TPU v7x, 32 devices: a whole 2x2x4 slice. The times are simulated.
32 devices in a mesh: fibre: 2 (over y), blk: 8 (over z, x), src: 2 (over core).
Axes of the slice: x: 2, y: 2, z: 4, core: 2. Of those that a mesh axis runs over, the one named last changes fastest.
Arguments:
- traces: float32 [96, 16, 512], P(('fibre', 'src'), 'blk'), parts along dimension 0, may hold values from -200 to 200
- valid_flags: int32 [96, 16], P(('fibre', 'src'), 'blk'), parts along dimension 0, may hold values 0 or 1
- source_index: int32 [256], replicated, may hold values from 0 to 47, as said below
Outputs:
- stacked: float32 [96, 129, 256], P(('fibre', 'src', 'blk')), parts along dimension 0
There are 2 independent parts, one for each index of `fibre`. A program takes and returns all parts, laid end to end along the dimension named above; an argument that names none is the same for every part. Nothing has to cross between parts.
Inputs may be any that keep to these rules, and one draw needn't show every extreme that they name: `source_index`: no channel appears twice where 256 <= 48; otherwise every channel appears, none more often than 256 / 48 rounded up.
All inputs are finite; a program needn't handle non-finite values. No bound on the sum of `valid_flags` on one device may be relied on, other than what follows from the above.
Results may differ from a plain program's by a relative error of at most 0.0026.
Values may be sent and summed in bfloat16 or wider, within the bound.
No kernel may reach another device: no remote copies, remote signals or barrier semaphores. Data moves between devices by JAX's collectives and lax.ppermute only.
A program may use at most 128 MiB of HBM per device.

v0:
```python
import math

import jax
import jax.numpy as jnp
from jax import lax
from jax.sharding import PartitionSpec as P

MAXLAG = 64


def broadcast(value, axis, source):
    kept = jnp.where(lax.axis_index(axis) == source, value, 0).astype(value.dtype)
    return lax.psum(kept, axis)


def toeplitz_rows(group, lag_count, segment):
    shifted = jnp.stack(
        [group[:, :, lag_step : lag_step + segment] for lag_step in range(lag_count)], axis=1
    )
    return shifted.reshape(group.shape[0] * lag_count, -1)


def body(traces, valid_flags, source_index):
    segment = traces.shape[2]
    centered = traces - jnp.mean(traces, axis=2, keepdims=True)
    mean_power = jnp.mean(centered * centered, axis=2, keepdims=True)
    flag_values = valid_flags[:, :, None].astype(jnp.float32)
    whitened = (centered * lax.rsqrt(mean_power + 1e-05) * flag_values).astype(jnp.bfloat16)
    pieces = []
    for owner in range(lax.axis_size("src")):
        pieces.append(broadcast(whitened, "src", owner))
    everyone = jnp.concatenate(pieces, axis=0)
    sources = jnp.take(everyone, source_index, axis=0)
    source_count = sources.shape[0]
    lag_count = 2 * MAXLAG + 1
    norm_factor = 1.0 / math.sqrt(traces.shape[1] * lax.axis_size("blk") * segment)
    own_rows = whitened.shape[0] // lax.axis_size("blk")
    flat_sources = sources.reshape(source_count, -1)
    padded = jnp.pad(whitened, ((0, 0), (0, 0), (MAXLAG, MAXLAG)))
    block_rows = math.gcd(lax.axis_size("blk") * own_rows, 16)
    grouped = padded.reshape(
        (lax.axis_size("blk") * own_rows // block_rows, block_rows) + padded.shape[1:]
    )

    def one_block(group):
        toeplitz = toeplitz_rows(group, lag_count, segment)
        products = lax.dot_general(
            toeplitz, flat_sources, (((1,), (1,)), ((), ())), preferred_element_type=jnp.float32
        )
        return (products * norm_factor).reshape(block_rows, lag_count, source_count)

    result = lax.map(one_block, grouped)
    return lax.psum_scatter(
        result.reshape(lax.axis_size("blk") * own_rows, lag_count, source_count),
        "blk",
        scatter_dimension=0,
        tiled=True,
    )


def solution(mesh):
    in_specs = (P(("fibre", "src"), "blk", None), P(("fibre", "src"), "blk"), P())
    out_specs = P(("fibre", "src", "blk"), None, None)
    return jax.shard_map(body, mesh=mesh, in_specs=in_specs, out_specs=out_specs, check_vma=False)
```

profile of v0, /device:TPU:0, one launch (start us, length us, event | category | flops | bytes accessed | tf_op | source)
XLA Modules:
  0.0 169.1 jit_solution(2660623632590289305)
XLA Ops:
  6.5 1.0 reduce_sum.18
  7.6 1.1 multiply_reduce_fusion
  8.7 0.7 convert_element_type.12
  9.4 1.7 broadcast_select_fusion.2
  11.1 0.7 broadcast_select_fusion.1
  11.8 0.7 compare_select_fusion
  12.5 0.7 compare_and_fusion
  13.2 0.1 pad.4
  13.4 19.2 %all-reduce.4.cloned.1.call-done = (bf16[24,2,512]{2,1,0:T(2,128)(2,1)}, bf16[24,2,512]{2,1,0:T(2,128)(2,1)}) async-done(((bf16[24,2,512]{2,1,0:T(2,128)(2,1)}, bf16[24,2,512]{2,1,0:T(2,128)(2,1)}), (bf16[24,2,512]{2,1,0:T(2,128)(2,1)}, bf16[24,2,512]{2,1,0:T(2,128)(2,1)})) %all-reduce.4.cloned.1.call-update) | async-done | bytes 98320 | tf_op jit(solution)/shard_map/psum | solution.py:13
  32.5 1.0 pad_maximum_fusion
  33.5 1.7 %gather_fusion = bf16[256,2,512]{2,1,0:T(2,128)(2,1)S(1)} fusion(bf16[48,2,512]{2,1,0:T(2,128)(2,1)S(1)} %pad_maximum_fusion, s32[1024]{0:T(1024)S(1)} %pad_clamp_fusion), kind=kCustom, calls=%fused_computation | custom fusion | bytes 1049600 | tf_op jit(solution)/shard_map/jit(_take)/gather | solution.py:33
  35.3 0.9 broadcast_select_fusion
  36.3 47.1 %while.10 = (s32[]{:T(128)}, f32[3,8,129,256]{3,2,1,0:T(8,128)}, bf16[3,8,2,640]{3,2,1,0:T(2,128)(2,1)S(1)}, bf16[256,1024]{1,0:T(8,128)(2,1)}, s32[]{:T(128)}) while((s32[]{:T(128)}, f32[3,8,129,256]{3,2,1,0:T(8,128)}, bf16[3,8,2,640]{3,2,1,0:T(2,128)(2,1)S(1)}, bf16[256,1024]{1,0:T(8,128)(2,1)}, s32[]{:T(128)}) %tuple.27), condition=%wide.region_5.6_spmd, body=%wide.region_4.5_spmd.sunk | while | flops 541329408 | bytes 18571868 | solution.py:52
  36.6 0.1 constant_dynamic-update-slice_fusion.264
  36.9 0.1 constant_dynamic-update-slice_fusion.267
  37.7 0.1 constant_dynamic-update-slice_fusion.275
  38.5 0.1 constant_dynamic-update-slice_fusion.283
  38.8 0.1 constant_dynamic-update-slice_fusion.286
  39.6 0.1 constant_dynamic-update-slice_fusion.294
  40.4 0.1 constant_dynamic-update-slice_fusion.302
  40.7 0.1 constant_dynamic-update-slice_fusion.305
  41.4 0.1 constant_dynamic-update-slice_fusion.313
  42.2 0.1 constant_dynamic-update-slice_fusion.321
  42.5 0.1 constant_dynamic-update-slice_fusion.324
  43.3 0.1 constant_dynamic-update-slice_fusion.332
  44.1 0.1 constant_dynamic-update-slice_fusion.340
  44.4 0.1 constant_dynamic-update-slice_fusion.343
  45.2 0.1 constant_dynamic-update-slice_fusion.351
  46.0 0.1 constant_dynamic-update-slice_fusion.359
  46.3 0.1 constant_dynamic-update-slice_fusion.362
  47.1 0.1 constant_dynamic-update-slice_fusion.370
  47.9 0.1 constant_dynamic-update-slice_fusion.378
  48.9 0.6 copy.137
  49.5 0.5 copy-done
  49.9 0.8 convolution_multiply_fusion.2
  50.7 0.1 broadcast_in_dim.37
  50.9 1.1 constant_dynamic-update-slice_fusion.389
  64.6 0.6 copy.137
  65.2 0.5 copy-done
  65.6 0.8 convolution_multiply_fusion.2
  66.4 0.1 broadcast_in_dim.37
  66.6 1.1 constant_dynamic-update-slice_fusion.389
  80.3 0.6 copy.137
  80.9 0.5 copy-done
  81.4 0.8 convolution_multiply_fusion.2
  82.2 0.1 broadcast_in_dim.37
  82.3 1.1 constant_dynamic-update-slice_fusion.389
  83.4 78.9 %reduce-scatter.2.cloned.1.call-done = f32[3,129,256]{2,1,0:T(8,128)} async-done(((f32[24,129,256]{2,1,0:T(8,128)}), f32[3,129,256]{2,1,0:T(8,128)}) %reduce-scatter.2.cloned.1.call-update) | async-done | bytes 396304 | tf_op jit(solution)/shard_map/reduce_scatter | solution.py:53
  (384 shorter events, 34.9 us)
Async XLA Ops:
  6.5 26.0 %all-reduce.4.cloned.1.call-start = ((), (), s32[]{:S(2)}) async-start(), calls=%async_computation.2 | async-start | bytes 196608 | tf_op jit(solution)/shard_map/psum | solution.py:13
  11.8 150.5 %reduce-scatter.2.cloned.1.call-start = ((), (), s32[]{:S(2)}) async-start(), calls=%async_computation.1 | async-start | bytes 3760128 | tf_op jit(solution)/shard_map/reduce_scatter | solution.py:53
  48.9 1.0 copy-start
  64.6 1.0 copy-start
  80.3 1.0 copy-start
Sparse Core Ops, SparseCore 0:
  11.9 20.5 all-reduce.3
  83.5 78.6 reduce-scatter.1
where the time goes:
time: 170 us; the launch traced here: 169 us
  waiting for transfers between devices  98.1 us (58%)
  local copies, waits for them, and re-layouts  45.2 us (27%)
  between operations  13.5 us (8%)
  other arithmetic  8.38 us (5%)
  matrix products  2.37 us (1%)
    reduce_scatter x1, waiting for transfers between devices, body(): lax.psum_scatter(result.reshape(lax.axis_size('blk') * own_rows, lag_coun...  78.9 us
    while x393, local copies, waits for them, and re-layouts  39.4 us
    psum x1, waiting for transfers between devices, broadcast(): return lax.psum(kept, axis)  19.2 us
  transfers between devices with their start and end apart: 2, of which 2 were waited for; matrix products, arithmetic and copies ran while one was open for 1% of the time, Pallas kernels for 0%

commit v1 on v0

--- a/solution.py
+++ b/solution.py
@@ -1,11 +1,17 @@
+import functools
 import math
 
 import jax
 import jax.numpy as jnp
 from jax import lax
+from jax.experimental import pallas as pl
+from jax.experimental.pallas import tpu as pltpu
 from jax.sharding import PartitionSpec as P
 
 MAXLAG = 64
+LAG_COUNT = 2 * MAXLAG + 1
+LANES = 256
+GROUP = 8
 
 
 def broadcast(value, axis, source):
@@ -20,7 +26,7 @@
     return shifted.reshape(group.shape[0] * lag_count, -1)
 
 
-def body(traces, valid_flags, source_index):
+def many_channels(traces, valid_flags, source_index):
     segment = traces.shape[2]
     centered = traces - jnp.mean(traces, axis=2, keepdims=True)
     mean_power = jnp.mean(centered * centered, axis=2, keepdims=True)
@@ -32,7 +38,6 @@
     everyone = jnp.concatenate(pieces, axis=0)
     sources = jnp.take(everyone, source_index, axis=0)
     source_count = sources.shape[0]
-    lag_count = 2 * MAXLAG + 1
     norm_factor = 1.0 / math.sqrt(traces.shape[1] * lax.axis_size("blk") * segment)
     own_rows = whitened.shape[0] // lax.axis_size("blk")
     flat_sources = sources.reshape(source_count, -1)
@@ -43,19 +48,196 @@
     )
 
     def one_block(group):
-        toeplitz = toeplitz_rows(group, lag_count, segment)
+        toeplitz = toeplitz_rows(group, LAG_COUNT, segment)
         products = lax.dot_general(
             toeplitz, flat_sources, (((1,), (1,)), ((), ())), preferred_element_type=jnp.float32
         )
-        return (products * norm_factor).reshape(block_rows, lag_count, source_count)
+        return (products * norm_factor).reshape(block_rows, LAG_COUNT, source_count)
 
     result = lax.map(one_block, grouped)
     return lax.psum_scatter(
-        result.reshape(lax.axis_size("blk") * own_rows, lag_count, source_count),
+        result.reshape(lax.axis_size("blk") * own_rows, LAG_COUNT, source_count),
         "blk",
         scatter_dimension=0,
         tiled=True,
     )
+
+
+class Plan:
+    def __init__(self, half, windows, segment, blk_size, src_size, source_count):
+        self.half = half
+        self.windows = windows
+        self.segment = segment
+        self.blk_size = blk_size
+        self.channels = half * src_size
+        self.source_count = source_count
+        self.coarse = LANES // self.channels if self.channels <= LANES else 0
+        if self.coarse == 0:
+            return
+        self.fine = -(-LAG_COUNT // self.coarse)
+        self.fine_padded = -(-self.fine // (2 * GROUP)) * 2 * GROUP
+        self.own = half // blk_size
+        reach = segment + (self.coarse - 1) * self.fine
+        self.span = -(-max(reach, segment + 2 * MAXLAG) // 128) * 128
+        self.whole_groups = self.fine // GROUP * GROUP
+        self.rest = self.fine - self.whole_groups
+        rows = self.own * self.fine
+        self.rows = -(-rows // 16) * 16
+        self.norm_factor = 1.0 / math.sqrt(windows * blk_size * segment)
+
+    def fits(self, src_size):
+        return (
+            self.coarse >= 2
+            and src_size == 2
+            and self.half % self.blk_size == 0
+            and self.half % GROUP == 0
+            and self.channels % 16 == 0
+            and self.blk_size & (self.blk_size - 1) == 0
+            and self.blk_size <= 16
+        )
+
+
+def whiten(plan, traces_ref, flags_ref, window):
+    values = traces_ref[:, window, :]
+    centered = values - jnp.mean(values, axis=1, keepdims=True)
+    mean_power = jnp.mean(centered * centered, axis=1, keepdims=True)
+    flag_values = flags_ref[:, window : window + 1].astype(jnp.float32)
+    whitened = centered * lax.rsqrt(mean_power + 1e-05) * flag_values
+    rounded = whitened.astype(jnp.bfloat16).astype(jnp.float32)
+    filler = jnp.zeros((plan.half, plan.span - plan.segment), jnp.float32)
+    return jnp.concatenate([rounded, filler], axis=1)
+
+
+def correlate_kernel(plan, traces_ref, flags_ref, peer_traces_ref, peer_flags_ref, *refs):
+    out_refs = refs[: plan.blk_size]
+    toeplitz_ref, columns_ref = refs[plan.blk_size :]
+    me = lax.axis_index("blk")
+    span = plan.span
+    filled = plan.coarse * plan.channels
+    if filled < LANES:
+        columns_ref[filled:, :] = jnp.zeros((LANES - filled, columns_ref.shape[1]), jnp.bfloat16)
+    for window in range(plan.windows):
+        at = slice(window * span, (window + 1) * span)
+        mine = whiten(plan, traces_ref, flags_ref, window)
+        other = whiten(plan, peer_traces_ref, peer_flags_ref, window)
+        both = jnp.concatenate([mine, other], axis=0)
+        for step in range(plan.coarse):
+            moved = pltpu.roll(both, step * plan.fine, 1) if step else both
+            columns_ref[step * plan.channels : (step + 1) * plan.channels, at] = moved.astype(jnp.bfloat16)
+        for block in range(plan.blk_size):
+            for member in range(plan.own):
+                channel = block * plan.own + member
+                row = jnp.broadcast_to(mine[channel : channel + 1, :], (GROUP, span))
+                pieces = [
+                    pltpu.roll(row, (MAXLAG - plan.fine + 1 + start) % span, 1, stride=1, stride_axis=0)
+                    for start in range(0, plan.fine_padded, GROUP)
+                ]
+                rows = slice(member * plan.fine_padded, (member + 1) * plan.fine_padded)
+                toeplitz_ref[block ^ me, rows, at] = jnp.concatenate(pieces, axis=0).astype(jnp.bfloat16)
+    height = plan.own * plan.fine_padded
+    products = lax.dot_general(
+        toeplitz_ref[...].reshape(plan.blk_size * height, -1),
+        columns_ref[...],
+        (((1,), (1,)), ((), ())),
+        preferred_element_type=jnp.float32,
+    ).reshape(plan.blk_size, plan.own, plan.fine_padded, LANES)
+    for hop in range(plan.blk_size):
+        part = products[hop]
+        pieces = [part[member, : plan.whole_groups] for member in range(plan.own)]
+        if plan.rest:
+            pieces += [part[member, plan.whole_groups : plan.fine] for member in range(plan.own)]
+        if plan.rows > plan.own * plan.fine:
+            pieces.append(jnp.zeros((plan.rows - plan.own * plan.fine, LANES), jnp.float32))
+        out_refs[hop][...] = jnp.concatenate(pieces, axis=0).astype(jnp.bfloat16)
+
+
+def expand_kernel(plan, index_ref, *refs):
+    part_refs = refs[: plan.blk_size]
+    out_ref = refs[plan.blk_size]
+    height = plan.own * plan.fine_padded
+    at_row = lax.broadcasted_iota(jnp.int32, (height, plan.rows), 0)
+    at_part = lax.broadcasted_iota(jnp.int32, (height, plan.rows), 1)
+    order = jnp.zeros((height, plan.rows), jnp.bool_)
+    for member in range(plan.own):
+        reverse = plan.fine - 1 - (at_row - member * plan.fine_padded)
+        whole = (reverse >= 0) & (reverse < plan.whole_groups) & (at_part == member * plan.whole_groups + reverse)
+        tail = plan.own * plan.whole_groups + member * plan.rest + reverse - plan.whole_groups
+        rest = (reverse >= plan.whole_groups) & (reverse < plan.fine) & (at_part == tail)
+        order = order | whole | rest
+    order = order.astype(jnp.float32).astype(jnp.bfloat16)
+    total = jnp.zeros((height, LANES), jnp.float32)
+    for part_ref in part_refs:
+        total += jnp.dot(order, part_ref[...], preferred_element_type=jnp.float32)
+    total = total * plan.norm_factor
+    first = lax.axis_index("src") * plan.half
+    index = index_ref[...] - first
+    index = jnp.where(index < 0, index + plan.channels, index)
+    at_column = lax.broadcasted_iota(jnp.int32, (LANES, plan.source_count), 0)
+    chosen = jnp.zeros((LANES, plan.source_count), jnp.bool_)
+    for step in range(plan.coarse):
+        chosen = chosen | (at_column == index + step * plan.channels)
+    chosen = chosen.astype(jnp.float32).astype(jnp.bfloat16)
+    lane = lax.broadcasted_iota(jnp.int32, (height, LANES), 1)
+    high = total.astype(jnp.bfloat16)
+    low = (total - high.astype(jnp.float32)).astype(jnp.bfloat16)
+    for step in range(plan.coarse):
+        inside = (lane >= step * plan.channels) & (lane < (step + 1) * plan.channels)
+        kept = jnp.concatenate(
+            [jnp.where(inside, total_part.astype(jnp.float32), 0.0).astype(jnp.bfloat16) for total_part in (high, low)],
+            axis=1,
+        )
+        expanded = jnp.dot(kept, jnp.concatenate([chosen, chosen], axis=0), preferred_element_type=jnp.float32)
+        count = min(plan.fine, LAG_COUNT - step * plan.fine)
+        for member in range(plan.own):
+            out_ref[member, step * plan.fine : step * plan.fine + count, :] = expanded[
+                member * plan.fine_padded : member * plan.fine_padded + count
+            ]
+
+
+def few_channels(plan, traces, valid_flags, source_index):
+    swap = [(0, 1), (1, 0)]
+    peer_traces = lax.ppermute(traces, "src", swap)
+    peer_flags = lax.ppermute(valid_flags, "src", swap)
+    vmem = pl.BlockSpec(memory_space=pltpu.VMEM)
+    width = plan.windows * plan.span
+    parts = pl.pallas_call(
+        functools.partial(correlate_kernel, plan),
+        out_shape=[jax.ShapeDtypeStruct((plan.rows, LANES), jnp.bfloat16)] * plan.blk_size,
+        in_specs=[vmem] * 4,
+        out_specs=[vmem] * plan.blk_size,
+        scratch_shapes=[
+            pltpu.VMEM((plan.blk_size, plan.own * plan.fine_padded, width), jnp.bfloat16),
+            pltpu.VMEM((LANES, width), jnp.bfloat16),
+        ],
+        compiler_params=pltpu.CompilerParams(vmem_limit_bytes=32 * 1024 * 1024),
+        name="correlate",
+    )(traces, valid_flags, peer_traces, peer_flags)
+    arrived = [parts[0]]
+    for hop in range(1, plan.blk_size):
+        pairs = [(place, place ^ hop) for place in range(plan.blk_size)]
+        arrived.append(lax.ppermute(parts[hop], "blk", pairs))
+    return pl.pallas_call(
+        functools.partial(expand_kernel, plan),
+        out_shape=jax.ShapeDtypeStruct((plan.own, LAG_COUNT, plan.source_count), jnp.float32),
+        in_specs=[vmem] * (1 + plan.blk_size),
+        out_specs=vmem,
+        compiler_params=pltpu.CompilerParams(vmem_limit_bytes=32 * 1024 * 1024),
+        name="expand",
+    )(source_index.reshape(1, -1), *arrived)
+
+
+def body(traces, valid_flags, source_index):
+    plan = Plan(
+        traces.shape[0],
+        traces.shape[1],
+        traces.shape[2],
+        lax.axis_size("blk"),
+        lax.axis_size("src"),
+        source_index.shape[0],
+    )
+    if plan.fits(lax.axis_size("src")):
+        return few_channels(plan, traces, valid_flags, source_index)
+    return many_channels(traces, valid_flags, source_index)
 
 
 def solution(mesh):

time: 170 us -> 26.1 us (0.15)
  waiting for transfers between devices: 98.1 us -> 7.78 us
  local copies, waits for them, and re-layouts: 45.2 us -> 2.33 us
  between operations: 13.5 us -> 0.02 us
  starting transfers between devices: 0.04 us -> 12.7 us
  other arithmetic: 8.38 us -> 0 us
  Pallas kernels: 0 us -> 3.05 us
  matrix products: 2.37 us -> 0 us
    reduce_scatter x1 -> x0, waiting for transfers between devices: 78.9 us -> none  [body(): lax.psum_scatter(result.reshape(lax.axis_size('blk') * own_rows, lag_coun...]
    while x393 -> x0, local copies, waits for them, and re-layouts: 39.4 us -> none
    psum x1 -> x0, waiting for transfers between devices: 19.2 us -> none  [broadcast(): return lax.psum(kept, axis)]
    ppermute x0 -> x9, starting transfers between devices: none -> 12.7 us  [the longest x7 12.2 us: few_channels(): arrived.append(lax.ppermute(parts[hop], 'blk', pairs))]
    ppermute x0 -> x9, waiting for transfers between devices: none -> 7.78 us  [the longest x7 6.66 us: few_channels(): arrived.append(lax.ppermute(parts[hop], 'blk', pairs))]
    select_n x4 -> x0, other arithmetic: 3.96 us -> none  [the longest x2 2.33 us: broadcast(): jnp.where(lax.axis_index(axis) == source, value, 0).astype(value.dtype)]
    dynamic_update_slice x3 -> x0, local copies, waits for them, and re-layouts: 3.28 us -> none  [body(): result = lax.map(one_block, grouped)]
    pallas_call x0 -> x2, Pallas kernels: none -> 3.05 us  [the longest x1 1.6 us: few_channels(): pl.pallas_call(functools.partial(correlate_kernel, plan), out_shape=[jax....]
  transfers between devices with their start and end apart: 2 -> 9, of which waited for: 2 -> 3; matrix products, arithmetic and copies ran while one was open for 1% -> 3% of each run, Pallas kernels for 0% -> 0%
where the time goes in v1:
time: 26.1 us; the launch traced here: 25.9 us
  starting transfers between devices  12.7 us (49%)
  waiting for transfers between devices  7.78 us (30%)
  Pallas kernels  3.05 us (12%)
  local copies, waits for them, and re-layouts  2.33 us (9%)
    ppermute x7, starting transfers between devices, few_channels(): arrived.append(lax.ppermute(parts[hop], 'blk', pairs))  12.2 us
    ppermute x7, waiting for transfers between devices, few_channels(): arrived.append(lax.ppermute(parts[hop], 'blk', pairs))  6.66 us
    unnamed x5, local copies, waits for them, and re-layouts  2.33 us
    pallas_call x1, Pallas kernels, few_channels(): pl.pallas_call(functools.partial(correlate_kernel, plan), out_shape=[jax....  1.6 us
    pallas_call x1, Pallas kernels, few_channels(): pl.pallas_call(functools.partial(expand_kernel, plan), out_shape=jax.Shap...  1.45 us
    ppermute x1, waiting for transfers between devices, few_channels(): peer_flags = lax.ppermute(valid_flags, 'src', swap)  1.12 us
  transfers between devices with their start and end apart: 9, of which 3 were waited for; matrix products, arithmetic and copies ran while one was open for 3% of the time, Pallas kernels for 0%

profile of v1, /device:TPU:0, one launch (start us, length us, event | category | flops | bytes accessed | tf_op | source)
XLA Modules:
  0.0 25.9 jit_solution(10316177785588910354)
XLA Ops:
  0.0 0.5 %collective-permute-start = (f32[24,2,512]{2,1,0:T(2,128)}, f32[24,2,512]{2,1,0:T(2,128)S(1)}, u32[]{:S(2)}, u32[]{:S(2)}) collective-permute-start(f32[24,2,512]{2,1,0:T(2,128)} %traces_ref.1), channel_id=1, source_target_pairs={{0,1},{1,0},{2,3},{3,2},{4,5},{5,4},{6,7},{7,6},{8,9},{9,8},{10,11... | collective-permute-start | bytes 294920 | tf_op jit(solution)/shard_map/ppermute | solution.py:199
  0.5 0.8 %copy.5.flags_ref = s32[24,2]{1,0:T(8,128)S(1)} copy(s32[24,2]{0,1:T(2,128)} %param.4) | data formatting | bytes 384 | tf_op args[1]
  1.2 0.1 collective-permute-start.1
  1.3 1.1 %collective-permute-done.1.peer_flags_ref = s32[24,2]{1,0:T(8,128)S(1)} collective-permute-done((s32[24,2]{1,0:T(8,128)S(1)}, s32[24,2]{1,0:T(8,128)S(1)}, u32[]{:S(2)}, u32[]{:S(2)}) %collective-permute-start.1) | collective-permute-done | bytes 224 | tf_op jit(solution)/shard_map/ppermute | solution.py:200
  2.4 0.0 collective-permute-done.peer_traces_ref
  2.4 0.0 copy-start
  2.4 0.9 %copy-done = f32[24,2,512]{2,1,0:T(2,128)S(1)} copy-done((f32[24,2,512]{2,1,0:T(2,128)S(1)}, f32[24,2,512]{2,1,0:T(2,128)}, u32[]{:S(2)}) %copy-start) | copy-done | bytes 98328
  3.3 1.6 %correlate.1 = (bf16[80,256]{1,0:T(8,128)(2,1)S(1)}, bf16[80,256]{1,0:T(8,128)(2,1)S(1)}, bf16[80,256]{1,0:T(8,128)(2,1)S(1)}, bf16[80,256]{1,0:T(8,128)(2,1)S(1...) custom-call(f32[24,2,512]{2,1,0:T(2,128)S(1)} %copy-done, ...), custom_call_target="tpu_custom_call" | custom-call | tf_op jit(solution)/shard_map/correlate/pallas_call | solution.py:203
  4.9 2.7 %collective-permute-start.2 = (bf16[80,256]{1,0:T(8,128)(2,1)S(1)}, bf16[80,256]{1,0:T(8,128)(2,1)S(1)}, u32[]{:S(2)}, u32[]{:S(2)}) collective-permute-start(bf16[80,256]{1,0:T(8,128)(2,1)S(1)} %get-tuple-element.14), channel_id=1, source_target_pairs={{0,2},{2,0},{4,6},{6,4},{8,10},{10,8},{12,14},{14,12},{1,3},{3,1},... | collective-permute-start | bytes 122888 | tf_op jit(solution)/shard_map/ppermute | solution.py:218
  7.6 1.6 %collective-permute-start.3 = (bf16[80,256]{1,0:T(8,128)(2,1)S(1)}, bf16[80,256]{1,0:T(8,128)(2,1)S(1)}, u32[]{:S(2)}, u32[]{:S(2)}) collective-permute-start(bf16[80,256]{1,0:T(8,128)(2,1)S(1)} %get-tuple-element.15), channel_id=1, source_target_pairs={{0,4},{2,6},{4,0},{6,2},{8,12},{10,14},{12,8},{14,10},{1,5},{3,7},... | collective-permute-start | bytes 122888 | tf_op jit(solution)/shard_map/ppermute | solution.py:218
  9.2 0.0 collective-permute-start.4
  9.2 3.0 %collective-permute-start.5 = (bf16[80,256]{1,0:T(8,128)(2,1)S(1)}, bf16[80,256]{1,0:T(8,128)(2,1)S(1)}, u32[]{:S(2)}, u32[]{:S(2)}) collective-permute-start(bf16[80,256]{1,0:T(8,128)(2,1)S(1)} %get-tuple-element.17), channel_id=1, source_target_pairs={{0,8},{2,10},{4,12},{6,14},{8,0},{10,2},{12,4},{14,6},{1,9},{3,11}... | collective-permute-start | bytes 122888 | tf_op jit(solution)/shard_map/ppermute | solution.py:218
  12.2 1.3 %collective-permute-start.6 = (bf16[80,256]{1,0:T(8,128)(2,1)S(1)}, bf16[80,256]{1,0:T(8,128)(2,1)S(1)}, u32[]{:S(2)}, u32[]{:S(2)}) collective-permute-start(bf16[80,256]{1,0:T(8,128)(2,1)S(1)} %get-tuple-element.18), channel_id=1, source_target_pairs={{0,10},{2,8},{4,14},{6,12},{8,2},{10,0},{12,6},{14,4},{1,11},{3,9}... | collective-permute-start | bytes 122888 | tf_op jit(solution)/shard_map/ppermute | solution.py:218
  13.5 0.0 collective-permute-done.2.refs_1_
  13.5 3.6 %collective-permute-start.7 = (bf16[80,256]{1,0:T(8,128)(2,1)S(1)}, bf16[80,256]{1,0:T(8,128)(2,1)S(1)}, u32[]{:S(2)}, u32[]{:S(2)}) collective-permute-start(bf16[80,256]{1,0:T(8,128)(2,1)S(1)} %get-tuple-element.19), channel_id=1, source_target_pairs={{0,12},{2,14},{4,8},{6,10},{8,4},{10,6},{12,0},{14,2},{1,13},{3,15... | collective-permute-start | bytes 122888 | tf_op jit(solution)/shard_map/ppermute | solution.py:218
  17.1 0.0 collective-permute-done.3.refs_2_
  17.1 0.0 collective-permute-start.8
  17.1 0.0 collective-permute-done.4.refs_3_
  17.1 0.0 collective-permute-done.5.refs_4_
  17.1 2.4 %collective-permute-done.6.refs_5_ = bf16[80,256]{1,0:T(8,128)(2,1)S(1)} collective-permute-done((bf16[80,256]{1,0:T(8,128)(2,1)S(1)}, bf16[80,256]{1,0:T(8,128)(2,1)S(1)}, u32[]{:S(2)}, u32[]{:S(2)}) %collective-permute-start.6) | collective-permute-done | bytes 40992 | tf_op jit(solution)/shard_map/ppermute | solution.py:218
  19.6 0.0 collective-permute-done.7.refs_6_
  19.6 4.2 %collective-permute-done.8.refs_7_ = bf16[80,256]{1,0:T(8,128)(2,1)S(1)} collective-permute-done((bf16[80,256]{1,0:T(8,128)(2,1)S(1)}, bf16[80,256]{1,0:T(8,128)(2,1)S(1)}, u32[]{:S(2)}, u32[]{:S(2)}) %collective-permute-start.8) | collective-permute-done | bytes 40992 | tf_op jit(solution)/shard_map/ppermute | solution.py:218
  23.8 0.0 copy-start.1
  23.8 0.7 %copy-done.1 = s32[256]{0:T(256)S(1)} copy-done((s32[256]{0:T(256)S(1)}, s32[256]{0:T(256)}, u32[]{:S(2)}) %copy-start.1) | copy-done | bytes 1048
  24.5 1.5 %expand.1 = f32[3,129,256]{2,1,0:T(8,128)} custom-call(s32[1,256]{1,0:T(1,128)S(1)} %bitcast.1, bf16[80,256]{1,0:T(8,128)(2,1)S(1)} %get-tuple-element.13.refs_0_, bf16[80,256]{1,0:T(8,128)(2,1)S(1)} %collective-permute-done.2.refs_1_, bf16[80,256]{1,0:T(8,128)(2,1)S(1)} %collective-permute-done.3.refs_2_, ...), custom_call_target="tpu_custom_call" | custom-call | tf_op jit(solution)/shard_map/expand/pallas_call | solution.py:219
Async XLA Ops:
  0.0 2.4 %collective-permute-start = (f32[24,2,512]{2,1,0:T(2,128)}, f32[24,2,512]{2,1,0:T(2,128)S(1)}, u32[]{:S(2)}, u32[]{:S(2)}) collective-permute-start(f32[24,2,512]{2,1,0:T(2,128)} %traces_ref.1), channel_id=1, source_target_pairs={{0,1},{1,0},{2,3},{3,2},{4,5},{5,4},{6,7},{7,6},{8,9},{9,8},{10,11... | collective-permute-start | bytes 294920 | tf_op jit(solution)/shard_map/ppermute | solution.py:199
  1.2 1.2 %collective-permute-start.1 = (s32[24,2]{1,0:T(8,128)S(1)}, s32[24,2]{1,0:T(8,128)S(1)}, u32[]{:S(2)}, u32[]{:S(2)}) collective-permute-start(s32[24,2]{1,0:T(8,128)S(1)} %copy.5.flags_ref), channel_id=1, source_target_pairs={{0,1},{1,0},{2,3},{3,2},{4,5},{5,4},{6,7},{7,6},{8,9},{9,8},{10,11... | collective-permute-start | bytes 584 | tf_op jit(solution)/shard_map/ppermute | solution.py:200
  2.4 0.9 %copy-start = (f32[24,2,512]{2,1,0:T(2,128)S(1)}, f32[24,2,512]{2,1,0:T(2,128)}, u32[]{:S(2)}) copy-start(f32[24,2,512]{2,1,0:T(2,128)} %traces_ref.1) | copy-start | bytes 294916
  4.9 8.6 %collective-permute-start.2 = (bf16[80,256]{1,0:T(8,128)(2,1)S(1)}, bf16[80,256]{1,0:T(8,128)(2,1)S(1)}, u32[]{:S(2)}, u32[]{:S(2)}) collective-permute-start(bf16[80,256]{1,0:T(8,128)(2,1)S(1)} %get-tuple-element.14), channel_id=1, source_target_pairs={{0,2},{2,0},{4,6},{6,4},{8,10},{10,8},{12,14},{14,12},{1,3},{3,1},... | collective-permute-start | bytes 122888 | tf_op jit(solution)/shard_map/ppermute | solution.py:218
  7.6 9.5 %collective-permute-start.3 = (bf16[80,256]{1,0:T(8,128)(2,1)S(1)}, bf16[80,256]{1,0:T(8,128)(2,1)S(1)}, u32[]{:S(2)}, u32[]{:S(2)}) collective-permute-start(bf16[80,256]{1,0:T(8,128)(2,1)S(1)} %get-tuple-element.15), channel_id=1, source_target_pairs={{0,4},{2,6},{4,0},{6,2},{8,12},{10,14},{12,8},{14,10},{1,5},{3,7},... | collective-permute-start | bytes 122888 | tf_op jit(solution)/shard_map/ppermute | solution.py:218
  9.2 7.9 %collective-permute-start.4 = (bf16[80,256]{1,0:T(8,128)(2,1)S(1)}, bf16[80,256]{1,0:T(8,128)(2,1)S(1)}, u32[]{:S(2)}, u32[]{:S(2)}) collective-permute-start(bf16[80,256]{1,0:T(8,128)(2,1)S(1)} %get-tuple-element.16), channel_id=1, source_target_pairs={{0,6},{2,4},{4,2},{6,0},{8,14},{10,12},{12,10},{14,8},{1,7},{3,5},... | collective-permute-start | bytes 122888 | tf_op jit(solution)/shard_map/ppermute | solution.py:218
  9.2 7.9 %collective-permute-start.5 = (bf16[80,256]{1,0:T(8,128)(2,1)S(1)}, bf16[80,256]{1,0:T(8,128)(2,1)S(1)}, u32[]{:S(2)}, u32[]{:S(2)}) collective-permute-start(bf16[80,256]{1,0:T(8,128)(2,1)S(1)} %get-tuple-element.17), channel_id=1, source_target_pairs={{0,8},{2,10},{4,12},{6,14},{8,0},{10,2},{12,4},{14,6},{1,9},{3,11}... | collective-permute-start | bytes 122888 | tf_op jit(solution)/shard_map/ppermute | solution.py:218
  12.2 7.4 %collective-permute-start.6 = (bf16[80,256]{1,0:T(8,128)(2,1)S(1)}, bf16[80,256]{1,0:T(8,128)(2,1)S(1)}, u32[]{:S(2)}, u32[]{:S(2)}) collective-permute-start(bf16[80,256]{1,0:T(8,128)(2,1)S(1)} %get-tuple-element.18), channel_id=1, source_target_pairs={{0,10},{2,8},{4,14},{6,12},{8,2},{10,0},{12,6},{14,4},{1,11},{3,9}... | collective-permute-start | bytes 122888 | tf_op jit(solution)/shard_map/ppermute | solution.py:218
  13.5 6.1 %collective-permute-start.7 = (bf16[80,256]{1,0:T(8,128)(2,1)S(1)}, bf16[80,256]{1,0:T(8,128)(2,1)S(1)}, u32[]{:S(2)}, u32[]{:S(2)}) collective-permute-start(bf16[80,256]{1,0:T(8,128)(2,1)S(1)} %get-tuple-element.19), channel_id=1, source_target_pairs={{0,12},{2,14},{4,8},{6,10},{8,4},{10,6},{12,0},{14,2},{1,13},{3,15... | collective-permute-start | bytes 122888 | tf_op jit(solution)/shard_map/ppermute | solution.py:218
  17.1 6.7 %collective-permute-start.8 = (bf16[80,256]{1,0:T(8,128)(2,1)S(1)}, bf16[80,256]{1,0:T(8,128)(2,1)S(1)}, u32[]{:S(2)}, u32[]{:S(2)}) collective-permute-start(bf16[80,256]{1,0:T(8,128)(2,1)S(1)} %get-tuple-element.20), channel_id=1, source_target_pairs={{0,14},{2,12},{4,10},{6,8},{8,6},{10,4},{12,2},{14,0},{1,15},{3,13... | collective-permute-start | bytes 122888 | tf_op jit(solution)/shard_map/ppermute | solution.py:218
  23.8 0.7 %copy-start.1 = (s32[256]{0:T(256)S(1)}, s32[256]{0:T(256)}, u32[]{:S(2)}) copy-start(s32[256]{0:T(256)} %param.5) | copy-start | bytes 3076

commit v2 on v1

--- a/solution.py
+++ b/solution.py
@@ -101,17 +101,14 @@
     values = traces_ref[:, window, :]
     centered = values - jnp.mean(values, axis=1, keepdims=True)
     mean_power = jnp.mean(centered * centered, axis=1, keepdims=True)
-    flag_values = flags_ref[:, window : window + 1].astype(jnp.float32)
+    flag_values = flags_ref[window : window + 1, :].astype(jnp.float32).reshape(plan.half, 1)
     whitened = centered * lax.rsqrt(mean_power + 1e-05) * flag_values
     rounded = whitened.astype(jnp.bfloat16).astype(jnp.float32)
     filler = jnp.zeros((plan.half, plan.span - plan.segment), jnp.float32)
     return jnp.concatenate([rounded, filler], axis=1)
 
 
-def correlate_kernel(plan, traces_ref, flags_ref, peer_traces_ref, peer_flags_ref, *refs):
-    out_refs = refs[: plan.blk_size]
-    toeplitz_ref, columns_ref = refs[plan.blk_size :]
-    me = lax.axis_index("blk")
+def correlate_kernel(plan, traces_ref, flags_ref, peer_traces_ref, peer_flags_ref, out_ref, toeplitz_ref, columns_ref):
     span = plan.span
     filled = plan.coarse * plan.channels
     if filled < LANES:
@@ -133,7 +130,7 @@
                     for start in range(0, plan.fine_padded, GROUP)
                 ]
                 rows = slice(member * plan.fine_padded, (member + 1) * plan.fine_padded)
-                toeplitz_ref[block ^ me, rows, at] = jnp.concatenate(pieces, axis=0).astype(jnp.bfloat16)
+                toeplitz_ref[block, rows, at] = jnp.concatenate(pieces, axis=0).astype(jnp.bfloat16)
     height = plan.own * plan.fine_padded
     products = lax.dot_general(
         toeplitz_ref[...].reshape(plan.blk_size * height, -1),
@@ -141,19 +138,17 @@
         (((1,), (1,)), ((), ())),
         preferred_element_type=jnp.float32,
     ).reshape(plan.blk_size, plan.own, plan.fine_padded, LANES)
-    for hop in range(plan.blk_size):
-        part = products[hop]
+    for block in range(plan.blk_size):
+        part = products[block]
         pieces = [part[member, : plan.whole_groups] for member in range(plan.own)]
         if plan.rest:
             pieces += [part[member, plan.whole_groups : plan.fine] for member in range(plan.own)]
         if plan.rows > plan.own * plan.fine:
             pieces.append(jnp.zeros((plan.rows - plan.own * plan.fine, LANES), jnp.float32))
-        out_refs[hop][...] = jnp.concatenate(pieces, axis=0).astype(jnp.bfloat16)
-
-
-def expand_kernel(plan, index_ref, *refs):
-    part_refs = refs[: plan.blk_size]
-    out_ref = refs[plan.blk_size]
+        out_ref[block] = jnp.concatenate(pieces, axis=0).astype(jnp.bfloat16)
+
+
+def expand_kernel(plan, index_ref, parts_ref, out_ref):
     height = plan.own * plan.fine_padded
     at_row = lax.broadcasted_iota(jnp.int32, (height, plan.rows), 0)
     at_part = lax.broadcasted_iota(jnp.int32, (height, plan.rows), 1)
@@ -166,8 +161,8 @@
         order = order | whole | rest
     order = order.astype(jnp.float32).astype(jnp.bfloat16)
     total = jnp.zeros((height, LANES), jnp.float32)
-    for part_ref in part_refs:
-        total += jnp.dot(order, part_ref[...], preferred_element_type=jnp.float32)
+    for block in range(plan.blk_size):
+        total += jnp.dot(order, parts_ref[block], preferred_element_type=jnp.float32)
     total = total * plan.norm_factor
     first = lax.axis_index("src") * plan.half
     index = index_ref[...] - first
@@ -197,33 +192,31 @@
 def few_channels(plan, traces, valid_flags, source_index):
     swap = [(0, 1), (1, 0)]
     peer_traces = lax.ppermute(traces, "src", swap)
-    peer_flags = lax.ppermute(valid_flags, "src", swap)
+    flags = valid_flags.T
+    peer_flags = lax.ppermute(flags, "src", swap)
     vmem = pl.BlockSpec(memory_space=pltpu.VMEM)
     width = plan.windows * plan.span
     parts = pl.pallas_call(
         functools.partial(correlate_kernel, plan),
-        out_shape=[jax.ShapeDtypeStruct((plan.rows, LANES), jnp.bfloat16)] * plan.blk_size,
+        out_shape=jax.ShapeDtypeStruct((plan.blk_size, plan.rows, LANES), jnp.bfloat16),
         in_specs=[vmem] * 4,
-        out_specs=[vmem] * plan.blk_size,
+        out_specs=vmem,
         scratch_shapes=[
             pltpu.VMEM((plan.blk_size, plan.own * plan.fine_padded, width), jnp.bfloat16),
             pltpu.VMEM((LANES, width), jnp.bfloat16),
         ],
         compiler_params=pltpu.CompilerParams(vmem_limit_bytes=32 * 1024 * 1024),
         name="correlate",
-    )(traces, valid_flags, peer_traces, peer_flags)
-    arrived = [parts[0]]
-    for hop in range(1, plan.blk_size):
-        pairs = [(place, place ^ hop) for place in range(plan.blk_size)]
-        arrived.append(lax.ppermute(parts[hop], "blk", pairs))
+    )(traces, flags, peer_traces, peer_flags)
+    arrived = lax.all_to_all(parts, "blk", 0, 0, tiled=True)
     return pl.pallas_call(
         functools.partial(expand_kernel, plan),
         out_shape=jax.ShapeDtypeStruct((plan.own, LAG_COUNT, plan.source_count), jnp.float32),
-        in_specs=[vmem] * (1 + plan.blk_size),
+        in_specs=[vmem] * 2,
         out_specs=vmem,
         compiler_params=pltpu.CompilerParams(vmem_limit_bytes=32 * 1024 * 1024),
         name="expand",
-    )(source_index.reshape(1, -1), *arrived)
+    )(source_index.reshape(1, -1), arrived)
 
 
 def body(traces, valid_flags, source_index):

time: 26.1 us -> 24.7 us (0.946)
  blocking collectives: 0 us -> 18.2 us
  starting transfers between devices: 12.7 us -> 0.91 us
  waiting for transfers between devices: 7.78 us -> 0.82 us
  local copies, waits for them, and re-layouts: 2.33 us -> 1.8 us
  Pallas kernels: 3.05 us -> 2.77 us
    all_to_all x0 -> x1, blocking collectives: none -> 18.2 us  [few_channels(): arrived = lax.all_to_all(parts, 'blk', 0, 0, tiled=True)]
    ppermute x8 -> x1, starting transfers between devices: 12.3 us -> 0.45 us  [few_channels(): peer_flags = lax.ppermute(flags, 'src', swap)]
    ppermute x8 -> x1, waiting for transfers between devices: 7.78 us -> 0.82 us  [few_channels(): peer_flags = lax.ppermute(flags, 'src', swap)]
    unnamed x5 -> x6, local copies, waits for them, and re-layouts: 2.33 us -> 1.8 us
    pallas_call x1, Pallas kernels: 1.6 us -> 1.32 us  [few_channels(): pl.pallas_call(functools.partial(correlate_kernel, plan), out_shape=jax.S...]
  transfers between devices with their start and end apart: 9 -> 2, of which waited for: 3 -> 1; matrix products, arithmetic and copies ran while one was open for 3% -> 0% of each run, Pallas kernels for 0% -> 0%
where the time goes in v2:
time: 24.7 us; the launch traced here: 24.5 us
  blocking collectives  18.2 us (74%)
  Pallas kernels  2.77 us (11%)
  local copies, waits for them, and re-layouts  1.8 us (7%)
  starting transfers between devices  0.91 us (4%)
  waiting for transfers between devices  0.82 us (3%)
    all_to_all x1, blocking collectives, few_channels(): arrived = lax.all_to_all(parts, 'blk', 0, 0, tiled=True)  18.2 us
    unnamed x6, local copies, waits for them, and re-layouts  1.8 us
    pallas_call x1, Pallas kernels, few_channels(): pl.pallas_call(functools.partial(expand_kernel, plan), out_shape=jax.Shap...  1.45 us
    pallas_call x1, Pallas kernels, few_channels(): pl.pallas_call(functools.partial(correlate_kernel, plan), out_shape=jax.S...  1.32 us
    ppermute x1, waiting for transfers between devices, few_channels(): peer_flags = lax.ppermute(flags, 'src', swap)  0.82 us
  transfers between devices with their start and end apart: 2, of which 1 were waited for; matrix products, arithmetic and copies ran while one was open for 0% of the time, Pallas kernels for 0%

profile of v2, /device:TPU:0, one launch (start us, length us, event | category | flops | bytes accessed | tf_op | source)
XLA Modules:
  0.0 24.5 jit_solution(18190258929229380799)
XLA Ops:
  0.0 0.0 copy-start.1
  0.0 0.5 %collective-permute-start = (f32[24,2,512]{2,1,0:T(2,128)}, f32[24,2,512]{2,1,0:T(2,128)S(1)}, u32[]{:S(2)}, u32[]{:S(2)}) collective-permute-start(f32[24,2,512]{2,1,0:T(2,128)} %traces_ref.1), channel_id=1, source_target_pairs={{0,1},{1,0},{2,3},{3,2},{4,5},{5,4},{6,7},{7,6},{8,9},{9,8},{10,11... | collective-permute-start | bytes 294920 | tf_op jit(solution)/shard_map/ppermute | solution.py:194
  0.5 0.2 copy-done.1
  0.7 0.5 %collective-permute-start.1 = (s32[2,24]{1,0:T(2,128)S(1)}, s32[2,24]{1,0:T(2,128)S(1)}, u32[]{:S(2)}, u32[]{:S(2)}) collective-permute-start(s32[2,24]{1,0:T(2,128)S(1)} %bitcast.2), channel_id=1, source_target_pairs={{0,1},{1,0},{2,3},{3,2},{4,5},{5,4},{6,7},{7,6},{8,9},{9,8},{10,11... | collective-permute-start | bytes 584 | tf_op jit(solution)/shard_map/ppermute | solution.py:196
  1.1 0.8 %collective-permute-done.1.peer_flags_ref = s32[2,24]{1,0:T(2,128)S(1)} collective-permute-done((s32[2,24]{1,0:T(2,128)S(1)}, s32[2,24]{1,0:T(2,128)S(1)}, u32[]{:S(2)}, u32[]{:S(2)}) %collective-permute-start.1) | collective-permute-done | bytes 224 | tf_op jit(solution)/shard_map/ppermute | solution.py:196
  2.0 0.0 collective-permute-done.peer_traces_ref
  2.0 0.0 copy-start
  2.0 0.9 %copy-done = f32[24,2,512]{2,1,0:T(2,128)S(1)} copy-done((f32[24,2,512]{2,1,0:T(2,128)S(1)}, f32[24,2,512]{2,1,0:T(2,128)}, u32[]{:S(2)}) %copy-start) | copy-done | bytes 98328
  2.9 1.3 %correlate.1 = bf16[8,80,256]{2,1,0:T(8,128)(2,1)S(1)} custom-call(f32[24,2,512]{2,1,0:T(2,128)S(1)} %copy-done, s32[2,24]{1,0:T(2,128)S(1)} %bitcast.3, f32[24,2,512]{2,1,0:T(2,128)S(1)} %collective-permute-done.peer_traces_ref, s32[2,24]{1,0:T(2,128)S(1)} %collective-permute-done.1.peer_flags_ref), custom_call_target="tpu_custom_call" | custom-call | tf_op jit(solution)/shard_map/correlate/pallas_call | solution.py:199
  4.2 18.2 %all_to_all.5.parts_ref = bf16[8,80,256]{2,1,0:T(8,128)(2,1)S(1)} all-to-all(bf16[8,80,256]{2,1,0:T(8,128)(2,1)S(1)} %correlate.1), channel_id=1, replica_groups=mesh['fibre'=2,'blk'=8,'src'=2] {'blk'}, dimensions={0} | all-to-all | bytes 655360 | tf_op jit(solution)/shard_map/all_to_all | solution.py:211
  22.4 0.0 copy-start.2
  22.4 0.7 %copy-done.2 = s32[256]{0:T(256)S(1)} copy-done((s32[256]{0:T(256)S(1)}, s32[256]{0:T(256)}, u32[]{:S(2)}) %copy-start.2) | copy-done | bytes 1048
  23.0 1.5 %expand.1 = f32[3,129,256]{2,1,0:T(8,128)} custom-call(s32[1,256]{1,0:T(1,128)S(1)} %bitcast.4, bf16[8,80,256]{2,1,0:T(8,128)(2,1)S(1)} %all_to_all.5.parts_ref), custom_call_target="tpu_custom_call" | custom-call | tf_op jit(solution)/shard_map/expand/pallas_call | solution.py:212
Async XLA Ops:
  0.0 0.7 %copy-start.1 = (s32[24,2]{0,1:T(2,128)S(1)}, s32[24,2]{0,1:T(2,128)}, u32[]{:S(2)}) copy-start(s32[24,2]{0,1:T(2,128)} %param.4) | copy-start | bytes 580
  0.0 2.0 %collective-permute-start = (f32[24,2,512]{2,1,0:T(2,128)}, f32[24,2,512]{2,1,0:T(2,128)S(1)}, u32[]{:S(2)}, u32[]{:S(2)}) collective-permute-start(f32[24,2,512]{2,1,0:T(2,128)} %traces_ref.1), channel_id=1, source_target_pairs={{0,1},{1,0},{2,3},{3,2},{4,5},{5,4},{6,7},{7,6},{8,9},{9,8},{10,11... | collective-permute-start | bytes 294920 | tf_op jit(solution)/shard_map/ppermute | solution.py:194
  0.7 1.3 %collective-permute-start.1 = (s32[2,24]{1,0:T(2,128)S(1)}, s32[2,24]{1,0:T(2,128)S(1)}, u32[]{:S(2)}, u32[]{:S(2)}) collective-permute-start(s32[2,24]{1,0:T(2,128)S(1)} %bitcast.2), channel_id=1, source_target_pairs={{0,1},{1,0},{2,3},{3,2},{4,5},{5,4},{6,7},{7,6},{8,9},{9,8},{10,11... | collective-permute-start | bytes 584 | tf_op jit(solution)/shard_map/ppermute | solution.py:196
  2.0 0.9 %copy-start = (f32[24,2,512]{2,1,0:T(2,128)S(1)}, f32[24,2,512]{2,1,0:T(2,128)}, u32[]{:S(2)}) copy-start(f32[24,2,512]{2,1,0:T(2,128)} %traces_ref.1) | copy-start | bytes 294916
  22.4 0.7 %copy-start.2 = (s32[256]{0:T(256)S(1)}, s32[256]{0:T(256)}, u32[]{:S(2)}) copy-start(s32[256]{0:T(256)} %param.5) | copy-start | bytes 3076

commit v3 on v2

v3 whole, which is shorter than its diff:
```python
import functools
import math

import jax
import jax.numpy as jnp
from jax import lax
from jax.experimental import pallas as pl
from jax.experimental.pallas import tpu as pltpu
from jax.sharding import PartitionSpec as P

MAXLAG = 64
LAG_COUNT = 2 * MAXLAG + 1
LANES = 256
GROUP = 8


def broadcast(value, axis, source):
    kept = jnp.where(lax.axis_index(axis) == source, value, 0).astype(value.dtype)
    return lax.psum(kept, axis)


def toeplitz_rows(group, lag_count, segment):
    shifted = jnp.stack(
        [group[:, :, lag_step : lag_step + segment] for lag_step in range(lag_count)], axis=1
    )
    return shifted.reshape(group.shape[0] * lag_count, -1)


def many_channels(traces, valid_flags, source_index):
    segment = traces.shape[2]
    centered = traces - jnp.mean(traces, axis=2, keepdims=True)
    mean_power = jnp.mean(centered * centered, axis=2, keepdims=True)
    flag_values = valid_flags[:, :, None].astype(jnp.float32)
    whitened = (centered * lax.rsqrt(mean_power + 1e-05) * flag_values).astype(jnp.bfloat16)
    pieces = []
    for owner in range(lax.axis_size("src")):
        pieces.append(broadcast(whitened, "src", owner))
    everyone = jnp.concatenate(pieces, axis=0)
    sources = jnp.take(everyone, source_index, axis=0)
    source_count = sources.shape[0]
    norm_factor = 1.0 / math.sqrt(traces.shape[1] * lax.axis_size("blk") * segment)
    own_rows = whitened.shape[0] // lax.axis_size("blk")
    flat_sources = sources.reshape(source_count, -1)
    padded = jnp.pad(whitened, ((0, 0), (0, 0), (MAXLAG, MAXLAG)))
    block_rows = math.gcd(lax.axis_size("blk") * own_rows, 16)
    grouped = padded.reshape(
        (lax.axis_size("blk") * own_rows // block_rows, block_rows) + padded.shape[1:]
    )

    def one_block(group):
        toeplitz = toeplitz_rows(group, LAG_COUNT, segment)
        products = lax.dot_general(
            toeplitz, flat_sources, (((1,), (1,)), ((), ())), preferred_element_type=jnp.float32
        )
        return (products * norm_factor).reshape(block_rows, LAG_COUNT, source_count)

    result = lax.map(one_block, grouped)
    return lax.psum_scatter(
        result.reshape(lax.axis_size("blk") * own_rows, LAG_COUNT, source_count),
        "blk",
        scatter_dimension=0,
        tiled=True,
    )


class Plan:
    def __init__(self, half, windows, segment, blk_size, src_size, source_count):
        self.half = half
        self.windows = windows
        self.segment = segment
        self.blk_size = blk_size
        self.src_size = src_size
        self.channels = half * src_size
        self.source_count = source_count
        self.coarse = LANES // self.channels
        if self.coarse == 0:
            return
        self.fine = -(-LAG_COUNT // self.coarse)
        self.fine_padded = -(-self.fine // (2 * GROUP)) * 2 * GROUP
        self.own = half // blk_size
        reach = segment + (self.coarse - 1) * self.fine
        self.span = -(-max(reach, segment + 2 * MAXLAG) // 128) * 128
        self.whole_groups = self.fine // GROUP * GROUP
        self.rest = self.fine - self.whole_groups
        rows = self.own * self.fine
        self.rows = -(-rows // 16) * 16
        self.height = self.own * self.fine_padded
        self.near = blk_size // 2
        self.norm_factor = 1.0 / math.sqrt(windows * blk_size * segment)

    def fits(self):
        return (
            self.coarse >= 2
            and self.src_size == 2
            and self.half % self.blk_size == 0
            and self.half % GROUP == 0
            and self.channels % 16 == 0
            and self.windows * self.half % 16 == 0
            and self.blk_size & (self.blk_size - 1) == 0
            and 2 <= self.blk_size <= 8
        )


def whiten_kernel(plan, traces_hbm, flags_hbm, out_ref, traces_ref, flags_ref, sems):
    copies = [
        pltpu.make_async_copy(traces_hbm, traces_ref, sems.at[0]),
        pltpu.make_async_copy(flags_hbm, flags_ref, sems.at[1]),
    ]
    for copy in copies:
        copy.start()
    for copy in copies:
        copy.wait()
    pieces = []
    for window in range(plan.windows):
        values = traces_ref[:, window, :]
        centered = values - jnp.mean(values, axis=1, keepdims=True)
        mean_power = jnp.mean(centered * centered, axis=1, keepdims=True)
        flag_values = flags_ref[window : window + 1, :].astype(jnp.float32).reshape(plan.half, 1)
        pieces.append(centered * lax.rsqrt(mean_power + 1e-05) * flag_values)
    out_ref[...] = jnp.concatenate(pieces, axis=0).astype(jnp.bfloat16)


def choose_kernel(plan, index_ref, after_ref, out_ref):
    first = lax.axis_index("src") * plan.half
    index = index_ref[...] - first
    index = jnp.where(index < 0, index + plan.channels, index)
    at_column = lax.broadcasted_iota(jnp.int32, (LANES, plan.source_count), 0)
    chosen = jnp.zeros((LANES, plan.source_count), jnp.bool_)
    for step in range(plan.coarse):
        chosen = chosen | (at_column == index + step * plan.channels)
    out_ref[...] = chosen.astype(jnp.float32).astype(jnp.bfloat16)


def correlate_kernel(plan, *refs):
    mine_refs = refs[: plan.near]
    other_refs = refs[plan.near : 2 * plan.near]
    kept_ref, sent_ref, rows_ref, toeplitz_ref, columns_ref = refs[2 * plan.near :]
    span = plan.span
    me = lax.axis_index("blk")
    targets = [me, me ^ plan.near]
    filled = plan.coarse * plan.channels
    if filled < LANES:
        columns_ref[filled:, :] = jnp.zeros((LANES - filled, columns_ref.shape[1]), jnp.bfloat16)
    filler = jnp.zeros((plan.channels, span - plan.segment), jnp.float32)
    for hop in range(plan.near):
        mine = mine_refs[hop][...].astype(jnp.float32)
        other = other_refs[hop][...].astype(jnp.float32)
        rows_ref[hop] = mine
        for window in range(plan.windows):
            start = (hop * plan.windows + window) * span
            at = slice(start, start + span)
            half = slice(window * plan.half, (window + 1) * plan.half)
            both = jnp.concatenate([mine[half], other[half]], axis=0)
            both = jnp.concatenate([both, filler], axis=1)
            for step in range(plan.coarse):
                moved = pltpu.roll(both, step * plan.fine, 1) if step else both
                columns_ref[step * plan.channels : (step + 1) * plan.channels, at] = moved.astype(jnp.bfloat16)
            for place, target in enumerate(targets):
                for member in range(plan.own):
                    channel = window * plan.half + target * plan.own + member
                    row = rows_ref[hop, pl.ds(channel, 1), :]
                    row = jnp.concatenate([row, filler[:1]], axis=1)
                    row = jnp.broadcast_to(row, (GROUP, span))
                    pieces = [
                        pltpu.roll(row, (MAXLAG - plan.fine + 1 + lag) % span, 1, stride=1, stride_axis=0)
                        for lag in range(0, plan.fine_padded, GROUP)
                    ]
                    first = place * plan.height + member * plan.fine_padded
                    toeplitz_ref[first : first + plan.fine_padded, at] = jnp.concatenate(pieces, axis=0).astype(
                        jnp.bfloat16
                    )
    products = lax.dot_general(
        toeplitz_ref[...],
        columns_ref[...],
        (((1,), (1,)), ((), ())),
        preferred_element_type=jnp.float32,
    ).reshape(len(targets), plan.own, plan.fine_padded, LANES)
    packed = []
    for place in range(len(targets)):
        part = products[place]
        pieces = [part[member, : plan.whole_groups] for member in range(plan.own)]
        if plan.rest:
            pieces += [part[member, plan.whole_groups : plan.fine] for member in range(plan.own)]
        if plan.rows > plan.own * plan.fine:
            pieces.append(jnp.zeros((plan.rows - plan.own * plan.fine, LANES), jnp.float32))
        packed.append(jnp.concatenate(pieces, axis=0))
    sent_ref[...] = packed[1].astype(jnp.bfloat16)
    kept_ref[...] = packed[0]


def halves(values):
    high = values.astype(jnp.bfloat16)
    return high, (values - high.astype(jnp.float32)).astype(jnp.bfloat16)


def expand_kernel(plan, chosen_ref, kept_ref, arrived_ref, out_ref):
    at_row = lax.broadcasted_iota(jnp.int32, (plan.height, plan.rows), 0)
    at_part = lax.broadcasted_iota(jnp.int32, (plan.height, plan.rows), 1)
    order = jnp.zeros((plan.height, plan.rows), jnp.bool_)
    for member in range(plan.own):
        reverse = plan.fine - 1 - (at_row - member * plan.fine_padded)
        whole = (reverse >= 0) & (reverse < plan.whole_groups) & (at_part == member * plan.whole_groups + reverse)
        tail = plan.own * plan.whole_groups + member * plan.rest + reverse - plan.whole_groups
        rest = (reverse >= plan.whole_groups) & (reverse < plan.fine) & (at_part == tail)
        order = order | whole | rest
    order = order.astype(jnp.float32).astype(jnp.bfloat16)
    total = (kept_ref[...] + arrived_ref[...].astype(jnp.float32)) * plan.norm_factor
    ordered = [jnp.dot(order, part, preferred_element_type=jnp.float32) for part in halves(total)]
    lane = lax.broadcasted_iota(jnp.int32, (plan.height, LANES), 1)
    chosen = chosen_ref[...]
    for step in range(plan.coarse):
        inside = (lane >= step * plan.channels) & (lane < (step + 1) * plan.channels)
        expanded = jnp.zeros((plan.height, plan.source_count), jnp.float32)
        for part in ordered:
            kept = jnp.where(inside, part, 0.0).astype(jnp.bfloat16)
            expanded += jnp.dot(kept, chosen, preferred_element_type=jnp.float32)
        count = min(plan.fine, LAG_COUNT - step * plan.fine)
        for member in range(plan.own):
            out_ref[member, step * plan.fine : step * plan.fine + count, :] = expanded[
                member * plan.fine_padded : member * plan.fine_padded + count
            ]


def few_channels(plan, traces, valid_flags, source_index):
    vmem = pl.BlockSpec(memory_space=pltpu.VMEM)
    anywhere = pl.BlockSpec(memory_space=pl.ANY)
    params = pltpu.CompilerParams(vmem_limit_bytes=32 * 1024 * 1024)
    packed_rows = plan.windows * plan.half
    flags = valid_flags.T

    def swap_cores(array):
        return lax.ppermute(array, "src", [(0, 1), (1, 0)])

    def swap_blk(array, hop):
        return lax.ppermute(array, "blk", [(place, place ^ hop) for place in range(plan.blk_size)])

    whitened = pl.pallas_call(
        functools.partial(whiten_kernel, plan),
        out_shape=jax.ShapeDtypeStruct((packed_rows, plan.segment), jnp.bfloat16),
        in_specs=[anywhere] * 2,
        out_specs=vmem,
        scratch_shapes=[
            pltpu.VMEM(traces.shape, jnp.float32),
            pltpu.VMEM(flags.shape, jnp.int32),
            pltpu.SemaphoreType.DMA((2,)),
        ],
        compiler_params=pltpu.CompilerParams(vmem_limit_bytes=60 * 1024 * 1024),
        name="whiten",
    )(traces, flags)
    mine = [whitened] + [swap_blk(whitened, hop) for hop in range(1, plan.near)]
    other = [swap_cores(array) for array in mine]
    chosen = pl.pallas_call(
        functools.partial(choose_kernel, plan),
        out_shape=jax.ShapeDtypeStruct((LANES, plan.source_count), jnp.bfloat16),
        in_specs=[vmem, pl.BlockSpec(memory_space=pl.ANY)],
        out_specs=vmem,
        compiler_params=params,
        name="choose",
    )(source_index.reshape(1, -1), whitened)
    width = plan.near * plan.windows * plan.span
    kept, sent = pl.pallas_call(
        functools.partial(correlate_kernel, plan),
        out_shape=[
            jax.ShapeDtypeStruct((plan.rows, LANES), jnp.float32),
            jax.ShapeDtypeStruct((plan.rows, LANES), jnp.bfloat16),
        ],
        in_specs=[vmem] * (2 * plan.near),
        out_specs=[vmem] * 2,
        scratch_shapes=[
            pltpu.VMEM((plan.near, packed_rows, plan.segment), jnp.float32),
            pltpu.VMEM((2 * plan.height, width), jnp.bfloat16),
            pltpu.VMEM((LANES, width), jnp.bfloat16),
        ],
        compiler_params=params,
        name="correlate",
    )(*mine, *other)
    arrived = swap_blk(sent, plan.near)
    return pl.pallas_call(
        functools.partial(expand_kernel, plan),
        out_shape=jax.ShapeDtypeStruct((plan.own, LAG_COUNT, plan.source_count), jnp.float32),
        in_specs=[vmem] * 3,
        out_specs=vmem,
        compiler_params=params,
        name="expand",
    )(chosen, kept, arrived)


def body(traces, valid_flags, source_index):
    plan = Plan(
        traces.shape[0],
        traces.shape[1],
        traces.shape[2],
        lax.axis_size("blk"),
        lax.axis_size("src"),
        source_index.shape[0],
    )
    if plan.fits():
        return few_channels(plan, traces, valid_flags, source_index)
    return many_channels(traces, valid_flags, source_index)


def solution(mesh):
    in_specs = (P(("fibre", "src"), "blk", None), P(("fibre", "src"), "blk"), P())
    out_specs = P(("fibre", "src", "blk"), None, None)
    return jax.shard_map(body, mesh=mesh, in_specs=in_specs, out_specs=out_specs, check_vma=False)
```

time: 24.7 us -> 20.8 us (0.84)
  blocking collectives: 18.2 us -> 0 us
  waiting for transfers between devices: 0.82 us -> 7.86 us
  starting transfers between devices: 0.91 us -> 7.38 us
  Pallas kernels: 2.77 us -> 4.53 us
  local copies, waits for them, and re-layouts: 1.8 us -> 0.8 us
    all_to_all x1 -> x0, blocking collectives: 18.2 us -> none  [few_channels(): arrived = lax.all_to_all(parts, 'blk', 0, 0, tiled=True)]
    ppermute x2 -> x8, waiting for transfers between devices: 0.82 us -> 7.86 us  [the longest x4 6.7 us: swap_blk(): lax.ppermute(array, 'blk', [(place, place ^ hop) for place in range(plan....]
    ppermute x2 -> x8, starting transfers between devices: 0.91 us -> 7.38 us  [the longest x4 7.31 us: swap_blk(): lax.ppermute(array, 'blk', [(place, place ^ hop) for place in range(plan....]
    pallas_call x1 -> x3, Pallas kernels: 1.32 us -> 3.32 us  [the longest x1 1.72 us: few_channels(): pl.pallas_call(functools.partial(whiten_kernel, plan), out_shape=jax.Shap...]
    unnamed x6 -> x4, local copies, waits for them, and re-layouts: 1.8 us -> 0.8 us
  transfers between devices with their start and end apart: 2 -> 8, of which waited for: 1 -> 6; matrix products, arithmetic and copies ran while one was open for 0% -> 0% of each run, Pallas kernels for 0% -> 1%
where the time goes in v3:
time: 20.8 us; the launch traced here: 20.6 us
  waiting for transfers between devices  7.86 us (38%)
  starting transfers between devices  7.38 us (35%)
  Pallas kernels  4.53 us (22%)
  local copies, waits for them, and re-layouts  0.8 us (4%)
    ppermute x4, starting transfers between devices, swap_blk(): lax.ppermute(array, 'blk', [(place, place ^ hop) for place in range(plan....  7.31 us
    ppermute x4, waiting for transfers between devices, swap_blk(): lax.ppermute(array, 'blk', [(place, place ^ hop) for place in range(plan....  6.7 us
    pallas_call x1, Pallas kernels, few_channels(): pl.pallas_call(functools.partial(whiten_kernel, plan), out_shape=jax.Shap...  1.72 us
    pallas_call x1, Pallas kernels, few_channels(): pl.pallas_call(functools.partial(correlate_kernel, plan), out_shape=[jax....  1.45 us
    pallas_call x1, Pallas kernels, few_channels(): pl.pallas_call(functools.partial(expand_kernel, plan), out_shape=jax.Shap...  1.21 us
    ppermute x4, waiting for transfers between devices, swap_cores(): return lax.ppermute(array, 'src', [(0, 1), (1, 0)])  1.16 us
    unnamed x4, local copies, waits for them, and re-layouts  0.8 us
  transfers between devices with their start and end apart: 8, of which 6 were waited for; matrix products, arithmetic and copies ran while one was open for 0% of the time, Pallas kernels for 1%

profile of v3, /device:TPU:0, one launch (start us, length us, event | category | flops | bytes accessed | tf_op | source)
XLA Modules:
  0.0 20.6 jit_solution(5159311382562249470)
XLA Ops:
  0.0 1.7 %whiten.1.after_ref.refs_0_ = bf16[48,512]{1,0:T(8,128)(2,1)} custom-call(f32[24,2,512]{2,1,0:T(2,128)} %traces_hbm.1, s32[2,24]{1,0:T(2,128)} %bitcast.3), custom_call_target="tpu_custom_call" | custom-call | tf_op jit(solution)/shard_map/whiten/pallas_call | solution.py:237
  1.7 4.0 %collective-permute-start.2 = (bf16[48,512]{1,0:T(8,128)(2,1)}, bf16[48,512]{1,0:T(8,128)(2,1)S(1)}, u32[]{:S(2)}, u32[]{:S(2)}) collective-permute-start(bf16[48,512]{1,0:T(8,128)(2,1)} %whiten.1.after_ref.refs_0_), channel_id=1, source_target_pairs={{0,6},{2,4},{4,2},{6,0},{8,14},{10,12},{12,10},{14,8},{1,7},{3,5},... | collective-permute-start | bytes 147464 | tf_op jit(solution)/shard_map/ppermute | solution.py:235
  5.7 0.4 %collective-permute-start.1 = (bf16[48,512]{1,0:T(8,128)(2,1)}, bf16[48,512]{1,0:T(8,128)(2,1)S(1)}, u32[]{:S(2)}, u32[]{:S(2)}) collective-permute-start(bf16[48,512]{1,0:T(8,128)(2,1)} %whiten.1.after_ref.refs_0_), channel_id=1, source_target_pairs={{0,4},{2,6},{4,0},{6,2},{8,12},{10,14},{12,8},{14,10},{1,5},{3,7},... | collective-permute-start | bytes 147464 | tf_op jit(solution)/shard_map/ppermute | solution.py:235
  6.2 0.2 collective-permute-start
  6.4 0.0 collective-permute-start.3
  6.4 1.6 %collective-permute-done.2.refs_3_ = bf16[48,512]{1,0:T(8,128)(2,1)S(1)} collective-permute-done((bf16[48,512]{1,0:T(8,128)(2,1)}, bf16[48,512]{1,0:T(8,128)(2,1)S(1)}, u32[]{:S(2)}, u32[]{:S(2)}) %collective-permute-start.2) | collective-permute-done | bytes 49184 | tf_op jit(solution)/shard_map/ppermute | solution.py:235
  8.0 0.0 collective-permute-start.6
  8.0 2.0 %collective-permute-done.1.refs_2_ = bf16[48,512]{1,0:T(8,128)(2,1)S(1)} collective-permute-done((bf16[48,512]{1,0:T(8,128)(2,1)}, bf16[48,512]{1,0:T(8,128)(2,1)S(1)}, u32[]{:S(2)}, u32[]{:S(2)}) %collective-permute-start.1) | collective-permute-done | bytes 49184 | tf_op jit(solution)/shard_map/ppermute | solution.py:235
  10.0 0.0 collective-permute-start.5
  10.1 0.4 %collective-permute-done.refs_1_ = bf16[48,512]{1,0:T(8,128)(2,1)S(1)} collective-permute-done((bf16[48,512]{1,0:T(8,128)(2,1)}, bf16[48,512]{1,0:T(8,128)(2,1)S(1)}, u32[]{:S(2)}, u32[]{:S(2)}) %collective-permute-start) | collective-permute-done | bytes 49184 | tf_op jit(solution)/shard_map/ppermute | solution.py:235
  10.5 0.1 collective-permute-start.4
  10.6 0.0 collective-permute-done.3.refs_4_
  10.6 0.0 collective-permute-done.6.refs_7_
  10.6 0.7 %collective-permute-done.5.refs_6_ = bf16[48,512]{1,0:T(8,128)(2,1)S(1)} collective-permute-done((bf16[48,512]{1,0:T(8,128)(2,1)S(1)}, bf16[48,512]{1,0:T(8,128)(2,1)S(1)}, u32[]{:S(2)}, u32[]{:S(2)}) %collective-permute-start.5) | collective-permute-done | bytes 49184 | tf_op jit(solution)/shard_map/ppermute | solution.py:232
  11.3 0.4 %collective-permute-done.4.refs_5_ = bf16[48,512]{1,0:T(8,128)(2,1)S(1)} collective-permute-done((bf16[48,512]{1,0:T(8,128)(2,1)S(1)}, bf16[48,512]{1,0:T(8,128)(2,1)S(1)}, u32[]{:S(2)}, u32[]{:S(2)}) %collective-permute-start.4) | collective-permute-done | bytes 49184 | tf_op jit(solution)/shard_map/ppermute | solution.py:232
  11.7 0.0 copy-start
  11.7 0.8 %copy-done = bf16[48,512]{1,0:T(8,128)(2,1)S(1)} copy-done((bf16[48,512]{1,0:T(8,128)(2,1)S(1)}, bf16[48,512]{1,0:T(8,128)(2,1)}, u32[]{:S(2)}) %copy-start) | copy-done | bytes 49176
  12.5 1.4 %correlate.1 = (f32[80,256]{1,0:T(8,128)S(1)}, bf16[80,256]{1,0:T(8,128)(2,1)S(1)}) custom-call(bf16[48,512]{1,0:T(8,128)(2,1)S(1)} %copy-done, bf16[48,512]{1,0:T(8,128)(2,1)S(1)} %collective-permute-done.refs_1_, bf16[48,512]{1,0:T(8,128)(2,1)S(1)} %collective-permute-done.1.refs_2_, bf16[48,512]{1,0:T(8,128)(2,1)S(1)} %collective-permute-done.2.refs_3_, ...), custom_call_target="tpu_custom_call" | custom-call | tf_op jit(solution)/shard_map/correlate/pallas_call | solution.py:261
  14.0 0.0 copy-start.1
  14.0 2.7 %collective-permute-start.7 = (bf16[80,256]{1,0:T(8,128)(2,1)S(1)}, bf16[80,256]{1,0:T(8,128)(2,1)S(1)}, u32[]{:S(2)}, u32[]{:S(2)}) collective-permute-start(bf16[80,256]{1,0:T(8,128)(2,1)S(1)} %get-tuple-element.8), channel_id=1, source_target_pairs={{0,8},{2,10},{4,12},{6,14},{8,0},{10,2},{12,4},{14,6},{1,9},{3,11}... | collective-permute-start | bytes 122888 | tf_op jit(solution)/shard_map/ppermute | solution.py:235
  16.7 0.0 copy-done.1
  16.7 0.1 choose.1.chosen_ref
  16.8 2.6 %collective-permute-done.7.arrived_ref = bf16[80,256]{1,0:T(8,128)(2,1)S(1)} collective-permute-done((bf16[80,256]{1,0:T(8,128)(2,1)S(1)}, bf16[80,256]{1,0:T(8,128)(2,1)S(1)}, u32[]{:S(2)}, u32[]{:S(2)}) %collective-permute-start.7) | collective-permute-done | bytes 40992 | tf_op jit(solution)/shard_map/ppermute | solution.py:235
  19.4 1.2 %expand.1 = f32[3,129,256]{2,1,0:T(8,128)} custom-call(bf16[256,256]{1,0:T(8,128)(2,1)S(1)} %choose.1.chosen_ref, f32[80,256]{1,0:T(8,128)S(1)} %get-tuple-element.7.kept_ref, bf16[80,256]{1,0:T(8,128)(2,1)S(1)} %collective-permute-done.7.arrived_ref), custom_call_target="tpu_custom_call" | custom-call | tf_op jit(solution)/shard_map/expand/pallas_call | solution.py:278
Async XLA Ops:
  1.7 6.3 %collective-permute-start.2 = (bf16[48,512]{1,0:T(8,128)(2,1)}, bf16[48,512]{1,0:T(8,128)(2,1)S(1)}, u32[]{:S(2)}, u32[]{:S(2)}) collective-permute-start(bf16[48,512]{1,0:T(8,128)(2,1)} %whiten.1.after_ref.refs_0_), channel_id=1, source_target_pairs={{0,6},{2,4},{4,2},{6,0},{8,14},{10,12},{12,10},{14,8},{1,7},{3,5},... | collective-permute-start | bytes 147464 | tf_op jit(solution)/shard_map/ppermute | solution.py:235
  5.7 4.3 %collective-permute-start.1 = (bf16[48,512]{1,0:T(8,128)(2,1)}, bf16[48,512]{1,0:T(8,128)(2,1)S(1)}, u32[]{:S(2)}, u32[]{:S(2)}) collective-permute-start(bf16[48,512]{1,0:T(8,128)(2,1)} %whiten.1.after_ref.refs_0_), channel_id=1, source_target_pairs={{0,4},{2,6},{4,0},{6,2},{8,12},{10,14},{12,8},{14,10},{1,5},{3,7},... | collective-permute-start | bytes 147464 | tf_op jit(solution)/shard_map/ppermute | solution.py:235
  6.2 4.3 %collective-permute-start = (bf16[48,512]{1,0:T(8,128)(2,1)}, bf16[48,512]{1,0:T(8,128)(2,1)S(1)}, u32[]{:S(2)}, u32[]{:S(2)}) collective-permute-start(bf16[48,512]{1,0:T(8,128)(2,1)} %whiten.1.after_ref.refs_0_), channel_id=1, source_target_pairs={{0,2},{2,0},{4,6},{6,4},{8,10},{10,8},{12,14},{14,12},{1,3},{3,1},... | collective-permute-start | bytes 147464 | tf_op jit(solution)/shard_map/ppermute | solution.py:235
  6.4 4.2 %collective-permute-start.3 = (bf16[48,512]{1,0:T(8,128)(2,1)}, bf16[48,512]{1,0:T(8,128)(2,1)S(1)}, u32[]{:S(2)}, u32[]{:S(2)}) collective-permute-start(bf16[48,512]{1,0:T(8,128)(2,1)} %whiten.1.after_ref.refs_0_), channel_id=1, source_target_pairs={{0,1},{1,0},{2,3},{3,2},{4,5},{5,4},{6,7},{7,6},{8,9},{9,8},{10,11... | collective-permute-start | bytes 147464 | tf_op jit(solution)/shard_map/ppermute | solution.py:232
  8.0 2.5 %collective-permute-start.6 = (bf16[48,512]{1,0:T(8,128)(2,1)S(1)}, bf16[48,512]{1,0:T(8,128)(2,1)S(1)}, u32[]{:S(2)}, u32[]{:S(2)}) collective-permute-start(bf16[48,512]{1,0:T(8,128)(2,1)S(1)} %collective-permute-done.2.refs_3_), channel_id=1, source_target_pairs={{0,1},{1,0},{2,3},{3,2},{4,5},{5,4},{6,7},{7,6},{8,9},{9,8},{10,11... | collective-permute-start | bytes 147464 | tf_op jit(solution)/shard_map/ppermute | solution.py:232
  10.0 1.2 %collective-permute-start.5 = (bf16[48,512]{1,0:T(8,128)(2,1)S(1)}, bf16[48,512]{1,0:T(8,128)(2,1)S(1)}, u32[]{:S(2)}, u32[]{:S(2)}) collective-permute-start(bf16[48,512]{1,0:T(8,128)(2,1)S(1)} %collective-permute-done.1.refs_2_), channel_id=1, source_target_pairs={{0,1},{1,0},{2,3},{3,2},{4,5},{5,4},{6,7},{7,6},{8,9},{9,8},{10,11... | collective-permute-start | bytes 147464 | tf_op jit(solution)/shard_map/ppermute | solution.py:232
  10.5 1.2 %collective-permute-start.4 = (bf16[48,512]{1,0:T(8,128)(2,1)S(1)}, bf16[48,512]{1,0:T(8,128)(2,1)S(1)}, u32[]{:S(2)}, u32[]{:S(2)}) collective-permute-start(bf16[48,512]{1,0:T(8,128)(2,1)S(1)} %collective-permute-done.refs_1_), channel_id=1, source_target_pairs={{0,1},{1,0},{2,3},{3,2},{4,5},{5,4},{6,7},{7,6},{8,9},{9,8},{10,11... | collective-permute-start | bytes 147464 | tf_op jit(solution)/shard_map/ppermute | solution.py:232
  11.7 0.8 %copy-start = (bf16[48,512]{1,0:T(8,128)(2,1)S(1)}, bf16[48,512]{1,0:T(8,128)(2,1)}, u32[]{:S(2)}) copy-start(bf16[48,512]{1,0:T(8,128)(2,1)} %whiten.1.after_ref.refs_0_) | copy-start | bytes 147460
  14.0 2.7 %copy-start.1 = (s32[256]{0:T(256)S(1)}, s32[256]{0:T(256)}, u32[]{:S(2)}) copy-start(s32[256]{0:T(256)} %param.5) | copy-start | bytes 3076
  14.0 5.4 %collective-permute-start.7 = (bf16[80,256]{1,0:T(8,128)(2,1)S(1)}, bf16[80,256]{1,0:T(8,128)(2,1)S(1)}, u32[]{:S(2)}, u32[]{:S(2)}) collective-permute-start(bf16[80,256]{1,0:T(8,128)(2,1)S(1)} %get-tuple-element.8), channel_id=1, source_target_pairs={{0,8},{2,10},{4,12},{6,14},{8,0},{10,2},{12,4},{14,6},{1,9},{3,11}... | collective-permute-start | bytes 122888 | tf_op jit(solution)/shard_map/ppermute | solution.py:235

commit v4 on v3

v4 whole, which is shorter than its diff:
```python
import functools
import math

import jax
import jax.numpy as jnp
from jax import lax
from jax.experimental import pallas as pl
from jax.experimental.pallas import tpu as pltpu
from jax.sharding import PartitionSpec as P

MAXLAG = 64
LAG_COUNT = 2 * MAXLAG + 1
LANES = 256
GROUP = 8


def broadcast(value, axis, source):
    kept = jnp.where(lax.axis_index(axis) == source, value, 0).astype(value.dtype)
    return lax.psum(kept, axis)


def toeplitz_rows(group, lag_count, segment):
    shifted = jnp.stack(
        [group[:, :, lag_step : lag_step + segment] for lag_step in range(lag_count)], axis=1
    )
    return shifted.reshape(group.shape[0] * lag_count, -1)


def many_channels(traces, valid_flags, source_index):
    segment = traces.shape[2]
    centered = traces - jnp.mean(traces, axis=2, keepdims=True)
    mean_power = jnp.mean(centered * centered, axis=2, keepdims=True)
    flag_values = valid_flags[:, :, None].astype(jnp.float32)
    whitened = (centered * lax.rsqrt(mean_power + 1e-05) * flag_values).astype(jnp.bfloat16)
    pieces = []
    for owner in range(lax.axis_size("src")):
        pieces.append(broadcast(whitened, "src", owner))
    everyone = jnp.concatenate(pieces, axis=0)
    sources = jnp.take(everyone, source_index, axis=0)
    source_count = sources.shape[0]
    norm_factor = 1.0 / math.sqrt(traces.shape[1] * lax.axis_size("blk") * segment)
    own_rows = whitened.shape[0] // lax.axis_size("blk")
    flat_sources = sources.reshape(source_count, -1)
    padded = jnp.pad(whitened, ((0, 0), (0, 0), (MAXLAG, MAXLAG)))
    block_rows = math.gcd(lax.axis_size("blk") * own_rows, 16)
    grouped = padded.reshape(
        (lax.axis_size("blk") * own_rows // block_rows, block_rows) + padded.shape[1:]
    )

    def one_block(group):
        toeplitz = toeplitz_rows(group, LAG_COUNT, segment)
        products = lax.dot_general(
            toeplitz, flat_sources, (((1,), (1,)), ((), ())), preferred_element_type=jnp.float32
        )
        return (products * norm_factor).reshape(block_rows, LAG_COUNT, source_count)

    result = lax.map(one_block, grouped)
    return lax.psum_scatter(
        result.reshape(lax.axis_size("blk") * own_rows, LAG_COUNT, source_count),
        "blk",
        scatter_dimension=0,
        tiled=True,
    )


class Plan:
    def __init__(self, half, windows, segment, blk_size, src_size, source_count):
        self.half = half
        self.windows = windows
        self.segment = segment
        self.blk_size = blk_size
        self.src_size = src_size
        self.channels = half * src_size
        self.source_count = source_count
        self.coarse = LANES // self.channels
        if self.coarse == 0:
            return
        self.fine = -(-LAG_COUNT // self.coarse)
        self.fine_padded = -(-self.fine // (2 * GROUP)) * 2 * GROUP
        self.own = half // blk_size
        reach = segment + (self.coarse - 1) * self.fine
        self.span = -(-max(reach, segment + 2 * MAXLAG) // 128) * 128
        self.whole_groups = self.fine // GROUP * GROUP
        self.rest = self.fine - self.whole_groups
        rows = self.own * self.fine
        self.rows = -(-rows // 16) * 16
        self.height = self.own * self.fine_padded
        self.near = blk_size // 2
        self.norm_factor = 1.0 / math.sqrt(windows * blk_size * segment)

    def fits(self):
        return (
            self.coarse >= 2
            and self.src_size == 2
            and self.half % self.blk_size == 0
            and self.half % GROUP == 0
            and self.channels % 16 == 0
            and self.windows * self.half % 16 == 0
            and self.blk_size == 8
        )


def whiten_kernel(plan, traces_hbm, flags_hbm, out_ref, traces_ref, flags_ref, sems):
    copies = [
        pltpu.make_async_copy(traces_hbm, traces_ref, sems.at[0]),
        pltpu.make_async_copy(flags_hbm, flags_ref, sems.at[1]),
    ]
    for copy in copies:
        copy.start()
    for copy in copies:
        copy.wait()
    pieces = []
    for window in range(plan.windows):
        values = traces_ref[:, window, :]
        centered = values - jnp.mean(values, axis=1, keepdims=True)
        mean_power = jnp.mean(centered * centered, axis=1, keepdims=True)
        flag_values = flags_ref[window : window + 1, :].astype(jnp.float32).reshape(plan.half, 1)
        pieces.append(centered * lax.rsqrt(mean_power + 1e-05) * flag_values)
    out_ref[...] = jnp.concatenate(pieces, axis=0).astype(jnp.bfloat16)


def lag_rows(plan, row):
    span = plan.span
    moved = jnp.broadcast_to(pltpu.roll(row, MAXLAG, 1), (GROUP, span))
    sublane = lax.broadcasted_iota(jnp.int32, (GROUP, span), 0)
    bit = 1
    while bit < GROUP:
        moved = jnp.where((sublane & bit) != 0, pltpu.roll(moved, span - bit, 1), moved)
        bit *= 2
    pieces = [moved]
    for lag in range(GROUP, plan.fine_padded, GROUP):
        pieces.append(pltpu.roll(moved, span - lag, 1))
    return jnp.concatenate(pieces, axis=0).astype(jnp.bfloat16)


def correlate_kernel(plan, pairs, prior, last, *refs):
    mine_refs, refs = refs[:pairs], refs[pairs:]
    other_refs, refs = refs[:pairs], refs[pairs:]
    if prior:
        prior_ref, refs = refs[0], refs[1:]
    out_refs, (rows_ref, toeplitz_ref, columns_ref) = refs[:-3], refs[-3:]
    span = plan.span
    me = lax.axis_index("blk")
    targets = [me, me ^ plan.near]
    filled = plan.coarse * plan.channels
    if filled < LANES:
        columns_ref[filled:, :] = jnp.zeros((LANES - filled, columns_ref.shape[1]), jnp.bfloat16)
    filler = jnp.zeros((plan.channels, span - plan.segment), jnp.float32)
    for pair in range(pairs):
        mine = mine_refs[pair][...].astype(jnp.float32)
        other = other_refs[pair][...].astype(jnp.float32)
        rows_ref[pair] = mine
        for window in range(plan.windows):
            start = (pair * plan.windows + window) * span
            at = slice(start, start + span)
            half = slice(window * plan.half, (window + 1) * plan.half)
            both = jnp.concatenate([mine[half], other[half]], axis=0)
            both = jnp.concatenate([both, filler], axis=1)
            for step in range(plan.coarse):
                moved = pltpu.roll(both, step * plan.fine, 1) if step else both
                columns_ref[step * plan.channels : (step + 1) * plan.channels, at] = moved.astype(jnp.bfloat16)
            for place, target in enumerate(targets):
                for member in range(plan.own):
                    channel = window * plan.half + target * plan.own + member
                    row = jnp.concatenate([rows_ref[pair, pl.ds(channel, 1), :], filler[:1]], axis=1)
                    first = place * plan.height + member * plan.fine_padded
                    toeplitz_ref[first : first + plan.fine_padded, at] = lag_rows(plan, row)
    products = lax.dot_general(
        toeplitz_ref[...],
        columns_ref[...],
        (((1,), (1,)), ((), ())),
        preferred_element_type=jnp.float32,
    )
    if prior:
        products = products + prior_ref[...]
    if not last:
        out_refs[0][...] = products
        return
    products = products.reshape(len(targets), plan.own, plan.fine_padded, LANES)
    packed = []
    for place in range(len(targets)):
        part = products[place]
        pieces = [part[member, : plan.whole_groups] for member in range(plan.own)]
        if plan.rest:
            pieces += [part[member, plan.whole_groups : plan.fine] for member in range(plan.own)]
        if plan.rows > plan.own * plan.fine:
            pieces.append(jnp.zeros((plan.rows - plan.own * plan.fine, LANES), jnp.float32))
        packed.append(jnp.concatenate(pieces, axis=0))
    out_refs[1][...] = packed[1].astype(jnp.bfloat16)
    out_refs[0][...] = packed[0]


def inside_step(plan, step, values):
    lane = lax.broadcasted_iota(jnp.int32, values.shape, 1)
    inside = (lane >= step * plan.channels) & (lane < (step + 1) * plan.channels)
    return jnp.where(inside, values, 0.0).astype(jnp.bfloat16)


def prepare_kernel(plan, index_ref, kept_ref, chosen_ref, base_ref):
    first = lax.axis_index("src") * plan.half
    index = index_ref[...] - first
    index = jnp.where(index < 0, index + plan.channels, index)
    at_column = lax.broadcasted_iota(jnp.int32, (LANES, plan.source_count), 0)
    chosen = jnp.zeros((LANES, plan.source_count), jnp.bool_)
    for step in range(plan.coarse):
        chosen = chosen | (at_column == index + step * plan.channels)
    chosen = chosen.astype(jnp.float32).astype(jnp.bfloat16)
    chosen_ref[...] = chosen
    kept = kept_ref[...] * plan.norm_factor
    high = kept.astype(jnp.bfloat16).astype(jnp.float32)
    for step in range(plan.coarse):
        base_ref[step] = sum(
            jnp.dot(inside_step(plan, step, part), chosen, preferred_element_type=jnp.float32)
            for part in (high, kept - high)
        )


def expand_kernel(plan, chosen_ref, base_ref, arrived_ref, out_hbm, out_ref, sems):
    arrived = arrived_ref[...].astype(jnp.float32)
    chosen = chosen_ref[...]
    expanded = []
    for step in range(plan.coarse):
        moved = jnp.dot(inside_step(plan, step, arrived), chosen, preferred_element_type=jnp.float32)
        expanded.append(base_ref[step] + moved * plan.norm_factor)
    copies = []
    for member in range(plan.own):
        for step in range(plan.coarse):
            start = step * plan.fine
            count = min(plan.whole_groups, LAG_COUNT - start)
            first = member * plan.whole_groups
            out_ref[member, start : start + count, :] = expanded[step][first : first + count]
            rest = min(plan.fine, LAG_COUNT - start) - count
            if rest > 0:
                start += plan.whole_groups
                first = plan.own * plan.whole_groups + member * plan.rest
                out_ref[member, start : start + rest, :] = expanded[step][first : first + rest]
        copies.append(pltpu.make_async_copy(out_ref.at[member], out_hbm.at[member], sems.at[member]))
        copies[-1].start()
    for copy in copies:
        copy.wait()


def few_channels(plan, traces, valid_flags, source_index):
    vmem = pl.BlockSpec(memory_space=pltpu.VMEM)
    params = pltpu.CompilerParams(vmem_limit_bytes=32 * 1024 * 1024)
    packed_rows = plan.windows * plan.half

    def swap_cores(array):
        return lax.ppermute(array, "src", [(0, 1), (1, 0)])

    def swap_blk(array, hops):
        pairs = []
        for place in range(plan.blk_size):
            for core in range(plan.src_size):
                pairs.append((place * plan.src_size + core, (place ^ hops[core]) * plan.src_size + core))
        return lax.ppermute(array, ("blk", "src"), pairs)

    flags = valid_flags.T
    whitened = pl.pallas_call(
        functools.partial(whiten_kernel, plan),
        out_shape=jax.ShapeDtypeStruct((packed_rows, plan.segment), jnp.bfloat16),
        in_specs=[pl.BlockSpec(memory_space=pl.ANY)] * 2,
        out_specs=vmem,
        scratch_shapes=[
            pltpu.VMEM(traces.shape, jnp.float32),
            pltpu.VMEM(flags.shape, jnp.int32),
            pltpu.SemaphoreType.DMA((2,)),
        ],
        compiler_params=pltpu.CompilerParams(vmem_limit_bytes=60 * 1024 * 1024),
        name="whiten",
    )(traces, flags)

    def correlate(mine, other, prior=None, last=False):
        pairs = len(mine)
        width = pairs * plan.windows * plan.span
        height = 2 * plan.height
        if last:
            shapes = [((plan.rows, LANES), jnp.float32), ((plan.rows, LANES), jnp.bfloat16)]
        else:
            shapes = [((height, LANES), jnp.float32)]
        operands = list(mine) + list(other) + ([] if prior is None else [prior])
        results = pl.pallas_call(
            functools.partial(correlate_kernel, plan, pairs, prior is not None, last),
            out_shape=[jax.ShapeDtypeStruct(*shape) for shape in shapes],
            in_specs=[vmem] * len(operands),
            out_specs=[vmem] * len(shapes),
            scratch_shapes=[
                pltpu.VMEM((pairs, packed_rows, plan.segment), jnp.float32),
                pltpu.VMEM((height, width), jnp.bfloat16),
                pltpu.VMEM((LANES, width), jnp.bfloat16),
            ],
            compiler_params=params,
            cost_estimate=pl.CostEstimate(
                flops=2 * height * width * LANES, bytes_accessed=4 * packed_rows * width, transcendentals=0
            ),
            name="correlate",
        )(*operands)
        return results if last else results[0]

    first = swap_blk(whitened, (1, 2))
    second = swap_blk(whitened, (2, 1))
    both = swap_blk(first, (2, 1))
    total = correlate([whitened], [swap_cores(whitened)])
    both, total = lax.optimization_barrier((both, total))
    total = correlate([first, second], [swap_cores(second), swap_cores(first)], total)
    kept, sent = correlate([both], [swap_cores(both)], total, last=True)
    arrived = swap_blk(sent, (4, 4))
    chosen, base = pl.pallas_call(
        functools.partial(prepare_kernel, plan),
        out_shape=[
            jax.ShapeDtypeStruct((LANES, plan.source_count), jnp.bfloat16),
            jax.ShapeDtypeStruct((plan.coarse, plan.rows, plan.source_count), jnp.float32),
        ],
        in_specs=[vmem] * 2,
        out_specs=[vmem] * 2,
        compiler_params=params,
        name="prepare",
    )(source_index.reshape(1, -1), kept)
    out_shape = (plan.own, LAG_COUNT, plan.source_count)
    return pl.pallas_call(
        functools.partial(expand_kernel, plan),
        out_shape=jax.ShapeDtypeStruct(out_shape, jnp.float32),
        in_specs=[vmem] * 3,
        out_specs=pl.BlockSpec(memory_space=pl.ANY),
        scratch_shapes=[pltpu.VMEM(out_shape, jnp.float32), pltpu.SemaphoreType.DMA((plan.own,))],
        compiler_params=params,
        name="expand",
    )(chosen, base, arrived)


def body(traces, valid_flags, source_index):
    plan = Plan(
        traces.shape[0],
        traces.shape[1],
        traces.shape[2],
        lax.axis_size("blk"),
        lax.axis_size("src"),
        source_index.shape[0],
    )
    if plan.fits():
        return few_channels(plan, traces, valid_flags, source_index)
    return many_channels(traces, valid_flags, source_index)


def solution(mesh):
    in_specs = (P(("fibre", "src"), "blk", None), P(("fibre", "src"), "blk"), P())
    out_specs = P(("fibre", "src", "blk"), None, None)
    return jax.shard_map(body, mesh=mesh, in_specs=in_specs, out_specs=out_specs, check_vma=False)
```

time: 20.8 us -> 23.1 us (1.11)
  waiting for transfers between devices: 7.86 us -> 2.7 us
  Pallas kernels: 4.53 us -> 8.16 us
  starting transfers between devices: 7.38 us -> 10.5 us
  local copies, waits for them, and re-layouts: 0.8 us -> 1.48 us
    ppermute x4, waiting for transfers between devices: 6.7 us -> 2.69 us  [swap_blk(): return lax.ppermute(array, ('blk', 'src'), pairs)]
    pallas_call x2 -> x4, Pallas kernels: 1.59 us -> 5.41 us  [the longest x3 4.95 us: correlate(): pl.pallas_call(functools.partial(correlate_kernel, plan, pairs, prior is...]
    ppermute x4, starting transfers between devices: 7.31 us -> 9.9 us  [swap_blk(): return lax.ppermute(array, ('blk', 'src'), pairs)]
    ppermute x4, waiting for transfers between devices: 1.16 us -> 0.01 us  [swap_cores(): return lax.ppermute(array, 'src', [(0, 1), (1, 0)])]
    unnamed x4, local copies, waits for them, and re-layouts: 0.8 us -> 1.48 us
    ppermute x4, starting transfers between devices: 0.07 us -> 0.58 us  [swap_cores(): return lax.ppermute(array, 'src', [(0, 1), (1, 0)])]
  transfers between devices with their start and end apart: 8 -> 8, of which waited for: 6 -> 2; matrix products, arithmetic and copies ran while one was open for 0% -> 0% of each run, Pallas kernels for 1% -> 20%
where the time goes in v4:
time: 23.1 us; the launch traced here: 22.9 us
  starting transfers between devices  10.5 us (45%)
  Pallas kernels  8.16 us (35%)
  waiting for transfers between devices  2.7 us (12%)
  local copies, waits for them, and re-layouts  1.48 us (6%)
    ppermute x4, starting transfers between devices, swap_blk(): return lax.ppermute(array, ('blk', 'src'), pairs)  9.9 us
    pallas_call x3, Pallas kernels, correlate(): pl.pallas_call(functools.partial(correlate_kernel, plan, pairs, prior is...  4.95 us
    ppermute x4, waiting for transfers between devices, swap_blk(): return lax.ppermute(array, ('blk', 'src'), pairs)  2.69 us
    pallas_call x1, Pallas kernels, few_channels(): pl.pallas_call(functools.partial(whiten_kernel, plan), out_shape=jax.Shap...  1.72 us
    unnamed x4, local copies, waits for them, and re-layouts  1.48 us
    pallas_call x1, Pallas kernels, few_channels(): pl.pallas_call(functools.partial(expand_kernel, plan), out_shape=jax.Shap...  1.02 us
    ppermute x4, starting transfers between devices, swap_cores(): return lax.ppermute(array, 'src', [(0, 1), (1, 0)])  0.58 us
  transfers between devices with their start and end apart: 8, of which 2 were waited for; matrix products, arithmetic and copies ran while one was open for 0% of the time, Pallas kernels for 20%

profile of v4, /device:TPU:0, one launch (start us, length us, event | category | flops | bytes accessed | tf_op | source)
XLA Modules:
  0.0 22.9 jit_solution(17852912094420776122)
XLA Ops:
  0.0 1.7 %whiten.1.refs_0_ = bf16[48,512]{1,0:T(8,128)(2,1)} custom-call(f32[24,2,512]{2,1,0:T(2,128)} %traces_hbm.1, s32[2,24]{1,0:T(2,128)} %bitcast.3), custom_call_target="tpu_custom_call" | custom-call | tf_op jit(solution)/shard_map/whiten/pallas_call | solution.py:259
  1.7 3.0 %collective-permute-start = (bf16[48,512]{1,0:T(8,128)(2,1)}, bf16[48,512]{1,0:T(8,128)(2,1)S(1)}, u32[]{:S(2)}, u32[]{:S(2)}) collective-permute-start(bf16[48,512]{1,0:T(8,128)(2,1)} %whiten.1.refs_0_), channel_id=1, source_target_pairs={{0,2},{1,5},{2,0},{3,7},{4,6},{5,1},{6,4},{7,3},{8,10},{9,13},{10,... | collective-permute-start | bytes 147464 | tf_op jit(solution)/shard_map/ppermute | solution.py:256
  4.7 1.6 %collective-permute-start.4 = (bf16[48,512]{1,0:T(8,128)(2,1)}, bf16[48,512]{1,0:T(8,128)(2,1)S(1)}, u32[]{:S(2)}, u32[]{:S(2)}) collective-permute-start(bf16[48,512]{1,0:T(8,128)(2,1)} %whiten.1.refs_0_), channel_id=1, source_target_pairs={{0,4},{1,3},{2,6},{3,1},{4,0},{5,7},{6,2},{7,5},{8,12},{9,11},{10,... | collective-permute-start | bytes 147464 | tf_op jit(solution)/shard_map/ppermute | solution.py:256
  6.3 0.0 collective-permute-start.2
  6.3 0.7 %collective-permute-done.refs_0_ = bf16[48,512]{1,0:T(8,128)(2,1)S(1)} collective-permute-done((bf16[48,512]{1,0:T(8,128)(2,1)}, bf16[48,512]{1,0:T(8,128)(2,1)S(1)}, u32[]{:S(2)}, u32[]{:S(2)}) %collective-permute-start) | collective-permute-done | bytes 49184 | tf_op jit(solution)/shard_map/ppermute | solution.py:256
  7.0 2.1 %collective-permute-start.1 = (bf16[48,512]{1,0:T(8,128)(2,1)S(1)}, bf16[48,512]{1,0:T(8,128)(2,1)S(1)}, u32[]{:S(2)}, u32[]{:S(2)}) collective-permute-start(bf16[48,512]{1,0:T(8,128)(2,1)S(1)} %collective-permute-done.refs_0_), channel_id=1, source_target_pairs={{0,4},{1,3},{2,6},{3,1},{4,0},{5,7},{6,2},{7,5},{8,12},{9,11},{10,... | collective-permute-start | bytes 147464 | tf_op jit(solution)/shard_map/ppermute | solution.py:256
  9.1 0.0 collective-permute-done.4.refs_1_
  9.1 0.0 collective-permute-start.5
  9.1 0.5 %collective-permute-start.6 = (bf16[48,512]{1,0:T(8,128)(2,1)S(1)}, bf16[48,512]{1,0:T(8,128)(2,1)S(1)}, u32[]{:S(2)}, u32[]{:S(2)}) collective-permute-start(bf16[48,512]{1,0:T(8,128)(2,1)S(1)} %collective-permute-done.refs_0_), channel_id=1, source_target_pairs={{0,1},{1,0},{2,3},{3,2},{4,5},{5,4},{6,7},{7,6},{8,9},{9,8},{10,11... | collective-permute-start | bytes 147464 | tf_op jit(solution)/shard_map/ppermute | solution.py:249
  9.6 0.0 collective-permute-done.2.refs_1_
  9.6 0.0 copy-start
  9.6 0.8 %copy-done = bf16[48,512]{1,0:T(8,128)(2,1)S(1)} copy-done((bf16[48,512]{1,0:T(8,128)(2,1)S(1)}, bf16[48,512]{1,0:T(8,128)(2,1)}, u32[]{:S(2)}) %copy-start) | copy-done | bytes 49176
  10.4 0.9 %correlate.3.refs_4_ = f32[192,256]{1,0:T(8,128)S(1)} custom-call(bf16[48,512]{1,0:T(8,128)(2,1)S(1)} %copy-done, bf16[48,512]{1,0:T(8,128)(2,1)S(1)} %collective-permute-done.2.refs_1_), custom_call_target="tpu_custom_call" | custom-call | flops 125829120 | bytes 245760 | tf_op jit(solution)/shard_map/correlate/pallas_call | solution.py:282
  11.3 0.0 collective-permute-done.1.refs_0_
  11.3 0.1 collective-permute-start.3
  11.4 0.0 collective-permute-done.5.refs_2_
  11.4 0.0 collective-permute-done.6.refs_3_
  11.4 3.2 %correlate.4.refs_2_ = f32[192,256]{1,0:T(8,128)S(1)} custom-call(bf16[48,512]{1,0:T(8,128)(2,1)S(1)} %collective-permute-done.refs_0_, bf16[48,512]{1,0:T(8,128)(2,1)S(1)} %collective-permute-done.4.refs_1_, bf16[48,512]{1,0:T(8,128)(2,1)S(1)} %collective-permute-done.5.refs_2_, bf16[48,512]{1,0:T(8,128)(2,1)S(1)} %collective-permute-done.6.refs_3_, ...), custom_call_target="tpu_custom_call" | custom-call | flops 251658240 | bytes 491520 | tf_op jit(solution)/shard_map/correlate/pallas_call | solution.py:282
  14.6 0.0 collective-permute-done.3.refs_1_
  14.7 0.9 %correlate.5 = (f32[80,256]{1,0:T(8,128)S(1)}, bf16[80,256]{1,0:T(8,128)(2,1)S(1)}) custom-call(bf16[48,512]{1,0:T(8,128)(2,1)S(1)} %collective-permute-done.1.refs_0_, bf16[48,512]{1,0:T(8,128)(2,1)S(1)} %collective-permute-done.3.refs_1_, f32[192,256]{1,0:T(8,128)S(1)} %correlate.4.refs_2_), custom_call_target="tpu_custom_call" | custom-call | flops 125829120 | bytes 245760 | tf_op jit(solution)/shard_map/correlate/pallas_call | solution.py:282
  15.5 3.2 %collective-permute-start.7 = (bf16[80,256]{1,0:T(8,128)(2,1)S(1)}, bf16[80,256]{1,0:T(8,128)(2,1)S(1)}, u32[]{:S(2)}, u32[]{:S(2)}) collective-permute-start(bf16[80,256]{1,0:T(8,128)(2,1)S(1)} %get-tuple-element.16), channel_id=1, source_target_pairs={{0,8},{1,9},{2,10},{3,11},{4,12},{5,13},{6,14},{7,15},{8,0},{9,1},... | collective-permute-start | bytes 122888 | tf_op jit(solution)/shard_map/ppermute | solution.py:256
  18.8 0.0 copy-start.1
  18.8 0.7 %copy-done.1 = s32[256]{0:T(256)S(1)} copy-done((s32[256]{0:T(256)S(1)}, s32[256]{0:T(256)}, u32[]{:S(2)}) %copy-start.1) | copy-done | bytes 1048
  19.4 0.5 %prepare.1 = (bf16[256,256]{1,0:T(8,128)(2,1)S(1)}, f32[5,80,256]{2,1,0:T(8,128)S(1)}) custom-call(s32[1,256]{1,0:T(1,128)S(1)} %bitcast.2, f32[80,256]{1,0:T(8,128)S(1)} %get-tuple-element.13.kept_ref), custom_call_target="tpu_custom_call" | custom-call | tf_op jit(solution)/shard_map/prepare/pallas_call | solution.py:308
  19.9 2.0 %collective-permute-done.7.arrived_ref = bf16[80,256]{1,0:T(8,128)(2,1)S(1)} collective-permute-done((bf16[80,256]{1,0:T(8,128)(2,1)S(1)}, bf16[80,256]{1,0:T(8,128)(2,1)S(1)}, u32[]{:S(2)}, u32[]{:S(2)}) %collective-permute-start.7) | collective-permute-done | bytes 40992 | tf_op jit(solution)/shard_map/ppermute | solution.py:256
  21.9 1.0 %expand.1 = f32[3,129,256]{2,1,0:T(8,128)} custom-call(bf16[256,256]{1,0:T(8,128)(2,1)S(1)} %get-tuple-element.14.chosen_ref, f32[5,80,256]{2,1,0:T(8,128)S(1)} %get-tuple-element.15.base_ref, bf16[80,256]{1,0:T(8,128)(2,1)S(1)} %collective-permute-done.7.arrived_ref), custom_call_target="tpu_custom_call" | custom-call | tf_op jit(solution)/shard_map/expand/pallas_call | solution.py:320
Async XLA Ops:
  1.7 5.3 %collective-permute-start = (bf16[48,512]{1,0:T(8,128)(2,1)}, bf16[48,512]{1,0:T(8,128)(2,1)S(1)}, u32[]{:S(2)}, u32[]{:S(2)}) collective-permute-start(bf16[48,512]{1,0:T(8,128)(2,1)} %whiten.1.refs_0_), channel_id=1, source_target_pairs={{0,2},{1,5},{2,0},{3,7},{4,6},{5,1},{6,4},{7,3},{8,10},{9,13},{10,... | collective-permute-start | bytes 147464 | tf_op jit(solution)/shard_map/ppermute | solution.py:256
  4.7 4.4 %collective-permute-start.4 = (bf16[48,512]{1,0:T(8,128)(2,1)}, bf16[48,512]{1,0:T(8,128)(2,1)S(1)}, u32[]{:S(2)}, u32[]{:S(2)}) collective-permute-start(bf16[48,512]{1,0:T(8,128)(2,1)} %whiten.1.refs_0_), channel_id=1, source_target_pairs={{0,4},{1,3},{2,6},{3,1},{4,0},{5,7},{6,2},{7,5},{8,12},{9,11},{10,... | collective-permute-start | bytes 147464 | tf_op jit(solution)/shard_map/ppermute | solution.py:256
  6.3 3.3 %collective-permute-start.2 = (bf16[48,512]{1,0:T(8,128)(2,1)}, bf16[48,512]{1,0:T(8,128)(2,1)S(1)}, u32[]{:S(2)}, u32[]{:S(2)}) collective-permute-start(bf16[48,512]{1,0:T(8,128)(2,1)} %whiten.1.refs_0_), channel_id=1, source_target_pairs={{0,1},{1,0},{2,3},{3,2},{4,5},{5,4},{6,7},{7,6},{8,9},{9,8},{10,11... | collective-permute-start | bytes 147464 | tf_op jit(solution)/shard_map/ppermute | solution.py:249
  7.0 4.3 %collective-permute-start.1 = (bf16[48,512]{1,0:T(8,128)(2,1)S(1)}, bf16[48,512]{1,0:T(8,128)(2,1)S(1)}, u32[]{:S(2)}, u32[]{:S(2)}) collective-permute-start(bf16[48,512]{1,0:T(8,128)(2,1)S(1)} %collective-permute-done.refs_0_), channel_id=1, source_target_pairs={{0,4},{1,3},{2,6},{3,1},{4,0},{5,7},{6,2},{7,5},{8,12},{9,11},{10,... | collective-permute-start | bytes 147464 | tf_op jit(solution)/shard_map/ppermute | solution.py:256
  9.1 2.3 %collective-permute-start.5 = (bf16[48,512]{1,0:T(8,128)(2,1)S(1)}, bf16[48,512]{1,0:T(8,128)(2,1)S(1)}, u32[]{:S(2)}, u32[]{:S(2)}) collective-permute-start(bf16[48,512]{1,0:T(8,128)(2,1)S(1)} %collective-permute-done.4.refs_1_), channel_id=1, source_target_pairs={{0,1},{1,0},{2,3},{3,2},{4,5},{5,4},{6,7},{7,6},{8,9},{9,8},{10,11... | collective-permute-start | bytes 147464 | tf_op jit(solution)/shard_map/ppermute | solution.py:249
  9.1 2.3 %collective-permute-start.6 = (bf16[48,512]{1,0:T(8,128)(2,1)S(1)}, bf16[48,512]{1,0:T(8,128)(2,1)S(1)}, u32[]{:S(2)}, u32[]{:S(2)}) collective-permute-start(bf16[48,512]{1,0:T(8,128)(2,1)S(1)} %collective-permute-done.refs_0_), channel_id=1, source_target_pairs={{0,1},{1,0},{2,3},{3,2},{4,5},{5,4},{6,7},{7,6},{8,9},{9,8},{10,11... | collective-permute-start | bytes 147464 | tf_op jit(solution)/shard_map/ppermute | solution.py:249
  9.6 0.8 %copy-start = (bf16[48,512]{1,0:T(8,128)(2,1)S(1)}, bf16[48,512]{1,0:T(8,128)(2,1)}, u32[]{:S(2)}) copy-start(bf16[48,512]{1,0:T(8,128)(2,1)} %whiten.1.refs_0_) | copy-start | bytes 147460
  11.3 3.3 %collective-permute-start.3 = (bf16[48,512]{1,0:T(8,128)(2,1)S(1)}, bf16[48,512]{1,0:T(8,128)(2,1)S(1)}, u32[]{:S(2)}, u32[]{:S(2)}) collective-permute-start(bf16[48,512]{1,0:T(8,128)(2,1)S(1)} %collective-permute-done.1.refs_0_), channel_id=1, source_target_pairs={{0,1},{1,0},{2,3},{3,2},{4,5},{5,4},{6,7},{7,6},{8,9},{9,8},{10,11... | collective-permute-start | bytes 147464 | tf_op jit(solution)/shard_map/ppermute | solution.py:249
  15.5 6.3 %collective-permute-start.7 = (bf16[80,256]{1,0:T(8,128)(2,1)S(1)}, bf16[80,256]{1,0:T(8,128)(2,1)S(1)}, u32[]{:S(2)}, u32[]{:S(2)}) collective-permute-start(bf16[80,256]{1,0:T(8,128)(2,1)S(1)} %get-tuple-element.16), channel_id=1, source_target_pairs={{0,8},{1,9},{2,10},{3,11},{4,12},{5,13},{6,14},{7,15},{8,0},{9,1},... | collective-permute-start | bytes 122888 | tf_op jit(solution)/shard_map/ppermute | solution.py:256
  18.8 0.7 %copy-start.1 = (s32[256]{0:T(256)S(1)}, s32[256]{0:T(256)}, u32[]{:S(2)}) copy-start(s32[256]{0:T(256)} %param.5) | copy-start | bytes 3076

commit v5 on v3

--- a/solution.py
+++ b/solution.py
@@ -96,8 +96,7 @@
             and self.half % GROUP == 0
             and self.channels % 16 == 0
             and self.windows * self.half % 16 == 0
-            and self.blk_size & (self.blk_size - 1) == 0
-            and 2 <= self.blk_size <= 8
+            and self.blk_size == 8
         )
 
 
@@ -117,24 +116,12 @@
         mean_power = jnp.mean(centered * centered, axis=1, keepdims=True)
         flag_values = flags_ref[window : window + 1, :].astype(jnp.float32).reshape(plan.half, 1)
         pieces.append(centered * lax.rsqrt(mean_power + 1e-05) * flag_values)
-    out_ref[...] = jnp.concatenate(pieces, axis=0).astype(jnp.bfloat16)
-
-
-def choose_kernel(plan, index_ref, after_ref, out_ref):
-    first = lax.axis_index("src") * plan.half
-    index = index_ref[...] - first
-    index = jnp.where(index < 0, index + plan.channels, index)
-    at_column = lax.broadcasted_iota(jnp.int32, (LANES, plan.source_count), 0)
-    chosen = jnp.zeros((LANES, plan.source_count), jnp.bool_)
-    for step in range(plan.coarse):
-        chosen = chosen | (at_column == index + step * plan.channels)
-    out_ref[...] = chosen.astype(jnp.float32).astype(jnp.bfloat16)
-
-
-def correlate_kernel(plan, *refs):
-    mine_refs = refs[: plan.near]
-    other_refs = refs[plan.near : 2 * plan.near]
-    kept_ref, sent_ref, rows_ref, toeplitz_ref, columns_ref = refs[2 * plan.near :]
+    whitened = jnp.concatenate(pieces, axis=0).astype(jnp.bfloat16)
+    for part in range(plan.near):
+        out_ref[part] = whitened
+
+
+def correlate_kernel(plan, mine_ref, other_ref, kept_ref, sent_ref, rows_ref, toeplitz_ref, columns_ref):
     span = plan.span
     me = lax.axis_index("blk")
     targets = [me, me ^ plan.near]
@@ -142,12 +129,12 @@
     if filled < LANES:
         columns_ref[filled:, :] = jnp.zeros((LANES - filled, columns_ref.shape[1]), jnp.bfloat16)
     filler = jnp.zeros((plan.channels, span - plan.segment), jnp.float32)
-    for hop in range(plan.near):
-        mine = mine_refs[hop][...].astype(jnp.float32)
-        other = other_refs[hop][...].astype(jnp.float32)
-        rows_ref[hop] = mine
+    for part in range(plan.near):
+        mine = mine_ref[part].astype(jnp.float32)
+        other = other_ref[part].astype(jnp.float32)
+        rows_ref[part] = mine
         for window in range(plan.windows):
-            start = (hop * plan.windows + window) * span
+            start = (part * plan.windows + window) * span
             at = slice(start, start + span)
             half = slice(window * plan.half, (window + 1) * plan.half)
             both = jnp.concatenate([mine[half], other[half]], axis=0)
@@ -158,8 +145,7 @@
             for place, target in enumerate(targets):
                 for member in range(plan.own):
                     channel = window * plan.half + target * plan.own + member
-                    row = rows_ref[hop, pl.ds(channel, 1), :]
-                    row = jnp.concatenate([row, filler[:1]], axis=1)
+                    row = jnp.concatenate([rows_ref[part, pl.ds(channel, 1), :], filler[:1]], axis=1)
                     row = jnp.broadcast_to(row, (GROUP, span))
                     pieces = [
                         pltpu.roll(row, (MAXLAG - plan.fine + 1 + lag) % span, 1, stride=1, stride_axis=0)
@@ -188,12 +174,7 @@
     kept_ref[...] = packed[0]
 
 
-def halves(values):
-    high = values.astype(jnp.bfloat16)
-    return high, (values - high.astype(jnp.float32)).astype(jnp.bfloat16)
-
-
-def expand_kernel(plan, chosen_ref, kept_ref, arrived_ref, out_ref):
+def order_matrix(plan):
     at_row = lax.broadcasted_iota(jnp.int32, (plan.height, plan.rows), 0)
     at_part = lax.broadcasted_iota(jnp.int32, (plan.height, plan.rows), 1)
     order = jnp.zeros((plan.height, plan.rows), jnp.bool_)
@@ -203,41 +184,66 @@
         tail = plan.own * plan.whole_groups + member * plan.rest + reverse - plan.whole_groups
         rest = (reverse >= plan.whole_groups) & (reverse < plan.fine) & (at_part == tail)
         order = order | whole | rest
-    order = order.astype(jnp.float32).astype(jnp.bfloat16)
-    total = (kept_ref[...] + arrived_ref[...].astype(jnp.float32)) * plan.norm_factor
-    ordered = [jnp.dot(order, part, preferred_element_type=jnp.float32) for part in halves(total)]
-    lane = lax.broadcasted_iota(jnp.int32, (plan.height, LANES), 1)
+    return order.astype(jnp.float32).astype(jnp.bfloat16)
+
+
+def inside_step(plan, step, values):
+    lane = lax.broadcasted_iota(jnp.int32, values.shape, 1)
+    inside = (lane >= step * plan.channels) & (lane < (step + 1) * plan.channels)
+    return jnp.where(inside, values, 0.0).astype(jnp.bfloat16)
+
+
+def prepare_kernel(plan, index_ref, kept_ref, order_ref, chosen_ref, base_ref):
+    first = lax.axis_index("src") * plan.half
+    index = index_ref[...] - first
+    index = jnp.where(index < 0, index + plan.channels, index)
+    at_column = lax.broadcasted_iota(jnp.int32, (LANES, plan.source_count), 0)
+    chosen = jnp.zeros((LANES, plan.source_count), jnp.bool_)
+    for step in range(plan.coarse):
+        chosen = chosen | (at_column == index + step * plan.channels)
+    chosen = chosen.astype(jnp.float32).astype(jnp.bfloat16)
+    chosen_ref[...] = chosen
+    order = order_matrix(plan)
+    order_ref[...] = order
+    kept = kept_ref[...] * plan.norm_factor
+    high = kept.astype(jnp.bfloat16)
+    low = (kept - high.astype(jnp.float32)).astype(jnp.bfloat16)
+    parts = [jnp.dot(order, part, preferred_element_type=jnp.float32) for part in (high, low)]
+    for step in range(plan.coarse):
+        base_ref[step] = sum(
+            jnp.dot(inside_step(plan, step, part), chosen, preferred_element_type=jnp.float32) for part in parts
+        )
+
+
+def expand_kernel(plan, order_ref, chosen_ref, base_ref, arrived_ref, out_hbm, out_ref, sems):
+    arrived = jnp.dot(order_ref[...], arrived_ref[...], preferred_element_type=jnp.float32)
     chosen = chosen_ref[...]
+    expanded = []
     for step in range(plan.coarse):
-        inside = (lane >= step * plan.channels) & (lane < (step + 1) * plan.channels)
-        expanded = jnp.zeros((plan.height, plan.source_count), jnp.float32)
-        for part in ordered:
-            kept = jnp.where(inside, part, 0.0).astype(jnp.bfloat16)
-            expanded += jnp.dot(kept, chosen, preferred_element_type=jnp.float32)
-        count = min(plan.fine, LAG_COUNT - step * plan.fine)
-        for member in range(plan.own):
-            out_ref[member, step * plan.fine : step * plan.fine + count, :] = expanded[
-                member * plan.fine_padded : member * plan.fine_padded + count
-            ]
+        moved = jnp.dot(inside_step(plan, step, arrived), chosen, preferred_element_type=jnp.float32)
+        expanded.append(base_ref[step] + moved * plan.norm_factor)
+    copies = []
+    for member in range(plan.own):
+        for step in range(plan.coarse):
+            start = step * plan.fine
+            count = min(plan.fine, LAG_COUNT - start)
+            first = member * plan.fine_padded
+            out_ref[member, start : start + count, :] = expanded[step][first : first + count]
+        copies.append(pltpu.make_async_copy(out_ref.at[member], out_hbm.at[member], sems.at[member]))
+        copies[-1].start()
+    for copy in copies:
+        copy.wait()
 
 
 def few_channels(plan, traces, valid_flags, source_index):
     vmem = pl.BlockSpec(memory_space=pltpu.VMEM)
-    anywhere = pl.BlockSpec(memory_space=pl.ANY)
     params = pltpu.CompilerParams(vmem_limit_bytes=32 * 1024 * 1024)
     packed_rows = plan.windows * plan.half
     flags = valid_flags.T
-
-    def swap_cores(array):
-        return lax.ppermute(array, "src", [(0, 1), (1, 0)])
-
-    def swap_blk(array, hop):
-        return lax.ppermute(array, "blk", [(place, place ^ hop) for place in range(plan.blk_size)])
-
-    whitened = pl.pallas_call(
+    copies = pl.pallas_call(
         functools.partial(whiten_kernel, plan),
-        out_shape=jax.ShapeDtypeStruct((packed_rows, plan.segment), jnp.bfloat16),
-        in_specs=[anywhere] * 2,
+        out_shape=jax.ShapeDtypeStruct((plan.near, packed_rows, plan.segment), jnp.bfloat16),
+        in_specs=[pl.BlockSpec(memory_space=pl.ANY)] * 2,
         out_specs=vmem,
         scratch_shapes=[
             pltpu.VMEM(traces.shape, jnp.float32),
@@ -247,16 +253,10 @@
         compiler_params=pltpu.CompilerParams(vmem_limit_bytes=60 * 1024 * 1024),
         name="whiten",
     )(traces, flags)
-    mine = [whitened] + [swap_blk(whitened, hop) for hop in range(1, plan.near)]
-    other = [swap_cores(array) for array in mine]
-    chosen = pl.pallas_call(
-        functools.partial(choose_kernel, plan),
-        out_shape=jax.ShapeDtypeStruct((LANES, plan.source_count), jnp.bfloat16),
-        in_specs=[vmem, pl.BlockSpec(memory_space=pl.ANY)],
-        out_specs=vmem,
-        compiler_params=params,
-        name="choose",
-    )(source_index.reshape(1, -1), whitened)
+    sides = [list(range(plan.near)), list(range(plan.near, plan.blk_size))]
+    mine = lax.all_to_all(copies, "blk", 0, 0, axis_index_groups=sides, tiled=True)
+    other = lax.ppermute(mine, "src", [(0, 1), (1, 0)])
+    height = 2 * plan.height
     width = plan.near * plan.windows * plan.span
     kept, sent = pl.pallas_call(
         functools.partial(correlate_kernel, plan),
@@ -264,25 +264,40 @@
             jax.ShapeDtypeStruct((plan.rows, LANES), jnp.float32),
             jax.ShapeDtypeStruct((plan.rows, LANES), jnp.bfloat16),
         ],
-        in_specs=[vmem] * (2 * plan.near),
+        in_specs=[vmem] * 2,
         out_specs=[vmem] * 2,
         scratch_shapes=[
             pltpu.VMEM((plan.near, packed_rows, plan.segment), jnp.float32),
-            pltpu.VMEM((2 * plan.height, width), jnp.bfloat16),
+            pltpu.VMEM((height, width), jnp.bfloat16),
             pltpu.VMEM((LANES, width), jnp.bfloat16),
         ],
         compiler_params=params,
         name="correlate",
-    )(*mine, *other)
-    arrived = swap_blk(sent, plan.near)
+    )(mine, other)
+    pairs = [(place, place ^ plan.near) for place in range(plan.blk_size)]
+    arrived = lax.ppermute(sent, "blk", pairs)
+    order, chosen, base = pl.pallas_call(
+        functools.partial(prepare_kernel, plan),
+        out_shape=[
+            jax.ShapeDtypeStruct((plan.height, plan.rows), jnp.bfloat16),
+            jax.ShapeDtypeStruct((LANES, plan.source_count), jnp.bfloat16),
+            jax.ShapeDtypeStruct((plan.coarse, plan.height, plan.source_count), jnp.float32),
+        ],
+        in_specs=[vmem] * 2,
+        out_specs=[vmem] * 3,
+        compiler_params=params,
+        name="prepare",
+    )(source_index.reshape(1, -1), kept)
+    out_shape = (plan.own, LAG_COUNT, plan.source_count)
     return pl.pallas_call(
         functools.partial(expand_kernel, plan),
-        out_shape=jax.ShapeDtypeStruct((plan.own, LAG_COUNT, plan.source_count), jnp.float32),
-        in_specs=[vmem] * 3,
-        out_specs=vmem,
+        out_shape=jax.ShapeDtypeStruct(out_shape, jnp.float32),
+        in_specs=[vmem] * 4,
+        out_specs=pl.BlockSpec(memory_space=pl.ANY),
+        scratch_shapes=[pltpu.VMEM(out_shape, jnp.float32), pltpu.SemaphoreType.DMA((plan.own,))],
         compiler_params=params,
         name="expand",
-    )(chosen, kept, arrived)
+    )(order, chosen, base, arrived)
 
 
 def body(traces, valid_flags, source_index):

time: 20.8 us -> 22.3 us (1.072)
  blocking collectives: 0 us -> 10.8 us
  waiting for transfers between devices: 7.86 us -> 3.06 us
  starting transfers between devices: 7.38 us -> 2.66 us
  Pallas kernels: 4.53 us -> 4.83 us
    all_to_all x0 -> x1, blocking collectives: none -> 10.8 us  [few_channels(): lax.all_to_all(copies, 'blk', 0, 0, axis_index_groups=sides, tiled=True)]
    ppermute x8 -> x2, waiting for transfers between devices: 7.86 us -> 3.06 us  [the longest x1 1.62 us: few_channels(): arrived = lax.ppermute(sent, 'blk', pairs)]
    ppermute x8 -> x2, starting transfers between devices: 7.38 us -> 2.66 us  [the longest x1 2.65 us: few_channels(): arrived = lax.ppermute(sent, 'blk', pairs)]
    pallas_call x1, Pallas kernels: 0.15 us -> 0.5 us  [few_channels(): pl.pallas_call(functools.partial(prepare_kernel, plan), out_shape=[jax.Sh...]
    unnamed x4 -> x2, local copies, waits for them, and re-layouts: 0.8 us -> 0.68 us
  transfers between devices with their start and end apart: 8 -> 2, of which waited for: 6 -> 2; matrix products, arithmetic and copies ran while one was open for 0% -> 0% of each run, Pallas kernels for 1% -> 2%
where the time goes in v5:
time: 22.3 us; the launch traced here: 22 us
  blocking collectives  10.8 us (48%)
  Pallas kernels  4.83 us (22%)
  waiting for transfers between devices  3.06 us (14%)
  starting transfers between devices  2.66 us (12%)
  local copies, waits for them, and re-layouts  0.68 us (3%)
    all_to_all x1, blocking collectives, few_channels(): lax.all_to_all(copies, 'blk', 0, 0, axis_index_groups=sides, tiled=True)  10.8 us
    ppermute x1, starting transfers between devices, few_channels(): arrived = lax.ppermute(sent, 'blk', pairs)  2.65 us
    pallas_call x1, Pallas kernels, few_channels(): pl.pallas_call(functools.partial(whiten_kernel, plan), out_shape=jax.Shap...  1.78 us
    ppermute x1, waiting for transfers between devices, few_channels(): arrived = lax.ppermute(sent, 'blk', pairs)  1.62 us
    pallas_call x1, Pallas kernels, few_channels(): pl.pallas_call(functools.partial(correlate_kernel, plan), out_shape=[jax....  1.45 us
    ppermute x1, waiting for transfers between devices, few_channels(): other = lax.ppermute(mine, 'src', [(0, 1), (1, 0)])  1.44 us
    pallas_call x1, Pallas kernels, few_channels(): pl.pallas_call(functools.partial(expand_kernel, plan), out_shape=jax.Shap...  1.11 us
    unnamed x2, local copies, waits for them, and re-layouts  0.68 us
  transfers between devices with their start and end apart: 2, of which 2 were waited for; matrix products, arithmetic and copies ran while one was open for 0% of the time, Pallas kernels for 2%

profile of v5, /device:TPU:0, one launch (start us, length us, event | category | flops | bytes accessed | tf_op | source)
XLA Modules:
  0.0 22.0 jit_solution(3691924854019006239)
XLA Ops:
  0.0 1.8 %whiten.1 = bf16[4,48,512]{2,1,0:T(8,128)(2,1)} custom-call(f32[24,2,512]{2,1,0:T(2,128)} %traces_hbm.1, s32[2,24]{1,0:T(2,128)} %bitcast.3), custom_call_target="tpu_custom_call" | custom-call | tf_op jit(solution)/shard_map/whiten/pallas_call | solution.py:243
  1.8 10.8 %all_to_all.5.mine_ref = bf16[4,48,512]{2,1,0:T(8,128)(2,1)S(1)} all-to-all(bf16[4,48,512]{2,1,0:T(8,128)(2,1)} %whiten.1), channel_id=1, replica_groups={{0,2,4,6},{8,10,12,14},{1,3,5,7},{9,11,13,15},{16,18,20,22},{24,26,28,3..., dimensions={0} | all-to-all | bytes 393216 | tf_op jit(solution)/shard_map/all_to_all | solution.py:257
  12.6 0.0 collective-permute-start
  12.6 1.4 %collective-permute-done.other_ref = bf16[4,48,512]{2,1,0:T(8,128)(2,1)S(1)} collective-permute-done((bf16[4,48,512]{2,1,0:T(8,128)(2,1)S(1)}, bf16[4,48,512]{2,1,0:T(8,128)(2,1)S(1)}, u32[]{:S(2)}, u32[]{:S(2)}) %collective-permute-start) | collective-permute-done | bytes 196640 | tf_op jit(solution)/shard_map/ppermute | solution.py:258
  14.0 1.4 %correlate.1 = (f32[80,256]{1,0:T(8,128)S(1)}, bf16[80,256]{1,0:T(8,128)(2,1)S(1)}) custom-call(bf16[4,48,512]{2,1,0:T(8,128)(2,1)S(1)} %all_to_all.5.mine_ref, bf16[4,48,512]{2,1,0:T(8,128)(2,1)S(1)} %collective-permute-done.other_ref), custom_call_target="tpu_custom_call" | custom-call | tf_op jit(solution)/shard_map/correlate/pallas_call | solution.py:261
  15.5 2.7 %collective-permute-start.1 = (bf16[80,256]{1,0:T(8,128)(2,1)S(1)}, bf16[80,256]{1,0:T(8,128)(2,1)S(1)}, u32[]{:S(2)}, u32[]{:S(2)}) collective-permute-start(bf16[80,256]{1,0:T(8,128)(2,1)S(1)} %get-tuple-element.14), channel_id=1, source_target_pairs={{0,8},{2,10},{4,12},{6,14},{8,0},{10,2},{12,4},{14,6},{1,9},{3,11}... | collective-permute-start | bytes 122888 | tf_op jit(solution)/shard_map/ppermute | solution.py:278
  18.1 0.0 copy-start
  18.1 0.7 %copy-done = s32[256]{0:T(256)S(1)} copy-done((s32[256]{0:T(256)S(1)}, s32[256]{0:T(256)}, u32[]{:S(2)}) %copy-start) | copy-done | bytes 1048
  18.8 0.5 %prepare.1 = (bf16[96,80]{1,0:T(8,128)(2,1)S(1)}, bf16[256,256]{1,0:T(8,128)(2,1)S(1)}, f32[5,96,256]{2,1,0:T(8,128)S(1)}) custom-call(s32[1,256]{1,0:T(1,128)S(1)} %bitcast.2, f32[80,256]{1,0:T(8,128)S(1)} %get-tuple-element.10.kept_ref), custom_call_target="tpu_custom_call" | custom-call | tf_op jit(solution)/shard_map/prepare/pallas_call | solution.py:279
  19.3 1.6 %collective-permute-done.1.arrived_ref = bf16[80,256]{1,0:T(8,128)(2,1)S(1)} collective-permute-done((bf16[80,256]{1,0:T(8,128)(2,1)S(1)}, bf16[80,256]{1,0:T(8,128)(2,1)S(1)}, u32[]{:S(2)}, u32[]{:S(2)}) %collective-permute-start.1) | collective-permute-done | bytes 40992 | tf_op jit(solution)/shard_map/ppermute | solution.py:278
  20.9 1.1 %expand.1 = f32[3,129,256]{2,1,0:T(8,128)} custom-call(bf16[96,80]{1,0:T(8,128)(2,1)S(1)} %get-tuple-element.11.order_ref, bf16[256,256]{1,0:T(8,128)(2,1)S(1)} %get-tuple-element.12.chosen_ref, f32[5,96,256]{2,1,0:T(8,128)S(1)} %get-tuple-element.13.base_ref, bf16[80,256]{1,0:T(8,128)(2,1)S(1)} %collective-permute-done.1.arrived_ref), custom_call_target="tpu_custom_call" | custom-call | tf_op jit(solution)/shard_map/expand/pallas_call | solution.py:292
Async XLA Ops:
  12.6 1.4 %collective-permute-start = (bf16[4,48,512]{2,1,0:T(8,128)(2,1)S(1)}, bf16[4,48,512]{2,1,0:T(8,128)(2,1)S(1)}, u32[]{:S(2)}, u32[]{:S(2)}) collective-permute-start(bf16[4,48,512]{2,1,0:T(8,128)(2,1)S(1)} %all_to_all.5.mine_ref), channel_id=1, source_target_pairs={{0,1},{1,0},{2,3},{3,2},{4,5},{5,4},{6,7},{7,6},{8,9},{9,8},{10,11... | collective-permute-start | bytes 589832 | tf_op jit(solution)/shard_map/ppermute | solution.py:258
  15.5 5.5 %collective-permute-start.1 = (bf16[80,256]{1,0:T(8,128)(2,1)S(1)}, bf16[80,256]{1,0:T(8,128)(2,1)S(1)}, u32[]{:S(2)}, u32[]{:S(2)}) collective-permute-start(bf16[80,256]{1,0:T(8,128)(2,1)S(1)} %get-tuple-element.14), channel_id=1, source_target_pairs={{0,8},{2,10},{4,12},{6,14},{8,0},{10,2},{12,4},{14,6},{1,9},{3,11}... | collective-permute-start | bytes 122888 | tf_op jit(solution)/shard_map/ppermute | solution.py:278
  18.1 0.7 %copy-start = (s32[256]{0:T(256)S(1)}, s32[256]{0:T(256)}, u32[]{:S(2)}) copy-start(s32[256]{0:T(256)} %param.5) | copy-start | bytes 3076

commit v6 on v5

--- a/solution.py
+++ b/solution.py
@@ -85,7 +85,8 @@
         rows = self.own * self.fine
         self.rows = -(-rows // 16) * 16
         self.height = self.own * self.fine_padded
-        self.near = blk_size // 2
+        self.columns = 2
+        self.targets = blk_size // self.columns
         self.norm_factor = 1.0 / math.sqrt(windows * blk_size * segment)
 
     def fits(self):
@@ -116,62 +117,64 @@
         mean_power = jnp.mean(centered * centered, axis=1, keepdims=True)
         flag_values = flags_ref[window : window + 1, :].astype(jnp.float32).reshape(plan.half, 1)
         pieces.append(centered * lax.rsqrt(mean_power + 1e-05) * flag_values)
-    whitened = jnp.concatenate(pieces, axis=0).astype(jnp.bfloat16)
-    for part in range(plan.near):
-        out_ref[part] = whitened
-
-
-def correlate_kernel(plan, mine_ref, other_ref, kept_ref, sent_ref, rows_ref, toeplitz_ref, columns_ref):
+    out_ref[...] = jnp.concatenate(pieces, axis=0).astype(jnp.bfloat16)
+
+
+def correlate_kernel(plan, last, mine_ref, other_ref, *refs):
+    if last:
+        prior_ref, *out_refs, rows_ref, toeplitz_ref, columns_ref = refs
+    else:
+        sum_ref, rows_ref, toeplitz_ref, columns_ref = refs
     span = plan.span
     me = lax.axis_index("blk")
-    targets = [me, me ^ plan.near]
     filled = plan.coarse * plan.channels
     if filled < LANES:
         columns_ref[filled:, :] = jnp.zeros((LANES - filled, columns_ref.shape[1]), jnp.bfloat16)
     filler = jnp.zeros((plan.channels, span - plan.segment), jnp.float32)
-    for part in range(plan.near):
-        mine = mine_ref[part].astype(jnp.float32)
-        other = other_ref[part].astype(jnp.float32)
-        rows_ref[part] = mine
-        for window in range(plan.windows):
-            start = (part * plan.windows + window) * span
-            at = slice(start, start + span)
-            half = slice(window * plan.half, (window + 1) * plan.half)
-            both = jnp.concatenate([mine[half], other[half]], axis=0)
-            both = jnp.concatenate([both, filler], axis=1)
-            for step in range(plan.coarse):
-                moved = pltpu.roll(both, step * plan.fine, 1) if step else both
-                columns_ref[step * plan.channels : (step + 1) * plan.channels, at] = moved.astype(jnp.bfloat16)
-            for place, target in enumerate(targets):
-                for member in range(plan.own):
-                    channel = window * plan.half + target * plan.own + member
-                    row = jnp.concatenate([rows_ref[part, pl.ds(channel, 1), :], filler[:1]], axis=1)
-                    row = jnp.broadcast_to(row, (GROUP, span))
-                    pieces = [
-                        pltpu.roll(row, (MAXLAG - plan.fine + 1 + lag) % span, 1, stride=1, stride_axis=0)
-                        for lag in range(0, plan.fine_padded, GROUP)
-                    ]
-                    first = place * plan.height + member * plan.fine_padded
-                    toeplitz_ref[first : first + plan.fine_padded, at] = jnp.concatenate(pieces, axis=0).astype(
-                        jnp.bfloat16
-                    )
+    mine = mine_ref[...].astype(jnp.float32)
+    other = other_ref[...].astype(jnp.float32)
+    rows_ref[...] = mine
+    for window in range(plan.windows):
+        at = slice(window * span, (window + 1) * span)
+        half = slice(window * plan.half, (window + 1) * plan.half)
+        both = jnp.concatenate([mine[half], other[half]], axis=0)
+        both = jnp.concatenate([both, filler], axis=1)
+        for step in range(plan.coarse):
+            moved = pltpu.roll(both, step * plan.fine, 1) if step else both
+            columns_ref[step * plan.channels : (step + 1) * plan.channels, at] = moved.astype(jnp.bfloat16)
+        for hop in range(plan.targets):
+            target = me ^ (hop * plan.columns)
+            for member in range(plan.own):
+                channel = window * plan.half + target * plan.own + member
+                row = jnp.concatenate([rows_ref[pl.ds(channel, 1), :], filler[:1]], axis=1)
+                row = jnp.broadcast_to(row, (GROUP, span))
+                pieces = [
+                    pltpu.roll(row, (MAXLAG - plan.fine + 1 + lag) % span, 1, stride=1, stride_axis=0)
+                    for lag in range(0, plan.fine_padded, GROUP)
+                ]
+                first = hop * plan.height + member * plan.fine_padded
+                toeplitz_ref[first : first + plan.fine_padded, at] = jnp.concatenate(pieces, axis=0).astype(
+                    jnp.bfloat16
+                )
     products = lax.dot_general(
         toeplitz_ref[...],
         columns_ref[...],
         (((1,), (1,)), ((), ())),
         preferred_element_type=jnp.float32,
-    ).reshape(len(targets), plan.own, plan.fine_padded, LANES)
-    packed = []
-    for place in range(len(targets)):
-        part = products[place]
+    )
+    if not last:
+        sum_ref[...] = products
+        return
+    products = (products + prior_ref[...]).reshape(plan.targets, plan.own, plan.fine_padded, LANES)
+    for hop in range(plan.targets):
+        part = products[hop]
         pieces = [part[member, : plan.whole_groups] for member in range(plan.own)]
         if plan.rest:
             pieces += [part[member, plan.whole_groups : plan.fine] for member in range(plan.own)]
         if plan.rows > plan.own * plan.fine:
             pieces.append(jnp.zeros((plan.rows - plan.own * plan.fine, LANES), jnp.float32))
-        packed.append(jnp.concatenate(pieces, axis=0))
-    sent_ref[...] = packed[1].astype(jnp.bfloat16)
-    kept_ref[...] = packed[0]
+        packed = jnp.concatenate(pieces, axis=0)
+        out_refs[hop][...] = packed.astype(out_refs[hop].dtype)
 
 
 def order_matrix(plan):
@@ -215,12 +218,18 @@
         )
 
 
-def expand_kernel(plan, order_ref, chosen_ref, base_ref, arrived_ref, out_hbm, out_ref, sems):
-    arrived = jnp.dot(order_ref[...], arrived_ref[...], preferred_element_type=jnp.float32)
+def expand_kernel(plan, order_ref, chosen_ref, base_ref, *refs):
+    *arrived_refs, out_hbm, out_ref, sems = refs
+    order = order_ref[...]
+    arrived = sum(jnp.dot(order, ref[...], preferred_element_type=jnp.float32) for ref in arrived_refs)
+    high = arrived.astype(jnp.bfloat16).astype(jnp.float32)
     chosen = chosen_ref[...]
     expanded = []
     for step in range(plan.coarse):
-        moved = jnp.dot(inside_step(plan, step, arrived), chosen, preferred_element_type=jnp.float32)
+        moved = sum(
+            jnp.dot(inside_step(plan, step, part), chosen, preferred_element_type=jnp.float32)
+            for part in (high, arrived - high)
+        )
         expanded.append(base_ref[step] + moved * plan.norm_factor)
     copies = []
     for member in range(plan.own):
@@ -240,9 +249,16 @@
     params = pltpu.CompilerParams(vmem_limit_bytes=32 * 1024 * 1024)
     packed_rows = plan.windows * plan.half
     flags = valid_flags.T
-    copies = pl.pallas_call(
+
+    def swap_cores(array):
+        return lax.ppermute(array, "src", [(0, 1), (1, 0)])
+
+    def swap_blk(array, hop):
+        return lax.ppermute(array, "blk", [(place, place ^ hop) for place in range(plan.blk_size)])
+
+    whitened = pl.pallas_call(
         functools.partial(whiten_kernel, plan),
-        out_shape=jax.ShapeDtypeStruct((plan.near, packed_rows, plan.segment), jnp.bfloat16),
+        out_shape=jax.ShapeDtypeStruct((packed_rows, plan.segment), jnp.bfloat16),
         in_specs=[pl.BlockSpec(memory_space=pl.ANY)] * 2,
         out_specs=vmem,
         scratch_shapes=[
@@ -253,29 +269,41 @@
         compiler_params=pltpu.CompilerParams(vmem_limit_bytes=60 * 1024 * 1024),
         name="whiten",
     )(traces, flags)
-    sides = [list(range(plan.near)), list(range(plan.near, plan.blk_size))]
-    mine = lax.all_to_all(copies, "blk", 0, 0, axis_index_groups=sides, tiled=True)
-    other = lax.ppermute(mine, "src", [(0, 1), (1, 0)])
-    height = 2 * plan.height
-    width = plan.near * plan.windows * plan.span
-    kept, sent = pl.pallas_call(
-        functools.partial(correlate_kernel, plan),
-        out_shape=[
-            jax.ShapeDtypeStruct((plan.rows, LANES), jnp.float32),
-            jax.ShapeDtypeStruct((plan.rows, LANES), jnp.bfloat16),
-        ],
-        in_specs=[vmem] * 2,
-        out_specs=[vmem] * 2,
-        scratch_shapes=[
-            pltpu.VMEM((plan.near, packed_rows, plan.segment), jnp.float32),
-            pltpu.VMEM((height, width), jnp.bfloat16),
-            pltpu.VMEM((LANES, width), jnp.bfloat16),
-        ],
-        compiler_params=params,
-        name="correlate",
-    )(mine, other)
-    pairs = [(place, place ^ plan.near) for place in range(plan.blk_size)]
-    arrived = lax.ppermute(sent, "blk", pairs)
+
+    height = plan.targets * plan.height
+    width = plan.windows * plan.span
+
+    def correlate(mine, other, prior=None):
+        last = prior is not None
+        if last:
+            types = [jnp.float32] + [jnp.bfloat16] * (plan.targets - 1)
+            shapes = [jax.ShapeDtypeStruct((plan.rows, LANES), dtype) for dtype in types]
+        else:
+            shapes = [jax.ShapeDtypeStruct((height, LANES), jnp.float32)]
+        operands = [mine, other] + ([prior] if last else [])
+        results = pl.pallas_call(
+            functools.partial(correlate_kernel, plan, last),
+            out_shape=shapes,
+            in_specs=[vmem] * len(operands),
+            out_specs=[vmem] * len(shapes),
+            scratch_shapes=[
+                pltpu.VMEM((packed_rows, plan.segment), jnp.float32),
+                pltpu.VMEM((height, width), jnp.bfloat16),
+                pltpu.VMEM((LANES, width), jnp.bfloat16),
+            ],
+            compiler_params=params,
+            cost_estimate=pl.CostEstimate(
+                flops=2 * height * width * LANES, bytes_accessed=4 * packed_rows * plan.segment, transcendentals=0
+            ),
+            name="correlate",
+        )(*operands)
+        return results if last else results[0]
+
+    beside = swap_blk(whitened, 1)
+    total = correlate(whitened, swap_cores(whitened))
+    beside, total = lax.optimization_barrier((beside, total))
+    kept, *sent = correlate(beside, swap_cores(beside), total)
+    arrived = [swap_blk(sent[hop - 1], hop * plan.columns) for hop in reversed(range(1, plan.targets))]
     order, chosen, base = pl.pallas_call(
         functools.partial(prepare_kernel, plan),
         out_shape=[
@@ -292,12 +320,12 @@
     return pl.pallas_call(
         functools.partial(expand_kernel, plan),
         out_shape=jax.ShapeDtypeStruct(out_shape, jnp.float32),
-        in_specs=[vmem] * 4,
+        in_specs=[vmem] * (3 + len(arrived)),
         out_specs=pl.BlockSpec(memory_space=pl.ANY),
         scratch_shapes=[pltpu.VMEM(out_shape, jnp.float32), pltpu.SemaphoreType.DMA((plan.own,))],
         compiler_params=params,
         name="expand",
-    )(order, chosen, base, arrived)
+    )(order, chosen, base, *arrived)
 
 
 def body(traces, valid_flags, source_index):

time: 22.3 us -> 19.6 us (0.88)
  blocking collectives: 10.8 us -> 0 us
  starting transfers between devices: 2.66 us -> 7.66 us
  waiting for transfers between devices: 3.06 us -> 5.39 us
  local copies, waits for them, and re-layouts: 0.68 us -> 1.51 us
    all_to_all x1 -> x0, blocking collectives: 10.8 us -> none  [few_channels(): lax.all_to_all(copies, 'blk', 0, 0, axis_index_groups=sides, tiled=True)]
    ppermute x2 -> x6, starting transfers between devices: 2.66 us -> 7.66 us  [the longest x4 7.14 us: swap_blk(): lax.ppermute(array, 'blk', [(place, place ^ hop) for place in range(plan....]
    ppermute x2 -> x6, waiting for transfers between devices: 3.06 us -> 5.39 us  [the longest x4 4.16 us: swap_blk(): lax.ppermute(array, 'blk', [(place, place ^ hop) for place in range(plan....]
    unnamed x2 -> x4, local copies, waits for them, and re-layouts: 0.68 us -> 1.51 us
    pallas_call x1 -> x2, Pallas kernels: 1.45 us -> 1.26 us  [correlate(): pl.pallas_call(functools.partial(correlate_kernel, plan, last), out_shape...]
  transfers between devices with their start and end apart: 2 -> 6, of which waited for: 2 -> 4; matrix products, arithmetic and copies ran while one was open for 0% -> 0% of each run, Pallas kernels for 2% -> 6%
where the time goes in v6:
time: 19.6 us; the launch traced here: 19.4 us
  starting transfers between devices  7.66 us (39%)
  waiting for transfers between devices  5.39 us (27%)
  Pallas kernels  4.77 us (24%)
  local copies, waits for them, and re-layouts  1.51 us (8%)
    ppermute x4, starting transfers between devices, swap_blk(): lax.ppermute(array, 'blk', [(place, place ^ hop) for place in range(plan....  7.14 us
    ppermute x4, waiting for transfers between devices, swap_blk(): lax.ppermute(array, 'blk', [(place, place ^ hop) for place in range(plan....  4.16 us
    pallas_call x1, Pallas kernels, few_channels(): pl.pallas_call(functools.partial(whiten_kernel, plan), out_shape=jax.Shap...  1.72 us
    unnamed x4, local copies, waits for them, and re-layouts  1.51 us
    pallas_call x1, Pallas kernels, few_channels(): pl.pallas_call(functools.partial(expand_kernel, plan), out_shape=jax.Shap...  1.29 us
    pallas_call x2, Pallas kernels, correlate(): pl.pallas_call(functools.partial(correlate_kernel, plan, last), out_shape...  1.26 us
    ppermute x2, waiting for transfers between devices, swap_cores(): return lax.ppermute(array, 'src', [(0, 1), (1, 0)])  1.23 us
    ppermute x2, starting transfers between devices, swap_cores(): return lax.ppermute(array, 'src', [(0, 1), (1, 0)])  0.52 us
  transfers between devices with their start and end apart: 6, of which 4 were waited for; matrix products, arithmetic and copies ran while one was open for 0% of the time, Pallas kernels for 6%

profile of v6, /device:TPU:0, one launch (start us, length us, event | category | flops | bytes accessed | tf_op | source)
XLA Modules:
  0.0 19.4 jit_solution(18422179534921682295)
XLA Ops:
  0.0 1.7 %whiten.1.mine_ref = bf16[48,512]{1,0:T(8,128)(2,1)} custom-call(f32[24,2,512]{2,1,0:T(2,128)} %traces_hbm.1, s32[2,24]{1,0:T(2,128)} %bitcast.3), custom_call_target="tpu_custom_call" | custom-call | tf_op jit(solution)/shard_map/whiten/pallas_call | solution.py:259
  1.7 0.5 %collective-permute-start.1 = (bf16[48,512]{1,0:T(8,128)(2,1)}, bf16[48,512]{1,0:T(8,128)(2,1)S(1)}, u32[]{:S(2)}, u32[]{:S(2)}) collective-permute-start(bf16[48,512]{1,0:T(8,128)(2,1)} %whiten.1.mine_ref), channel_id=1, source_target_pairs={{0,1},{1,0},{2,3},{3,2},{4,5},{5,4},{6,7},{7,6},{8,9},{9,8},{10,11... | collective-permute-start | bytes 147464 | tf_op jit(solution)/shard_map/ppermute | solution.py:254
  2.2 2.6 %collective-permute-start = (bf16[48,512]{1,0:T(8,128)(2,1)}, bf16[48,512]{1,0:T(8,128)(2,1)S(1)}, u32[]{:S(2)}, u32[]{:S(2)}) collective-permute-start(bf16[48,512]{1,0:T(8,128)(2,1)} %whiten.1.mine_ref), channel_id=1, source_target_pairs={{0,2},{2,0},{4,6},{6,4},{8,10},{10,8},{12,14},{14,12},{1,3},{3,1},... | collective-permute-start | bytes 147464 | tf_op jit(solution)/shard_map/ppermute | solution.py:257
  4.8 0.0 collective-permute-done.1.other_ref
  4.8 0.0 copy-start
  4.8 0.8 %copy-done = bf16[48,512]{1,0:T(8,128)(2,1)S(1)} copy-done((bf16[48,512]{1,0:T(8,128)(2,1)S(1)}, bf16[48,512]{1,0:T(8,128)(2,1)}, u32[]{:S(2)}) %copy-start) | copy-done | bytes 49176
  5.6 0.6 %correlate.2.refs_0_ = f32[384,256]{1,0:T(8,128)S(1)} custom-call(bf16[48,512]{1,0:T(8,128)(2,1)S(1)} %copy-done, bf16[48,512]{1,0:T(8,128)(2,1)S(1)} %collective-permute-done.1.other_ref), custom_call_target="tpu_custom_call" | custom-call | flops 251658240 | bytes 98304 | tf_op jit(solution)/shard_map/correlate/pallas_call | solution.py:284
  6.3 1.1 %collective-permute-done.mine_ref = bf16[48,512]{1,0:T(8,128)(2,1)S(1)} collective-permute-done((bf16[48,512]{1,0:T(8,128)(2,1)}, bf16[48,512]{1,0:T(8,128)(2,1)S(1)}, u32[]{:S(2)}, u32[]{:S(2)}) %collective-permute-start) | collective-permute-done | bytes 49184 | tf_op jit(solution)/shard_map/ppermute | solution.py:257
  7.4 0.0 collective-permute-start.2
  7.4 1.2 %collective-permute-done.2.other_ref = bf16[48,512]{1,0:T(8,128)(2,1)S(1)} collective-permute-done((bf16[48,512]{1,0:T(8,128)(2,1)S(1)}, bf16[48,512]{1,0:T(8,128)(2,1)S(1)}, u32[]{:S(2)}, u32[]{:S(2)}) %collective-permute-start.2) | collective-permute-done | bytes 49184 | tf_op jit(solution)/shard_map/ppermute | solution.py:254
  8.6 0.6 %correlate.3 = (f32[80,256]{1,0:T(8,128)S(1)}, bf16[80,256]{1,0:T(8,128)(2,1)S(1)}, bf16[80,256]{1,0:T(8,128)(2,1)S(1)}, bf16[80,256]{1,0:T(8,128)(2,1)S(1)}) custom-call(bf16[48,512]{1,0:T(8,128)(2,1)S(1)} %collective-permute-done.mine_ref, bf16[48,512]{1,0:T(8,128)(2,1)S(1)} %collective-permute-done.2.other_ref, f32[384,256]{1,0:T(8,128)S(1)} %correlate.2.refs_0_), custom_call_target="tpu_custom_call" | custom-call | flops 251658240 | bytes 98304 | tf_op jit(solution)/shard_map/correlate/pallas_call | solution.py:284
  9.2 3.9 %collective-permute-start.3 = (bf16[80,256]{1,0:T(8,128)(2,1)S(1)}, bf16[80,256]{1,0:T(8,128)(2,1)S(1)}, u32[]{:S(2)}, u32[]{:S(2)}) collective-permute-start(bf16[80,256]{1,0:T(8,128)(2,1)S(1)} %get-tuple-element.20), channel_id=1, source_target_pairs={{0,12},{2,14},{4,8},{6,10},{8,4},{10,6},{12,0},{14,2},{1,13},{3,15... | collective-permute-start | bytes 122888 | tf_op jit(solution)/shard_map/ppermute | solution.py:257
  13.2 0.0 collective-permute-start.4
  13.2 0.6 %collective-permute-start.5 = (bf16[80,256]{1,0:T(8,128)(2,1)S(1)}, bf16[80,256]{1,0:T(8,128)(2,1)S(1)}, u32[]{:S(2)}, u32[]{:S(2)}) collective-permute-start(bf16[80,256]{1,0:T(8,128)(2,1)S(1)} %get-tuple-element.22), channel_id=1, source_target_pairs={{0,4},{2,6},{4,0},{6,2},{8,12},{10,14},{12,8},{14,10},{1,5},{3,7},... | collective-permute-start | bytes 122888 | tf_op jit(solution)/shard_map/ppermute | solution.py:257
  13.8 0.0 copy-start.1
  13.8 0.7 %copy-done.1 = s32[256]{0:T(256)S(1)} copy-done((s32[256]{0:T(256)S(1)}, s32[256]{0:T(256)}, u32[]{:S(2)}) %copy-start.1) | copy-done | bytes 1048
  14.5 0.5 %prepare.1 = (bf16[96,80]{1,0:T(8,128)(2,1)S(1)}, bf16[256,256]{1,0:T(8,128)(2,1)S(1)}, f32[5,96,256]{2,1,0:T(8,128)S(1)}) custom-call(s32[1,256]{1,0:T(1,128)S(1)} %bitcast.2, f32[80,256]{1,0:T(8,128)S(1)} %get-tuple-element.16.kept_ref), custom_call_target="tpu_custom_call" | custom-call | tf_op jit(solution)/shard_map/prepare/pallas_call | solution.py:307
  15.0 0.2 %collective-permute-done.3.refs_0_ = bf16[80,256]{1,0:T(8,128)(2,1)S(1)} collective-permute-done((bf16[80,256]{1,0:T(8,128)(2,1)S(1)}, bf16[80,256]{1,0:T(8,128)(2,1)S(1)}, u32[]{:S(2)}, u32[]{:S(2)}) %collective-permute-start.3) | collective-permute-done | bytes 40992 | tf_op jit(solution)/shard_map/ppermute | solution.py:257
  15.2 2.9 %collective-permute-done.4.refs_1_ = bf16[80,256]{1,0:T(8,128)(2,1)S(1)} collective-permute-done((bf16[80,256]{1,0:T(8,128)(2,1)S(1)}, bf16[80,256]{1,0:T(8,128)(2,1)S(1)}, u32[]{:S(2)}, u32[]{:S(2)}) %collective-permute-start.4) | collective-permute-done | bytes 40992 | tf_op jit(solution)/shard_map/ppermute | solution.py:257
  18.1 0.0 collective-permute-done.5.refs_2_
  18.1 1.3 %expand.1 = f32[3,129,256]{2,1,0:T(8,128)} custom-call(bf16[96,80]{1,0:T(8,128)(2,1)S(1)} %get-tuple-element.17.order_ref, bf16[256,256]{1,0:T(8,128)(2,1)S(1)} %get-tuple-element.18.chosen_ref, f32[5,96,256]{2,1,0:T(8,128)S(1)} %get-tuple-element.19.base_ref, bf16[80,256]{1,0:T(8,128)(2,1)S(1)} %collective-permute-done.3.refs_0_, ...), custom_call_target="tpu_custom_call" | custom-call | tf_op jit(solution)/shard_map/expand/pallas_call | solution.py:320
Async XLA Ops:
  1.7 3.1 %collective-permute-start.1 = (bf16[48,512]{1,0:T(8,128)(2,1)}, bf16[48,512]{1,0:T(8,128)(2,1)S(1)}, u32[]{:S(2)}, u32[]{:S(2)}) collective-permute-start(bf16[48,512]{1,0:T(8,128)(2,1)} %whiten.1.mine_ref), channel_id=1, source_target_pairs={{0,1},{1,0},{2,3},{3,2},{4,5},{5,4},{6,7},{7,6},{8,9},{9,8},{10,11... | collective-permute-start | bytes 147464 | tf_op jit(solution)/shard_map/ppermute | solution.py:254
  2.2 5.1 %collective-permute-start = (bf16[48,512]{1,0:T(8,128)(2,1)}, bf16[48,512]{1,0:T(8,128)(2,1)S(1)}, u32[]{:S(2)}, u32[]{:S(2)}) collective-permute-start(bf16[48,512]{1,0:T(8,128)(2,1)} %whiten.1.mine_ref), channel_id=1, source_target_pairs={{0,2},{2,0},{4,6},{6,4},{8,10},{10,8},{12,14},{14,12},{1,3},{3,1},... | collective-permute-start | bytes 147464 | tf_op jit(solution)/shard_map/ppermute | solution.py:257
  4.8 0.8 %copy-start = (bf16[48,512]{1,0:T(8,128)(2,1)S(1)}, bf16[48,512]{1,0:T(8,128)(2,1)}, u32[]{:S(2)}) copy-start(bf16[48,512]{1,0:T(8,128)(2,1)} %whiten.1.mine_ref) | copy-start | bytes 147460
  7.4 1.2 %collective-permute-start.2 = (bf16[48,512]{1,0:T(8,128)(2,1)S(1)}, bf16[48,512]{1,0:T(8,128)(2,1)S(1)}, u32[]{:S(2)}, u32[]{:S(2)}) collective-permute-start(bf16[48,512]{1,0:T(8,128)(2,1)S(1)} %collective-permute-done.mine_ref), channel_id=1, source_target_pairs={{0,1},{1,0},{2,3},{3,2},{4,5},{5,4},{6,7},{7,6},{8,9},{9,8},{10,11... | collective-permute-start | bytes 147464 | tf_op jit(solution)/shard_map/ppermute | solution.py:254
  9.2 6.0 %collective-permute-start.3 = (bf16[80,256]{1,0:T(8,128)(2,1)S(1)}, bf16[80,256]{1,0:T(8,128)(2,1)S(1)}, u32[]{:S(2)}, u32[]{:S(2)}) collective-permute-start(bf16[80,256]{1,0:T(8,128)(2,1)S(1)} %get-tuple-element.20), channel_id=1, source_target_pairs={{0,12},{2,14},{4,8},{6,10},{8,4},{10,6},{12,0},{14,2},{1,13},{3,15... | collective-permute-start | bytes 122888 | tf_op jit(solution)/shard_map/ppermute | solution.py:257
  13.2 4.9 %collective-permute-start.4 = (bf16[80,256]{1,0:T(8,128)(2,1)S(1)}, bf16[80,256]{1,0:T(8,128)(2,1)S(1)}, u32[]{:S(2)}, u32[]{:S(2)}) collective-permute-start(bf16[80,256]{1,0:T(8,128)(2,1)S(1)} %get-tuple-element.21), channel_id=1, source_target_pairs={{0,8},{2,10},{4,12},{6,14},{8,0},{10,2},{12,4},{14,6},{1,9},{3,11}... | collective-permute-start | bytes 122888 | tf_op jit(solution)/shard_map/ppermute | solution.py:257
  13.2 4.9 %collective-permute-start.5 = (bf16[80,256]{1,0:T(8,128)(2,1)S(1)}, bf16[80,256]{1,0:T(8,128)(2,1)S(1)}, u32[]{:S(2)}, u32[]{:S(2)}) collective-permute-start(bf16[80,256]{1,0:T(8,128)(2,1)S(1)} %get-tuple-element.22), channel_id=1, source_target_pairs={{0,4},{2,6},{4,0},{6,2},{8,12},{10,14},{12,8},{14,10},{1,5},{3,7},... | collective-permute-start | bytes 122888 | tf_op jit(solution)/shard_map/ppermute | solution.py:257
  13.8 0.7 %copy-start.1 = (s32[256]{0:T(256)S(1)}, s32[256]{0:T(256)}, u32[]{:S(2)}) copy-start(s32[256]{0:T(256)} %param.5) | copy-start | bytes 3076

commit v7 on v6

--- a/solution.py
+++ b/solution.py
@@ -258,7 +258,7 @@
 
     whitened = pl.pallas_call(
         functools.partial(whiten_kernel, plan),
-        out_shape=jax.ShapeDtypeStruct((packed_rows, plan.segment), jnp.bfloat16),
+        out_shape=pltpu.VMEM((packed_rows, plan.segment), jnp.bfloat16),
         in_specs=[pl.BlockSpec(memory_space=pl.ANY)] * 2,
         out_specs=vmem,
         scratch_shapes=[
@@ -303,7 +303,7 @@
     total = correlate(whitened, swap_cores(whitened))
     beside, total = lax.optimization_barrier((beside, total))
     kept, *sent = correlate(beside, swap_cores(beside), total)
-    arrived = [swap_blk(sent[hop - 1], hop * plan.columns) for hop in reversed(range(1, plan.targets))]
+    arrived = [swap_blk(sent[hop - 1], hop * plan.columns) for hop in (2, 3, 1)]
     order, chosen, base = pl.pallas_call(
         functools.partial(prepare_kernel, plan),
         out_shape=[

time: 19.6 us -> 18.6 us (0.949)
  local copies, waits for them, and re-layouts: 1.51 us -> 0.68 us
  Pallas kernels: 4.77 us -> 4.16 us
  waiting for transfers between devices: 5.39 us -> 5.96 us
    unnamed x4 -> x2, local copies, waits for them, and re-layouts: 1.51 us -> 0.68 us
    pallas_call x1, Pallas kernels: 1.72 us -> 1.1 us  [few_channels(): pl.pallas_call(functools.partial(whiten_kernel, plan), out_shape=pltpu.VM...]
    ppermute x4, waiting for transfers between devices: 4.16 us -> 4.73 us  [swap_blk(): lax.ppermute(array, 'blk', [(place, place ^ hop) for place in range(plan....]
  transfers between devices with their start and end apart: 6 -> 6, of which waited for: 4 -> 3; matrix products, arithmetic and copies ran while one was open for 0% -> 0% of each run, Pallas kernels for 6% -> 6%
where the time goes in v7:
time: 18.6 us; the launch traced here: 18.4 us
  starting transfers between devices  7.58 us (41%)
  waiting for transfers between devices  5.96 us (32%)
  Pallas kernels  4.16 us (22%)
  local copies, waits for them, and re-layouts  0.68 us (4%)
    ppermute x4, starting transfers between devices, swap_blk(): lax.ppermute(array, 'blk', [(place, place ^ hop) for place in range(plan....  7.06 us
    ppermute x4, waiting for transfers between devices, swap_blk(): lax.ppermute(array, 'blk', [(place, place ^ hop) for place in range(plan....  4.73 us
    pallas_call x1, Pallas kernels, few_channels(): pl.pallas_call(functools.partial(expand_kernel, plan), out_shape=jax.Shap...  1.29 us
    pallas_call x2, Pallas kernels, correlate(): pl.pallas_call(functools.partial(correlate_kernel, plan, last), out_shape...  1.26 us
    ppermute x2, waiting for transfers between devices, swap_cores(): return lax.ppermute(array, 'src', [(0, 1), (1, 0)])  1.23 us
    pallas_call x1, Pallas kernels, few_channels(): pl.pallas_call(functools.partial(whiten_kernel, plan), out_shape=pltpu.VM...  1.1 us
    unnamed x2, local copies, waits for them, and re-layouts  0.68 us
    ppermute x2, starting transfers between devices, swap_cores(): return lax.ppermute(array, 'src', [(0, 1), (1, 0)])  0.52 us
  transfers between devices with their start and end apart: 6, of which 3 were waited for; matrix products, arithmetic and copies ran while one was open for 0% of the time, Pallas kernels for 6%

profile of v7, /device:TPU:0, one launch (start us, length us, event | category | flops | bytes accessed | tf_op | source)
XLA Modules:
  0.0 18.4 jit_solution(15980865551977740495)
XLA Ops:
  0.0 1.1 %whiten.1.mine_ref = bf16[48,512]{1,0:T(8,128)(2,1)S(1)} custom-call(f32[24,2,512]{2,1,0:T(2,128)} %traces_hbm.1, s32[2,24]{1,0:T(2,128)} %bitcast.3), custom_call_target="tpu_custom_call" | custom-call | tf_op jit(solution)/shard_map/whiten/pallas_call | solution.py:259
  1.1 0.5 %collective-permute-start.1 = (bf16[48,512]{1,0:T(8,128)(2,1)S(1)}, bf16[48,512]{1,0:T(8,128)(2,1)S(1)}, u32[]{:S(2)}, u32[]{:S(2)}) collective-permute-start(bf16[48,512]{1,0:T(8,128)(2,1)S(1)} %whiten.1.mine_ref), channel_id=1, source_target_pairs={{0,1},{1,0},{2,3},{3,2},{4,5},{5,4},{6,7},{7,6},{8,9},{9,8},{10,11... | collective-permute-start | bytes 147464 | tf_op jit(solution)/shard_map/ppermute | solution.py:254
  1.6 2.6 %collective-permute-start = (bf16[48,512]{1,0:T(8,128)(2,1)S(1)}, bf16[48,512]{1,0:T(8,128)(2,1)S(1)}, u32[]{:S(2)}, u32[]{:S(2)}) collective-permute-start(bf16[48,512]{1,0:T(8,128)(2,1)S(1)} %whiten.1.mine_ref), channel_id=1, source_target_pairs={{0,2},{2,0},{4,6},{6,4},{8,10},{10,8},{12,14},{14,12},{1,3},{3,1},... | collective-permute-start | bytes 147464 | tf_op jit(solution)/shard_map/ppermute | solution.py:257
  4.2 0.0 collective-permute-done.1.other_ref
  4.2 0.6 %correlate.2.refs_0_ = f32[384,256]{1,0:T(8,128)S(1)} custom-call(bf16[48,512]{1,0:T(8,128)(2,1)S(1)} %whiten.1.mine_ref, bf16[48,512]{1,0:T(8,128)(2,1)S(1)} %collective-permute-done.1.other_ref), custom_call_target="tpu_custom_call" | custom-call | flops 251658240 | bytes 98304 | tf_op jit(solution)/shard_map/correlate/pallas_call | solution.py:284
  4.8 1.7 %collective-permute-done.mine_ref = bf16[48,512]{1,0:T(8,128)(2,1)S(1)} collective-permute-done((bf16[48,512]{1,0:T(8,128)(2,1)S(1)}, bf16[48,512]{1,0:T(8,128)(2,1)S(1)}, u32[]{:S(2)}, u32[]{:S(2)}) %collective-permute-start) | collective-permute-done | bytes 49184 | tf_op jit(solution)/shard_map/ppermute | solution.py:257
  6.5 0.0 collective-permute-start.2
  6.5 1.2 %collective-permute-done.2.other_ref = bf16[48,512]{1,0:T(8,128)(2,1)S(1)} collective-permute-done((bf16[48,512]{1,0:T(8,128)(2,1)S(1)}, bf16[48,512]{1,0:T(8,128)(2,1)S(1)}, u32[]{:S(2)}, u32[]{:S(2)}) %collective-permute-start.2) | collective-permute-done | bytes 49184 | tf_op jit(solution)/shard_map/ppermute | solution.py:254
  7.8 0.6 %correlate.3 = (f32[80,256]{1,0:T(8,128)S(1)}, bf16[80,256]{1,0:T(8,128)(2,1)S(1)}, bf16[80,256]{1,0:T(8,128)(2,1)S(1)}, bf16[80,256]{1,0:T(8,128)(2,1)S(1)}) custom-call(bf16[48,512]{1,0:T(8,128)(2,1)S(1)} %collective-permute-done.mine_ref, bf16[48,512]{1,0:T(8,128)(2,1)S(1)} %collective-permute-done.2.other_ref, f32[384,256]{1,0:T(8,128)S(1)} %correlate.2.refs_0_), custom_call_target="tpu_custom_call" | custom-call | flops 251658240 | bytes 98304 | tf_op jit(solution)/shard_map/correlate/pallas_call | solution.py:284
  8.4 2.9 %collective-permute-start.3 = (bf16[80,256]{1,0:T(8,128)(2,1)S(1)}, bf16[80,256]{1,0:T(8,128)(2,1)S(1)}, u32[]{:S(2)}, u32[]{:S(2)}) collective-permute-start(bf16[80,256]{1,0:T(8,128)(2,1)S(1)} %get-tuple-element.20), channel_id=1, source_target_pairs={{0,8},{2,10},{4,12},{6,14},{8,0},{10,2},{12,4},{14,6},{1,9},{3,11}... | collective-permute-start | bytes 122888 | tf_op jit(solution)/shard_map/ppermute | solution.py:257
  11.3 1.3 %collective-permute-start.4 = (bf16[80,256]{1,0:T(8,128)(2,1)S(1)}, bf16[80,256]{1,0:T(8,128)(2,1)S(1)}, u32[]{:S(2)}, u32[]{:S(2)}) collective-permute-start(bf16[80,256]{1,0:T(8,128)(2,1)S(1)} %get-tuple-element.21), channel_id=1, source_target_pairs={{0,12},{2,14},{4,8},{6,10},{8,4},{10,6},{12,0},{14,2},{1,13},{3,15... | collective-permute-start | bytes 122888 | tf_op jit(solution)/shard_map/ppermute | solution.py:257
  12.7 0.2 %collective-permute-start.5 = (bf16[80,256]{1,0:T(8,128)(2,1)S(1)}, bf16[80,256]{1,0:T(8,128)(2,1)S(1)}, u32[]{:S(2)}, u32[]{:S(2)}) collective-permute-start(bf16[80,256]{1,0:T(8,128)(2,1)S(1)} %get-tuple-element.22), channel_id=1, source_target_pairs={{0,4},{2,6},{4,0},{6,2},{8,12},{10,14},{12,8},{14,10},{1,5},{3,7},... | collective-permute-start | bytes 122888 | tf_op jit(solution)/shard_map/ppermute | solution.py:257
  12.9 0.0 copy-start
  12.9 0.7 %copy-done = s32[256]{0:T(256)S(1)} copy-done((s32[256]{0:T(256)S(1)}, s32[256]{0:T(256)}, u32[]{:S(2)}) %copy-start) | copy-done | bytes 1048
  13.6 0.5 %prepare.1 = (bf16[96,80]{1,0:T(8,128)(2,1)S(1)}, bf16[256,256]{1,0:T(8,128)(2,1)S(1)}, f32[5,96,256]{2,1,0:T(8,128)S(1)}) custom-call(s32[1,256]{1,0:T(1,128)S(1)} %bitcast.2, f32[80,256]{1,0:T(8,128)S(1)} %get-tuple-element.16.kept_ref), custom_call_target="tpu_custom_call" | custom-call | tf_op jit(solution)/shard_map/prepare/pallas_call | solution.py:307
  14.1 0.0 collective-permute-done.3.refs_0_
  14.1 3.0 %collective-permute-done.4.refs_1_ = bf16[80,256]{1,0:T(8,128)(2,1)S(1)} collective-permute-done((bf16[80,256]{1,0:T(8,128)(2,1)S(1)}, bf16[80,256]{1,0:T(8,128)(2,1)S(1)}, u32[]{:S(2)}, u32[]{:S(2)}) %collective-permute-start.4) | collective-permute-done | bytes 40992 | tf_op jit(solution)/shard_map/ppermute | solution.py:257
  17.1 0.0 collective-permute-done.5.refs_2_
  17.1 1.3 %expand.1 = f32[3,129,256]{2,1,0:T(8,128)} custom-call(bf16[96,80]{1,0:T(8,128)(2,1)S(1)} %get-tuple-element.17.order_ref, bf16[256,256]{1,0:T(8,128)(2,1)S(1)} %get-tuple-element.18.chosen_ref, f32[5,96,256]{2,1,0:T(8,128)S(1)} %get-tuple-element.19.base_ref, bf16[80,256]{1,0:T(8,128)(2,1)S(1)} %collective-permute-done.3.refs_0_, ...), custom_call_target="tpu_custom_call" | custom-call | tf_op jit(solution)/shard_map/expand/pallas_call | solution.py:320
Async XLA Ops:
  1.1 3.1 %collective-permute-start.1 = (bf16[48,512]{1,0:T(8,128)(2,1)S(1)}, bf16[48,512]{1,0:T(8,128)(2,1)S(1)}, u32[]{:S(2)}, u32[]{:S(2)}) collective-permute-start(bf16[48,512]{1,0:T(8,128)(2,1)S(1)} %whiten.1.mine_ref), channel_id=1, source_target_pairs={{0,1},{1,0},{2,3},{3,2},{4,5},{5,4},{6,7},{7,6},{8,9},{9,8},{10,11... | collective-permute-start | bytes 147464 | tf_op jit(solution)/shard_map/ppermute | solution.py:254
  1.6 4.9 %collective-permute-start = (bf16[48,512]{1,0:T(8,128)(2,1)S(1)}, bf16[48,512]{1,0:T(8,128)(2,1)S(1)}, u32[]{:S(2)}, u32[]{:S(2)}) collective-permute-start(bf16[48,512]{1,0:T(8,128)(2,1)S(1)} %whiten.1.mine_ref), channel_id=1, source_target_pairs={{0,2},{2,0},{4,6},{6,4},{8,10},{10,8},{12,14},{14,12},{1,3},{3,1},... | collective-permute-start | bytes 147464 | tf_op jit(solution)/shard_map/ppermute | solution.py:257
  6.5 1.2 %collective-permute-start.2 = (bf16[48,512]{1,0:T(8,128)(2,1)S(1)}, bf16[48,512]{1,0:T(8,128)(2,1)S(1)}, u32[]{:S(2)}, u32[]{:S(2)}) collective-permute-start(bf16[48,512]{1,0:T(8,128)(2,1)S(1)} %collective-permute-done.mine_ref), channel_id=1, source_target_pairs={{0,1},{1,0},{2,3},{3,2},{4,5},{5,4},{6,7},{7,6},{8,9},{9,8},{10,11... | collective-permute-start | bytes 147464 | tf_op jit(solution)/shard_map/ppermute | solution.py:254
  8.4 5.7 %collective-permute-start.3 = (bf16[80,256]{1,0:T(8,128)(2,1)S(1)}, bf16[80,256]{1,0:T(8,128)(2,1)S(1)}, u32[]{:S(2)}, u32[]{:S(2)}) collective-permute-start(bf16[80,256]{1,0:T(8,128)(2,1)S(1)} %get-tuple-element.20), channel_id=1, source_target_pairs={{0,8},{2,10},{4,12},{6,14},{8,0},{10,2},{12,4},{14,6},{1,9},{3,11}... | collective-permute-start | bytes 122888 | tf_op jit(solution)/shard_map/ppermute | solution.py:257
  11.3 5.8 %collective-permute-start.4 = (bf16[80,256]{1,0:T(8,128)(2,1)S(1)}, bf16[80,256]{1,0:T(8,128)(2,1)S(1)}, u32[]{:S(2)}, u32[]{:S(2)}) collective-permute-start(bf16[80,256]{1,0:T(8,128)(2,1)S(1)} %get-tuple-element.21), channel_id=1, source_target_pairs={{0,12},{2,14},{4,8},{6,10},{8,4},{10,6},{12,0},{14,2},{1,13},{3,15... | collective-permute-start | bytes 122888 | tf_op jit(solution)/shard_map/ppermute | solution.py:257
  12.7 4.5 %collective-permute-start.5 = (bf16[80,256]{1,0:T(8,128)(2,1)S(1)}, bf16[80,256]{1,0:T(8,128)(2,1)S(1)}, u32[]{:S(2)}, u32[]{:S(2)}) collective-permute-start(bf16[80,256]{1,0:T(8,128)(2,1)S(1)} %get-tuple-element.22), channel_id=1, source_target_pairs={{0,4},{2,6},{4,0},{6,2},{8,12},{10,14},{12,8},{14,10},{1,5},{3,7},... | collective-permute-start | bytes 122888 | tf_op jit(solution)/shard_map/ppermute | solution.py:257
  12.9 0.7 %copy-start = (s32[256]{0:T(256)S(1)}, s32[256]{0:T(256)}, u32[]{:S(2)}) copy-start(s32[256]{0:T(256)} %param.5) | copy-start | bytes 3076

commit v8 on v7

--- a/solution.py
+++ b/solution.py
@@ -175,6 +175,8 @@
             pieces.append(jnp.zeros((plan.rows - plan.own * plan.fine, LANES), jnp.float32))
         packed = jnp.concatenate(pieces, axis=0)
         out_refs[hop][...] = packed.astype(out_refs[hop].dtype)
+        if hop == plan.targets - 1:
+            out_refs[hop + 1][...] = packed.astype(out_refs[hop + 1].dtype)
 
 
 def order_matrix(plan):
@@ -219,9 +221,12 @@
 
 
 def expand_kernel(plan, order_ref, chosen_ref, base_ref, *refs):
-    *arrived_refs, out_hbm, out_ref, sems = refs
+    inner_ref, *arrived_refs, outer_ref, out_hbm, out_ref, sems = refs
     order = order_ref[...]
-    arrived = sum(jnp.dot(order, ref[...], preferred_element_type=jnp.float32) for ref in arrived_refs)
+    line = lax.axis_index("blk") // plan.columns
+    is_outer = (line == 0) | (line == plan.targets - 1)
+    blocks = [ref[...] for ref in arrived_refs] + [jnp.where(is_outer, outer_ref[...], inner_ref[...])]
+    arrived = sum(jnp.dot(order, block, preferred_element_type=jnp.float32) for block in blocks)
     high = arrived.astype(jnp.bfloat16).astype(jnp.float32)
     chosen = chosen_ref[...]
     expanded = []
@@ -253,8 +258,9 @@
     def swap_cores(array):
         return lax.ppermute(array, "src", [(0, 1), (1, 0)])
 
-    def swap_blk(array, hop):
-        return lax.ppermute(array, "blk", [(place, place ^ hop) for place in range(plan.blk_size)])
+    def swap_blk(array, hop, places):
+        pairs = [(place, place ^ hop if place in places else place) for place in range(plan.blk_size)]
+        return lax.ppermute(array, "blk", pairs)
 
     whitened = pl.pallas_call(
         functools.partial(whiten_kernel, plan),
@@ -276,7 +282,7 @@
     def correlate(mine, other, prior=None):
         last = prior is not None
         if last:
-            types = [jnp.float32] + [jnp.bfloat16] * (plan.targets - 1)
+            types = [jnp.float32] + [jnp.bfloat16] * plan.targets
             shapes = [jax.ShapeDtypeStruct((plan.rows, LANES), dtype) for dtype in types]
         else:
             shapes = [jax.ShapeDtypeStruct((height, LANES), jnp.float32)]
@@ -299,11 +305,15 @@
         )(*operands)
         return results if last else results[0]
 
-    beside = swap_blk(whitened, 1)
+    beside = swap_blk(whitened, 1, range(plan.blk_size))
     total = correlate(whitened, swap_cores(whitened))
     beside, total = lax.optimization_barrier((beside, total))
     kept, *sent = correlate(beside, swap_cores(beside), total)
-    arrived = [swap_blk(sent[hop - 1], hop * plan.columns) for hop in (2, 3, 1)]
+    every = range(plan.blk_size)
+    outer = [place for place in every if place // plan.columns in (0, plan.targets - 1)]
+    inner = [place for place in every if place not in outer]
+    steps = [(sent[3], 3, inner), (sent[1], 2, every), (sent[0], 1, every), (sent[2], 3, outer)]
+    arrived = [swap_blk(array, hop * plan.columns, who) for array, hop, who in steps]
     order, chosen, base = pl.pallas_call(
         functools.partial(prepare_kernel, plan),
         out_shape=[

time: 18.6 us -> 23 us (1.24)
  starting transfers between devices: 7.58 us -> 12.7 us
  waiting for transfers between devices: 5.96 us -> 5.22 us
    ppermute x4 -> x5, starting transfers between devices: 7.06 us -> 12.2 us  [swap_blk(): return lax.ppermute(array, 'blk', pairs)]
    ppermute x4 -> x5, waiting for transfers between devices: 4.73 us -> 3.98 us  [swap_blk(): return lax.ppermute(array, 'blk', pairs)]
  transfers between devices with their start and end apart: 6 -> 7, of which waited for: 3 -> 3; matrix products, arithmetic and copies ran while one was open for 0% -> 0% of each run, Pallas kernels for 6% -> 5%
where the time goes in v8:
time: 23 us; the launch traced here: 22.9 us
  starting transfers between devices  12.7 us (55%)
  waiting for transfers between devices  5.22 us (23%)
  Pallas kernels  4.15 us (18%)
  local copies, waits for them, and re-layouts  0.67 us (3%)
    ppermute x5, starting transfers between devices, swap_blk(): return lax.ppermute(array, 'blk', pairs)  12.2 us
    ppermute x5, waiting for transfers between devices, swap_blk(): return lax.ppermute(array, 'blk', pairs)  3.98 us
    pallas_call x1, Pallas kernels, few_channels(): pl.pallas_call(functools.partial(expand_kernel, plan), out_shape=jax.Shap...  1.29 us
    pallas_call x2, Pallas kernels, correlate(): pl.pallas_call(functools.partial(correlate_kernel, plan, last), out_shape...  1.26 us
    ppermute x2, waiting for transfers between devices, swap_cores(): return lax.ppermute(array, 'src', [(0, 1), (1, 0)])  1.23 us
    pallas_call x1, Pallas kernels, few_channels(): pl.pallas_call(functools.partial(whiten_kernel, plan), out_shape=pltpu.VM...  1.1 us
    unnamed x2, local copies, waits for them, and re-layouts  0.67 us
    ppermute x2, starting transfers between devices, swap_cores(): return lax.ppermute(array, 'src', [(0, 1), (1, 0)])  0.52 us
  transfers between devices with their start and end apart: 7, of which 3 were waited for; matrix products, arithmetic and copies ran while one was open for 0% of the time, Pallas kernels for 5%

profile of v8, /device:TPU:0, one launch (start us, length us, event | category | flops | bytes accessed | tf_op | source)
XLA Modules:
  0.0 22.9 jit_solution(13421659398691229676)
XLA Ops:
  0.0 1.1 %whiten.1.mine_ref = bf16[48,512]{1,0:T(8,128)(2,1)S(1)} custom-call(f32[24,2,512]{2,1,0:T(2,128)} %traces_hbm.1, s32[2,24]{1,0:T(2,128)} %bitcast.3), custom_call_target="tpu_custom_call" | custom-call | tf_op jit(solution)/shard_map/whiten/pallas_call | solution.py:265
  1.1 0.5 %collective-permute-start.1 = (bf16[48,512]{1,0:T(8,128)(2,1)S(1)}, bf16[48,512]{1,0:T(8,128)(2,1)S(1)}, u32[]{:S(2)}, u32[]{:S(2)}) collective-permute-start(bf16[48,512]{1,0:T(8,128)(2,1)S(1)} %whiten.1.mine_ref), channel_id=1, source_target_pairs={{0,1},{1,0},{2,3},{3,2},{4,5},{5,4},{6,7},{7,6},{8,9},{9,8},{10,11... | collective-permute-start | bytes 147464 | tf_op jit(solution)/shard_map/ppermute | solution.py:259
  1.6 2.6 %collective-permute-start = (bf16[48,512]{1,0:T(8,128)(2,1)S(1)}, bf16[48,512]{1,0:T(8,128)(2,1)S(1)}, u32[]{:S(2)}, u32[]{:S(2)}) collective-permute-start(bf16[48,512]{1,0:T(8,128)(2,1)S(1)} %whiten.1.mine_ref), channel_id=1, source_target_pairs={{0,2},{2,0},{4,6},{6,4},{8,10},{10,8},{12,14},{14,12},{1,3},{3,1},... | collective-permute-start | bytes 147464 | tf_op jit(solution)/shard_map/ppermute | solution.py:263
  4.2 0.0 collective-permute-done.1.other_ref
  4.2 0.6 %correlate.2.refs_0_ = f32[384,256]{1,0:T(8,128)S(1)} custom-call(bf16[48,512]{1,0:T(8,128)(2,1)S(1)} %whiten.1.mine_ref, bf16[48,512]{1,0:T(8,128)(2,1)S(1)} %collective-permute-done.1.other_ref), custom_call_target="tpu_custom_call" | custom-call | flops 251658240 | bytes 98304 | tf_op jit(solution)/shard_map/correlate/pallas_call | solution.py:290
  4.8 1.7 %collective-permute-done.mine_ref = bf16[48,512]{1,0:T(8,128)(2,1)S(1)} collective-permute-done((bf16[48,512]{1,0:T(8,128)(2,1)S(1)}, bf16[48,512]{1,0:T(8,128)(2,1)S(1)}, u32[]{:S(2)}, u32[]{:S(2)}) %collective-permute-start) | collective-permute-done | bytes 49184 | tf_op jit(solution)/shard_map/ppermute | solution.py:263
  6.5 0.0 collective-permute-start.2
  6.5 1.2 %collective-permute-done.2.other_ref = bf16[48,512]{1,0:T(8,128)(2,1)S(1)} collective-permute-done((bf16[48,512]{1,0:T(8,128)(2,1)S(1)}, bf16[48,512]{1,0:T(8,128)(2,1)S(1)}, u32[]{:S(2)}, u32[]{:S(2)}) %collective-permute-start.2) | collective-permute-done | bytes 49184 | tf_op jit(solution)/shard_map/ppermute | solution.py:259
  7.8 0.6 %correlate.3 = (f32[80,256]{1,0:T(8,128)S(1)}, bf16[80,256]{1,0:T(8,128)(2,1)S(1)}, bf16[80,256]{1,0:T(8,128)(2,1)S(1)}, bf16[80,256]{1,0:T(8,128)(2,1)S(1)}, bf16[80,256]{1,0:T(8,128)(2,1)S(1)}) custom-call(bf16[48,512]{1,0:T(8,128)(2,1)S(1)} %collective-permute-done.mine_ref, bf16[48,512]{1,0:T(8,128)(2,1)S(1)} %collective-permute-done.2.other_ref, ...), custom_call_target="tpu_custom_call" | custom-call | flops 251658240 | bytes 98304 | tf_op jit(solution)/shard_map/correlate/pallas_call | solution.py:290
  8.4 0.7 %collective-permute-start.3 = (bf16[80,256]{1,0:T(8,128)(2,1)S(1)}, bf16[80,256]{1,0:T(8,128)(2,1)S(1)}, u32[]{:S(2)}, u32[]{:S(2)}) collective-permute-start(bf16[80,256]{1,0:T(8,128)(2,1)S(1)} %get-tuple-element.21), channel_id=1, source_target_pairs={{0,0},{2,2},{4,8},{6,10},{8,4},{10,6},{12,12},{14,14},{1,1},{3,3},... | collective-permute-start | bytes 122888 | tf_op jit(solution)/shard_map/ppermute | solution.py:263
  9.1 4.6 %collective-permute-start.4 = (bf16[80,256]{1,0:T(8,128)(2,1)S(1)}, bf16[80,256]{1,0:T(8,128)(2,1)S(1)}, u32[]{:S(2)}, u32[]{:S(2)}) collective-permute-start(bf16[80,256]{1,0:T(8,128)(2,1)S(1)} %get-tuple-element.22), channel_id=1, source_target_pairs={{0,8},{2,10},{4,12},{6,14},{8,0},{10,2},{12,4},{14,6},{1,9},{3,11}... | collective-permute-start | bytes 122888 | tf_op jit(solution)/shard_map/ppermute | solution.py:263
  13.7 0.2 collective-permute-start.5
  13.9 4.2 %collective-permute-start.6 = (bf16[80,256]{1,0:T(8,128)(2,1)S(1)}, bf16[80,256]{1,0:T(8,128)(2,1)S(1)}, u32[]{:S(2)}, u32[]{:S(2)}) collective-permute-start(bf16[80,256]{1,0:T(8,128)(2,1)S(1)} %get-tuple-element.24), channel_id=1, source_target_pairs={{0,12},{2,14},{4,4},{6,6},{8,8},{10,10},{12,0},{14,2},{1,13},{3,15... | collective-permute-start | bytes 122888 | tf_op jit(solution)/shard_map/ppermute | solution.py:263
  18.1 0.0 copy-start
  18.1 0.7 %copy-done = s32[256]{0:T(256)S(1)} copy-done((s32[256]{0:T(256)S(1)}, s32[256]{0:T(256)}, u32[]{:S(2)}) %copy-start) | copy-done | bytes 1048
  18.8 0.5 %prepare.1 = (bf16[96,80]{1,0:T(8,128)(2,1)S(1)}, bf16[256,256]{1,0:T(8,128)(2,1)S(1)}, f32[5,96,256]{2,1,0:T(8,128)S(1)}) custom-call(s32[1,256]{1,0:T(1,128)S(1)} %bitcast.2, f32[80,256]{1,0:T(8,128)S(1)} %get-tuple-element.17.kept_ref), custom_call_target="tpu_custom_call" | custom-call | tf_op jit(solution)/shard_map/prepare/pallas_call | solution.py:317
  19.2 0.0 collective-permute-done.3.refs_0_
  19.3 0.0 collective-permute-done.4.refs_1_
  19.3 0.0 collective-permute-done.5.refs_2_
  19.3 2.3 %collective-permute-done.6.refs_3_ = bf16[80,256]{1,0:T(8,128)(2,1)S(1)} collective-permute-done((bf16[80,256]{1,0:T(8,128)(2,1)S(1)}, bf16[80,256]{1,0:T(8,128)(2,1)S(1)}, u32[]{:S(2)}, u32[]{:S(2)}) %collective-permute-start.6) | collective-permute-done | bytes 40992 | tf_op jit(solution)/shard_map/ppermute | solution.py:263
  21.6 1.3 %expand.1 = f32[3,129,256]{2,1,0:T(8,128)} custom-call(bf16[96,80]{1,0:T(8,128)(2,1)S(1)} %get-tuple-element.18.order_ref, bf16[256,256]{1,0:T(8,128)(2,1)S(1)} %get-tuple-element.19.chosen_ref, f32[5,96,256]{2,1,0:T(8,128)S(1)} %get-tuple-element.20.base_ref, bf16[80,256]{1,0:T(8,128)(2,1)S(1)} %collective-permute-done.3.refs_0_, ...), custom_call_target="tpu_custom_call" | custom-call | tf_op jit(solution)/shard_map/expand/pallas_call | solution.py:330
Async XLA Ops:
  1.1 3.1 %collective-permute-start.1 = (bf16[48,512]{1,0:T(8,128)(2,1)S(1)}, bf16[48,512]{1,0:T(8,128)(2,1)S(1)}, u32[]{:S(2)}, u32[]{:S(2)}) collective-permute-start(bf16[48,512]{1,0:T(8,128)(2,1)S(1)} %whiten.1.mine_ref), channel_id=1, source_target_pairs={{0,1},{1,0},{2,3},{3,2},{4,5},{5,4},{6,7},{7,6},{8,9},{9,8},{10,11... | collective-permute-start | bytes 147464 | tf_op jit(solution)/shard_map/ppermute | solution.py:259
  1.6 4.9 %collective-permute-start = (bf16[48,512]{1,0:T(8,128)(2,1)S(1)}, bf16[48,512]{1,0:T(8,128)(2,1)S(1)}, u32[]{:S(2)}, u32[]{:S(2)}) collective-permute-start(bf16[48,512]{1,0:T(8,128)(2,1)S(1)} %whiten.1.mine_ref), channel_id=1, source_target_pairs={{0,2},{2,0},{4,6},{6,4},{8,10},{10,8},{12,14},{14,12},{1,3},{3,1},... | collective-permute-start | bytes 147464 | tf_op jit(solution)/shard_map/ppermute | solution.py:263
  6.5 1.2 %collective-permute-start.2 = (bf16[48,512]{1,0:T(8,128)(2,1)S(1)}, bf16[48,512]{1,0:T(8,128)(2,1)S(1)}, u32[]{:S(2)}, u32[]{:S(2)}) collective-permute-start(bf16[48,512]{1,0:T(8,128)(2,1)S(1)} %collective-permute-done.mine_ref), channel_id=1, source_target_pairs={{0,1},{1,0},{2,3},{3,2},{4,5},{5,4},{6,7},{7,6},{8,9},{9,8},{10,11... | collective-permute-start | bytes 147464 | tf_op jit(solution)/shard_map/ppermute | solution.py:259
  8.4 10.8 %collective-permute-start.3 = (bf16[80,256]{1,0:T(8,128)(2,1)S(1)}, bf16[80,256]{1,0:T(8,128)(2,1)S(1)}, u32[]{:S(2)}, u32[]{:S(2)}) collective-permute-start(bf16[80,256]{1,0:T(8,128)(2,1)S(1)} %get-tuple-element.21), channel_id=1, source_target_pairs={{0,0},{2,2},{4,8},{6,10},{8,4},{10,6},{12,12},{14,14},{1,1},{3,3},... | collective-permute-start | bytes 122888 | tf_op jit(solution)/shard_map/ppermute | solution.py:263
  9.1 10.2 %collective-permute-start.4 = (bf16[80,256]{1,0:T(8,128)(2,1)S(1)}, bf16[80,256]{1,0:T(8,128)(2,1)S(1)}, u32[]{:S(2)}, u32[]{:S(2)}) collective-permute-start(bf16[80,256]{1,0:T(8,128)(2,1)S(1)} %get-tuple-element.22), channel_id=1, source_target_pairs={{0,8},{2,10},{4,12},{6,14},{8,0},{10,2},{12,4},{14,6},{1,9},{3,11}... | collective-permute-start | bytes 122888 | tf_op jit(solution)/shard_map/ppermute | solution.py:263
  13.7 5.6 %collective-permute-start.5 = (bf16[80,256]{1,0:T(8,128)(2,1)S(1)}, bf16[80,256]{1,0:T(8,128)(2,1)S(1)}, u32[]{:S(2)}, u32[]{:S(2)}) collective-permute-start(bf16[80,256]{1,0:T(8,128)(2,1)S(1)} %get-tuple-element.23), channel_id=1, source_target_pairs={{0,4},{2,6},{4,0},{6,2},{8,12},{10,14},{12,8},{14,10},{1,5},{3,7},... | collective-permute-start | bytes 122888 | tf_op jit(solution)/shard_map/ppermute | solution.py:263
  13.9 7.7 %collective-permute-start.6 = (bf16[80,256]{1,0:T(8,128)(2,1)S(1)}, bf16[80,256]{1,0:T(8,128)(2,1)S(1)}, u32[]{:S(2)}, u32[]{:S(2)}) collective-permute-start(bf16[80,256]{1,0:T(8,128)(2,1)S(1)} %get-tuple-element.24), channel_id=1, source_target_pairs={{0,12},{2,14},{4,4},{6,6},{8,8},{10,10},{12,0},{14,2},{1,13},{3,15... | collective-permute-start | bytes 122888 | tf_op jit(solution)/shard_map/ppermute | solution.py:263
  18.1 0.7 %copy-start = (s32[256]{0:T(256)S(1)}, s32[256]{0:T(256)}, u32[]{:S(2)}) copy-start(s32[256]{0:T(256)} %param.5) | copy-start | bytes 3076

commit v9 on v8

--- a/solution.py
+++ b/solution.py
@@ -259,8 +259,7 @@
         return lax.ppermute(array, "src", [(0, 1), (1, 0)])
 
     def swap_blk(array, hop, places):
-        pairs = [(place, place ^ hop if place in places else place) for place in range(plan.blk_size)]
-        return lax.ppermute(array, "blk", pairs)
+        return lax.ppermute(array, "blk", [(place, place ^ hop) for place in places])
 
     whitened = pl.pallas_call(
         functools.partial(whiten_kernel, plan),

time: 23 us -> 23 us (level)
  no operation moved by 1% of the time
where the time goes in v9:
time: 23 us; the launch traced here: 22.9 us
  starting transfers between devices  12.7 us (55%)
  waiting for transfers between devices  5.22 us (23%)
  Pallas kernels  4.15 us (18%)
  local copies, waits for them, and re-layouts  0.67 us (3%)
    ppermute x5, starting transfers between devices, swap_blk(): lax.ppermute(array, 'blk', [(place, place ^ hop) for place in places])  12.2 us
    ppermute x5, waiting for transfers between devices, swap_blk(): lax.ppermute(array, 'blk', [(place, place ^ hop) for place in places])  3.98 us
    pallas_call x1, Pallas kernels, few_channels(): pl.pallas_call(functools.partial(expand_kernel, plan), out_shape=jax.Shap...  1.29 us
    pallas_call x2, Pallas kernels, correlate(): pl.pallas_call(functools.partial(correlate_kernel, plan, last), out_shape...  1.26 us
    ppermute x2, waiting for transfers between devices, swap_cores(): return lax.ppermute(array, 'src', [(0, 1), (1, 0)])  1.23 us
    pallas_call x1, Pallas kernels, few_channels(): pl.pallas_call(functools.partial(whiten_kernel, plan), out_shape=pltpu.VM...  1.1 us
    unnamed x2, local copies, waits for them, and re-layouts  0.67 us
    ppermute x2, starting transfers between devices, swap_cores(): return lax.ppermute(array, 'src', [(0, 1), (1, 0)])  0.52 us
  transfers between devices with their start and end apart: 7, of which 3 were waited for; matrix products, arithmetic and copies ran while one was open for 0% of the time, Pallas kernels for 5%

profile of v9, /device:TPU:0, one launch (start us, length us, event | category | flops | bytes accessed | tf_op | source)
XLA Modules:
  0.0 22.9 jit_solution(8564578658016103744)
XLA Ops:
  0.0 1.1 %whiten.1.mine_ref = bf16[48,512]{1,0:T(8,128)(2,1)S(1)} custom-call(f32[24,2,512]{2,1,0:T(2,128)} %traces_hbm.1, s32[2,24]{1,0:T(2,128)} %bitcast.3), custom_call_target="tpu_custom_call" | custom-call | tf_op jit(solution)/shard_map/whiten/pallas_call | solution.py:264
  1.1 0.5 %collective-permute-start.1 = (bf16[48,512]{1,0:T(8,128)(2,1)S(1)}, bf16[48,512]{1,0:T(8,128)(2,1)S(1)}, u32[]{:S(2)}, u32[]{:S(2)}) collective-permute-start(bf16[48,512]{1,0:T(8,128)(2,1)S(1)} %whiten.1.mine_ref), channel_id=1, source_target_pairs={{0,1},{1,0},{2,3},{3,2},{4,5},{5,4},{6,7},{7,6},{8,9},{9,8},{10,11... | collective-permute-start | bytes 147464 | tf_op jit(solution)/shard_map/ppermute | solution.py:259
  1.6 2.6 %collective-permute-start = (bf16[48,512]{1,0:T(8,128)(2,1)S(1)}, bf16[48,512]{1,0:T(8,128)(2,1)S(1)}, u32[]{:S(2)}, u32[]{:S(2)}) collective-permute-start(bf16[48,512]{1,0:T(8,128)(2,1)S(1)} %whiten.1.mine_ref), channel_id=1, source_target_pairs={{0,2},{2,0},{4,6},{6,4},{8,10},{10,8},{12,14},{14,12},{1,3},{3,1},... | collective-permute-start | bytes 147464 | tf_op jit(solution)/shard_map/ppermute | solution.py:262
  4.2 0.0 collective-permute-done.1.other_ref
  4.2 0.6 %correlate.2.refs_0_ = f32[384,256]{1,0:T(8,128)S(1)} custom-call(bf16[48,512]{1,0:T(8,128)(2,1)S(1)} %whiten.1.mine_ref, bf16[48,512]{1,0:T(8,128)(2,1)S(1)} %collective-permute-done.1.other_ref), custom_call_target="tpu_custom_call" | custom-call | flops 251658240 | bytes 98304 | tf_op jit(solution)/shard_map/correlate/pallas_call | solution.py:289
  4.8 1.7 %collective-permute-done.mine_ref = bf16[48,512]{1,0:T(8,128)(2,1)S(1)} collective-permute-done((bf16[48,512]{1,0:T(8,128)(2,1)S(1)}, bf16[48,512]{1,0:T(8,128)(2,1)S(1)}, u32[]{:S(2)}, u32[]{:S(2)}) %collective-permute-start) | collective-permute-done | bytes 49184 | tf_op jit(solution)/shard_map/ppermute | solution.py:262
  6.5 0.0 collective-permute-start.2
  6.5 1.2 %collective-permute-done.2.other_ref = bf16[48,512]{1,0:T(8,128)(2,1)S(1)} collective-permute-done((bf16[48,512]{1,0:T(8,128)(2,1)S(1)}, bf16[48,512]{1,0:T(8,128)(2,1)S(1)}, u32[]{:S(2)}, u32[]{:S(2)}) %collective-permute-start.2) | collective-permute-done | bytes 49184 | tf_op jit(solution)/shard_map/ppermute | solution.py:259
  7.8 0.6 %correlate.3 = (f32[80,256]{1,0:T(8,128)S(1)}, bf16[80,256]{1,0:T(8,128)(2,1)S(1)}, bf16[80,256]{1,0:T(8,128)(2,1)S(1)}, bf16[80,256]{1,0:T(8,128)(2,1)S(1)}, bf16[80,256]{1,0:T(8,128)(2,1)S(1)}) custom-call(bf16[48,512]{1,0:T(8,128)(2,1)S(1)} %collective-permute-done.mine_ref, bf16[48,512]{1,0:T(8,128)(2,1)S(1)} %collective-permute-done.2.other_ref, ...), custom_call_target="tpu_custom_call" | custom-call | flops 251658240 | bytes 98304 | tf_op jit(solution)/shard_map/correlate/pallas_call | solution.py:289
  8.4 0.7 %collective-permute-start.3 = (bf16[80,256]{1,0:T(8,128)(2,1)S(1)}, bf16[80,256]{1,0:T(8,128)(2,1)S(1)}, u32[]{:S(2)}, u32[]{:S(2)}) collective-permute-start(bf16[80,256]{1,0:T(8,128)(2,1)S(1)} %get-tuple-element.21), channel_id=1, source_target_pairs={{4,8},{6,10},{8,4},{10,6},{5,9},{7,11},{9,5},{11,7},{20,24},{22,26... | collective-permute-start | bytes 122888 | tf_op jit(solution)/shard_map/ppermute | solution.py:262
  9.1 4.6 %collective-permute-start.4 = (bf16[80,256]{1,0:T(8,128)(2,1)S(1)}, bf16[80,256]{1,0:T(8,128)(2,1)S(1)}, u32[]{:S(2)}, u32[]{:S(2)}) collective-permute-start(bf16[80,256]{1,0:T(8,128)(2,1)S(1)} %get-tuple-element.22), channel_id=1, source_target_pairs={{0,8},{2,10},{4,12},{6,14},{8,0},{10,2},{12,4},{14,6},{1,9},{3,11}... | collective-permute-start | bytes 122888 | tf_op jit(solution)/shard_map/ppermute | solution.py:262
  13.7 0.2 collective-permute-start.5
  13.9 4.2 %collective-permute-start.6 = (bf16[80,256]{1,0:T(8,128)(2,1)S(1)}, bf16[80,256]{1,0:T(8,128)(2,1)S(1)}, u32[]{:S(2)}, u32[]{:S(2)}) collective-permute-start(bf16[80,256]{1,0:T(8,128)(2,1)S(1)} %get-tuple-element.24), channel_id=1, source_target_pairs={{0,12},{2,14},{12,0},{14,2},{1,13},{3,15},{13,1},{15,3},{16,28},{1... | collective-permute-start | bytes 122888 | tf_op jit(solution)/shard_map/ppermute | solution.py:262
  18.1 0.0 copy-start
  18.1 0.7 %copy-done = s32[256]{0:T(256)S(1)} copy-done((s32[256]{0:T(256)S(1)}, s32[256]{0:T(256)}, u32[]{:S(2)}) %copy-start) | copy-done | bytes 1048
  18.8 0.5 %prepare.1 = (bf16[96,80]{1,0:T(8,128)(2,1)S(1)}, bf16[256,256]{1,0:T(8,128)(2,1)S(1)}, f32[5,96,256]{2,1,0:T(8,128)S(1)}) custom-call(s32[1,256]{1,0:T(1,128)S(1)} %bitcast.2, f32[80,256]{1,0:T(8,128)S(1)} %get-tuple-element.17.kept_ref), custom_call_target="tpu_custom_call" | custom-call | tf_op jit(solution)/shard_map/prepare/pallas_call | solution.py:316
  19.2 0.0 collective-permute-done.3.refs_0_
  19.3 0.0 collective-permute-done.4.refs_1_
  19.3 0.0 collective-permute-done.5.refs_2_
  19.3 2.3 %collective-permute-done.6.refs_3_ = bf16[80,256]{1,0:T(8,128)(2,1)S(1)} collective-permute-done((bf16[80,256]{1,0:T(8,128)(2,1)S(1)}, bf16[80,256]{1,0:T(8,128)(2,1)S(1)}, u32[]{:S(2)}, u32[]{:S(2)}) %collective-permute-start.6) | collective-permute-done | bytes 40992 | tf_op jit(solution)/shard_map/ppermute | solution.py:262
  21.6 1.3 %expand.1 = f32[3,129,256]{2,1,0:T(8,128)} custom-call(bf16[96,80]{1,0:T(8,128)(2,1)S(1)} %get-tuple-element.18.order_ref, bf16[256,256]{1,0:T(8,128)(2,1)S(1)} %get-tuple-element.19.chosen_ref, f32[5,96,256]{2,1,0:T(8,128)S(1)} %get-tuple-element.20.base_ref, bf16[80,256]{1,0:T(8,128)(2,1)S(1)} %collective-permute-done.3.refs_0_, ...), custom_call_target="tpu_custom_call" | custom-call | tf_op jit(solution)/shard_map/expand/pallas_call | solution.py:329
Async XLA Ops:
  1.1 3.1 %collective-permute-start.1 = (bf16[48,512]{1,0:T(8,128)(2,1)S(1)}, bf16[48,512]{1,0:T(8,128)(2,1)S(1)}, u32[]{:S(2)}, u32[]{:S(2)}) collective-permute-start(bf16[48,512]{1,0:T(8,128)(2,1)S(1)} %whiten.1.mine_ref), channel_id=1, source_target_pairs={{0,1},{1,0},{2,3},{3,2},{4,5},{5,4},{6,7},{7,6},{8,9},{9,8},{10,11... | collective-permute-start | bytes 147464 | tf_op jit(solution)/shard_map/ppermute | solution.py:259
  1.6 4.9 %collective-permute-start = (bf16[48,512]{1,0:T(8,128)(2,1)S(1)}, bf16[48,512]{1,0:T(8,128)(2,1)S(1)}, u32[]{:S(2)}, u32[]{:S(2)}) collective-permute-start(bf16[48,512]{1,0:T(8,128)(2,1)S(1)} %whiten.1.mine_ref), channel_id=1, source_target_pairs={{0,2},{2,0},{4,6},{6,4},{8,10},{10,8},{12,14},{14,12},{1,3},{3,1},... | collective-permute-start | bytes 147464 | tf_op jit(solution)/shard_map/ppermute | solution.py:262
  6.5 1.2 %collective-permute-start.2 = (bf16[48,512]{1,0:T(8,128)(2,1)S(1)}, bf16[48,512]{1,0:T(8,128)(2,1)S(1)}, u32[]{:S(2)}, u32[]{:S(2)}) collective-permute-start(bf16[48,512]{1,0:T(8,128)(2,1)S(1)} %collective-permute-done.mine_ref), channel_id=1, source_target_pairs={{0,1},{1,0},{2,3},{3,2},{4,5},{5,4},{6,7},{7,6},{8,9},{9,8},{10,11... | collective-permute-start | bytes 147464 | tf_op jit(solution)/shard_map/ppermute | solution.py:259
  8.4 10.8 %collective-permute-start.3 = (bf16[80,256]{1,0:T(8,128)(2,1)S(1)}, bf16[80,256]{1,0:T(8,128)(2,1)S(1)}, u32[]{:S(2)}, u32[]{:S(2)}) collective-permute-start(bf16[80,256]{1,0:T(8,128)(2,1)S(1)} %get-tuple-element.21), channel_id=1, source_target_pairs={{4,8},{6,10},{8,4},{10,6},{5,9},{7,11},{9,5},{11,7},{20,24},{22,26... | collective-permute-start | bytes 122888 | tf_op jit(solution)/shard_map/ppermute | solution.py:262
  9.1 10.2 %collective-permute-start.4 = (bf16[80,256]{1,0:T(8,128)(2,1)S(1)}, bf16[80,256]{1,0:T(8,128)(2,1)S(1)}, u32[]{:S(2)}, u32[]{:S(2)}) collective-permute-start(bf16[80,256]{1,0:T(8,128)(2,1)S(1)} %get-tuple-element.22), channel_id=1, source_target_pairs={{0,8},{2,10},{4,12},{6,14},{8,0},{10,2},{12,4},{14,6},{1,9},{3,11}... | collective-permute-start | bytes 122888 | tf_op jit(solution)/shard_map/ppermute | solution.py:262
  13.7 5.6 %collective-permute-start.5 = (bf16[80,256]{1,0:T(8,128)(2,1)S(1)}, bf16[80,256]{1,0:T(8,128)(2,1)S(1)}, u32[]{:S(2)}, u32[]{:S(2)}) collective-permute-start(bf16[80,256]{1,0:T(8,128)(2,1)S(1)} %get-tuple-element.23), channel_id=1, source_target_pairs={{0,4},{2,6},{4,0},{6,2},{8,12},{10,14},{12,8},{14,10},{1,5},{3,7},... | collective-permute-start | bytes 122888 | tf_op jit(solution)/shard_map/ppermute | solution.py:262
  13.9 7.7 %collective-permute-start.6 = (bf16[80,256]{1,0:T(8,128)(2,1)S(1)}, bf16[80,256]{1,0:T(8,128)(2,1)S(1)}, u32[]{:S(2)}, u32[]{:S(2)}) collective-permute-start(bf16[80,256]{1,0:T(8,128)(2,1)S(1)} %get-tuple-element.24), channel_id=1, source_target_pairs={{0,12},{2,14},{12,0},{14,2},{1,13},{3,15},{13,1},{15,3},{16,28},{1... | collective-permute-start | bytes 122888 | tf_op jit(solution)/shard_map/ppermute | solution.py:262
  18.1 0.7 %copy-start = (s32[256]{0:T(256)S(1)}, s32[256]{0:T(256)}, u32[]{:S(2)}) copy-start(s32[256]{0:T(256)} %param.5) | copy-start | bytes 3076

commit v10 on v7

--- a/solution.py
+++ b/solution.py
@@ -85,8 +85,8 @@
         rows = self.own * self.fine
         self.rows = -(-rows // 16) * 16
         self.height = self.own * self.fine_padded
-        self.columns = 2
-        self.targets = blk_size // self.columns
+        self.far = blk_size // 2
+        self.targets = 2
         self.norm_factor = 1.0 / math.sqrt(windows * blk_size * segment)
 
     def fits(self):
@@ -120,11 +120,10 @@
     out_ref[...] = jnp.concatenate(pieces, axis=0).astype(jnp.bfloat16)
 
 
-def correlate_kernel(plan, last, mine_ref, other_ref, *refs):
-    if last:
-        prior_ref, *out_refs, rows_ref, toeplitz_ref, columns_ref = refs
-    else:
-        sum_ref, rows_ref, toeplitz_ref, columns_ref = refs
+def correlate_kernel(plan, prior, last, mine_ref, other_ref, *refs):
+    if prior:
+        prior_ref, *refs = refs
+    *out_refs, rows_ref, toeplitz_ref, columns_ref = refs
     span = plan.span
     me = lax.axis_index("blk")
     filled = plan.coarse * plan.channels
@@ -143,7 +142,7 @@
             moved = pltpu.roll(both, step * plan.fine, 1) if step else both
             columns_ref[step * plan.channels : (step + 1) * plan.channels, at] = moved.astype(jnp.bfloat16)
         for hop in range(plan.targets):
-            target = me ^ (hop * plan.columns)
+            target = me ^ (hop * plan.far)
             for member in range(plan.own):
                 channel = window * plan.half + target * plan.own + member
                 row = jnp.concatenate([rows_ref[pl.ds(channel, 1), :], filler[:1]], axis=1)
@@ -162,10 +161,12 @@
         (((1,), (1,)), ((), ())),
         preferred_element_type=jnp.float32,
     )
+    if prior:
+        products = products + prior_ref[...]
     if not last:
-        sum_ref[...] = products
+        out_refs[0][...] = products
         return
-    products = (products + prior_ref[...]).reshape(plan.targets, plan.own, plan.fine_padded, LANES)
+    products = products.reshape(plan.targets, plan.own, plan.fine_padded, LANES)
     for hop in range(plan.targets):
         part = products[hop]
         pieces = [part[member, : plan.whole_groups] for member in range(plan.own)]
@@ -218,18 +219,12 @@
         )
 
 
-def expand_kernel(plan, order_ref, chosen_ref, base_ref, *refs):
-    *arrived_refs, out_hbm, out_ref, sems = refs
-    order = order_ref[...]
-    arrived = sum(jnp.dot(order, ref[...], preferred_element_type=jnp.float32) for ref in arrived_refs)
-    high = arrived.astype(jnp.bfloat16).astype(jnp.float32)
+def expand_kernel(plan, order_ref, chosen_ref, base_ref, arrived_ref, out_hbm, out_ref, sems):
+    arrived = jnp.dot(order_ref[...], arrived_ref[...], preferred_element_type=jnp.float32)
     chosen = chosen_ref[...]
     expanded = []
     for step in range(plan.coarse):
-        moved = sum(
-            jnp.dot(inside_step(plan, step, part), chosen, preferred_element_type=jnp.float32)
-            for part in (high, arrived - high)
-        )
+        moved = jnp.dot(inside_step(plan, step, arrived), chosen, preferred_element_type=jnp.float32)
         expanded.append(base_ref[step] + moved * plan.norm_factor)
     copies = []
     for member in range(plan.own):
@@ -273,16 +268,14 @@
     height = plan.targets * plan.height
     width = plan.windows * plan.span
 
-    def correlate(mine, other, prior=None):
-        last = prior is not None
+    def correlate(mine, other, prior=None, last=False):
         if last:
-            types = [jnp.float32] + [jnp.bfloat16] * (plan.targets - 1)
-            shapes = [jax.ShapeDtypeStruct((plan.rows, LANES), dtype) for dtype in types]
+            shapes = [jax.ShapeDtypeStruct((plan.rows, LANES), dtype) for dtype in (jnp.float32, jnp.bfloat16)]
         else:
             shapes = [jax.ShapeDtypeStruct((height, LANES), jnp.float32)]
-        operands = [mine, other] + ([prior] if last else [])
+        operands = [mine, other] + ([] if prior is None else [prior])
         results = pl.pallas_call(
-            functools.partial(correlate_kernel, plan, last),
+            functools.partial(correlate_kernel, plan, prior is not None, last),
             out_shape=shapes,
             in_specs=[vmem] * len(operands),
             out_specs=[vmem] * len(shapes),
@@ -299,11 +292,15 @@
         )(*operands)
         return results if last else results[0]
 
-    beside = swap_blk(whitened, 1)
+    diagonal, along, beside = [swap_blk(whitened, hop) for hop in (3, 2, 1)]
     total = correlate(whitened, swap_cores(whitened))
-    beside, total = lax.optimization_barrier((beside, total))
-    kept, *sent = correlate(beside, swap_cores(beside), total)
-    arrived = [swap_blk(sent[hop - 1], hop * plan.columns) for hop in (2, 3, 1)]
+    beside, along, total = lax.optimization_barrier((beside, along, total))
+    other_beside, other_along = swap_cores(beside), swap_cores(along)
+    diagonal, other_beside = lax.optimization_barrier((diagonal, other_beside))
+    total = correlate(beside, other_beside, total)
+    total = correlate(along, other_along, total)
+    kept, sent = correlate(diagonal, swap_cores(diagonal), total, last=True)
+    arrived = swap_blk(sent, plan.far)
     order, chosen, base = pl.pallas_call(
         functools.partial(prepare_kernel, plan),
         out_shape=[
@@ -320,12 +317,12 @@
     return pl.pallas_call(
         functools.partial(expand_kernel, plan),
         out_shape=jax.ShapeDtypeStruct(out_shape, jnp.float32),
-        in_specs=[vmem] * (3 + len(arrived)),
+        in_specs=[vmem] * 4,
         out_specs=pl.BlockSpec(memory_space=pl.ANY),
         scratch_shapes=[pltpu.VMEM(out_shape, jnp.float32), pltpu.SemaphoreType.DMA((plan.own,))],
         compiler_params=params,
         name="expand",
-    )(order, chosen, base, *arrived)
+    )(order, chosen, base, arrived)
 
 
 def body(traces, valid_flags, source_index):

time: 18.6 us -> 19.3 us (1.038)
  Pallas kernels: 4.16 us -> 4.76 us
  starting transfers between devices: 7.58 us -> 7.87 us
    ppermute x2 -> x4, waiting for transfers between devices: 1.23 us -> 0.2 us  [swap_cores(): return lax.ppermute(array, 'src', [(0, 1), (1, 0)])]
    ppermute x4, waiting for transfers between devices: 4.73 us -> 5.6 us  [swap_blk(): lax.ppermute(array, 'blk', [(place, place ^ hop) for place in range(plan....]
    pallas_call x2 -> x4, Pallas kernels: 1.26 us -> 2.05 us  [correlate(): pl.pallas_call(functools.partial(correlate_kernel, plan, prior is not Non...]
    ppermute x2 -> x4, starting transfers between devices: 0.52 us -> 1.03 us  [swap_cores(): return lax.ppermute(array, 'src', [(0, 1), (1, 0)])]
    ppermute x4, starting transfers between devices: 7.06 us -> 6.84 us  [swap_blk(): lax.ppermute(array, 'blk', [(place, place ^ hop) for place in range(plan....]
  transfers between devices with their start and end apart: 6 -> 8, of which waited for: 3 -> 5; matrix products, arithmetic and copies ran while one was open for 0% -> 0% of each run, Pallas kernels for 6% -> 11%
where the time goes in v10:
time: 19.3 us; the launch traced here: 19.1 us
  starting transfers between devices  7.87 us (41%)
  waiting for transfers between devices  5.8 us (30%)
  Pallas kernels  4.76 us (25%)
  local copies, waits for them, and re-layouts  0.68 us (4%)
    ppermute x4, starting transfers between devices, swap_blk(): lax.ppermute(array, 'blk', [(place, place ^ hop) for place in range(plan....  6.84 us
    ppermute x4, waiting for transfers between devices, swap_blk(): lax.ppermute(array, 'blk', [(place, place ^ hop) for place in range(plan....  5.6 us
    pallas_call x4, Pallas kernels, correlate(): pl.pallas_call(functools.partial(correlate_kernel, plan, prior is not Non...  2.05 us
    pallas_call x1, Pallas kernels, few_channels(): pl.pallas_call(functools.partial(expand_kernel, plan), out_shape=jax.Shap...  1.11 us
    pallas_call x1, Pallas kernels, few_channels(): pl.pallas_call(functools.partial(whiten_kernel, plan), out_shape=pltpu.VM...  1.1 us
    ppermute x4, starting transfers between devices, swap_cores(): return lax.ppermute(array, 'src', [(0, 1), (1, 0)])  1.03 us
    unnamed x2, local copies, waits for them, and re-layouts  0.68 us
    pallas_call x1, Pallas kernels, few_channels(): pl.pallas_call(functools.partial(prepare_kernel, plan), out_shape=[jax.Sh...  0.5 us
  transfers between devices with their start and end apart: 8, of which 5 were waited for; matrix products, arithmetic and copies ran while one was open for 0% of the time, Pallas kernels for 11%

profile of v10, /device:TPU:0, one launch (start us, length us, event | category | flops | bytes accessed | tf_op | source)
XLA Modules:
  0.0 19.1 jit_solution(12167154219398157669)
XLA Ops:
  0.0 1.1 %whiten.1.mine_ref = bf16[48,512]{1,0:T(8,128)(2,1)S(1)} custom-call(f32[24,2,512]{2,1,0:T(2,128)} %traces_hbm.1, s32[2,24]{1,0:T(2,128)} %bitcast.3), custom_call_target="tpu_custom_call" | custom-call | tf_op jit(solution)/shard_map/whiten/pallas_call | solution.py:254
  1.1 0.5 %collective-permute-start.3 = (bf16[48,512]{1,0:T(8,128)(2,1)S(1)}, bf16[48,512]{1,0:T(8,128)(2,1)S(1)}, u32[]{:S(2)}, u32[]{:S(2)}) collective-permute-start(bf16[48,512]{1,0:T(8,128)(2,1)S(1)} %whiten.1.mine_ref), channel_id=1, source_target_pairs={{0,1},{1,0},{2,3},{3,2},{4,5},{5,4},{6,7},{7,6},{8,9},{9,8},{10,11... | collective-permute-start | bytes 147464 | tf_op jit(solution)/shard_map/ppermute | solution.py:249
  1.6 2.6 %collective-permute-start.2 = (bf16[48,512]{1,0:T(8,128)(2,1)S(1)}, bf16[48,512]{1,0:T(8,128)(2,1)S(1)}, u32[]{:S(2)}, u32[]{:S(2)}) collective-permute-start(bf16[48,512]{1,0:T(8,128)(2,1)S(1)} %whiten.1.mine_ref), channel_id=1, source_target_pairs={{0,4},{2,6},{4,0},{6,2},{8,12},{10,14},{12,8},{14,10},{1,5},{3,7},... | collective-permute-start | bytes 147464 | tf_op jit(solution)/shard_map/ppermute | solution.py:252
  4.3 1.5 %collective-permute-start.1 = (bf16[48,512]{1,0:T(8,128)(2,1)S(1)}, bf16[48,512]{1,0:T(8,128)(2,1)S(1)}, u32[]{:S(2)}, u32[]{:S(2)}) collective-permute-start(bf16[48,512]{1,0:T(8,128)(2,1)S(1)} %whiten.1.mine_ref), channel_id=1, source_target_pairs={{0,2},{2,0},{4,6},{6,4},{8,10},{10,8},{12,14},{14,12},{1,3},{3,1},... | collective-permute-start | bytes 147464 | tf_op jit(solution)/shard_map/ppermute | solution.py:252
  5.8 0.0 collective-permute-start
  5.8 0.0 collective-permute-done.3.other_ref
  5.8 0.5 %correlate.4.refs_0_ = f32[192,256]{1,0:T(8,128)S(1)} custom-call(bf16[48,512]{1,0:T(8,128)(2,1)S(1)} %whiten.1.mine_ref, bf16[48,512]{1,0:T(8,128)(2,1)S(1)} %collective-permute-done.3.other_ref), custom_call_target="tpu_custom_call" | custom-call | flops 125829120 | bytes 98304 | tf_op jit(solution)/shard_map/correlate/pallas_call | solution.py:277
  6.3 0.3 %collective-permute-done.2.mine_ref = bf16[48,512]{1,0:T(8,128)(2,1)S(1)} collective-permute-done((bf16[48,512]{1,0:T(8,128)(2,1)S(1)}, bf16[48,512]{1,0:T(8,128)(2,1)S(1)}, u32[]{:S(2)}, u32[]{:S(2)}) %collective-permute-start.2) | collective-permute-done | bytes 49184 | tf_op jit(solution)/shard_map/ppermute | solution.py:252
  6.6 1.8 %collective-permute-done.1.mine_ref = bf16[48,512]{1,0:T(8,128)(2,1)S(1)} collective-permute-done((bf16[48,512]{1,0:T(8,128)(2,1)S(1)}, bf16[48,512]{1,0:T(8,128)(2,1)S(1)}, u32[]{:S(2)}, u32[]{:S(2)}) %collective-permute-start.1) | collective-permute-done | bytes 49184 | tf_op jit(solution)/shard_map/ppermute | solution.py:252
  8.4 0.0 collective-permute-start.4
  8.4 0.5 %collective-permute-start.6 = (bf16[48,512]{1,0:T(8,128)(2,1)S(1)}, bf16[48,512]{1,0:T(8,128)(2,1)S(1)}, u32[]{:S(2)}, u32[]{:S(2)}) collective-permute-start(bf16[48,512]{1,0:T(8,128)(2,1)S(1)} %collective-permute-done.2.mine_ref), channel_id=1, source_target_pairs={{0,1},{1,0},{2,3},{3,2},{4,5},{5,4},{6,7},{7,6},{8,9},{9,8},{10,11... | collective-permute-start | bytes 147464 | tf_op jit(solution)/shard_map/ppermute | solution.py:249
  8.9 1.9 %collective-permute-done.mine_ref = bf16[48,512]{1,0:T(8,128)(2,1)S(1)} collective-permute-done((bf16[48,512]{1,0:T(8,128)(2,1)S(1)}, bf16[48,512]{1,0:T(8,128)(2,1)S(1)}, u32[]{:S(2)}, u32[]{:S(2)}) %collective-permute-start) | collective-permute-done | bytes 49184 | tf_op jit(solution)/shard_map/ppermute | solution.py:252
  10.8 0.0 collective-permute-done.4.other_ref
  10.8 0.0 collective-permute-start.5
  10.8 0.5 %correlate.5.refs_0_ = f32[192,256]{1,0:T(8,128)S(1)} custom-call(bf16[48,512]{1,0:T(8,128)(2,1)S(1)} %collective-permute-done.1.mine_ref, bf16[48,512]{1,0:T(8,128)(2,1)S(1)} %collective-permute-done.4.other_ref, f32[192,256]{1,0:T(8,128)S(1)} %correlate.4.refs_0_), custom_call_target="tpu_custom_call" | custom-call | flops 125829120 | bytes 98304 | tf_op jit(solution)/shard_map/correlate/pallas_call | solution.py:277
  11.3 0.0 collective-permute-done.6.other_ref
  11.3 0.5 %correlate.6.refs_0_ = f32[192,256]{1,0:T(8,128)S(1)} custom-call(bf16[48,512]{1,0:T(8,128)(2,1)S(1)} %collective-permute-done.2.mine_ref, bf16[48,512]{1,0:T(8,128)(2,1)S(1)} %collective-permute-done.6.other_ref, f32[192,256]{1,0:T(8,128)S(1)} %correlate.5.refs_0_), custom_call_target="tpu_custom_call" | custom-call | flops 125829120 | bytes 98304 | tf_op jit(solution)/shard_map/correlate/pallas_call | solution.py:277
  11.8 0.2 %collective-permute-done.5.other_ref = bf16[48,512]{1,0:T(8,128)(2,1)S(1)} collective-permute-done((bf16[48,512]{1,0:T(8,128)(2,1)S(1)}, bf16[48,512]{1,0:T(8,128)(2,1)S(1)}, u32[]{:S(2)}, u32[]{:S(2)}) %collective-permute-start.5) | collective-permute-done | bytes 49184 | tf_op jit(solution)/shard_map/ppermute | solution.py:249
  12.0 0.5 %correlate.7 = (f32[80,256]{1,0:T(8,128)S(1)}, bf16[80,256]{1,0:T(8,128)(2,1)S(1)}) custom-call(bf16[48,512]{1,0:T(8,128)(2,1)S(1)} %collective-permute-done.mine_ref, bf16[48,512]{1,0:T(8,128)(2,1)S(1)} %collective-permute-done.5.other_ref, f32[192,256]{1,0:T(8,128)S(1)} %correlate.6.refs_0_), custom_call_target="tpu_custom_call" | custom-call | flops 125829120 | bytes 98304 | tf_op jit(solution)/shard_map/correlate/pallas_call | solution.py:277
  12.5 2.7 %collective-permute-start.7 = (bf16[80,256]{1,0:T(8,128)(2,1)S(1)}, bf16[80,256]{1,0:T(8,128)(2,1)S(1)}, u32[]{:S(2)}, u32[]{:S(2)}) collective-permute-start(bf16[80,256]{1,0:T(8,128)(2,1)S(1)} %get-tuple-element.24), channel_id=1, source_target_pairs={{0,8},{2,10},{4,12},{6,14},{8,0},{10,2},{12,4},{14,6},{1,9},{3,11}... | collective-permute-start | bytes 122888 | tf_op jit(solution)/shard_map/ppermute | solution.py:252
  15.2 0.0 copy-start
  15.2 0.7 %copy-done = s32[256]{0:T(256)S(1)} copy-done((s32[256]{0:T(256)S(1)}, s32[256]{0:T(256)}, u32[]{:S(2)}) %copy-start) | copy-done | bytes 1048
  15.8 0.5 %prepare.1 = (bf16[96,80]{1,0:T(8,128)(2,1)S(1)}, bf16[256,256]{1,0:T(8,128)(2,1)S(1)}, f32[5,96,256]{2,1,0:T(8,128)S(1)}) custom-call(s32[1,256]{1,0:T(1,128)S(1)} %bitcast.2, f32[80,256]{1,0:T(8,128)S(1)} %get-tuple-element.20.kept_ref), custom_call_target="tpu_custom_call" | custom-call | tf_op jit(solution)/shard_map/prepare/pallas_call | solution.py:304
  16.3 1.7 %collective-permute-done.7.arrived_ref = bf16[80,256]{1,0:T(8,128)(2,1)S(1)} collective-permute-done((bf16[80,256]{1,0:T(8,128)(2,1)S(1)}, bf16[80,256]{1,0:T(8,128)(2,1)S(1)}, u32[]{:S(2)}, u32[]{:S(2)}) %collective-permute-start.7) | collective-permute-done | bytes 40992 | tf_op jit(solution)/shard_map/ppermute | solution.py:252
  18.0 1.1 %expand.1 = f32[3,129,256]{2,1,0:T(8,128)} custom-call(bf16[96,80]{1,0:T(8,128)(2,1)S(1)} %get-tuple-element.21.order_ref, bf16[256,256]{1,0:T(8,128)(2,1)S(1)} %get-tuple-element.22.chosen_ref, f32[5,96,256]{2,1,0:T(8,128)S(1)} %get-tuple-element.23.base_ref, bf16[80,256]{1,0:T(8,128)(2,1)S(1)} %collective-permute-done.7.arrived_ref), custom_call_target="tpu_custom_call" | custom-call | tf_op jit(solution)/shard_map/expand/pallas_call | solution.py:317
Async XLA Ops:
  1.1 4.7 %collective-permute-start.3 = (bf16[48,512]{1,0:T(8,128)(2,1)S(1)}, bf16[48,512]{1,0:T(8,128)(2,1)S(1)}, u32[]{:S(2)}, u32[]{:S(2)}) collective-permute-start(bf16[48,512]{1,0:T(8,128)(2,1)S(1)} %whiten.1.mine_ref), channel_id=1, source_target_pairs={{0,1},{1,0},{2,3},{3,2},{4,5},{5,4},{6,7},{7,6},{8,9},{9,8},{10,11... | collective-permute-start | bytes 147464 | tf_op jit(solution)/shard_map/ppermute | solution.py:249
  1.6 5.0 %collective-permute-start.2 = (bf16[48,512]{1,0:T(8,128)(2,1)S(1)}, bf16[48,512]{1,0:T(8,128)(2,1)S(1)}, u32[]{:S(2)}, u32[]{:S(2)}) collective-permute-start(bf16[48,512]{1,0:T(8,128)(2,1)S(1)} %whiten.1.mine_ref), channel_id=1, source_target_pairs={{0,4},{2,6},{4,0},{6,2},{8,12},{10,14},{12,8},{14,10},{1,5},{3,7},... | collective-permute-start | bytes 147464 | tf_op jit(solution)/shard_map/ppermute | solution.py:252
  4.3 4.1 %collective-permute-start.1 = (bf16[48,512]{1,0:T(8,128)(2,1)S(1)}, bf16[48,512]{1,0:T(8,128)(2,1)S(1)}, u32[]{:S(2)}, u32[]{:S(2)}) collective-permute-start(bf16[48,512]{1,0:T(8,128)(2,1)S(1)} %whiten.1.mine_ref), channel_id=1, source_target_pairs={{0,2},{2,0},{4,6},{6,4},{8,10},{10,8},{12,14},{14,12},{1,3},{3,1},... | collective-permute-start | bytes 147464 | tf_op jit(solution)/shard_map/ppermute | solution.py:252
  5.8 5.0 %collective-permute-start = (bf16[48,512]{1,0:T(8,128)(2,1)S(1)}, bf16[48,512]{1,0:T(8,128)(2,1)S(1)}, u32[]{:S(2)}, u32[]{:S(2)}) collective-permute-start(bf16[48,512]{1,0:T(8,128)(2,1)S(1)} %whiten.1.mine_ref), channel_id=1, source_target_pairs={{0,6},{2,4},{4,2},{6,0},{8,14},{10,12},{12,10},{14,8},{1,7},{3,5},... | collective-permute-start | bytes 147464 | tf_op jit(solution)/shard_map/ppermute | solution.py:252
  8.4 2.4 %collective-permute-start.4 = (bf16[48,512]{1,0:T(8,128)(2,1)S(1)}, bf16[48,512]{1,0:T(8,128)(2,1)S(1)}, u32[]{:S(2)}, u32[]{:S(2)}) collective-permute-start(bf16[48,512]{1,0:T(8,128)(2,1)S(1)} %collective-permute-done.1.mine_ref), channel_id=1, source_target_pairs={{0,1},{1,0},{2,3},{3,2},{4,5},{5,4},{6,7},{7,6},{8,9},{9,8},{10,11... | collective-permute-start | bytes 147464 | tf_op jit(solution)/shard_map/ppermute | solution.py:249
  8.4 2.9 %collective-permute-start.6 = (bf16[48,512]{1,0:T(8,128)(2,1)S(1)}, bf16[48,512]{1,0:T(8,128)(2,1)S(1)}, u32[]{:S(2)}, u32[]{:S(2)}) collective-permute-start(bf16[48,512]{1,0:T(8,128)(2,1)S(1)} %collective-permute-done.2.mine_ref), channel_id=1, source_target_pairs={{0,1},{1,0},{2,3},{3,2},{4,5},{5,4},{6,7},{7,6},{8,9},{9,8},{10,11... | collective-permute-start | bytes 147464 | tf_op jit(solution)/shard_map/ppermute | solution.py:249
  10.8 1.2 %collective-permute-start.5 = (bf16[48,512]{1,0:T(8,128)(2,1)S(1)}, bf16[48,512]{1,0:T(8,128)(2,1)S(1)}, u32[]{:S(2)}, u32[]{:S(2)}) collective-permute-start(bf16[48,512]{1,0:T(8,128)(2,1)S(1)} %collective-permute-done.mine_ref), channel_id=1, source_target_pairs={{0,1},{1,0},{2,3},{3,2},{4,5},{5,4},{6,7},{7,6},{8,9},{9,8},{10,11... | collective-permute-start | bytes 147464 | tf_op jit(solution)/shard_map/ppermute | solution.py:249
  12.5 5.5 %collective-permute-start.7 = (bf16[80,256]{1,0:T(8,128)(2,1)S(1)}, bf16[80,256]{1,0:T(8,128)(2,1)S(1)}, u32[]{:S(2)}, u32[]{:S(2)}) collective-permute-start(bf16[80,256]{1,0:T(8,128)(2,1)S(1)} %get-tuple-element.24), channel_id=1, source_target_pairs={{0,8},{2,10},{4,12},{6,14},{8,0},{10,2},{12,4},{14,6},{1,9},{3,11}... | collective-permute-start | bytes 122888 | tf_op jit(solution)/shard_map/ppermute | solution.py:252
  15.2 0.7 %copy-start = (s32[256]{0:T(256)S(1)}, s32[256]{0:T(256)}, u32[]{:S(2)}) copy-start(s32[256]{0:T(256)} %param.5) | copy-start | bytes 3076

commit v11 on v7

--- a/solution.py
+++ b/solution.py
@@ -85,8 +85,7 @@
         rows = self.own * self.fine
         self.rows = -(-rows // 16) * 16
         self.height = self.own * self.fine_padded
-        self.columns = 2
-        self.targets = blk_size // self.columns
+        self.targets = blk_size // 2
         self.norm_factor = 1.0 / math.sqrt(windows * blk_size * segment)
 
     def fits(self):
@@ -143,7 +142,7 @@
             moved = pltpu.roll(both, step * plan.fine, 1) if step else both
             columns_ref[step * plan.channels : (step + 1) * plan.channels, at] = moved.astype(jnp.bfloat16)
         for hop in range(plan.targets):
-            target = me ^ (hop * plan.columns)
+            target = me ^ hop
             for member in range(plan.own):
                 channel = window * plan.half + target * plan.own + member
                 row = jnp.concatenate([rows_ref[pl.ds(channel, 1), :], filler[:1]], axis=1)
@@ -299,11 +298,11 @@
         )(*operands)
         return results if last else results[0]
 
-    beside = swap_blk(whitened, 1)
-    total = correlate(whitened, swap_cores(whitened))
-    beside, total = lax.optimization_barrier((beside, total))
-    kept, *sent = correlate(beside, swap_cores(beside), total)
-    arrived = [swap_blk(sent[hop - 1], hop * plan.columns) for hop in (2, 3, 1)]
+    other = swap_cores(whitened)
+    across = swap_blk(whitened, plan.targets)
+    total = correlate(whitened, other)
+    kept, *sent = correlate(across, swap_cores(across), total)
+    arrived = [swap_blk(sent[hop - 1], hop) for hop in reversed(range(1, plan.targets))]
     order, chosen, base = pl.pallas_call(
         functools.partial(prepare_kernel, plan),
         out_shape=[

time: 18.6 us -> 18.4 us (0.989)
  waiting for transfers between devices: 5.96 us -> 5.68 us
    ppermute x2, waiting for transfers between devices: 1.23 us -> 0.59 us  [swap_cores(): return lax.ppermute(array, 'src', [(0, 1), (1, 0)])]
    ppermute x4, starting transfers between devices: 7.06 us -> 7.66 us  [swap_blk(): lax.ppermute(array, 'blk', [(place, place ^ hop) for place in range(plan....]
    ppermute x2, starting transfers between devices: 0.52 us -> 0.01 us  [swap_cores(): return lax.ppermute(array, 'src', [(0, 1), (1, 0)])]
    ppermute x4, waiting for transfers between devices: 4.73 us -> 5.09 us  [swap_blk(): lax.ppermute(array, 'blk', [(place, place ^ hop) for place in range(plan....]
  transfers between devices with their start and end apart: 6 -> 6, of which waited for: 3 -> 5; matrix products, arithmetic and copies ran while one was open for 0% -> 0% of each run, Pallas kernels for 6% -> 6%
where the time goes in v11:
time: 18.4 us; the launch traced here: 18.2 us
  starting transfers between devices  7.66 us (42%)
  waiting for transfers between devices  5.68 us (31%)
  Pallas kernels  4.16 us (23%)
  local copies, waits for them, and re-layouts  0.68 us (4%)
    ppermute x4, starting transfers between devices, swap_blk(): lax.ppermute(array, 'blk', [(place, place ^ hop) for place in range(plan....  7.66 us
    ppermute x4, waiting for transfers between devices, swap_blk(): lax.ppermute(array, 'blk', [(place, place ^ hop) for place in range(plan....  5.09 us
    pallas_call x1, Pallas kernels, few_channels(): pl.pallas_call(functools.partial(expand_kernel, plan), out_shape=jax.Shap...  1.3 us
    pallas_call x2, Pallas kernels, correlate(): pl.pallas_call(functools.partial(correlate_kernel, plan, last), out_shape...  1.26 us
    pallas_call x1, Pallas kernels, few_channels(): pl.pallas_call(functools.partial(whiten_kernel, plan), out_shape=pltpu.VM...  1.1 us
    unnamed x2, local copies, waits for them, and re-layouts  0.68 us
    ppermute x2, waiting for transfers between devices, swap_cores(): return lax.ppermute(array, 'src', [(0, 1), (1, 0)])  0.59 us
    pallas_call x1, Pallas kernels, few_channels(): pl.pallas_call(functools.partial(prepare_kernel, plan), out_shape=[jax.Sh...  0.49 us
  transfers between devices with their start and end apart: 6, of which 5 were waited for; matrix products, arithmetic and copies ran while one was open for 0% of the time, Pallas kernels for 6%

profile of v11, /device:TPU:0, one launch (start us, length us, event | category | flops | bytes accessed | tf_op | source)
XLA Modules:
  0.0 18.2 jit_solution(12360766396807488666)
XLA Ops:
  0.0 1.1 %whiten.1.mine_ref = bf16[48,512]{1,0:T(8,128)(2,1)S(1)} custom-call(f32[24,2,512]{2,1,0:T(2,128)} %traces_hbm.1, s32[2,24]{1,0:T(2,128)} %bitcast.3), custom_call_target="tpu_custom_call" | custom-call | tf_op jit(solution)/shard_map/whiten/pallas_call | solution.py:258
  1.1 4.1 %collective-permute-start = (bf16[48,512]{1,0:T(8,128)(2,1)S(1)}, bf16[48,512]{1,0:T(8,128)(2,1)S(1)}, u32[]{:S(2)}, u32[]{:S(2)}) collective-permute-start(bf16[48,512]{1,0:T(8,128)(2,1)S(1)} %whiten.1.mine_ref), channel_id=1, source_target_pairs={{0,8},{2,10},{4,12},{6,14},{8,0},{10,2},{12,4},{14,6},{1,9},{3,11}... | collective-permute-start | bytes 147464 | tf_op jit(solution)/shard_map/ppermute | solution.py:256
  5.2 0.0 collective-permute-start.2
  5.2 2.6 %collective-permute-done.mine_ref = bf16[48,512]{1,0:T(8,128)(2,1)S(1)} collective-permute-done((bf16[48,512]{1,0:T(8,128)(2,1)S(1)}, bf16[48,512]{1,0:T(8,128)(2,1)S(1)}, u32[]{:S(2)}, u32[]{:S(2)}) %collective-permute-start) | collective-permute-done | bytes 49184 | tf_op jit(solution)/shard_map/ppermute | solution.py:256
  7.8 0.0 collective-permute-start.1
  7.8 0.0 collective-permute-done.2.other_ref
  7.8 0.6 %correlate.2.refs_0_ = f32[384,256]{1,0:T(8,128)S(1)} custom-call(bf16[48,512]{1,0:T(8,128)(2,1)S(1)} %whiten.1.mine_ref, bf16[48,512]{1,0:T(8,128)(2,1)S(1)} %collective-permute-done.2.other_ref), custom_call_target="tpu_custom_call" | custom-call | flops 251658240 | bytes 98304 | tf_op jit(solution)/shard_map/correlate/pallas_call | solution.py:283
  8.5 0.6 %collective-permute-done.1.other_ref = bf16[48,512]{1,0:T(8,128)(2,1)S(1)} collective-permute-done((bf16[48,512]{1,0:T(8,128)(2,1)S(1)}, bf16[48,512]{1,0:T(8,128)(2,1)S(1)}, u32[]{:S(2)}, u32[]{:S(2)}) %collective-permute-start.1) | collective-permute-done | bytes 49184 | tf_op jit(solution)/shard_map/ppermute | solution.py:253
  9.0 0.6 %correlate.3 = (f32[80,256]{1,0:T(8,128)S(1)}, bf16[80,256]{1,0:T(8,128)(2,1)S(1)}, bf16[80,256]{1,0:T(8,128)(2,1)S(1)}, bf16[80,256]{1,0:T(8,128)(2,1)S(1)}) custom-call(bf16[48,512]{1,0:T(8,128)(2,1)S(1)} %collective-permute-done.mine_ref, bf16[48,512]{1,0:T(8,128)(2,1)S(1)} %collective-permute-done.1.other_ref, f32[384,256]{1,0:T(8,128)S(1)} %correlate.2.refs_0_), custom_call_target="tpu_custom_call" | custom-call | flops 251658240 | bytes 98304 | tf_op jit(solution)/shard_map/correlate/pallas_call | solution.py:283
  9.7 2.4 %collective-permute-start.3 = (bf16[80,256]{1,0:T(8,128)(2,1)S(1)}, bf16[80,256]{1,0:T(8,128)(2,1)S(1)}, u32[]{:S(2)}, u32[]{:S(2)}) collective-permute-start(bf16[80,256]{1,0:T(8,128)(2,1)S(1)} %get-tuple-element.16), channel_id=1, source_target_pairs={{0,6},{2,4},{4,2},{6,0},{8,14},{10,12},{12,10},{14,8},{1,7},{3,5},... | collective-permute-start | bytes 122888 | tf_op jit(solution)/shard_map/ppermute | solution.py:256
  12.1 0.9 %collective-permute-start.4 = (bf16[80,256]{1,0:T(8,128)(2,1)S(1)}, bf16[80,256]{1,0:T(8,128)(2,1)S(1)}, u32[]{:S(2)}, u32[]{:S(2)}) collective-permute-start(bf16[80,256]{1,0:T(8,128)(2,1)S(1)} %get-tuple-element.17), channel_id=1, source_target_pairs={{0,4},{2,6},{4,0},{6,2},{8,12},{10,14},{12,8},{14,10},{1,5},{3,7},... | collective-permute-start | bytes 122888 | tf_op jit(solution)/shard_map/ppermute | solution.py:256
  12.9 0.3 %collective-permute-start.5 = (bf16[80,256]{1,0:T(8,128)(2,1)S(1)}, bf16[80,256]{1,0:T(8,128)(2,1)S(1)}, u32[]{:S(2)}, u32[]{:S(2)}) collective-permute-start(bf16[80,256]{1,0:T(8,128)(2,1)S(1)} %get-tuple-element.18), channel_id=1, source_target_pairs={{0,2},{2,0},{4,6},{6,4},{8,10},{10,8},{12,14},{14,12},{1,3},{3,1},... | collective-permute-start | bytes 122888 | tf_op jit(solution)/shard_map/ppermute | solution.py:256
  13.2 0.0 copy-start
  13.2 0.7 %copy-done = s32[256]{0:T(256)S(1)} copy-done((s32[256]{0:T(256)S(1)}, s32[256]{0:T(256)}, u32[]{:S(2)}) %copy-start) | copy-done | bytes 1048
  13.9 0.5 %prepare.1 = (bf16[96,80]{1,0:T(8,128)(2,1)S(1)}, bf16[256,256]{1,0:T(8,128)(2,1)S(1)}, f32[5,96,256]{2,1,0:T(8,128)S(1)}) custom-call(s32[1,256]{1,0:T(1,128)S(1)} %bitcast.2, f32[80,256]{1,0:T(8,128)S(1)} %get-tuple-element.12.kept_ref), custom_call_target="tpu_custom_call" | custom-call | tf_op jit(solution)/shard_map/prepare/pallas_call | solution.py:306
  14.4 0.4 %collective-permute-done.3.refs_0_ = bf16[80,256]{1,0:T(8,128)(2,1)S(1)} collective-permute-done((bf16[80,256]{1,0:T(8,128)(2,1)S(1)}, bf16[80,256]{1,0:T(8,128)(2,1)S(1)}, u32[]{:S(2)}, u32[]{:S(2)}) %collective-permute-start.3) | collective-permute-done | bytes 40992 | tf_op jit(solution)/shard_map/ppermute | solution.py:256
  14.8 1.3 %collective-permute-done.4.refs_1_ = bf16[80,256]{1,0:T(8,128)(2,1)S(1)} collective-permute-done((bf16[80,256]{1,0:T(8,128)(2,1)S(1)}, bf16[80,256]{1,0:T(8,128)(2,1)S(1)}, u32[]{:S(2)}, u32[]{:S(2)}) %collective-permute-start.4) | collective-permute-done | bytes 40992 | tf_op jit(solution)/shard_map/ppermute | solution.py:256
  16.1 0.9 %collective-permute-done.5.refs_2_ = bf16[80,256]{1,0:T(8,128)(2,1)S(1)} collective-permute-done((bf16[80,256]{1,0:T(8,128)(2,1)S(1)}, bf16[80,256]{1,0:T(8,128)(2,1)S(1)}, u32[]{:S(2)}, u32[]{:S(2)}) %collective-permute-start.5) | collective-permute-done | bytes 40992 | tf_op jit(solution)/shard_map/ppermute | solution.py:256
  16.9 1.3 %expand.1 = f32[3,129,256]{2,1,0:T(8,128)} custom-call(bf16[96,80]{1,0:T(8,128)(2,1)S(1)} %get-tuple-element.13.order_ref, bf16[256,256]{1,0:T(8,128)(2,1)S(1)} %get-tuple-element.14.chosen_ref, f32[5,96,256]{2,1,0:T(8,128)S(1)} %get-tuple-element.15.base_ref, bf16[80,256]{1,0:T(8,128)(2,1)S(1)} %collective-permute-done.3.refs_0_, ...), custom_call_target="tpu_custom_call" | custom-call | tf_op jit(solution)/shard_map/expand/pallas_call | solution.py:319
Async XLA Ops:
  1.1 6.7 %collective-permute-start = (bf16[48,512]{1,0:T(8,128)(2,1)S(1)}, bf16[48,512]{1,0:T(8,128)(2,1)S(1)}, u32[]{:S(2)}, u32[]{:S(2)}) collective-permute-start(bf16[48,512]{1,0:T(8,128)(2,1)S(1)} %whiten.1.mine_ref), channel_id=1, source_target_pairs={{0,8},{2,10},{4,12},{6,14},{8,0},{10,2},{12,4},{14,6},{1,9},{3,11}... | collective-permute-start | bytes 147464 | tf_op jit(solution)/shard_map/ppermute | solution.py:256
  5.2 2.6 %collective-permute-start.2 = (bf16[48,512]{1,0:T(8,128)(2,1)S(1)}, bf16[48,512]{1,0:T(8,128)(2,1)S(1)}, u32[]{:S(2)}, u32[]{:S(2)}) collective-permute-start(bf16[48,512]{1,0:T(8,128)(2,1)S(1)} %whiten.1.mine_ref), channel_id=1, source_target_pairs={{0,1},{1,0},{2,3},{3,2},{4,5},{5,4},{6,7},{7,6},{8,9},{9,8},{10,11... | collective-permute-start | bytes 147464 | tf_op jit(solution)/shard_map/ppermute | solution.py:253
  7.8 1.2 %collective-permute-start.1 = (bf16[48,512]{1,0:T(8,128)(2,1)S(1)}, bf16[48,512]{1,0:T(8,128)(2,1)S(1)}, u32[]{:S(2)}, u32[]{:S(2)}) collective-permute-start(bf16[48,512]{1,0:T(8,128)(2,1)S(1)} %collective-permute-done.mine_ref), channel_id=1, source_target_pairs={{0,1},{1,0},{2,3},{3,2},{4,5},{5,4},{6,7},{7,6},{8,9},{9,8},{10,11... | collective-permute-start | bytes 147464 | tf_op jit(solution)/shard_map/ppermute | solution.py:253
  9.7 5.1 %collective-permute-start.3 = (bf16[80,256]{1,0:T(8,128)(2,1)S(1)}, bf16[80,256]{1,0:T(8,128)(2,1)S(1)}, u32[]{:S(2)}, u32[]{:S(2)}) collective-permute-start(bf16[80,256]{1,0:T(8,128)(2,1)S(1)} %get-tuple-element.16), channel_id=1, source_target_pairs={{0,6},{2,4},{4,2},{6,0},{8,14},{10,12},{12,10},{14,8},{1,7},{3,5},... | collective-permute-start | bytes 122888 | tf_op jit(solution)/shard_map/ppermute | solution.py:256
  12.1 4.0 %collective-permute-start.4 = (bf16[80,256]{1,0:T(8,128)(2,1)S(1)}, bf16[80,256]{1,0:T(8,128)(2,1)S(1)}, u32[]{:S(2)}, u32[]{:S(2)}) collective-permute-start(bf16[80,256]{1,0:T(8,128)(2,1)S(1)} %get-tuple-element.17), channel_id=1, source_target_pairs={{0,4},{2,6},{4,0},{6,2},{8,12},{10,14},{12,8},{14,10},{1,5},{3,7},... | collective-permute-start | bytes 122888 | tf_op jit(solution)/shard_map/ppermute | solution.py:256
  12.9 4.0 %collective-permute-start.5 = (bf16[80,256]{1,0:T(8,128)(2,1)S(1)}, bf16[80,256]{1,0:T(8,128)(2,1)S(1)}, u32[]{:S(2)}, u32[]{:S(2)}) collective-permute-start(bf16[80,256]{1,0:T(8,128)(2,1)S(1)} %get-tuple-element.18), channel_id=1, source_target_pairs={{0,2},{2,0},{4,6},{6,4},{8,10},{10,8},{12,14},{14,12},{1,3},{3,1},... | collective-permute-start | bytes 122888 | tf_op jit(solution)/shard_map/ppermute | solution.py:256
  13.2 0.7 %copy-start = (s32[256]{0:T(256)S(1)}, s32[256]{0:T(256)}, u32[]{:S(2)}) copy-start(s32[256]{0:T(256)} %param.5) | copy-start | bytes 3076

commit v12 on v11

--- a/solution.py
+++ b/solution.py
@@ -206,7 +206,8 @@
     chosen = chosen.astype(jnp.float32).astype(jnp.bfloat16)
     chosen_ref[...] = chosen
     order = order_matrix(plan)
-    order_ref[...] = order
+    for block in range(plan.targets - 1):
+        order_ref[:, block * plan.rows : (block + 1) * plan.rows] = order
     kept = kept_ref[...] * plan.norm_factor
     high = kept.astype(jnp.bfloat16)
     low = (kept - high.astype(jnp.float32)).astype(jnp.bfloat16)
@@ -219,17 +220,13 @@
 
 def expand_kernel(plan, order_ref, chosen_ref, base_ref, *refs):
     *arrived_refs, out_hbm, out_ref, sems = refs
-    order = order_ref[...]
-    arrived = sum(jnp.dot(order, ref[...], preferred_element_type=jnp.float32) for ref in arrived_refs)
+    blocks = jnp.concatenate([ref[...] for ref in arrived_refs], axis=0)
+    arrived = jnp.dot(order_ref[...], blocks, preferred_element_type=jnp.float32) * plan.norm_factor
     high = arrived.astype(jnp.bfloat16).astype(jnp.float32)
-    chosen = chosen_ref[...]
-    expanded = []
-    for step in range(plan.coarse):
-        moved = sum(
-            jnp.dot(inside_step(plan, step, part), chosen, preferred_element_type=jnp.float32)
-            for part in (high, arrived - high)
-        )
-        expanded.append(base_ref[step] + moved * plan.norm_factor)
+    steps = [inside_step(plan, step, part) for part in (high, arrived - high) for step in range(plan.coarse)]
+    moved = jnp.dot(jnp.concatenate(steps, axis=0), chosen_ref[...], preferred_element_type=jnp.float32)
+    moved = moved.reshape(2, plan.coarse, plan.height, plan.source_count)
+    expanded = [base_ref[step] + (moved[0, step] + moved[1, step]) for step in range(plan.coarse)]
     copies = []
     for member in range(plan.own):
         for step in range(plan.coarse):
@@ -302,11 +299,11 @@
     across = swap_blk(whitened, plan.targets)
     total = correlate(whitened, other)
     kept, *sent = correlate(across, swap_cores(across), total)
-    arrived = [swap_blk(sent[hop - 1], hop) for hop in reversed(range(1, plan.targets))]
+    arrived = [swap_blk(sent[hop - 1], hop) for hop in (3, 1, 2)]
     order, chosen, base = pl.pallas_call(
         functools.partial(prepare_kernel, plan),
         out_shape=[
-            jax.ShapeDtypeStruct((plan.height, plan.rows), jnp.bfloat16),
+            jax.ShapeDtypeStruct((plan.height, (plan.targets - 1) * plan.rows), jnp.bfloat16),
             jax.ShapeDtypeStruct((LANES, plan.source_count), jnp.bfloat16),
             jax.ShapeDtypeStruct((plan.coarse, plan.height, plan.source_count), jnp.float32),
         ],

time: 18.4 us -> 17.9 us (0.973)
  waiting for transfers between devices: 5.68 us -> 5.36 us
    ppermute x4, waiting for transfers between devices: 5.09 us -> 4.77 us  [swap_blk(): lax.ppermute(array, 'blk', [(place, place ^ hop) for place in range(plan....]
where the time goes in v12:
time: 17.9 us; the launch traced here: 17.8 us
  starting transfers between devices  7.66 us (43%)
  waiting for transfers between devices  5.36 us (30%)
  Pallas kernels  4.06 us (23%)
  local copies, waits for them, and re-layouts  0.68 us (4%)
    ppermute x4, starting transfers between devices, swap_blk(): lax.ppermute(array, 'blk', [(place, place ^ hop) for place in range(plan....  7.66 us
    ppermute x4, waiting for transfers between devices, swap_blk(): lax.ppermute(array, 'blk', [(place, place ^ hop) for place in range(plan....  4.77 us
    pallas_call x2, Pallas kernels, correlate(): pl.pallas_call(functools.partial(correlate_kernel, plan, last), out_shape...  1.26 us
    pallas_call x1, Pallas kernels, few_channels(): pl.pallas_call(functools.partial(expand_kernel, plan), out_shape=jax.Shap...  1.2 us
    pallas_call x1, Pallas kernels, few_channels(): pl.pallas_call(functools.partial(whiten_kernel, plan), out_shape=pltpu.VM...  1.1 us
    unnamed x2, local copies, waits for them, and re-layouts  0.68 us
    ppermute x2, waiting for transfers between devices, swap_cores(): return lax.ppermute(array, 'src', [(0, 1), (1, 0)])  0.59 us
    pallas_call x1, Pallas kernels, few_channels(): pl.pallas_call(functools.partial(prepare_kernel, plan), out_shape=[jax.Sh...  0.49 us
  transfers between devices with their start and end apart: 6, of which 5 were waited for; matrix products, arithmetic and copies ran while one was open for 0% of the time, Pallas kernels for 6%

profile of v12, /device:TPU:0, one launch (start us, length us, event | category | flops | bytes accessed | tf_op | source)
XLA Modules:
  0.0 17.8 jit_solution(17061285625916450497)
XLA Ops:
  0.0 1.1 %whiten.1.mine_ref = bf16[48,512]{1,0:T(8,128)(2,1)S(1)} custom-call(f32[24,2,512]{2,1,0:T(2,128)} %traces_hbm.1, s32[2,24]{1,0:T(2,128)} %bitcast.3), custom_call_target="tpu_custom_call" | custom-call | tf_op jit(solution)/shard_map/whiten/pallas_call | solution.py:255
  1.1 4.1 %collective-permute-start = (bf16[48,512]{1,0:T(8,128)(2,1)S(1)}, bf16[48,512]{1,0:T(8,128)(2,1)S(1)}, u32[]{:S(2)}, u32[]{:S(2)}) collective-permute-start(bf16[48,512]{1,0:T(8,128)(2,1)S(1)} %whiten.1.mine_ref), channel_id=1, source_target_pairs={{0,8},{2,10},{4,12},{6,14},{8,0},{10,2},{12,4},{14,6},{1,9},{3,11}... | collective-permute-start | bytes 147464 | tf_op jit(solution)/shard_map/ppermute | solution.py:253
  5.2 0.0 collective-permute-start.2
  5.2 2.6 %collective-permute-done.mine_ref = bf16[48,512]{1,0:T(8,128)(2,1)S(1)} collective-permute-done((bf16[48,512]{1,0:T(8,128)(2,1)S(1)}, bf16[48,512]{1,0:T(8,128)(2,1)S(1)}, u32[]{:S(2)}, u32[]{:S(2)}) %collective-permute-start) | collective-permute-done | bytes 49184 | tf_op jit(solution)/shard_map/ppermute | solution.py:253
  7.8 0.0 collective-permute-start.1
  7.8 0.0 collective-permute-done.2.other_ref
  7.8 0.6 %correlate.2.refs_0_ = f32[384,256]{1,0:T(8,128)S(1)} custom-call(bf16[48,512]{1,0:T(8,128)(2,1)S(1)} %whiten.1.mine_ref, bf16[48,512]{1,0:T(8,128)(2,1)S(1)} %collective-permute-done.2.other_ref), custom_call_target="tpu_custom_call" | custom-call | flops 251658240 | bytes 98304 | tf_op jit(solution)/shard_map/correlate/pallas_call | solution.py:280
  8.5 0.6 %collective-permute-done.1.other_ref = bf16[48,512]{1,0:T(8,128)(2,1)S(1)} collective-permute-done((bf16[48,512]{1,0:T(8,128)(2,1)S(1)}, bf16[48,512]{1,0:T(8,128)(2,1)S(1)}, u32[]{:S(2)}, u32[]{:S(2)}) %collective-permute-start.1) | collective-permute-done | bytes 49184 | tf_op jit(solution)/shard_map/ppermute | solution.py:250
  9.0 0.6 %correlate.3 = (f32[80,256]{1,0:T(8,128)S(1)}, bf16[80,256]{1,0:T(8,128)(2,1)S(1)}, bf16[80,256]{1,0:T(8,128)(2,1)S(1)}, bf16[80,256]{1,0:T(8,128)(2,1)S(1)}) custom-call(bf16[48,512]{1,0:T(8,128)(2,1)S(1)} %collective-permute-done.mine_ref, bf16[48,512]{1,0:T(8,128)(2,1)S(1)} %collective-permute-done.1.other_ref, f32[384,256]{1,0:T(8,128)S(1)} %correlate.2.refs_0_), custom_call_target="tpu_custom_call" | custom-call | flops 251658240 | bytes 98304 | tf_op jit(solution)/shard_map/correlate/pallas_call | solution.py:280
  9.7 2.4 %collective-permute-start.3 = (bf16[80,256]{1,0:T(8,128)(2,1)S(1)}, bf16[80,256]{1,0:T(8,128)(2,1)S(1)}, u32[]{:S(2)}, u32[]{:S(2)}) collective-permute-start(bf16[80,256]{1,0:T(8,128)(2,1)S(1)} %get-tuple-element.16), channel_id=1, source_target_pairs={{0,6},{2,4},{4,2},{6,0},{8,14},{10,12},{12,10},{14,8},{1,7},{3,5},... | collective-permute-start | bytes 122888 | tf_op jit(solution)/shard_map/ppermute | solution.py:253
  12.1 0.5 %collective-permute-start.4 = (bf16[80,256]{1,0:T(8,128)(2,1)S(1)}, bf16[80,256]{1,0:T(8,128)(2,1)S(1)}, u32[]{:S(2)}, u32[]{:S(2)}) collective-permute-start(bf16[80,256]{1,0:T(8,128)(2,1)S(1)} %get-tuple-element.17), channel_id=1, source_target_pairs={{0,2},{2,0},{4,6},{6,4},{8,10},{10,8},{12,14},{14,12},{1,3},{3,1},... | collective-permute-start | bytes 122888 | tf_op jit(solution)/shard_map/ppermute | solution.py:253
  12.6 0.6 %collective-permute-start.5 = (bf16[80,256]{1,0:T(8,128)(2,1)S(1)}, bf16[80,256]{1,0:T(8,128)(2,1)S(1)}, u32[]{:S(2)}, u32[]{:S(2)}) collective-permute-start(bf16[80,256]{1,0:T(8,128)(2,1)S(1)} %get-tuple-element.18), channel_id=1, source_target_pairs={{0,4},{2,6},{4,0},{6,2},{8,12},{10,14},{12,8},{14,10},{1,5},{3,7},... | collective-permute-start | bytes 122888 | tf_op jit(solution)/shard_map/ppermute | solution.py:253
  13.2 0.0 copy-start
  13.2 0.7 %copy-done = s32[256]{0:T(256)S(1)} copy-done((s32[256]{0:T(256)S(1)}, s32[256]{0:T(256)}, u32[]{:S(2)}) %copy-start) | copy-done | bytes 1048
  13.9 0.5 %prepare.1 = (bf16[96,240]{1,0:T(8,128)(2,1)S(1)}, bf16[256,256]{1,0:T(8,128)(2,1)S(1)}, f32[5,96,256]{2,1,0:T(8,128)S(1)}) custom-call(s32[1,256]{1,0:T(1,128)S(1)} %bitcast.2, f32[80,256]{1,0:T(8,128)S(1)} %get-tuple-element.12.kept_ref), custom_call_target="tpu_custom_call" | custom-call | tf_op jit(solution)/shard_map/prepare/pallas_call | solution.py:303
  14.4 0.2 %collective-permute-done.3.refs_0_ = bf16[80,256]{1,0:T(8,128)(2,1)S(1)} collective-permute-done((bf16[80,256]{1,0:T(8,128)(2,1)S(1)}, bf16[80,256]{1,0:T(8,128)(2,1)S(1)}, u32[]{:S(2)}, u32[]{:S(2)}) %collective-permute-start.3) | collective-permute-done | bytes 40992 | tf_op jit(solution)/shard_map/ppermute | solution.py:253
  14.7 1.4 %collective-permute-done.4.refs_1_ = bf16[80,256]{1,0:T(8,128)(2,1)S(1)} collective-permute-done((bf16[80,256]{1,0:T(8,128)(2,1)S(1)}, bf16[80,256]{1,0:T(8,128)(2,1)S(1)}, u32[]{:S(2)}, u32[]{:S(2)}) %collective-permute-start.4) | collective-permute-done | bytes 40992 | tf_op jit(solution)/shard_map/ppermute | solution.py:253
  16.1 0.5 %collective-permute-done.5.refs_2_ = bf16[80,256]{1,0:T(8,128)(2,1)S(1)} collective-permute-done((bf16[80,256]{1,0:T(8,128)(2,1)S(1)}, bf16[80,256]{1,0:T(8,128)(2,1)S(1)}, u32[]{:S(2)}, u32[]{:S(2)}) %collective-permute-start.5) | collective-permute-done | bytes 40992 | tf_op jit(solution)/shard_map/ppermute | solution.py:253
  16.6 1.2 %expand.1 = f32[3,129,256]{2,1,0:T(8,128)} custom-call(bf16[96,240]{1,0:T(8,128)(2,1)S(1)} %get-tuple-element.13.order_ref, bf16[256,256]{1,0:T(8,128)(2,1)S(1)} %get-tuple-element.14.chosen_ref, f32[5,96,256]{2,1,0:T(8,128)S(1)} %get-tuple-element.15.base_ref, bf16[80,256]{1,0:T(8,128)(2,1)S(1)} %collective-permute-done.3.refs_0_, ...), custom_call_target="tpu_custom_call" | custom-call | tf_op jit(solution)/shard_map/expand/pallas_call | solution.py:316
Async XLA Ops:
  1.1 6.7 %collective-permute-start = (bf16[48,512]{1,0:T(8,128)(2,1)S(1)}, bf16[48,512]{1,0:T(8,128)(2,1)S(1)}, u32[]{:S(2)}, u32[]{:S(2)}) collective-permute-start(bf16[48,512]{1,0:T(8,128)(2,1)S(1)} %whiten.1.mine_ref), channel_id=1, source_target_pairs={{0,8},{2,10},{4,12},{6,14},{8,0},{10,2},{12,4},{14,6},{1,9},{3,11}... | collective-permute-start | bytes 147464 | tf_op jit(solution)/shard_map/ppermute | solution.py:253
  5.2 2.6 %collective-permute-start.2 = (bf16[48,512]{1,0:T(8,128)(2,1)S(1)}, bf16[48,512]{1,0:T(8,128)(2,1)S(1)}, u32[]{:S(2)}, u32[]{:S(2)}) collective-permute-start(bf16[48,512]{1,0:T(8,128)(2,1)S(1)} %whiten.1.mine_ref), channel_id=1, source_target_pairs={{0,1},{1,0},{2,3},{3,2},{4,5},{5,4},{6,7},{7,6},{8,9},{9,8},{10,11... | collective-permute-start | bytes 147464 | tf_op jit(solution)/shard_map/ppermute | solution.py:250
  7.8 1.2 %collective-permute-start.1 = (bf16[48,512]{1,0:T(8,128)(2,1)S(1)}, bf16[48,512]{1,0:T(8,128)(2,1)S(1)}, u32[]{:S(2)}, u32[]{:S(2)}) collective-permute-start(bf16[48,512]{1,0:T(8,128)(2,1)S(1)} %collective-permute-done.mine_ref), channel_id=1, source_target_pairs={{0,1},{1,0},{2,3},{3,2},{4,5},{5,4},{6,7},{7,6},{8,9},{9,8},{10,11... | collective-permute-start | bytes 147464 | tf_op jit(solution)/shard_map/ppermute | solution.py:250
  9.7 5.0 %collective-permute-start.3 = (bf16[80,256]{1,0:T(8,128)(2,1)S(1)}, bf16[80,256]{1,0:T(8,128)(2,1)S(1)}, u32[]{:S(2)}, u32[]{:S(2)}) collective-permute-start(bf16[80,256]{1,0:T(8,128)(2,1)S(1)} %get-tuple-element.16), channel_id=1, source_target_pairs={{0,6},{2,4},{4,2},{6,0},{8,14},{10,12},{12,10},{14,8},{1,7},{3,5},... | collective-permute-start | bytes 122888 | tf_op jit(solution)/shard_map/ppermute | solution.py:253
  12.1 4.0 %collective-permute-start.4 = (bf16[80,256]{1,0:T(8,128)(2,1)S(1)}, bf16[80,256]{1,0:T(8,128)(2,1)S(1)}, u32[]{:S(2)}, u32[]{:S(2)}) collective-permute-start(bf16[80,256]{1,0:T(8,128)(2,1)S(1)} %get-tuple-element.17), channel_id=1, source_target_pairs={{0,2},{2,0},{4,6},{6,4},{8,10},{10,8},{12,14},{14,12},{1,3},{3,1},... | collective-permute-start | bytes 122888 | tf_op jit(solution)/shard_map/ppermute | solution.py:253
  12.6 4.0 %collective-permute-start.5 = (bf16[80,256]{1,0:T(8,128)(2,1)S(1)}, bf16[80,256]{1,0:T(8,128)(2,1)S(1)}, u32[]{:S(2)}, u32[]{:S(2)}) collective-permute-start(bf16[80,256]{1,0:T(8,128)(2,1)S(1)} %get-tuple-element.18), channel_id=1, source_target_pairs={{0,4},{2,6},{4,0},{6,2},{8,12},{10,14},{12,8},{14,10},{1,5},{3,7},... | collective-permute-start | bytes 122888 | tf_op jit(solution)/shard_map/ppermute | solution.py:253
  13.2 0.7 %copy-start = (s32[256]{0:T(256)S(1)}, s32[256]{0:T(256)}, u32[]{:S(2)}) copy-start(s32[256]{0:T(256)} %param.5) | copy-start | bytes 3076

commit v13 on v12

--- a/solution.py
+++ b/solution.py
@@ -299,7 +299,7 @@
     across = swap_blk(whitened, plan.targets)
     total = correlate(whitened, other)
     kept, *sent = correlate(across, swap_cores(across), total)
-    arrived = [swap_blk(sent[hop - 1], hop) for hop in (3, 1, 2)]
+    arrived = [swap_blk(sent[hop - 1], hop) for hop in (1, 3, 2)]
     order, chosen, base = pl.pallas_call(
         functools.partial(prepare_kernel, plan),
         out_shape=[

time: 17.9 us -> 17.9 us (level)
  transfers between devices with their start and end apart: 6 -> 6, of which waited for: 5 -> 3; matrix products, arithmetic and copies ran while one was open for 0% -> 0% of each run, Pallas kernels for 6% -> 6%
where the time goes in v13:
time: 17.9 us; the launch traced here: 17.8 us
  starting transfers between devices  7.66 us (43%)
  waiting for transfers between devices  5.36 us (30%)
  Pallas kernels  4.06 us (23%)
  local copies, waits for them, and re-layouts  0.68 us (4%)
    ppermute x4, starting transfers between devices, swap_blk(): lax.ppermute(array, 'blk', [(place, place ^ hop) for place in range(plan....  7.65 us
    ppermute x4, waiting for transfers between devices, swap_blk(): lax.ppermute(array, 'blk', [(place, place ^ hop) for place in range(plan....  4.77 us
    pallas_call x2, Pallas kernels, correlate(): pl.pallas_call(functools.partial(correlate_kernel, plan, last), out_shape...  1.26 us
    pallas_call x1, Pallas kernels, few_channels(): pl.pallas_call(functools.partial(expand_kernel, plan), out_shape=jax.Shap...  1.2 us
    pallas_call x1, Pallas kernels, few_channels(): pl.pallas_call(functools.partial(whiten_kernel, plan), out_shape=pltpu.VM...  1.1 us
    unnamed x2, local copies, waits for them, and re-layouts  0.68 us
    ppermute x2, waiting for transfers between devices, swap_cores(): return lax.ppermute(array, 'src', [(0, 1), (1, 0)])  0.59 us
    pallas_call x1, Pallas kernels, few_channels(): pl.pallas_call(functools.partial(prepare_kernel, plan), out_shape=[jax.Sh...  0.49 us
  transfers between devices with their start and end apart: 6, of which 3 were waited for; matrix products, arithmetic and copies ran while one was open for 0% of the time, Pallas kernels for 6%

profile of v13, /device:TPU:0, one launch (start us, length us, event | category | flops | bytes accessed | tf_op | source)
XLA Modules:
  0.0 17.8 jit_solution(4330788878979234640)
XLA Ops:
  0.0 1.1 %whiten.1.mine_ref = bf16[48,512]{1,0:T(8,128)(2,1)S(1)} custom-call(f32[24,2,512]{2,1,0:T(2,128)} %traces_hbm.1, s32[2,24]{1,0:T(2,128)} %bitcast.3), custom_call_target="tpu_custom_call" | custom-call | tf_op jit(solution)/shard_map/whiten/pallas_call | solution.py:255
  1.1 4.1 %collective-permute-start = (bf16[48,512]{1,0:T(8,128)(2,1)S(1)}, bf16[48,512]{1,0:T(8,128)(2,1)S(1)}, u32[]{:S(2)}, u32[]{:S(2)}) collective-permute-start(bf16[48,512]{1,0:T(8,128)(2,1)S(1)} %whiten.1.mine_ref), channel_id=1, source_target_pairs={{0,8},{2,10},{4,12},{6,14},{8,0},{10,2},{12,4},{14,6},{1,9},{3,11}... | collective-permute-start | bytes 147464 | tf_op jit(solution)/shard_map/ppermute | solution.py:253
  5.2 0.0 collective-permute-start.2
  5.2 2.6 %collective-permute-done.mine_ref = bf16[48,512]{1,0:T(8,128)(2,1)S(1)} collective-permute-done((bf16[48,512]{1,0:T(8,128)(2,1)S(1)}, bf16[48,512]{1,0:T(8,128)(2,1)S(1)}, u32[]{:S(2)}, u32[]{:S(2)}) %collective-permute-start) | collective-permute-done | bytes 49184 | tf_op jit(solution)/shard_map/ppermute | solution.py:253
  7.8 0.0 collective-permute-start.1
  7.8 0.0 collective-permute-done.2.other_ref
  7.8 0.6 %correlate.2.refs_0_ = f32[384,256]{1,0:T(8,128)S(1)} custom-call(bf16[48,512]{1,0:T(8,128)(2,1)S(1)} %whiten.1.mine_ref, bf16[48,512]{1,0:T(8,128)(2,1)S(1)} %collective-permute-done.2.other_ref), custom_call_target="tpu_custom_call" | custom-call | flops 251658240 | bytes 98304 | tf_op jit(solution)/shard_map/correlate/pallas_call | solution.py:280
  8.5 0.6 %collective-permute-done.1.other_ref = bf16[48,512]{1,0:T(8,128)(2,1)S(1)} collective-permute-done((bf16[48,512]{1,0:T(8,128)(2,1)S(1)}, bf16[48,512]{1,0:T(8,128)(2,1)S(1)}, u32[]{:S(2)}, u32[]{:S(2)}) %collective-permute-start.1) | collective-permute-done | bytes 49184 | tf_op jit(solution)/shard_map/ppermute | solution.py:250
  9.0 0.6 %correlate.3 = (f32[80,256]{1,0:T(8,128)S(1)}, bf16[80,256]{1,0:T(8,128)(2,1)S(1)}, bf16[80,256]{1,0:T(8,128)(2,1)S(1)}, bf16[80,256]{1,0:T(8,128)(2,1)S(1)}) custom-call(bf16[48,512]{1,0:T(8,128)(2,1)S(1)} %collective-permute-done.mine_ref, bf16[48,512]{1,0:T(8,128)(2,1)S(1)} %collective-permute-done.1.other_ref, f32[384,256]{1,0:T(8,128)S(1)} %correlate.2.refs_0_), custom_call_target="tpu_custom_call" | custom-call | flops 251658240 | bytes 98304 | tf_op jit(solution)/shard_map/correlate/pallas_call | solution.py:280
  9.7 1.8 %collective-permute-start.3 = (bf16[80,256]{1,0:T(8,128)(2,1)S(1)}, bf16[80,256]{1,0:T(8,128)(2,1)S(1)}, u32[]{:S(2)}, u32[]{:S(2)}) collective-permute-start(bf16[80,256]{1,0:T(8,128)(2,1)S(1)} %get-tuple-element.16), channel_id=1, source_target_pairs={{0,2},{2,0},{4,6},{6,4},{8,10},{10,8},{12,14},{14,12},{1,3},{3,1},... | collective-permute-start | bytes 122888 | tf_op jit(solution)/shard_map/ppermute | solution.py:253
  11.4 1.1 %collective-permute-start.4 = (bf16[80,256]{1,0:T(8,128)(2,1)S(1)}, bf16[80,256]{1,0:T(8,128)(2,1)S(1)}, u32[]{:S(2)}, u32[]{:S(2)}) collective-permute-start(bf16[80,256]{1,0:T(8,128)(2,1)S(1)} %get-tuple-element.17), channel_id=1, source_target_pairs={{0,6},{2,4},{4,2},{6,0},{8,14},{10,12},{12,10},{14,8},{1,7},{3,5},... | collective-permute-start | bytes 122888 | tf_op jit(solution)/shard_map/ppermute | solution.py:253
  12.6 0.6 %collective-permute-start.5 = (bf16[80,256]{1,0:T(8,128)(2,1)S(1)}, bf16[80,256]{1,0:T(8,128)(2,1)S(1)}, u32[]{:S(2)}, u32[]{:S(2)}) collective-permute-start(bf16[80,256]{1,0:T(8,128)(2,1)S(1)} %get-tuple-element.18), channel_id=1, source_target_pairs={{0,4},{2,6},{4,0},{6,2},{8,12},{10,14},{12,8},{14,10},{1,5},{3,7},... | collective-permute-start | bytes 122888 | tf_op jit(solution)/shard_map/ppermute | solution.py:253
  13.2 0.0 copy-start
  13.2 0.7 %copy-done = s32[256]{0:T(256)S(1)} copy-done((s32[256]{0:T(256)S(1)}, s32[256]{0:T(256)}, u32[]{:S(2)}) %copy-start) | copy-done | bytes 1048
  13.9 0.5 %prepare.1 = (bf16[96,240]{1,0:T(8,128)(2,1)S(1)}, bf16[256,256]{1,0:T(8,128)(2,1)S(1)}, f32[5,96,256]{2,1,0:T(8,128)S(1)}) custom-call(s32[1,256]{1,0:T(1,128)S(1)} %bitcast.2, f32[80,256]{1,0:T(8,128)S(1)} %get-tuple-element.12.kept_ref), custom_call_target="tpu_custom_call" | custom-call | tf_op jit(solution)/shard_map/prepare/pallas_call | solution.py:303
  14.4 0.0 collective-permute-done.3.refs_0_
  14.4 2.2 %collective-permute-done.4.refs_1_ = bf16[80,256]{1,0:T(8,128)(2,1)S(1)} collective-permute-done((bf16[80,256]{1,0:T(8,128)(2,1)S(1)}, bf16[80,256]{1,0:T(8,128)(2,1)S(1)}, u32[]{:S(2)}, u32[]{:S(2)}) %collective-permute-start.4) | collective-permute-done | bytes 40992 | tf_op jit(solution)/shard_map/ppermute | solution.py:253
  16.6 0.0 collective-permute-done.5.refs_2_
  16.6 1.2 %expand.1 = f32[3,129,256]{2,1,0:T(8,128)} custom-call(bf16[96,240]{1,0:T(8,128)(2,1)S(1)} %get-tuple-element.13.order_ref, bf16[256,256]{1,0:T(8,128)(2,1)S(1)} %get-tuple-element.14.chosen_ref, f32[5,96,256]{2,1,0:T(8,128)S(1)} %get-tuple-element.15.base_ref, bf16[80,256]{1,0:T(8,128)(2,1)S(1)} %collective-permute-done.3.refs_0_, ...), custom_call_target="tpu_custom_call" | custom-call | tf_op jit(solution)/shard_map/expand/pallas_call | solution.py:316
Async XLA Ops:
  1.1 6.7 %collective-permute-start = (bf16[48,512]{1,0:T(8,128)(2,1)S(1)}, bf16[48,512]{1,0:T(8,128)(2,1)S(1)}, u32[]{:S(2)}, u32[]{:S(2)}) collective-permute-start(bf16[48,512]{1,0:T(8,128)(2,1)S(1)} %whiten.1.mine_ref), channel_id=1, source_target_pairs={{0,8},{2,10},{4,12},{6,14},{8,0},{10,2},{12,4},{14,6},{1,9},{3,11}... | collective-permute-start | bytes 147464 | tf_op jit(solution)/shard_map/ppermute | solution.py:253
  5.2 2.6 %collective-permute-start.2 = (bf16[48,512]{1,0:T(8,128)(2,1)S(1)}, bf16[48,512]{1,0:T(8,128)(2,1)S(1)}, u32[]{:S(2)}, u32[]{:S(2)}) collective-permute-start(bf16[48,512]{1,0:T(8,128)(2,1)S(1)} %whiten.1.mine_ref), channel_id=1, source_target_pairs={{0,1},{1,0},{2,3},{3,2},{4,5},{5,4},{6,7},{7,6},{8,9},{9,8},{10,11... | collective-permute-start | bytes 147464 | tf_op jit(solution)/shard_map/ppermute | solution.py:250
  7.8 1.2 %collective-permute-start.1 = (bf16[48,512]{1,0:T(8,128)(2,1)S(1)}, bf16[48,512]{1,0:T(8,128)(2,1)S(1)}, u32[]{:S(2)}, u32[]{:S(2)}) collective-permute-start(bf16[48,512]{1,0:T(8,128)(2,1)S(1)} %collective-permute-done.mine_ref), channel_id=1, source_target_pairs={{0,1},{1,0},{2,3},{3,2},{4,5},{5,4},{6,7},{7,6},{8,9},{9,8},{10,11... | collective-permute-start | bytes 147464 | tf_op jit(solution)/shard_map/ppermute | solution.py:250
  9.7 4.7 %collective-permute-start.3 = (bf16[80,256]{1,0:T(8,128)(2,1)S(1)}, bf16[80,256]{1,0:T(8,128)(2,1)S(1)}, u32[]{:S(2)}, u32[]{:S(2)}) collective-permute-start(bf16[80,256]{1,0:T(8,128)(2,1)S(1)} %get-tuple-element.16), channel_id=1, source_target_pairs={{0,2},{2,0},{4,6},{6,4},{8,10},{10,8},{12,14},{14,12},{1,3},{3,1},... | collective-permute-start | bytes 122888 | tf_op jit(solution)/shard_map/ppermute | solution.py:253
  11.4 5.1 %collective-permute-start.4 = (bf16[80,256]{1,0:T(8,128)(2,1)S(1)}, bf16[80,256]{1,0:T(8,128)(2,1)S(1)}, u32[]{:S(2)}, u32[]{:S(2)}) collective-permute-start(bf16[80,256]{1,0:T(8,128)(2,1)S(1)} %get-tuple-element.17), channel_id=1, source_target_pairs={{0,6},{2,4},{4,2},{6,0},{8,14},{10,12},{12,10},{14,8},{1,7},{3,5},... | collective-permute-start | bytes 122888 | tf_op jit(solution)/shard_map/ppermute | solution.py:253
  12.6 4.0 %collective-permute-start.5 = (bf16[80,256]{1,0:T(8,128)(2,1)S(1)}, bf16[80,256]{1,0:T(8,128)(2,1)S(1)}, u32[]{:S(2)}, u32[]{:S(2)}) collective-permute-start(bf16[80,256]{1,0:T(8,128)(2,1)S(1)} %get-tuple-element.18), channel_id=1, source_target_pairs={{0,4},{2,6},{4,0},{6,2},{8,12},{10,14},{12,8},{14,10},{1,5},{3,7},... | collective-permute-start | bytes 122888 | tf_op jit(solution)/shard_map/ppermute | solution.py:253
  13.2 0.7 %copy-start = (s32[256]{0:T(256)S(1)}, s32[256]{0:T(256)}, u32[]{:S(2)}) copy-start(s32[256]{0:T(256)} %param.5) | copy-start | bytes 3076

commit v14 on v13

--- a/solution.py
+++ b/solution.py
@@ -72,7 +72,8 @@
         self.src_size = src_size
         self.channels = half * src_size
         self.source_count = source_count
-        self.coarse = LANES // self.channels
+        self.half_lanes = LANES // 2
+        self.coarse = self.half_lanes // half
         if self.coarse == 0:
             return
         self.fine = -(-LAG_COUNT // self.coarse)
@@ -119,33 +120,16 @@
     out_ref[...] = jnp.concatenate(pieces, axis=0).astype(jnp.bfloat16)
 
 
-def correlate_kernel(plan, last, mine_ref, other_ref, *refs):
-    if last:
-        prior_ref, *out_refs, rows_ref, toeplitz_ref, columns_ref = refs
-    else:
-        sum_ref, rows_ref, toeplitz_ref, columns_ref = refs
+def lag_rows(plan, rows_ref, toeplitz_ref):
     span = plan.span
     me = lax.axis_index("blk")
-    filled = plan.coarse * plan.channels
-    if filled < LANES:
-        columns_ref[filled:, :] = jnp.zeros((LANES - filled, columns_ref.shape[1]), jnp.bfloat16)
-    filler = jnp.zeros((plan.channels, span - plan.segment), jnp.float32)
-    mine = mine_ref[...].astype(jnp.float32)
-    other = other_ref[...].astype(jnp.float32)
-    rows_ref[...] = mine
+    filler = jnp.zeros((1, span - plan.segment), jnp.float32)
     for window in range(plan.windows):
         at = slice(window * span, (window + 1) * span)
-        half = slice(window * plan.half, (window + 1) * plan.half)
-        both = jnp.concatenate([mine[half], other[half]], axis=0)
-        both = jnp.concatenate([both, filler], axis=1)
-        for step in range(plan.coarse):
-            moved = pltpu.roll(both, step * plan.fine, 1) if step else both
-            columns_ref[step * plan.channels : (step + 1) * plan.channels, at] = moved.astype(jnp.bfloat16)
         for hop in range(plan.targets):
-            target = me ^ hop
             for member in range(plan.own):
-                channel = window * plan.half + target * plan.own + member
-                row = jnp.concatenate([rows_ref[pl.ds(channel, 1), :], filler[:1]], axis=1)
+                channel = window * plan.half + (me ^ hop) * plan.own + member
+                row = jnp.concatenate([rows_ref[pl.ds(channel, 1), :], filler], axis=1)
                 row = jnp.broadcast_to(row, (GROUP, span))
                 pieces = [
                     pltpu.roll(row, (MAXLAG - plan.fine + 1 + lag) % span, 1, stride=1, stride_axis=0)
@@ -155,16 +139,49 @@
                 toeplitz_ref[first : first + plan.fine_padded, at] = jnp.concatenate(pieces, axis=0).astype(
                     jnp.bfloat16
                 )
-    products = lax.dot_general(
-        toeplitz_ref[...],
-        columns_ref[...],
-        (((1,), (1,)), ((), ())),
-        preferred_element_type=jnp.float32,
-    )
-    if not last:
-        sum_ref[...] = products
-        return
-    products = (products + prior_ref[...]).reshape(plan.targets, plan.own, plan.fine_padded, LANES)
+
+
+def half_product(plan, values, toeplitz_ref, columns_ref):
+    span = plan.span
+    filled = plan.coarse * plan.half
+    if filled < plan.half_lanes:
+        columns_ref[filled:, :] = jnp.zeros((plan.half_lanes - filled, columns_ref.shape[1]), jnp.bfloat16)
+    filler = jnp.zeros((plan.half, span - plan.segment), jnp.float32)
+    for window in range(plan.windows):
+        at = slice(window * span, (window + 1) * span)
+        rows = jnp.concatenate([values[window * plan.half : (window + 1) * plan.half], filler], axis=1)
+        for step in range(plan.coarse):
+            moved = pltpu.roll(rows, step * plan.fine, 1) if step else rows
+            columns_ref[step * plan.half : (step + 1) * plan.half, at] = moved.astype(jnp.bfloat16)
+    return lax.dot_general(
+        toeplitz_ref[...], columns_ref[...], (((1,), (1,)), ((), ())), preferred_element_type=jnp.float32
+    )
+
+
+def near_kernel(plan, mine_ref, other_ref, sum_ref, rows_ref, toeplitz_ref, columns_ref):
+    rows_ref[...] = mine_ref[...].astype(jnp.float32)
+    lag_rows(plan, rows_ref, toeplitz_ref)
+    other = other_ref[...].astype(jnp.float32)
+    sum_ref[:, : plan.half_lanes] = half_product(plan, rows_ref[...], toeplitz_ref, columns_ref.at[0])
+    sum_ref[:, plan.half_lanes :] = half_product(plan, other, toeplitz_ref, columns_ref.at[1])
+
+
+def across_kernel(plan, mine_ref, prior_ref, toeplitz_ref, sum_ref, rows_ref, columns_ref):
+    rows_ref[...] = mine_ref[...].astype(jnp.float32)
+    lag_rows(plan, rows_ref, toeplitz_ref)
+    sum_ref[:, : plan.half_lanes] = prior_ref[:, : plan.half_lanes] + half_product(
+        plan, rows_ref[...], toeplitz_ref, columns_ref
+    )
+    sum_ref[:, plan.half_lanes :] = prior_ref[:, plan.half_lanes :]
+
+
+def finish_kernel(plan, other_ref, toeplitz_ref, prior_ref, *refs):
+    *out_refs, columns_ref = refs
+    right = prior_ref[:, plan.half_lanes :] + half_product(
+        plan, other_ref[...].astype(jnp.float32), toeplitz_ref, columns_ref
+    )
+    products = jnp.concatenate([prior_ref[:, : plan.half_lanes], right], axis=1)
+    products = products.reshape(plan.targets, plan.own, plan.fine_padded, LANES)
     for hop in range(plan.targets):
         part = products[hop]
         pieces = [part[member, : plan.whole_groups] for member in range(plan.own)]
@@ -191,23 +208,30 @@
 
 def inside_step(plan, step, values):
     lane = lax.broadcasted_iota(jnp.int32, values.shape, 1)
-    inside = (lane >= step * plan.channels) & (lane < (step + 1) * plan.channels)
+    lane = jnp.where(lane >= plan.half_lanes, lane - plan.half_lanes, lane)
+    inside = (lane >= step * plan.half) & (lane < (step + 1) * plan.half)
     return jnp.where(inside, values, 0.0).astype(jnp.bfloat16)
 
 
-def prepare_kernel(plan, index_ref, kept_ref, order_ref, chosen_ref, base_ref):
+def choose_kernel(plan, index_ref, whitened_ref, order_ref, chosen_ref, same_ref):
     first = lax.axis_index("src") * plan.half
     index = index_ref[...] - first
     index = jnp.where(index < 0, index + plan.channels, index)
+    lane = jnp.where(index >= plan.half, index - plan.half + plan.half_lanes, index)
     at_column = lax.broadcasted_iota(jnp.int32, (LANES, plan.source_count), 0)
     chosen = jnp.zeros((LANES, plan.source_count), jnp.bool_)
     for step in range(plan.coarse):
-        chosen = chosen | (at_column == index + step * plan.channels)
-    chosen = chosen.astype(jnp.float32).astype(jnp.bfloat16)
-    chosen_ref[...] = chosen
+        chosen = chosen | (at_column == lane + step * plan.half)
+    chosen_ref[...] = chosen.astype(jnp.float32).astype(jnp.bfloat16)
     order = order_matrix(plan)
     for block in range(plan.targets - 1):
         order_ref[:, block * plan.rows : (block + 1) * plan.rows] = order
+    same_ref[...] = whitened_ref[...]
+
+
+def prepare_kernel(plan, order_ref, chosen_ref, kept_ref, base_ref):
+    order = order_ref[:, : plan.rows]
+    chosen = chosen_ref[...]
     kept = kept_ref[...] * plan.norm_factor
     high = kept.astype(jnp.bfloat16)
     low = (kept - high.astype(jnp.float32)).astype(jnp.bfloat16)
@@ -268,50 +292,65 @@
 
     height = plan.targets * plan.height
     width = plan.windows * plan.span
-
-    def correlate(mine, other, prior=None):
-        last = prior is not None
-        if last:
-            types = [jnp.float32] + [jnp.bfloat16] * (plan.targets - 1)
-            shapes = [jax.ShapeDtypeStruct((plan.rows, LANES), dtype) for dtype in types]
-        else:
-            shapes = [jax.ShapeDtypeStruct((height, LANES), jnp.float32)]
-        operands = [mine, other] + ([prior] if last else [])
-        results = pl.pallas_call(
-            functools.partial(correlate_kernel, plan, last),
-            out_shape=shapes,
+    rows = pltpu.VMEM((packed_rows, plan.segment), jnp.float32)
+    toeplitz = (height, width)
+    columns = (plan.half_lanes, width)
+    sums = jax.ShapeDtypeStruct((height, LANES), jnp.float32)
+
+    def call(kernel, name, operands, outputs, scratch=()):
+        return pl.pallas_call(
+            functools.partial(kernel, plan),
+            out_shape=outputs,
             in_specs=[vmem] * len(operands),
-            out_specs=[vmem] * len(shapes),
-            scratch_shapes=[
-                pltpu.VMEM((packed_rows, plan.segment), jnp.float32),
-                pltpu.VMEM((height, width), jnp.bfloat16),
-                pltpu.VMEM((LANES, width), jnp.bfloat16),
-            ],
+            out_specs=[vmem] * len(outputs),
+            scratch_shapes=scratch,
             compiler_params=params,
-            cost_estimate=pl.CostEstimate(
-                flops=2 * height * width * LANES, bytes_accessed=4 * packed_rows * plan.segment, transcendentals=0
-            ),
-            name="correlate",
+            name=name,
         )(*operands)
-        return results if last else results[0]
-
-    other = swap_cores(whitened)
+
     across = swap_blk(whitened, plan.targets)
-    total = correlate(whitened, other)
-    kept, *sent = correlate(across, swap_cores(across), total)
-    arrived = [swap_blk(sent[hop - 1], hop) for hop in (1, 3, 2)]
-    order, chosen, base = pl.pallas_call(
-        functools.partial(prepare_kernel, plan),
-        out_shape=[
+    order, chosen, same = call(
+        choose_kernel,
+        "choose",
+        (source_index.reshape(1, -1), whitened),
+        (
             jax.ShapeDtypeStruct((plan.height, (plan.targets - 1) * plan.rows), jnp.bfloat16),
             jax.ShapeDtypeStruct((LANES, plan.source_count), jnp.bfloat16),
-            jax.ShapeDtypeStruct((plan.coarse, plan.height, plan.source_count), jnp.float32),
-        ],
-        in_specs=[vmem] * 2,
-        out_specs=[vmem] * 3,
-        compiler_params=params,
-        name="prepare",
-    )(source_index.reshape(1, -1), kept)
+            jax.ShapeDtypeStruct(whitened.shape, whitened.dtype),
+        ),
+    )
+    (total,) = call(
+        near_kernel,
+        "near",
+        (whitened, swap_cores(same)),
+        (sums,),
+        (rows, pltpu.VMEM(toeplitz, jnp.bfloat16), pltpu.VMEM((2,) + columns, jnp.bfloat16)),
+    )
+    across_other = swap_cores(across)
+    lagged, total = call(
+        across_kernel,
+        "across",
+        (across, total),
+        (jax.ShapeDtypeStruct(toeplitz, jnp.bfloat16), sums),
+        (rows, pltpu.VMEM(columns, jnp.bfloat16)),
+    )
+    kept, *sent = call(
+        finish_kernel,
+        "finish",
+        (across_other, lagged, total),
+        tuple(
+            jax.ShapeDtypeStruct((plan.rows, LANES), jnp.bfloat16 if hop else jnp.float32)
+            for hop in range(plan.targets)
+        ),
+        (pltpu.VMEM(columns, jnp.bfloat16),),
+    )
+    arrived = [swap_blk(sent[hop - 1], hop) for hop in (1, 3, 2)]
+    (base,) = call(
+        prepare_kernel,
+        "prepare",
+        (order, chosen, kept),
+        (jax.ShapeDtypeStruct((plan.coarse, plan.height, plan.source_count), jnp.float32),),
+    )
     out_shape = (plan.own, LAG_COUNT, plan.source_count)
     return pl.pallas_call(
         functools.partial(expand_kernel, plan),

time: 17.9 us -> 18 us (level)
  Pallas kernels: 4.06 us -> 4.81 us
  local copies, waits for them, and re-layouts: 0.68 us -> 0.01 us
    pallas_call x3 -> x5, Pallas kernels: 1.76 us -> 2.51 us  [call(): pl.pallas_call(functools.partial(kernel, plan), out_shape=outputs, in_spe...]
    unnamed x2, local copies, waits for them, and re-layouts: 0.68 us -> 0.01 us
    ppermute x2, waiting for transfers between devices: 0.59 us -> 0.01 us  [swap_cores(): return lax.ppermute(array, 'src', [(0, 1), (1, 0)])]
    ppermute x4, waiting for transfers between devices: 4.77 us -> 5.24 us  [swap_blk(): lax.ppermute(array, 'blk', [(place, place ^ hop) for place in range(plan....]
  transfers between devices with their start and end apart: 6 -> 6, of which waited for: 3 -> 3; matrix products, arithmetic and copies ran while one was open for 0% -> 0% of each run, Pallas kernels for 6% -> 11%
where the time goes in v14:
time: 18 us; the launch traced here: 17.9 us
  starting transfers between devices  7.73 us (43%)
  waiting for transfers between devices  5.24 us (29%)
  Pallas kernels  4.81 us (27%)
    ppermute x4, starting transfers between devices, swap_blk(): lax.ppermute(array, 'blk', [(place, place ^ hop) for place in range(plan....  7.65 us
    ppermute x4, waiting for transfers between devices, swap_blk(): lax.ppermute(array, 'blk', [(place, place ^ hop) for place in range(plan....  5.24 us
    pallas_call x5, Pallas kernels, call(): pl.pallas_call(functools.partial(kernel, plan), out_shape=outputs, in_spe...  2.51 us
    pallas_call x1, Pallas kernels, few_channels(): pl.pallas_call(functools.partial(expand_kernel, plan), out_shape=jax.Shap...  1.19 us
    pallas_call x1, Pallas kernels, few_channels(): pl.pallas_call(functools.partial(whiten_kernel, plan), out_shape=pltpu.VM...  1.1 us
  transfers between devices with their start and end apart: 6, of which 3 were waited for; matrix products, arithmetic and copies ran while one was open for 0% of the time, Pallas kernels for 11%

profile of v14, /device:TPU:0, one launch (start us, length us, event | category | flops | bytes accessed | tf_op | source)
XLA Modules:
  0.0 17.9 jit_solution(11651659105415771609)
XLA Ops:
  0.0 1.1 %whiten.1.whitened_ref.mine_ref = bf16[48,512]{1,0:T(8,128)(2,1)S(1)} custom-call(f32[24,2,512]{2,1,0:T(2,128)} %traces_hbm.1, s32[2,24]{1,0:T(2,128)} %bitcast.3), custom_call_target="tpu_custom_call" | custom-call | tf_op jit(solution)/shard_map/whiten/pallas_call | solution.py:279
  1.1 0.0 copy-start
  1.1 4.1 %collective-permute-start = (bf16[48,512]{1,0:T(8,128)(2,1)S(1)}, bf16[48,512]{1,0:T(8,128)(2,1)S(1)}, u32[]{:S(2)}, u32[]{:S(2)}) collective-permute-start(bf16[48,512]{1,0:T(8,128)(2,1)S(1)} %whiten.1.whitened_ref.mine_ref), channel_id=1, source_target_pairs={{0,8},{2,10},{4,12},{6,14},{8,0},{10,2},{12,4},{14,6},{1,9},{3,11}... | collective-permute-start | bytes 147464 | tf_op jit(solution)/shard_map/ppermute | solution.py:277
  5.2 0.0 copy-done
  5.2 0.2 %choose.1 = (bf16[96,240]{1,0:T(8,128)(2,1)S(1)}, bf16[256,256]{1,0:T(8,128)(2,1)S(1)}, bf16[48,512]{1,0:T(8,128)(2,1)S(1)}) custom-call(s32[1,256]{1,0:T(1,128)S(1)} %bitcast.2, bf16[48,512]{1,0:T(8,128)(2,1)S(1)} %whiten.1.whitened_ref.mine_ref), custom_call_target="tpu_custom_call" | custom-call | tf_op jit(solution)/shard_map/choose/pallas_call | solution.py:301
  5.5 0.1 collective-permute-start.2
  5.5 2.3 %collective-permute-done.mine_ref = bf16[48,512]{1,0:T(8,128)(2,1)S(1)} collective-permute-done((bf16[48,512]{1,0:T(8,128)(2,1)S(1)}, bf16[48,512]{1,0:T(8,128)(2,1)S(1)}, u32[]{:S(2)}, u32[]{:S(2)}) %collective-permute-start) | collective-permute-done | bytes 49184 | tf_op jit(solution)/shard_map/ppermute | solution.py:277
  7.8 0.0 collective-permute-start.1
  7.8 0.0 collective-permute-done.2.other_ref
  7.8 0.8 %near.1.prior_ref = f32[384,256]{1,0:T(8,128)S(1)} custom-call(bf16[48,512]{1,0:T(8,128)(2,1)S(1)} %whiten.1.whitened_ref.mine_ref, bf16[48,512]{1,0:T(8,128)(2,1)S(1)} %collective-permute-done.2.other_ref), custom_call_target="tpu_custom_call" | custom-call | tf_op jit(solution)/shard_map/near/pallas_call | solution.py:301
  8.6 0.6 %across.1 = (bf16[384,1280]{1,0:T(8,128)(2,1)S(1)}, f32[384,256]{1,0:T(8,128)S(1)}) custom-call(bf16[48,512]{1,0:T(8,128)(2,1)S(1)} %collective-permute-done.mine_ref, f32[384,256]{1,0:T(8,128)S(1)} %near.1.prior_ref), custom_call_target="tpu_custom_call" | custom-call | tf_op jit(solution)/shard_map/across/pallas_call | solution.py:301
  9.2 0.0 collective-permute-done.1.other_ref
  9.2 0.5 %finish.1 = (f32[80,256]{1,0:T(8,128)S(1)}, bf16[80,256]{1,0:T(8,128)(2,1)S(1)}, bf16[80,256]{1,0:T(8,128)(2,1)S(1)}, bf16[80,256]{1,0:T(8,128)(2,1)S(1)}) custom-call(bf16[48,512]{1,0:T(8,128)(2,1)S(1)} %collective-permute-done.1.other_ref, bf16[384,1280]{1,0:T(8,128)(2,1)S(1)} %get-tuple-element.17.toeplitz_ref, f32[384,256]{1,0:T(8,128)S(1)} %get-tuple-element.18.prior_ref), custom_call_target="tpu_custom_call" | custom-call | tf_op jit(solution)/shard_map/finish/pallas_call | solution.py:301
  9.7 1.8 %collective-permute-start.3 = (bf16[80,256]{1,0:T(8,128)(2,1)S(1)}, bf16[80,256]{1,0:T(8,128)(2,1)S(1)}, u32[]{:S(2)}, u32[]{:S(2)}) collective-permute-start(bf16[80,256]{1,0:T(8,128)(2,1)S(1)} %get-tuple-element.20), channel_id=1, source_target_pairs={{0,2},{2,0},{4,6},{6,4},{8,10},{10,8},{12,14},{14,12},{1,3},{3,1},... | collective-permute-start | bytes 122888 | tf_op jit(solution)/shard_map/ppermute | solution.py:277
  11.5 1.1 %collective-permute-start.4 = (bf16[80,256]{1,0:T(8,128)(2,1)S(1)}, bf16[80,256]{1,0:T(8,128)(2,1)S(1)}, u32[]{:S(2)}, u32[]{:S(2)}) collective-permute-start(bf16[80,256]{1,0:T(8,128)(2,1)S(1)} %get-tuple-element.21), channel_id=1, source_target_pairs={{0,6},{2,4},{4,2},{6,0},{8,14},{10,12},{12,10},{14,8},{1,7},{3,5},... | collective-permute-start | bytes 122888 | tf_op jit(solution)/shard_map/ppermute | solution.py:277
  12.6 0.6 %collective-permute-start.5 = (bf16[80,256]{1,0:T(8,128)(2,1)S(1)}, bf16[80,256]{1,0:T(8,128)(2,1)S(1)}, u32[]{:S(2)}, u32[]{:S(2)}) collective-permute-start(bf16[80,256]{1,0:T(8,128)(2,1)S(1)} %get-tuple-element.22), channel_id=1, source_target_pairs={{0,4},{2,6},{4,0},{6,2},{8,12},{10,14},{12,8},{14,10},{1,5},{3,7},... | collective-permute-start | bytes 122888 | tf_op jit(solution)/shard_map/ppermute | solution.py:277
  13.3 0.5 %prepare.1.base_ref = f32[5,96,256]{2,1,0:T(8,128)S(1)} custom-call(bf16[96,240]{1,0:T(8,128)(2,1)S(1)} %get-tuple-element.14.order_ref, bf16[256,256]{1,0:T(8,128)(2,1)S(1)} %get-tuple-element.15.chosen_ref, f32[80,256]{1,0:T(8,128)S(1)} %get-tuple-element.19.kept_ref), custom_call_target="tpu_custom_call" | custom-call | tf_op jit(solution)/shard_map/prepare/pallas_call | solution.py:301
  13.7 0.1 collective-permute-done.3.refs_0_
  13.8 2.9 %collective-permute-done.4.refs_1_ = bf16[80,256]{1,0:T(8,128)(2,1)S(1)} collective-permute-done((bf16[80,256]{1,0:T(8,128)(2,1)S(1)}, bf16[80,256]{1,0:T(8,128)(2,1)S(1)}, u32[]{:S(2)}, u32[]{:S(2)}) %collective-permute-start.4) | collective-permute-done | bytes 40992 | tf_op jit(solution)/shard_map/ppermute | solution.py:277
  16.7 0.0 collective-permute-done.5.refs_2_
  16.7 1.2 %expand.1 = f32[3,129,256]{2,1,0:T(8,128)} custom-call(bf16[96,240]{1,0:T(8,128)(2,1)S(1)} %get-tuple-element.14.order_ref, bf16[256,256]{1,0:T(8,128)(2,1)S(1)} %get-tuple-element.15.chosen_ref, f32[5,96,256]{2,1,0:T(8,128)S(1)} %prepare.1.base_ref, bf16[80,256]{1,0:T(8,128)(2,1)S(1)} %collective-permute-done.3.refs_0_, ...), custom_call_target="tpu_custom_call" | custom-call | tf_op jit(solution)/shard_map/expand/pallas_call | solution.py:355
Async XLA Ops:
  1.1 4.1 %copy-start = (s32[256]{0:T(256)S(1)}, s32[256]{0:T(256)}, u32[]{:S(2)}) copy-start(s32[256]{0:T(256)} %param.5) | copy-start | bytes 3076
  1.1 6.7 %collective-permute-start = (bf16[48,512]{1,0:T(8,128)(2,1)S(1)}, bf16[48,512]{1,0:T(8,128)(2,1)S(1)}, u32[]{:S(2)}, u32[]{:S(2)}) collective-permute-start(bf16[48,512]{1,0:T(8,128)(2,1)S(1)} %whiten.1.whitened_ref.mine_ref), channel_id=1, source_target_pairs={{0,8},{2,10},{4,12},{6,14},{8,0},{10,2},{12,4},{14,6},{1,9},{3,11}... | collective-permute-start | bytes 147464 | tf_op jit(solution)/shard_map/ppermute | solution.py:277
  5.5 2.4 %collective-permute-start.2 = (bf16[48,512]{1,0:T(8,128)(2,1)S(1)}, bf16[48,512]{1,0:T(8,128)(2,1)S(1)}, u32[]{:S(2)}, u32[]{:S(2)}) collective-permute-start(bf16[48,512]{1,0:T(8,128)(2,1)S(1)} %get-tuple-element.16), channel_id=1, source_target_pairs={{0,1},{1,0},{2,3},{3,2},{4,5},{5,4},{6,7},{7,6},{8,9},{9,8},{10,11... | collective-permute-start | bytes 147464 | tf_op jit(solution)/shard_map/ppermute | solution.py:274
  7.8 1.4 %collective-permute-start.1 = (bf16[48,512]{1,0:T(8,128)(2,1)S(1)}, bf16[48,512]{1,0:T(8,128)(2,1)S(1)}, u32[]{:S(2)}, u32[]{:S(2)}) collective-permute-start(bf16[48,512]{1,0:T(8,128)(2,1)S(1)} %collective-permute-done.mine_ref), channel_id=1, source_target_pairs={{0,1},{1,0},{2,3},{3,2},{4,5},{5,4},{6,7},{7,6},{8,9},{9,8},{10,11... | collective-permute-start | bytes 147464 | tf_op jit(solution)/shard_map/ppermute | solution.py:274
  9.7 4.1 %collective-permute-start.3 = (bf16[80,256]{1,0:T(8,128)(2,1)S(1)}, bf16[80,256]{1,0:T(8,128)(2,1)S(1)}, u32[]{:S(2)}, u32[]{:S(2)}) collective-permute-start(bf16[80,256]{1,0:T(8,128)(2,1)S(1)} %get-tuple-element.20), channel_id=1, source_target_pairs={{0,2},{2,0},{4,6},{6,4},{8,10},{10,8},{12,14},{14,12},{1,3},{3,1},... | collective-permute-start | bytes 122888 | tf_op jit(solution)/shard_map/ppermute | solution.py:277
  11.5 5.2 %collective-permute-start.4 = (bf16[80,256]{1,0:T(8,128)(2,1)S(1)}, bf16[80,256]{1,0:T(8,128)(2,1)S(1)}, u32[]{:S(2)}, u32[]{:S(2)}) collective-permute-start(bf16[80,256]{1,0:T(8,128)(2,1)S(1)} %get-tuple-element.21), channel_id=1, source_target_pairs={{0,6},{2,4},{4,2},{6,0},{8,14},{10,12},{12,10},{14,8},{1,7},{3,5},... | collective-permute-start | bytes 122888 | tf_op jit(solution)/shard_map/ppermute | solution.py:277
  12.6 4.0 %collective-permute-start.5 = (bf16[80,256]{1,0:T(8,128)(2,1)S(1)}, bf16[80,256]{1,0:T(8,128)(2,1)S(1)}, u32[]{:S(2)}, u32[]{:S(2)}) collective-permute-start(bf16[80,256]{1,0:T(8,128)(2,1)S(1)} %get-tuple-element.22), channel_id=1, source_target_pairs={{0,4},{2,6},{4,0},{6,2},{8,12},{10,14},{12,8},{14,10},{1,5},{3,7},... | collective-permute-start | bytes 122888 | tf_op jit(solution)/shard_map/ppermute | solution.py:277

commit v15 on v14

--- a/solution.py
+++ b/solution.py
@@ -12,6 +12,7 @@
 LAG_COUNT = 2 * MAXLAG + 1
 LANES = 256
 GROUP = 8
+HOPS = ((3, 2), (1, 3), (2, 1))
 
 
 def broadcast(value, axis, source):
@@ -123,10 +124,12 @@
 def lag_rows(plan, rows_ref, toeplitz_ref):
     span = plan.span
     me = lax.axis_index("blk")
+    on_first = lax.axis_index("src") == 0
+    hops = [0] + [jnp.where(on_first, *pair) for pair in HOPS]
     filler = jnp.zeros((1, span - plan.segment), jnp.float32)
     for window in range(plan.windows):
         at = slice(window * span, (window + 1) * span)
-        for hop in range(plan.targets):
+        for place, hop in enumerate(hops):
             for member in range(plan.own):
                 channel = window * plan.half + (me ^ hop) * plan.own + member
                 row = jnp.concatenate([rows_ref[pl.ds(channel, 1), :], filler], axis=1)
@@ -135,7 +138,7 @@
                     pltpu.roll(row, (MAXLAG - plan.fine + 1 + lag) % span, 1, stride=1, stride_axis=0)
                     for lag in range(0, plan.fine_padded, GROUP)
                 ]
-                first = hop * plan.height + member * plan.fine_padded
+                first = place * plan.height + member * plan.fine_padded
                 toeplitz_ref[first : first + plan.fine_padded, at] = jnp.concatenate(pieces, axis=0).astype(
                     jnp.bfloat16
                 )
@@ -273,8 +276,13 @@
     def swap_cores(array):
         return lax.ppermute(array, "src", [(0, 1), (1, 0)])
 
-    def swap_blk(array, hop):
-        return lax.ppermute(array, "blk", [(place, place ^ hop) for place in range(plan.blk_size)])
+    def swap_blk(array, hops):
+        pairs = [
+            (place * plan.src_size + core, (place ^ hops[core]) * plan.src_size + core)
+            for place in range(plan.blk_size)
+            for core in range(plan.src_size)
+        ]
+        return lax.ppermute(array, ("blk", "src"), pairs)
 
     whitened = pl.pallas_call(
         functools.partial(whiten_kernel, plan),
@@ -308,7 +316,7 @@
             name=name,
         )(*operands)
 
-    across = swap_blk(whitened, plan.targets)
+    across = swap_blk(whitened, (plan.targets, plan.targets))
     order, chosen, same = call(
         choose_kernel,
         "choose",
@@ -344,7 +352,7 @@
         ),
         (pltpu.VMEM(columns, jnp.bfloat16),),
     )
-    arrived = [swap_blk(sent[hop - 1], hop) for hop in (1, 3, 2)]
+    arrived = [swap_blk(array, hops) for array, hops in zip(sent, HOPS)]
     (base,) = call(
         prepare_kernel,
         "prepare",

time: 18 us -> 17.9 us (level)
  transfers between devices with their start and end apart: 6 -> 6, of which waited for: 3 -> 4; matrix products, arithmetic and copies ran while one was open for 0% -> 0% of each run, Pallas kernels for 11% -> 11%
where the time goes in v15:
time: 17.9 us; the launch traced here: 17.8 us
  starting transfers between devices  7.73 us (43%)
  waiting for transfers between devices  5.2 us (29%)
  Pallas kernels  4.81 us (27%)
    ppermute x4, starting transfers between devices, swap_blk(): return lax.ppermute(array, ('blk', 'src'), pairs)  7.65 us
    ppermute x4, waiting for transfers between devices, swap_blk(): return lax.ppermute(array, ('blk', 'src'), pairs)  5.19 us
    pallas_call x5, Pallas kernels, call(): pl.pallas_call(functools.partial(kernel, plan), out_shape=outputs, in_spe...  2.51 us
    pallas_call x1, Pallas kernels, few_channels(): pl.pallas_call(functools.partial(expand_kernel, plan), out_shape=jax.Shap...  1.19 us
    pallas_call x1, Pallas kernels, few_channels(): pl.pallas_call(functools.partial(whiten_kernel, plan), out_shape=pltpu.VM...  1.1 us
  transfers between devices with their start and end apart: 6, of which 4 were waited for; matrix products, arithmetic and copies ran while one was open for 0% of the time, Pallas kernels for 11%

profile of v15, /device:TPU:0, one launch (start us, length us, event | category | flops | bytes accessed | tf_op | source)
XLA Modules:
  0.0 17.8 jit_solution(3836841868138691244)
XLA Ops:
  0.0 1.1 %whiten.1.whitened_ref.mine_ref = bf16[48,512]{1,0:T(8,128)(2,1)S(1)} custom-call(f32[24,2,512]{2,1,0:T(2,128)} %traces_hbm.1, s32[2,24]{1,0:T(2,128)} %bitcast.3), custom_call_target="tpu_custom_call" | custom-call | tf_op jit(solution)/shard_map/whiten/pallas_call | solution.py:287
  1.1 0.0 copy-start
  1.1 4.1 %collective-permute-start = (bf16[48,512]{1,0:T(8,128)(2,1)S(1)}, bf16[48,512]{1,0:T(8,128)(2,1)S(1)}, u32[]{:S(2)}, u32[]{:S(2)}) collective-permute-start(bf16[48,512]{1,0:T(8,128)(2,1)S(1)} %whiten.1.whitened_ref.mine_ref), channel_id=1, source_target_pairs={{0,8},{1,9},{2,10},{3,11},{4,12},{5,13},{6,14},{7,15},{8,0},{9,1},... | collective-permute-start | bytes 147464 | tf_op jit(solution)/shard_map/ppermute | solution.py:285
  5.2 0.0 copy-done
  5.2 0.2 %choose.1 = (bf16[96,240]{1,0:T(8,128)(2,1)S(1)}, bf16[256,256]{1,0:T(8,128)(2,1)S(1)}, bf16[48,512]{1,0:T(8,128)(2,1)S(1)}) custom-call(s32[1,256]{1,0:T(1,128)S(1)} %bitcast.2, bf16[48,512]{1,0:T(8,128)(2,1)S(1)} %whiten.1.whitened_ref.mine_ref), custom_call_target="tpu_custom_call" | custom-call | tf_op jit(solution)/shard_map/choose/pallas_call | solution.py:309
  5.5 0.1 collective-permute-start.2
  5.5 2.3 %collective-permute-done.mine_ref = bf16[48,512]{1,0:T(8,128)(2,1)S(1)} collective-permute-done((bf16[48,512]{1,0:T(8,128)(2,1)S(1)}, bf16[48,512]{1,0:T(8,128)(2,1)S(1)}, u32[]{:S(2)}, u32[]{:S(2)}) %collective-permute-start) | collective-permute-done | bytes 49184 | tf_op jit(solution)/shard_map/ppermute | solution.py:285
  7.8 0.0 collective-permute-start.1
  7.8 0.0 collective-permute-done.2.other_ref
  7.8 0.8 %near.1.prior_ref = f32[384,256]{1,0:T(8,128)S(1)} custom-call(bf16[48,512]{1,0:T(8,128)(2,1)S(1)} %whiten.1.whitened_ref.mine_ref, bf16[48,512]{1,0:T(8,128)(2,1)S(1)} %collective-permute-done.2.other_ref), custom_call_target="tpu_custom_call" | custom-call | tf_op jit(solution)/shard_map/near/pallas_call | solution.py:309
  8.6 0.6 %across.1 = (bf16[384,1280]{1,0:T(8,128)(2,1)S(1)}, f32[384,256]{1,0:T(8,128)S(1)}) custom-call(bf16[48,512]{1,0:T(8,128)(2,1)S(1)} %collective-permute-done.mine_ref, f32[384,256]{1,0:T(8,128)S(1)} %near.1.prior_ref), custom_call_target="tpu_custom_call" | custom-call | tf_op jit(solution)/shard_map/across/pallas_call | solution.py:309
  9.2 0.0 collective-permute-done.1.other_ref
  9.2 0.5 %finish.1 = (f32[80,256]{1,0:T(8,128)S(1)}, bf16[80,256]{1,0:T(8,128)(2,1)S(1)}, bf16[80,256]{1,0:T(8,128)(2,1)S(1)}, bf16[80,256]{1,0:T(8,128)(2,1)S(1)}) custom-call(bf16[48,512]{1,0:T(8,128)(2,1)S(1)} %collective-permute-done.1.other_ref, bf16[384,1280]{1,0:T(8,128)(2,1)S(1)} %get-tuple-element.17.toeplitz_ref, f32[384,256]{1,0:T(8,128)S(1)} %get-tuple-element.18.prior_ref), custom_call_target="tpu_custom_call" | custom-call | tf_op jit(solution)/shard_map/finish/pallas_call | solution.py:309
  9.7 2.4 %collective-permute-start.3 = (bf16[80,256]{1,0:T(8,128)(2,1)S(1)}, bf16[80,256]{1,0:T(8,128)(2,1)S(1)}, u32[]{:S(2)}, u32[]{:S(2)}) collective-permute-start(bf16[80,256]{1,0:T(8,128)(2,1)S(1)} %get-tuple-element.20), channel_id=1, source_target_pairs={{0,6},{1,5},{2,4},{3,7},{4,2},{5,1},{6,0},{7,3},{8,14},{9,13},{10,... | collective-permute-start | bytes 122888 | tf_op jit(solution)/shard_map/ppermute | solution.py:285
  12.1 0.5 %collective-permute-start.4 = (bf16[80,256]{1,0:T(8,128)(2,1)S(1)}, bf16[80,256]{1,0:T(8,128)(2,1)S(1)}, u32[]{:S(2)}, u32[]{:S(2)}) collective-permute-start(bf16[80,256]{1,0:T(8,128)(2,1)S(1)} %get-tuple-element.21), channel_id=1, source_target_pairs={{0,2},{1,7},{2,0},{3,5},{4,6},{5,3},{6,4},{7,1},{8,10},{9,15},{10,... | collective-permute-start | bytes 122888 | tf_op jit(solution)/shard_map/ppermute | solution.py:285
  12.6 0.6 %collective-permute-start.5 = (bf16[80,256]{1,0:T(8,128)(2,1)S(1)}, bf16[80,256]{1,0:T(8,128)(2,1)S(1)}, u32[]{:S(2)}, u32[]{:S(2)}) collective-permute-start(bf16[80,256]{1,0:T(8,128)(2,1)S(1)} %get-tuple-element.22), channel_id=1, source_target_pairs={{0,4},{1,3},{2,6},{3,1},{4,0},{5,7},{6,2},{7,5},{8,12},{9,11},{10,... | collective-permute-start | bytes 122888 | tf_op jit(solution)/shard_map/ppermute | solution.py:285
  13.3 0.5 %prepare.1.base_ref = f32[5,96,256]{2,1,0:T(8,128)S(1)} custom-call(bf16[96,240]{1,0:T(8,128)(2,1)S(1)} %get-tuple-element.14.order_ref, bf16[256,256]{1,0:T(8,128)(2,1)S(1)} %get-tuple-element.15.chosen_ref, f32[80,256]{1,0:T(8,128)S(1)} %get-tuple-element.19.kept_ref), custom_call_target="tpu_custom_call" | custom-call | tf_op jit(solution)/shard_map/prepare/pallas_call | solution.py:309
  13.7 1.2 %collective-permute-done.3.refs_0_ = bf16[80,256]{1,0:T(8,128)(2,1)S(1)} collective-permute-done((bf16[80,256]{1,0:T(8,128)(2,1)S(1)}, bf16[80,256]{1,0:T(8,128)(2,1)S(1)}, u32[]{:S(2)}, u32[]{:S(2)}) %collective-permute-start.3) | collective-permute-done | bytes 40992 | tf_op jit(solution)/shard_map/ppermute | solution.py:285
  14.9 1.4 %collective-permute-done.4.refs_1_ = bf16[80,256]{1,0:T(8,128)(2,1)S(1)} collective-permute-done((bf16[80,256]{1,0:T(8,128)(2,1)S(1)}, bf16[80,256]{1,0:T(8,128)(2,1)S(1)}, u32[]{:S(2)}, u32[]{:S(2)}) %collective-permute-start.4) | collective-permute-done | bytes 40992 | tf_op jit(solution)/shard_map/ppermute | solution.py:285
  16.3 0.3 %collective-permute-done.5.refs_2_ = bf16[80,256]{1,0:T(8,128)(2,1)S(1)} collective-permute-done((bf16[80,256]{1,0:T(8,128)(2,1)S(1)}, bf16[80,256]{1,0:T(8,128)(2,1)S(1)}, u32[]{:S(2)}, u32[]{:S(2)}) %collective-permute-start.5) | collective-permute-done | bytes 40992 | tf_op jit(solution)/shard_map/ppermute | solution.py:285
  16.6 1.2 %expand.1 = f32[3,129,256]{2,1,0:T(8,128)} custom-call(bf16[96,240]{1,0:T(8,128)(2,1)S(1)} %get-tuple-element.14.order_ref, bf16[256,256]{1,0:T(8,128)(2,1)S(1)} %get-tuple-element.15.chosen_ref, f32[5,96,256]{2,1,0:T(8,128)S(1)} %prepare.1.base_ref, bf16[80,256]{1,0:T(8,128)(2,1)S(1)} %collective-permute-done.3.refs_0_, ...), custom_call_target="tpu_custom_call" | custom-call | tf_op jit(solution)/shard_map/expand/pallas_call | solution.py:363
Async XLA Ops:
  1.1 4.1 %copy-start = (s32[256]{0:T(256)S(1)}, s32[256]{0:T(256)}, u32[]{:S(2)}) copy-start(s32[256]{0:T(256)} %param.5) | copy-start | bytes 3076
  1.1 6.7 %collective-permute-start = (bf16[48,512]{1,0:T(8,128)(2,1)S(1)}, bf16[48,512]{1,0:T(8,128)(2,1)S(1)}, u32[]{:S(2)}, u32[]{:S(2)}) collective-permute-start(bf16[48,512]{1,0:T(8,128)(2,1)S(1)} %whiten.1.whitened_ref.mine_ref), channel_id=1, source_target_pairs={{0,8},{1,9},{2,10},{3,11},{4,12},{5,13},{6,14},{7,15},{8,0},{9,1},... | collective-permute-start | bytes 147464 | tf_op jit(solution)/shard_map/ppermute | solution.py:285
  5.5 2.4 %collective-permute-start.2 = (bf16[48,512]{1,0:T(8,128)(2,1)S(1)}, bf16[48,512]{1,0:T(8,128)(2,1)S(1)}, u32[]{:S(2)}, u32[]{:S(2)}) collective-permute-start(bf16[48,512]{1,0:T(8,128)(2,1)S(1)} %get-tuple-element.16), channel_id=1, source_target_pairs={{0,1},{1,0},{2,3},{3,2},{4,5},{5,4},{6,7},{7,6},{8,9},{9,8},{10,11... | collective-permute-start | bytes 147464 | tf_op jit(solution)/shard_map/ppermute | solution.py:277
  7.8 1.4 %collective-permute-start.1 = (bf16[48,512]{1,0:T(8,128)(2,1)S(1)}, bf16[48,512]{1,0:T(8,128)(2,1)S(1)}, u32[]{:S(2)}, u32[]{:S(2)}) collective-permute-start(bf16[48,512]{1,0:T(8,128)(2,1)S(1)} %collective-permute-done.mine_ref), channel_id=1, source_target_pairs={{0,1},{1,0},{2,3},{3,2},{4,5},{5,4},{6,7},{7,6},{8,9},{9,8},{10,11... | collective-permute-start | bytes 147464 | tf_op jit(solution)/shard_map/ppermute | solution.py:277
  9.7 5.2 %collective-permute-start.3 = (bf16[80,256]{1,0:T(8,128)(2,1)S(1)}, bf16[80,256]{1,0:T(8,128)(2,1)S(1)}, u32[]{:S(2)}, u32[]{:S(2)}) collective-permute-start(bf16[80,256]{1,0:T(8,128)(2,1)S(1)} %get-tuple-element.20), channel_id=1, source_target_pairs={{0,6},{1,5},{2,4},{3,7},{4,2},{5,1},{6,0},{7,3},{8,14},{9,13},{10,... | collective-permute-start | bytes 122888 | tf_op jit(solution)/shard_map/ppermute | solution.py:285
  12.1 4.3 %collective-permute-start.4 = (bf16[80,256]{1,0:T(8,128)(2,1)S(1)}, bf16[80,256]{1,0:T(8,128)(2,1)S(1)}, u32[]{:S(2)}, u32[]{:S(2)}) collective-permute-start(bf16[80,256]{1,0:T(8,128)(2,1)S(1)} %get-tuple-element.21), channel_id=1, source_target_pairs={{0,2},{1,7},{2,0},{3,5},{4,6},{5,3},{6,4},{7,1},{8,10},{9,15},{10,... | collective-permute-start | bytes 122888 | tf_op jit(solution)/shard_map/ppermute | solution.py:285
  12.6 4.0 %collective-permute-start.5 = (bf16[80,256]{1,0:T(8,128)(2,1)S(1)}, bf16[80,256]{1,0:T(8,128)(2,1)S(1)}, u32[]{:S(2)}, u32[]{:S(2)}) collective-permute-start(bf16[80,256]{1,0:T(8,128)(2,1)S(1)} %get-tuple-element.22), channel_id=1, source_target_pairs={{0,4},{1,3},{2,6},{3,1},{4,0},{5,7},{6,2},{7,5},{8,12},{9,11},{10,... | collective-permute-start | bytes 122888 | tf_op jit(solution)/shard_map/ppermute | solution.py:285

commit v16 on v15

--- a/solution.py
+++ b/solution.py
@@ -161,12 +161,10 @@
     )
 
 
-def near_kernel(plan, mine_ref, other_ref, sum_ref, rows_ref, toeplitz_ref, columns_ref):
-    rows_ref[...] = mine_ref[...].astype(jnp.float32)
-    lag_rows(plan, rows_ref, toeplitz_ref)
+def near_kernel(plan, other_ref, toeplitz_ref, prior_ref, sum_ref, columns_ref):
     other = other_ref[...].astype(jnp.float32)
-    sum_ref[:, : plan.half_lanes] = half_product(plan, rows_ref[...], toeplitz_ref, columns_ref.at[0])
-    sum_ref[:, plan.half_lanes :] = half_product(plan, other, toeplitz_ref, columns_ref.at[1])
+    sum_ref[:, : plan.half_lanes] = prior_ref[...]
+    sum_ref[:, plan.half_lanes :] = half_product(plan, other, toeplitz_ref, columns_ref)
 
 
 def across_kernel(plan, mine_ref, prior_ref, toeplitz_ref, sum_ref, rows_ref, columns_ref):
@@ -197,11 +195,11 @@
 
 
 def order_matrix(plan):
-    at_row = lax.broadcasted_iota(jnp.int32, (plan.height, plan.rows), 0)
-    at_part = lax.broadcasted_iota(jnp.int32, (plan.height, plan.rows), 1)
-    order = jnp.zeros((plan.height, plan.rows), jnp.bool_)
+    at_row = lax.broadcasted_iota(jnp.int32, (plan.rows, plan.rows), 0)
+    at_part = lax.broadcasted_iota(jnp.int32, (plan.rows, plan.rows), 1)
+    order = jnp.zeros((plan.rows, plan.rows), jnp.bool_)
     for member in range(plan.own):
-        reverse = plan.fine - 1 - (at_row - member * plan.fine_padded)
+        reverse = plan.fine - 1 - (at_row - member * plan.fine)
         whole = (reverse >= 0) & (reverse < plan.whole_groups) & (at_part == member * plan.whole_groups + reverse)
         tail = plan.own * plan.whole_groups + member * plan.rest + reverse - plan.whole_groups
         rest = (reverse >= plan.whole_groups) & (reverse < plan.fine) & (at_part == tail)
@@ -209,14 +207,29 @@
     return order.astype(jnp.float32).astype(jnp.bfloat16)
 
 
-def inside_step(plan, step, values):
+def spread(plan, values):
+    high = values.astype(jnp.bfloat16).astype(jnp.float32)
+    low = values - high
     lane = lax.broadcasted_iota(jnp.int32, values.shape, 1)
     lane = jnp.where(lane >= plan.half_lanes, lane - plan.half_lanes, lane)
-    inside = (lane >= step * plan.half) & (lane < (step + 1) * plan.half)
-    return jnp.where(inside, values, 0.0).astype(jnp.bfloat16)
-
-
-def choose_kernel(plan, index_ref, whitened_ref, order_ref, chosen_ref, same_ref):
+    up = pltpu.roll(low, plan.half, 1)
+    down = pltpu.roll(low, LANES - plan.half, 1)
+    pieces = []
+    for step in range(plan.coarse):
+        beside, moved = (step + 1, up) if step + 1 < plan.coarse else (step - 1, down)
+        kept = jnp.where((lane >= step * plan.half) & (lane < (step + 1) * plan.half), high, 0.0)
+        there = (lane >= beside * plan.half) & (lane < (beside + 1) * plan.half)
+        pieces.append(jnp.where(there, moved, kept).astype(jnp.bfloat16))
+    return jnp.concatenate(pieces, axis=0)
+
+
+def first_kernel(
+    plan, index_ref, mine_ref, order_ref, chosen_ref, same_ref, toeplitz_ref, sum_ref, rows_ref, columns_ref
+):
+    same_ref[...] = mine_ref[...]
+    rows_ref[...] = mine_ref[...].astype(jnp.float32)
+    lag_rows(plan, rows_ref, toeplitz_ref)
+    sum_ref[...] = half_product(plan, rows_ref[...], toeplitz_ref, columns_ref)
     first = lax.axis_index("src") * plan.half
     index = index_ref[...] - first
     index = jnp.where(index < 0, index + plan.channels, index)
@@ -229,38 +242,29 @@
     order = order_matrix(plan)
     for block in range(plan.targets - 1):
         order_ref[:, block * plan.rows : (block + 1) * plan.rows] = order
-    same_ref[...] = whitened_ref[...]
 
 
 def prepare_kernel(plan, order_ref, chosen_ref, kept_ref, base_ref):
-    order = order_ref[:, : plan.rows]
-    chosen = chosen_ref[...]
     kept = kept_ref[...] * plan.norm_factor
     high = kept.astype(jnp.bfloat16)
     low = (kept - high.astype(jnp.float32)).astype(jnp.bfloat16)
-    parts = [jnp.dot(order, part, preferred_element_type=jnp.float32) for part in (high, low)]
-    for step in range(plan.coarse):
-        base_ref[step] = sum(
-            jnp.dot(inside_step(plan, step, part), chosen, preferred_element_type=jnp.float32) for part in parts
-        )
+    order = order_ref[:, : plan.rows]
+    ordered = sum(jnp.dot(order, part, preferred_element_type=jnp.float32) for part in (high, low))
+    base_ref[...] = jnp.dot(spread(plan, ordered), chosen_ref[...], preferred_element_type=jnp.float32)
 
 
 def expand_kernel(plan, order_ref, chosen_ref, base_ref, *refs):
     *arrived_refs, out_hbm, out_ref, sems = refs
     blocks = jnp.concatenate([ref[...] for ref in arrived_refs], axis=0)
     arrived = jnp.dot(order_ref[...], blocks, preferred_element_type=jnp.float32) * plan.norm_factor
-    high = arrived.astype(jnp.bfloat16).astype(jnp.float32)
-    steps = [inside_step(plan, step, part) for part in (high, arrived - high) for step in range(plan.coarse)]
-    moved = jnp.dot(jnp.concatenate(steps, axis=0), chosen_ref[...], preferred_element_type=jnp.float32)
-    moved = moved.reshape(2, plan.coarse, plan.height, plan.source_count)
-    expanded = [base_ref[step] + (moved[0, step] + moved[1, step]) for step in range(plan.coarse)]
+    expanded = base_ref[...] + jnp.dot(spread(plan, arrived), chosen_ref[...], preferred_element_type=jnp.float32)
     copies = []
     for member in range(plan.own):
         for step in range(plan.coarse):
             start = step * plan.fine
             count = min(plan.fine, LAG_COUNT - start)
-            first = member * plan.fine_padded
-            out_ref[member, start : start + count, :] = expanded[step][first : first + count]
+            first = step * plan.rows + member * plan.fine
+            out_ref[member, start : start + count, :] = expanded[first : first + count]
         copies.append(pltpu.make_async_copy(out_ref.at[member], out_hbm.at[member], sems.at[member]))
         copies[-1].start()
     for copy in copies:
@@ -317,22 +321,21 @@
         )(*operands)
 
     across = swap_blk(whitened, (plan.targets, plan.targets))
-    order, chosen, same = call(
-        choose_kernel,
-        "choose",
+    order, chosen, same, lagged, total = call(
+        first_kernel,
+        "first",
         (source_index.reshape(1, -1), whitened),
         (
-            jax.ShapeDtypeStruct((plan.height, (plan.targets - 1) * plan.rows), jnp.bfloat16),
+            jax.ShapeDtypeStruct((plan.rows, (plan.targets - 1) * plan.rows), jnp.bfloat16),
             jax.ShapeDtypeStruct((LANES, plan.source_count), jnp.bfloat16),
             jax.ShapeDtypeStruct(whitened.shape, whitened.dtype),
+            jax.ShapeDtypeStruct(toeplitz, jnp.bfloat16),
+            jax.ShapeDtypeStruct((height, plan.half_lanes), jnp.float32),
         ),
+        (rows, pltpu.VMEM(columns, jnp.bfloat16)),
     )
     (total,) = call(
-        near_kernel,
-        "near",
-        (whitened, swap_cores(same)),
-        (sums,),
-        (rows, pltpu.VMEM(toeplitz, jnp.bfloat16), pltpu.VMEM((2,) + columns, jnp.bfloat16)),
+        near_kernel, "near", (swap_cores(same), lagged, total), (sums,), (pltpu.VMEM(columns, jnp.bfloat16),)
     )
     across_other = swap_cores(across)
     lagged, total = call(
@@ -357,7 +360,7 @@
         prepare_kernel,
         "prepare",
         (order, chosen, kept),
-        (jax.ShapeDtypeStruct((plan.coarse, plan.height, plan.source_count), jnp.float32),),
+        (jax.ShapeDtypeStruct((plan.coarse * plan.rows, plan.source_count), jnp.float32),),
     )
     out_shape = (plan.own, LAG_COUNT, plan.source_count)
     return pl.pallas_call(

time: 17.9 us -> 17.8 us (level)
  waiting for transfers between devices: 5.2 us -> 4.77 us
  Pallas kernels: 4.81 us -> 5.11 us
    ppermute x4, waiting for transfers between devices: 5.19 us -> 4.65 us  [swap_blk(): return lax.ppermute(array, ('blk', 'src'), pairs)]
    pallas_call x5, Pallas kernels: 2.51 us -> 2.79 us  [call(): pl.pallas_call(functools.partial(kernel, plan), out_shape=outputs, in_spe...]
  transfers between devices with their start and end apart: 6 -> 6, of which waited for: 4 -> 5; matrix products, arithmetic and copies ran while one was open for 0% -> 0% of each run, Pallas kernels for 11% -> 13%
where the time goes in v16:
time: 17.8 us; the launch traced here: 17.7 us
  starting transfers between devices  7.73 us (43%)
  Pallas kernels  5.11 us (29%)
  waiting for transfers between devices  4.77 us (27%)
    ppermute x4, starting transfers between devices, swap_blk(): return lax.ppermute(array, ('blk', 'src'), pairs)  7.65 us
    ppermute x4, waiting for transfers between devices, swap_blk(): return lax.ppermute(array, ('blk', 'src'), pairs)  4.65 us
    pallas_call x5, Pallas kernels, call(): pl.pallas_call(functools.partial(kernel, plan), out_shape=outputs, in_spe...  2.79 us
    pallas_call x1, Pallas kernels, few_channels(): pl.pallas_call(functools.partial(expand_kernel, plan), out_shape=jax.Shap...  1.21 us
    pallas_call x1, Pallas kernels, few_channels(): pl.pallas_call(functools.partial(whiten_kernel, plan), out_shape=pltpu.VM...  1.1 us
  transfers between devices with their start and end apart: 6, of which 5 were waited for; matrix products, arithmetic and copies ran while one was open for 0% of the time, Pallas kernels for 13%

profile of v16, /device:TPU:0, one launch (start us, length us, event | category | flops | bytes accessed | tf_op | source)
XLA Modules:
  0.0 17.7 jit_solution(687161635876052226)
XLA Ops:
  0.0 1.1 %whiten.1.mine_ref = bf16[48,512]{1,0:T(8,128)(2,1)S(1)} custom-call(f32[24,2,512]{2,1,0:T(2,128)} %traces_hbm.1, s32[2,24]{1,0:T(2,128)} %bitcast.3), custom_call_target="tpu_custom_call" | custom-call | tf_op jit(solution)/shard_map/whiten/pallas_call | solution.py:291
  1.1 0.0 copy-start
  1.1 4.1 %collective-permute-start = (bf16[48,512]{1,0:T(8,128)(2,1)S(1)}, bf16[48,512]{1,0:T(8,128)(2,1)S(1)}, u32[]{:S(2)}, u32[]{:S(2)}) collective-permute-start(bf16[48,512]{1,0:T(8,128)(2,1)S(1)} %whiten.1.mine_ref), channel_id=1, source_target_pairs={{0,8},{1,9},{2,10},{3,11},{4,12},{5,13},{6,14},{7,15},{8,0},{9,1},... | collective-permute-start | bytes 147464 | tf_op jit(solution)/shard_map/ppermute | solution.py:289
  5.2 0.0 copy-done
  5.2 0.8 %first.1 = (bf16[80,240]{1,0:T(8,128)(2,1)S(1)}, bf16[256,256]{1,0:T(8,128)(2,1)S(1)}, bf16[48,512]{1,0:T(8,128)(2,1)S(1)}, bf16[384,1280]{1,0:T(8,128)(2,1)S(1)}, f32[384,128]{1,0:T(8,128)S(1)}) custom-call(s32[1,256]{1,0:T(1,128)S(1)} %bitcast.2, bf16[48,512]{1,0:T(8,128)(2,1)S(1)} %whiten.1.mine_ref), custom_call_target="tpu_custom_call" | custom-call | tf_op jit(solution)/shard_map/first/pallas_call | solution.py:313
  6.0 0.1 collective-permute-start.2
  6.1 1.7 %collective-permute-done.mine_ref = bf16[48,512]{1,0:T(8,128)(2,1)S(1)} collective-permute-done((bf16[48,512]{1,0:T(8,128)(2,1)S(1)}, bf16[48,512]{1,0:T(8,128)(2,1)S(1)}, u32[]{:S(2)}, u32[]{:S(2)}) %collective-permute-start) | collective-permute-done | bytes 49184 | tf_op jit(solution)/shard_map/ppermute | solution.py:289
  7.8 0.0 collective-permute-start.1
  7.8 0.0 collective-permute-done.2.other_ref
  7.8 0.5 %near.1.prior_ref = f32[384,256]{1,0:T(8,128)S(1)} custom-call(bf16[48,512]{1,0:T(8,128)(2,1)S(1)} %collective-permute-done.2.other_ref, bf16[384,1280]{1,0:T(8,128)(2,1)S(1)} %get-tuple-element.19.toeplitz_ref, f32[384,128]{1,0:T(8,128)S(1)} %get-tuple-element.20.prior_ref), custom_call_target="tpu_custom_call" | custom-call | tf_op jit(solution)/shard_map/near/pallas_call | solution.py:313
  8.3 0.6 %across.1 = (bf16[384,1280]{1,0:T(8,128)(2,1)S(1)}, f32[384,256]{1,0:T(8,128)S(1)}) custom-call(bf16[48,512]{1,0:T(8,128)(2,1)S(1)} %collective-permute-done.mine_ref, f32[384,256]{1,0:T(8,128)S(1)} %near.1.prior_ref), custom_call_target="tpu_custom_call" | custom-call | tf_op jit(solution)/shard_map/across/pallas_call | solution.py:313
  8.9 0.1 collective-permute-done.1.other_ref
  9.1 0.5 %finish.1 = (f32[80,256]{1,0:T(8,128)S(1)}, bf16[80,256]{1,0:T(8,128)(2,1)S(1)}, bf16[80,256]{1,0:T(8,128)(2,1)S(1)}, bf16[80,256]{1,0:T(8,128)(2,1)S(1)}) custom-call(bf16[48,512]{1,0:T(8,128)(2,1)S(1)} %collective-permute-done.1.other_ref, bf16[384,1280]{1,0:T(8,128)(2,1)S(1)} %get-tuple-element.21.toeplitz_ref, f32[384,256]{1,0:T(8,128)S(1)} %get-tuple-element.22.prior_ref), custom_call_target="tpu_custom_call" | custom-call | tf_op jit(solution)/shard_map/finish/pallas_call | solution.py:313
  9.6 2.4 %collective-permute-start.3 = (bf16[80,256]{1,0:T(8,128)(2,1)S(1)}, bf16[80,256]{1,0:T(8,128)(2,1)S(1)}, u32[]{:S(2)}, u32[]{:S(2)}) collective-permute-start(bf16[80,256]{1,0:T(8,128)(2,1)S(1)} %get-tuple-element.24), channel_id=1, source_target_pairs={{0,6},{1,5},{2,4},{3,7},{4,2},{5,1},{6,0},{7,3},{8,14},{9,13},{10,... | collective-permute-start | bytes 122888 | tf_op jit(solution)/shard_map/ppermute | solution.py:289
  11.9 0.5 %collective-permute-start.4 = (bf16[80,256]{1,0:T(8,128)(2,1)S(1)}, bf16[80,256]{1,0:T(8,128)(2,1)S(1)}, u32[]{:S(2)}, u32[]{:S(2)}) collective-permute-start(bf16[80,256]{1,0:T(8,128)(2,1)S(1)} %get-tuple-element.25), channel_id=1, source_target_pairs={{0,2},{1,7},{2,0},{3,5},{4,6},{5,3},{6,4},{7,1},{8,10},{9,15},{10,... | collective-permute-start | bytes 122888 | tf_op jit(solution)/shard_map/ppermute | solution.py:289
  12.5 0.6 %collective-permute-start.5 = (bf16[80,256]{1,0:T(8,128)(2,1)S(1)}, bf16[80,256]{1,0:T(8,128)(2,1)S(1)}, u32[]{:S(2)}, u32[]{:S(2)}) collective-permute-start(bf16[80,256]{1,0:T(8,128)(2,1)S(1)} %get-tuple-element.26), channel_id=1, source_target_pairs={{0,4},{1,3},{2,6},{3,1},{4,0},{5,7},{6,2},{7,5},{8,12},{9,11},{10,... | collective-permute-start | bytes 122888 | tf_op jit(solution)/shard_map/ppermute | solution.py:289
  13.1 0.4 %prepare.1.base_ref = f32[400,256]{1,0:T(8,128)S(1)} custom-call(bf16[80,240]{1,0:T(8,128)(2,1)S(1)} %get-tuple-element.16.order_ref, bf16[256,256]{1,0:T(8,128)(2,1)S(1)} %get-tuple-element.17.chosen_ref, f32[80,256]{1,0:T(8,128)S(1)} %get-tuple-element.23.kept_ref), custom_call_target="tpu_custom_call" | custom-call | tf_op jit(solution)/shard_map/prepare/pallas_call | solution.py:313
  13.6 1.1 %collective-permute-done.3.refs_0_ = bf16[80,256]{1,0:T(8,128)(2,1)S(1)} collective-permute-done((bf16[80,256]{1,0:T(8,128)(2,1)S(1)}, bf16[80,256]{1,0:T(8,128)(2,1)S(1)}, u32[]{:S(2)}, u32[]{:S(2)}) %collective-permute-start.3) | collective-permute-done | bytes 40992 | tf_op jit(solution)/shard_map/ppermute | solution.py:289
  14.7 1.4 %collective-permute-done.4.refs_1_ = bf16[80,256]{1,0:T(8,128)(2,1)S(1)} collective-permute-done((bf16[80,256]{1,0:T(8,128)(2,1)S(1)}, bf16[80,256]{1,0:T(8,128)(2,1)S(1)}, u32[]{:S(2)}, u32[]{:S(2)}) %collective-permute-start.4) | collective-permute-done | bytes 40992 | tf_op jit(solution)/shard_map/ppermute | solution.py:289
  16.1 0.4 %collective-permute-done.5.refs_2_ = bf16[80,256]{1,0:T(8,128)(2,1)S(1)} collective-permute-done((bf16[80,256]{1,0:T(8,128)(2,1)S(1)}, bf16[80,256]{1,0:T(8,128)(2,1)S(1)}, u32[]{:S(2)}, u32[]{:S(2)}) %collective-permute-start.5) | collective-permute-done | bytes 40992 | tf_op jit(solution)/shard_map/ppermute | solution.py:289
  16.5 1.2 %expand.1 = f32[3,129,256]{2,1,0:T(8,128)} custom-call(bf16[80,240]{1,0:T(8,128)(2,1)S(1)} %get-tuple-element.16.order_ref, bf16[256,256]{1,0:T(8,128)(2,1)S(1)} %get-tuple-element.17.chosen_ref, f32[400,256]{1,0:T(8,128)S(1)} %prepare.1.base_ref, bf16[80,256]{1,0:T(8,128)(2,1)S(1)} %collective-permute-done.3.refs_0_, ...), custom_call_target="tpu_custom_call" | custom-call | tf_op jit(solution)/shard_map/expand/pallas_call | solution.py:366
Async XLA Ops:
  1.1 4.1 %copy-start = (s32[256]{0:T(256)S(1)}, s32[256]{0:T(256)}, u32[]{:S(2)}) copy-start(s32[256]{0:T(256)} %param.5) | copy-start | bytes 3076
  1.1 6.7 %collective-permute-start = (bf16[48,512]{1,0:T(8,128)(2,1)S(1)}, bf16[48,512]{1,0:T(8,128)(2,1)S(1)}, u32[]{:S(2)}, u32[]{:S(2)}) collective-permute-start(bf16[48,512]{1,0:T(8,128)(2,1)S(1)} %whiten.1.mine_ref), channel_id=1, source_target_pairs={{0,8},{1,9},{2,10},{3,11},{4,12},{5,13},{6,14},{7,15},{8,0},{9,1},... | collective-permute-start | bytes 147464 | tf_op jit(solution)/shard_map/ppermute | solution.py:289
  6.0 1.8 %collective-permute-start.2 = (bf16[48,512]{1,0:T(8,128)(2,1)S(1)}, bf16[48,512]{1,0:T(8,128)(2,1)S(1)}, u32[]{:S(2)}, u32[]{:S(2)}) collective-permute-start(bf16[48,512]{1,0:T(8,128)(2,1)S(1)} %get-tuple-element.18), channel_id=1, source_target_pairs={{0,1},{1,0},{2,3},{3,2},{4,5},{5,4},{6,7},{7,6},{8,9},{9,8},{10,11... | collective-permute-start | bytes 147464 | tf_op jit(solution)/shard_map/ppermute | solution.py:281
  7.8 1.2 %collective-permute-start.1 = (bf16[48,512]{1,0:T(8,128)(2,1)S(1)}, bf16[48,512]{1,0:T(8,128)(2,1)S(1)}, u32[]{:S(2)}, u32[]{:S(2)}) collective-permute-start(bf16[48,512]{1,0:T(8,128)(2,1)S(1)} %collective-permute-done.mine_ref), channel_id=1, source_target_pairs={{0,1},{1,0},{2,3},{3,2},{4,5},{5,4},{6,7},{7,6},{8,9},{9,8},{10,11... | collective-permute-start | bytes 147464 | tf_op jit(solution)/shard_map/ppermute | solution.py:281
  9.6 5.1 %collective-permute-start.3 = (bf16[80,256]{1,0:T(8,128)(2,1)S(1)}, bf16[80,256]{1,0:T(8,128)(2,1)S(1)}, u32[]{:S(2)}, u32[]{:S(2)}) collective-permute-start(bf16[80,256]{1,0:T(8,128)(2,1)S(1)} %get-tuple-element.24), channel_id=1, source_target_pairs={{0,6},{1,5},{2,4},{3,7},{4,2},{5,1},{6,0},{7,3},{8,14},{9,13},{10,... | collective-permute-start | bytes 122888 | tf_op jit(solution)/shard_map/ppermute | solution.py:289
  11.9 4.2 %collective-permute-start.4 = (bf16[80,256]{1,0:T(8,128)(2,1)S(1)}, bf16[80,256]{1,0:T(8,128)(2,1)S(1)}, u32[]{:S(2)}, u32[]{:S(2)}) collective-permute-start(bf16[80,256]{1,0:T(8,128)(2,1)S(1)} %get-tuple-element.25), channel_id=1, source_target_pairs={{0,2},{1,7},{2,0},{3,5},{4,6},{5,3},{6,4},{7,1},{8,10},{9,15},{10,... | collective-permute-start | bytes 122888 | tf_op jit(solution)/shard_map/ppermute | solution.py:289
  12.5 4.0 %collective-permute-start.5 = (bf16[80,256]{1,0:T(8,128)(2,1)S(1)}, bf16[80,256]{1,0:T(8,128)(2,1)S(1)}, u32[]{:S(2)}, u32[]{:S(2)}) collective-permute-start(bf16[80,256]{1,0:T(8,128)(2,1)S(1)} %get-tuple-element.26), channel_id=1, source_target_pairs={{0,4},{1,3},{2,6},{3,1},{4,0},{5,7},{6,2},{7,5},{8,12},{9,11},{10,... | collective-permute-start | bytes 122888 | tf_op jit(solution)/shard_map/ppermute | solution.py:289

commit v17 on v16

--- a/solution.py
+++ b/solution.py
@@ -12,7 +12,11 @@
 LAG_COUNT = 2 * MAXLAG + 1
 LANES = 256
 GROUP = 8
-HOPS = ((3, 2), (1, 3), (2, 1))
+FIRST_HOP = (1, 2)
+SECOND_HOP = (2, 1)
+BOTH_HOPS = (3, 3)
+ARRIVALS = 2
+TARGETS = (SECOND_HOP, BOTH_HOPS, FIRST_HOP)
 
 
 def broadcast(value, axis, source):
@@ -125,7 +129,7 @@
     span = plan.span
     me = lax.axis_index("blk")
     on_first = lax.axis_index("src") == 0
-    hops = [0] + [jnp.where(on_first, *pair) for pair in HOPS]
+    hops = [0] + [jnp.where(on_first, *pair) for pair in TARGETS]
     filler = jnp.zeros((1, span - plan.segment), jnp.float32)
     for window in range(plan.windows):
         at = slice(window * span, (window + 1) * span)
@@ -192,6 +196,10 @@
             pieces.append(jnp.zeros((plan.rows - plan.own * plan.fine, LANES), jnp.float32))
         packed = jnp.concatenate(pieces, axis=0)
         out_refs[hop][...] = packed.astype(out_refs[hop].dtype)
+
+
+def complete_kernel(plan, part_ref, passed_ref, out_ref):
+    out_ref[...] = (part_ref[...] + passed_ref[...].astype(jnp.float32)).astype(jnp.bfloat16)
 
 
 def order_matrix(plan):
@@ -240,7 +248,7 @@
         chosen = chosen | (at_column == lane + step * plan.half)
     chosen_ref[...] = chosen.astype(jnp.float32).astype(jnp.bfloat16)
     order = order_matrix(plan)
-    for block in range(plan.targets - 1):
+    for block in range(ARRIVALS):
         order_ref[:, block * plan.rows : (block + 1) * plan.rows] = order
 
 
@@ -326,7 +334,7 @@
         "first",
         (source_index.reshape(1, -1), whitened),
         (
-            jax.ShapeDtypeStruct((plan.rows, (plan.targets - 1) * plan.rows), jnp.bfloat16),
+            jax.ShapeDtypeStruct((plan.rows, ARRIVALS * plan.rows), jnp.bfloat16),
             jax.ShapeDtypeStruct((LANES, plan.source_count), jnp.bfloat16),
             jax.ShapeDtypeStruct(whitened.shape, whitened.dtype),
             jax.ShapeDtypeStruct(toeplitz, jnp.bfloat16),
@@ -350,12 +358,18 @@
         "finish",
         (across_other, lagged, total),
         tuple(
-            jax.ShapeDtypeStruct((plan.rows, LANES), jnp.bfloat16 if hop else jnp.float32)
-            for hop in range(plan.targets)
+            jax.ShapeDtypeStruct((plan.rows, LANES), dtype)
+            for dtype in (jnp.float32, jnp.float32, jnp.bfloat16, jnp.bfloat16)
         ),
         (pltpu.VMEM(columns, jnp.bfloat16),),
     )
-    arrived = [swap_blk(array, hops) for array, hops in zip(sent, HOPS)]
+    to_complete, to_pass_on, first_sent = sent
+    passed_on = swap_blk(to_pass_on, FIRST_HOP)
+    first_arrived = swap_blk(first_sent, FIRST_HOP)
+    (completed,) = call(
+        complete_kernel, "complete", (to_complete, passed_on), (jax.ShapeDtypeStruct(passed_on.shape, jnp.bfloat16),)
+    )
+    arrived = [first_arrived, swap_blk(completed, SECOND_HOP)]
     (base,) = call(
         prepare_kernel,
         "prepare",

time: 17.8 us -> 19 us (1.067)
  waiting for transfers between devices: 4.77 us -> 6 us
    ppermute x4, waiting for transfers between devices: 4.65 us -> 5.87 us  [swap_blk(): return lax.ppermute(array, ('blk', 'src'), pairs)]
    pallas_call x5 -> x6, Pallas kernels: 2.79 us -> 2.82 us  [call(): pl.pallas_call(functools.partial(kernel, plan), out_shape=outputs, in_spe...]
  transfers between devices with their start and end apart: 6 -> 6, of which waited for: 5 -> 4; matrix products, arithmetic and copies ran while one was open for 0% -> 0% of each run, Pallas kernels for 13% -> 12%
where the time goes in v17:
time: 19 us; the launch traced here: 18.9 us
  starting transfers between devices  7.71 us (41%)
  waiting for transfers between devices  6 us (32%)
  Pallas kernels  5.1 us (27%)
    ppermute x4, starting transfers between devices, swap_blk(): return lax.ppermute(array, ('blk', 'src'), pairs)  7.64 us
    ppermute x4, waiting for transfers between devices, swap_blk(): return lax.ppermute(array, ('blk', 'src'), pairs)  5.87 us
    pallas_call x6, Pallas kernels, call(): pl.pallas_call(functools.partial(kernel, plan), out_shape=outputs, in_spe...  2.82 us
    pallas_call x1, Pallas kernels, few_channels(): pl.pallas_call(functools.partial(expand_kernel, plan), out_shape=jax.Shap...  1.18 us
    pallas_call x1, Pallas kernels, few_channels(): pl.pallas_call(functools.partial(whiten_kernel, plan), out_shape=pltpu.VM...  1.1 us
  transfers between devices with their start and end apart: 6, of which 4 were waited for; matrix products, arithmetic and copies ran while one was open for 0% of the time, Pallas kernels for 12%

profile of v17, /device:TPU:0, one launch (start us, length us, event | category | flops | bytes accessed | tf_op | source)
XLA Modules:
  0.0 18.9 jit_solution(8203754091311649319)
XLA Ops:
  0.0 1.1 %whiten.1.mine_ref = bf16[48,512]{1,0:T(8,128)(2,1)S(1)} custom-call(f32[24,2,512]{2,1,0:T(2,128)} %traces_hbm.1, s32[2,24]{1,0:T(2,128)} %bitcast.3), custom_call_target="tpu_custom_call" | custom-call | tf_op jit(solution)/shard_map/whiten/pallas_call | solution.py:299
  1.1 0.0 copy-start
  1.1 4.1 %collective-permute-start = (bf16[48,512]{1,0:T(8,128)(2,1)S(1)}, bf16[48,512]{1,0:T(8,128)(2,1)S(1)}, u32[]{:S(2)}, u32[]{:S(2)}) collective-permute-start(bf16[48,512]{1,0:T(8,128)(2,1)S(1)} %whiten.1.mine_ref), channel_id=1, source_target_pairs={{0,8},{1,9},{2,10},{3,11},{4,12},{5,13},{6,14},{7,15},{8,0},{9,1},... | collective-permute-start | bytes 147464 | tf_op jit(solution)/shard_map/ppermute | solution.py:297
  5.2 0.0 copy-done
  5.2 0.8 %first.1 = (bf16[80,160]{1,0:T(8,128)(2,1)S(1)}, bf16[256,256]{1,0:T(8,128)(2,1)S(1)}, bf16[48,512]{1,0:T(8,128)(2,1)S(1)}, bf16[384,1280]{1,0:T(8,128)(2,1)S(1)}, f32[384,128]{1,0:T(8,128)S(1)}) custom-call(s32[1,256]{1,0:T(1,128)S(1)} %bitcast.2, bf16[48,512]{1,0:T(8,128)(2,1)S(1)} %whiten.1.mine_ref), custom_call_target="tpu_custom_call" | custom-call | tf_op jit(solution)/shard_map/first/pallas_call | solution.py:321
  6.0 0.1 collective-permute-start.2
  6.1 1.7 %collective-permute-done.mine_ref = bf16[48,512]{1,0:T(8,128)(2,1)S(1)} collective-permute-done((bf16[48,512]{1,0:T(8,128)(2,1)S(1)}, bf16[48,512]{1,0:T(8,128)(2,1)S(1)}, u32[]{:S(2)}, u32[]{:S(2)}) %collective-permute-start) | collective-permute-done | bytes 49184 | tf_op jit(solution)/shard_map/ppermute | solution.py:297
  7.8 0.0 collective-permute-start.1
  7.8 0.0 collective-permute-done.2.other_ref
  7.8 0.5 %near.1.prior_ref = f32[384,256]{1,0:T(8,128)S(1)} custom-call(bf16[48,512]{1,0:T(8,128)(2,1)S(1)} %collective-permute-done.2.other_ref, bf16[384,1280]{1,0:T(8,128)(2,1)S(1)} %get-tuple-element.19.toeplitz_ref, f32[384,128]{1,0:T(8,128)S(1)} %get-tuple-element.20.prior_ref), custom_call_target="tpu_custom_call" | custom-call | tf_op jit(solution)/shard_map/near/pallas_call | solution.py:321
  8.3 0.6 %across.1 = (bf16[384,1280]{1,0:T(8,128)(2,1)S(1)}, f32[384,256]{1,0:T(8,128)S(1)}) custom-call(bf16[48,512]{1,0:T(8,128)(2,1)S(1)} %collective-permute-done.mine_ref, f32[384,256]{1,0:T(8,128)S(1)} %near.1.prior_ref), custom_call_target="tpu_custom_call" | custom-call | tf_op jit(solution)/shard_map/across/pallas_call | solution.py:321
  8.9 0.1 collective-permute-done.1.other_ref
  9.1 0.5 %finish.1 = (f32[80,256]{1,0:T(8,128)S(1)}, f32[80,256]{1,0:T(8,128)S(1)}, bf16[80,256]{1,0:T(8,128)(2,1)S(1)}, bf16[80,256]{1,0:T(8,128)(2,1)S(1)}) custom-call(bf16[48,512]{1,0:T(8,128)(2,1)S(1)} %collective-permute-done.1.other_ref, bf16[384,1280]{1,0:T(8,128)(2,1)S(1)} %get-tuple-element.21.toeplitz_ref, f32[384,256]{1,0:T(8,128)S(1)} %get-tuple-element.22.prior_ref), custom_call_target="tpu_custom_call" | custom-call | tf_op jit(solution)/shard_map/finish/pallas_call | solution.py:321
  9.6 1.8 %collective-permute-start.4 = (bf16[80,256]{1,0:T(8,128)(2,1)S(1)}, bf16[80,256]{1,0:T(8,128)(2,1)S(1)}, u32[]{:S(2)}, u32[]{:S(2)}) collective-permute-start(bf16[80,256]{1,0:T(8,128)(2,1)S(1)} %get-tuple-element.26), channel_id=1, source_target_pairs={{0,2},{1,5},{2,0},{3,7},{4,6},{5,1},{6,4},{7,3},{8,10},{9,13},{10,... | collective-permute-start | bytes 122888 | tf_op jit(solution)/shard_map/ppermute | solution.py:297
  11.3 0.3 %collective-permute-start.3 = (bf16[80,256]{1,0:T(8,128)(2,1)S(1)}, bf16[80,256]{1,0:T(8,128)(2,1)S(1)}, u32[]{:S(2)}, u32[]{:S(2)}) collective-permute-start(bf16[80,256]{1,0:T(8,128)(2,1)S(1)} %get-tuple-element.24), channel_id=1, source_target_pairs={{0,2},{1,5},{2,0},{3,7},{4,6},{5,1},{6,4},{7,3},{8,10},{9,13},{10,... | collective-permute-start | bytes 122888 | tf_op jit(solution)/shard_map/ppermute | solution.py:297
  11.6 2.0 %collective-permute-done.4.passed_ref = bf16[80,256]{1,0:T(8,128)(2,1)S(1)} collective-permute-done((bf16[80,256]{1,0:T(8,128)(2,1)S(1)}, bf16[80,256]{1,0:T(8,128)(2,1)S(1)}, u32[]{:S(2)}, u32[]{:S(2)}) %collective-permute-start.4) | collective-permute-done | bytes 40992 | tf_op jit(solution)/shard_map/ppermute | solution.py:297
  13.6 1.4 %collective-permute-start.5 = (bf16[80,256]{1,0:T(8,128)(2,1)S(1)}, bf16[80,256]{1,0:T(8,128)(2,1)S(1)}, u32[]{:S(2)}, u32[]{:S(2)}) collective-permute-start(bf16[80,256]{1,0:T(8,128)(2,1)S(1)} %complete.1), channel_id=1, source_target_pairs={{0,4},{1,3},{2,6},{3,1},{4,0},{5,7},{6,2},{7,5},{8,12},{9,11},{10,... | collective-permute-start | bytes 122888 | tf_op jit(solution)/shard_map/ppermute | solution.py:297
  15.1 0.4 %prepare.1.base_ref = f32[400,256]{1,0:T(8,128)S(1)} custom-call(bf16[80,160]{1,0:T(8,128)(2,1)S(1)} %get-tuple-element.16.order_ref, bf16[256,256]{1,0:T(8,128)(2,1)S(1)} %get-tuple-element.17.chosen_ref, f32[80,256]{1,0:T(8,128)S(1)} %get-tuple-element.23.kept_ref), custom_call_target="tpu_custom_call" | custom-call | tf_op jit(solution)/shard_map/prepare/pallas_call | solution.py:321
  15.5 0.0 collective-permute-done.3.refs_0_
  15.5 2.2 %collective-permute-done.5.refs_1_ = bf16[80,256]{1,0:T(8,128)(2,1)S(1)} collective-permute-done((bf16[80,256]{1,0:T(8,128)(2,1)S(1)}, bf16[80,256]{1,0:T(8,128)(2,1)S(1)}, u32[]{:S(2)}, u32[]{:S(2)}) %collective-permute-start.5) | collective-permute-done | bytes 40992 | tf_op jit(solution)/shard_map/ppermute | solution.py:297
  17.7 1.2 %expand.1 = f32[3,129,256]{2,1,0:T(8,128)} custom-call(bf16[80,160]{1,0:T(8,128)(2,1)S(1)} %get-tuple-element.16.order_ref, bf16[256,256]{1,0:T(8,128)(2,1)S(1)} %get-tuple-element.17.chosen_ref, f32[400,256]{1,0:T(8,128)S(1)} %prepare.1.base_ref, bf16[80,256]{1,0:T(8,128)(2,1)S(1)} %collective-permute-done.3.refs_0_, ...), custom_call_target="tpu_custom_call" | custom-call | tf_op jit(solution)/shard_map/expand/pallas_call | solution.py:380
  (1 shorter events, 0.0 us)
Async XLA Ops:
  1.1 4.1 %copy-start = (s32[256]{0:T(256)S(1)}, s32[256]{0:T(256)}, u32[]{:S(2)}) copy-start(s32[256]{0:T(256)} %param.5) | copy-start | bytes 3076
  1.1 6.7 %collective-permute-start = (bf16[48,512]{1,0:T(8,128)(2,1)S(1)}, bf16[48,512]{1,0:T(8,128)(2,1)S(1)}, u32[]{:S(2)}, u32[]{:S(2)}) collective-permute-start(bf16[48,512]{1,0:T(8,128)(2,1)S(1)} %whiten.1.mine_ref), channel_id=1, source_target_pairs={{0,8},{1,9},{2,10},{3,11},{4,12},{5,13},{6,14},{7,15},{8,0},{9,1},... | collective-permute-start | bytes 147464 | tf_op jit(solution)/shard_map/ppermute | solution.py:297
  6.0 1.8 %collective-permute-start.2 = (bf16[48,512]{1,0:T(8,128)(2,1)S(1)}, bf16[48,512]{1,0:T(8,128)(2,1)S(1)}, u32[]{:S(2)}, u32[]{:S(2)}) collective-permute-start(bf16[48,512]{1,0:T(8,128)(2,1)S(1)} %get-tuple-element.18), channel_id=1, source_target_pairs={{0,1},{1,0},{2,3},{3,2},{4,5},{5,4},{6,7},{7,6},{8,9},{9,8},{10,11... | collective-permute-start | bytes 147464 | tf_op jit(solution)/shard_map/ppermute | solution.py:289
  7.8 1.2 %collective-permute-start.1 = (bf16[48,512]{1,0:T(8,128)(2,1)S(1)}, bf16[48,512]{1,0:T(8,128)(2,1)S(1)}, u32[]{:S(2)}, u32[]{:S(2)}) collective-permute-start(bf16[48,512]{1,0:T(8,128)(2,1)S(1)} %collective-permute-done.mine_ref), channel_id=1, source_target_pairs={{0,1},{1,0},{2,3},{3,2},{4,5},{5,4},{6,7},{7,6},{8,9},{9,8},{10,11... | collective-permute-start | bytes 147464 | tf_op jit(solution)/shard_map/ppermute | solution.py:289
  9.6 4.1 %collective-permute-start.4 = (bf16[80,256]{1,0:T(8,128)(2,1)S(1)}, bf16[80,256]{1,0:T(8,128)(2,1)S(1)}, u32[]{:S(2)}, u32[]{:S(2)}) collective-permute-start(bf16[80,256]{1,0:T(8,128)(2,1)S(1)} %get-tuple-element.26), channel_id=1, source_target_pairs={{0,2},{1,5},{2,0},{3,7},{4,6},{5,1},{6,4},{7,3},{8,10},{9,13},{10,... | collective-permute-start | bytes 122888 | tf_op jit(solution)/shard_map/ppermute | solution.py:297
  11.3 4.2 %collective-permute-start.3 = (bf16[80,256]{1,0:T(8,128)(2,1)S(1)}, bf16[80,256]{1,0:T(8,128)(2,1)S(1)}, u32[]{:S(2)}, u32[]{:S(2)}) collective-permute-start(bf16[80,256]{1,0:T(8,128)(2,1)S(1)} %get-tuple-element.24), channel_id=1, source_target_pairs={{0,2},{1,5},{2,0},{3,7},{4,6},{5,1},{6,4},{7,3},{8,10},{9,13},{10,... | collective-permute-start | bytes 122888 | tf_op jit(solution)/shard_map/ppermute | solution.py:297
  13.6 4.1 %collective-permute-start.5 = (bf16[80,256]{1,0:T(8,128)(2,1)S(1)}, bf16[80,256]{1,0:T(8,128)(2,1)S(1)}, u32[]{:S(2)}, u32[]{:S(2)}) collective-permute-start(bf16[80,256]{1,0:T(8,128)(2,1)S(1)} %complete.1), channel_id=1, source_target_pairs={{0,4},{1,3},{2,6},{3,1},{4,0},{5,7},{6,2},{7,5},{8,12},{9,11},{10,... | collective-permute-start | bytes 122888 | tf_op jit(solution)/shard_map/ppermute | solution.py:297

commit v18 on v16

--- a/solution.py
+++ b/solution.py
@@ -102,7 +102,8 @@
         )
 
 
-def whiten_kernel(plan, traces_hbm, flags_hbm, out_ref, traces_ref, flags_ref, sems):
+def whiten_kernel(plan, traces_hbm, flags_hbm, *refs):
+    *out_refs, traces_ref, flags_ref, sems = refs
     copies = [
         pltpu.make_async_copy(traces_hbm, traces_ref, sems.at[0]),
         pltpu.make_async_copy(flags_hbm, flags_ref, sems.at[1]),
@@ -111,14 +112,12 @@
         copy.start()
     for copy in copies:
         copy.wait()
-    pieces = []
     for window in range(plan.windows):
         values = traces_ref[:, window, :]
         centered = values - jnp.mean(values, axis=1, keepdims=True)
         mean_power = jnp.mean(centered * centered, axis=1, keepdims=True)
         flag_values = flags_ref[window : window + 1, :].astype(jnp.float32).reshape(plan.half, 1)
-        pieces.append(centered * lax.rsqrt(mean_power + 1e-05) * flag_values)
-    out_ref[...] = jnp.concatenate(pieces, axis=0).astype(jnp.bfloat16)
+        out_refs[window][...] = (centered * lax.rsqrt(mean_power + 1e-05) * flag_values).astype(jnp.bfloat16)
 
 
 def lag_rows(plan, rows_ref, toeplitz_ref):
@@ -152,7 +151,7 @@
     filler = jnp.zeros((plan.half, span - plan.segment), jnp.float32)
     for window in range(plan.windows):
         at = slice(window * span, (window + 1) * span)
-        rows = jnp.concatenate([values[window * plan.half : (window + 1) * plan.half], filler], axis=1)
+        rows = jnp.concatenate([values[window].astype(jnp.float32), filler], axis=1)
         for step in range(plan.coarse):
             moved = pltpu.roll(rows, step * plan.fine, 1) if step else rows
             columns_ref[step * plan.half : (step + 1) * plan.half, at] = moved.astype(jnp.bfloat16)
@@ -161,27 +160,31 @@
     )
 
 
-def near_kernel(plan, other_ref, toeplitz_ref, prior_ref, sum_ref, columns_ref):
-    other = other_ref[...].astype(jnp.float32)
-    sum_ref[:, : plan.half_lanes] = prior_ref[...]
-    sum_ref[:, plan.half_lanes :] = half_product(plan, other, toeplitz_ref, columns_ref)
-
-
-def across_kernel(plan, mine_ref, prior_ref, toeplitz_ref, sum_ref, rows_ref, columns_ref):
-    rows_ref[...] = mine_ref[...].astype(jnp.float32)
+def load_rows(plan, refs, rows_ref):
+    values = [ref[...].astype(jnp.float32) for ref in refs]
+    for window, array in enumerate(values):
+        rows_ref[window * plan.half : (window + 1) * plan.half, :] = array
+    return values
+
+
+def near_kernel(plan, other_ref, toeplitz_ref, sum_ref, columns_ref):
+    packed = other_ref[...].astype(jnp.float32)
+    other = [packed[window * plan.half : (window + 1) * plan.half] for window in range(plan.windows)]
+    sum_ref[...] = half_product(plan, other, toeplitz_ref, columns_ref)
+
+
+def across_kernel(plan, *refs):
+    mine_refs, (prior_ref, toeplitz_ref, sum_ref, rows_ref, columns_ref) = refs[: plan.windows], refs[plan.windows :]
+    mine = load_rows(plan, mine_refs, rows_ref)
     lag_rows(plan, rows_ref, toeplitz_ref)
-    sum_ref[:, : plan.half_lanes] = prior_ref[:, : plan.half_lanes] + half_product(
-        plan, rows_ref[...], toeplitz_ref, columns_ref
-    )
-    sum_ref[:, plan.half_lanes :] = prior_ref[:, plan.half_lanes :]
-
-
-def finish_kernel(plan, other_ref, toeplitz_ref, prior_ref, *refs):
-    *out_refs, columns_ref = refs
-    right = prior_ref[:, plan.half_lanes :] + half_product(
-        plan, other_ref[...].astype(jnp.float32), toeplitz_ref, columns_ref
-    )
-    products = jnp.concatenate([prior_ref[:, : plan.half_lanes], right], axis=1)
+    sum_ref[...] = prior_ref[...] + half_product(plan, mine, toeplitz_ref, columns_ref)
+
+
+def finish_kernel(plan, *refs):
+    other_refs, refs = refs[: plan.windows], refs[plan.windows :]
+    toeplitz_ref, left_ref, right_ref, *out_refs, columns_ref = refs
+    right = right_ref[...] + half_product(plan, [ref[...] for ref in other_refs], toeplitz_ref, columns_ref)
+    products = jnp.concatenate([left_ref[...], right], axis=1)
     products = products.reshape(plan.targets, plan.own, plan.fine_padded, LANES)
     for hop in range(plan.targets):
         part = products[hop]
@@ -223,13 +226,13 @@
     return jnp.concatenate(pieces, axis=0)
 
 
-def first_kernel(
-    plan, index_ref, mine_ref, order_ref, chosen_ref, same_ref, toeplitz_ref, sum_ref, rows_ref, columns_ref
-):
-    same_ref[...] = mine_ref[...]
-    rows_ref[...] = mine_ref[...].astype(jnp.float32)
+def first_kernel(plan, index_ref, *refs):
+    mine_refs, refs = refs[: plan.windows], refs[plan.windows :]
+    order_ref, chosen_ref, same_ref, toeplitz_ref, sum_ref, rows_ref, columns_ref = refs
+    mine = load_rows(plan, mine_refs, rows_ref)
+    same_ref[...] = rows_ref[...].astype(jnp.bfloat16)
     lag_rows(plan, rows_ref, toeplitz_ref)
-    sum_ref[...] = half_product(plan, rows_ref[...], toeplitz_ref, columns_ref)
+    sum_ref[...] = half_product(plan, mine, toeplitz_ref, columns_ref)
     first = lax.axis_index("src") * plan.half
     index = index_ref[...] - first
     index = jnp.where(index < 0, index + plan.channels, index)
@@ -290,9 +293,9 @@
 
     whitened = pl.pallas_call(
         functools.partial(whiten_kernel, plan),
-        out_shape=pltpu.VMEM((packed_rows, plan.segment), jnp.bfloat16),
+        out_shape=[pltpu.VMEM((plan.half, plan.segment), jnp.bfloat16)] * plan.windows,
         in_specs=[pl.BlockSpec(memory_space=pl.ANY)] * 2,
-        out_specs=vmem,
+        out_specs=[vmem] * plan.windows,
         scratch_shapes=[
             pltpu.VMEM(traces.shape, jnp.float32),
             pltpu.VMEM(flags.shape, jnp.int32),
@@ -307,7 +310,7 @@
     rows = pltpu.VMEM((packed_rows, plan.segment), jnp.float32)
     toeplitz = (height, width)
     columns = (plan.half_lanes, width)
-    sums = jax.ShapeDtypeStruct((height, LANES), jnp.float32)
+    sums = jax.ShapeDtypeStruct((height, plan.half_lanes), jnp.float32)
 
     def call(kernel, name, operands, outputs, scratch=()):
         return pl.pallas_call(
@@ -320,35 +323,34 @@
             name=name,
         )(*operands)
 
-    across = swap_blk(whitened, (plan.targets, plan.targets))
-    order, chosen, same, lagged, total = call(
+    across = [swap_blk(array, (plan.targets, plan.targets)) for array in whitened]
+    order, chosen, same, lagged, left = call(
         first_kernel,
         "first",
-        (source_index.reshape(1, -1), whitened),
+        (source_index.reshape(1, -1), *whitened),
         (
             jax.ShapeDtypeStruct((plan.rows, (plan.targets - 1) * plan.rows), jnp.bfloat16),
             jax.ShapeDtypeStruct((LANES, plan.source_count), jnp.bfloat16),
-            jax.ShapeDtypeStruct(whitened.shape, whitened.dtype),
+            jax.ShapeDtypeStruct((packed_rows, plan.segment), jnp.bfloat16),
             jax.ShapeDtypeStruct(toeplitz, jnp.bfloat16),
-            jax.ShapeDtypeStruct((height, plan.half_lanes), jnp.float32),
+            sums,
         ),
         (rows, pltpu.VMEM(columns, jnp.bfloat16)),
     )
-    (total,) = call(
-        near_kernel, "near", (swap_cores(same), lagged, total), (sums,), (pltpu.VMEM(columns, jnp.bfloat16),)
-    )
-    across_other = swap_cores(across)
-    lagged, total = call(
+    *across, same = lax.optimization_barrier((*across, same))
+    (right,) = call(near_kernel, "near", (swap_cores(same), lagged), (sums,), (pltpu.VMEM(columns, jnp.bfloat16),))
+    across_other = [swap_cores(array) for array in across]
+    lagged, left = call(
         across_kernel,
         "across",
-        (across, total),
+        (*across, left),
         (jax.ShapeDtypeStruct(toeplitz, jnp.bfloat16), sums),
         (rows, pltpu.VMEM(columns, jnp.bfloat16)),
     )
     kept, *sent = call(
         finish_kernel,
         "finish",
-        (across_other, lagged, total),
+        (*across_other, lagged, left, right),
         tuple(
             jax.ShapeDtypeStruct((plan.rows, LANES), jnp.bfloat16 if hop else jnp.float32)
             for hop in range(plan.targets)

time: 17.8 us -> 20.7 us (1.16)
  waiting for transfers between devices: 4.77 us -> 6.52 us
  local copies, waits for them, and re-layouts: 0.01 us -> 0.59 us
  starting transfers between devices: 7.73 us -> 8.26 us
    ppermute x4 -> x5, waiting for transfers between devices: 4.65 us -> 6.38 us  [swap_blk(): return lax.ppermute(array, ('blk', 'src'), pairs)]
    unnamed x2, local copies, waits for them, and re-layouts: 0.01 us -> 0.59 us
    ppermute x2 -> x3, starting transfers between devices: 0.07 us -> 0.51 us  [swap_cores(): return lax.ppermute(array, 'src', [(0, 1), (1, 0)])]
    ppermute x4 -> x5, starting transfers between devices: 7.65 us -> 7.74 us  [swap_blk(): return lax.ppermute(array, ('blk', 'src'), pairs)]
  transfers between devices with their start and end apart: 6 -> 8, of which waited for: 5 -> 6; matrix products, arithmetic and copies ran while one was open for 0% -> 0% of each run, Pallas kernels for 13% -> 11%
where the time goes in v18:
time: 20.7 us; the launch traced here: 20.5 us
  starting transfers between devices  8.26 us (40%)
  waiting for transfers between devices  6.52 us (31%)
  Pallas kernels  5.12 us (25%)
  local copies, waits for them, and re-layouts  0.59 us (3%)
    ppermute x5, starting transfers between devices, swap_blk(): return lax.ppermute(array, ('blk', 'src'), pairs)  7.74 us
    ppermute x5, waiting for transfers between devices, swap_blk(): return lax.ppermute(array, ('blk', 'src'), pairs)  6.38 us
    pallas_call x5, Pallas kernels, call(): pl.pallas_call(functools.partial(kernel, plan), out_shape=outputs, in_spe...  2.81 us
    pallas_call x1, Pallas kernels, few_channels(): pl.pallas_call(functools.partial(expand_kernel, plan), out_shape=jax.Shap...  1.21 us
    pallas_call x1, Pallas kernels, few_channels(): pl.pallas_call(functools.partial(whiten_kernel, plan), out_shape=[pltpu.V...  1.1 us
    unnamed x2, local copies, waits for them, and re-layouts  0.59 us
    ppermute x3, starting transfers between devices, swap_cores(): return lax.ppermute(array, 'src', [(0, 1), (1, 0)])  0.51 us
  transfers between devices with their start and end apart: 8, of which 6 were waited for; matrix products, arithmetic and copies ran while one was open for 0% of the time, Pallas kernels for 11%

profile of v18, /device:TPU:0, one launch (start us, length us, event | category | flops | bytes accessed | tf_op | source)
XLA Modules:
  0.0 20.5 jit_solution(5840428774678876401)
XLA Ops:
  0.0 1.1 %whiten.1 = (bf16[24,512]{1,0:T(8,128)(2,1)S(1)}, bf16[24,512]{1,0:T(8,128)(2,1)S(1)}) custom-call(f32[24,2,512]{2,1,0:T(2,128)} %traces_hbm.1, s32[2,24]{1,0:T(2,128)} %bitcast.3), custom_call_target="tpu_custom_call" | custom-call | tf_op jit(solution)/shard_map/whiten/pallas_call | solution.py:294
  1.1 4.1 %collective-permute-start = (bf16[24,512]{1,0:T(8,128)(2,1)S(1)}, bf16[24,512]{1,0:T(8,128)(2,1)S(1)}, u32[]{:S(2)}, u32[]{:S(2)}) collective-permute-start(bf16[24,512]{1,0:T(8,128)(2,1)S(1)} %get-tuple-element.21.refs_0_), channel_id=1, source_target_pairs={{0,8},{1,9},{2,10},{3,11},{4,12},{5,13},{6,14},{7,15},{8,0},{9,1},... | collective-permute-start | bytes 73736 | tf_op jit(solution)/shard_map/ppermute | solution.py:292
  5.2 0.0 copy-start
  5.2 0.1 collective-permute-start.1
  5.3 0.6 %copy-done = s32[256]{0:T(256)S(1)} copy-done((s32[256]{0:T(256)S(1)}, s32[256]{0:T(256)}, u32[]{:S(2)}) %copy-start) | copy-done | bytes 1048
  5.9 0.8 %first.1 = (bf16[80,240]{1,0:T(8,128)(2,1)S(1)}, bf16[256,256]{1,0:T(8,128)(2,1)S(1)}, bf16[48,512]{1,0:T(8,128)(2,1)S(1)}, bf16[384,1280]{1,0:T(8,128)(2,1)S(1)}, f32[384,128]{1,0:T(8,128)S(1)}) custom-call(s32[1,256]{1,0:T(1,128)S(1)} %bitcast.2, bf16[24,512]{1,0:T(8,128)(2,1)S(1)} %get-tuple-element.21.refs_0_, bf16[24,512]{1,0:T(8,128)(2,1)S(1)} %get-tuple-element.22.refs_1_), custom_call_target="tpu_custom_call" | custom-call | tf_op jit(solution)/shard_map/first/pallas_call | solution.py:316
  6.7 0.4 %collective-permute-done.refs_0_ = bf16[24,512]{1,0:T(8,128)(2,1)S(1)} collective-permute-done((bf16[24,512]{1,0:T(8,128)(2,1)S(1)}, bf16[24,512]{1,0:T(8,128)(2,1)S(1)}, u32[]{:S(2)}, u32[]{:S(2)}) %collective-permute-start) | collective-permute-done | bytes 24608 | tf_op jit(solution)/shard_map/ppermute | solution.py:292
  7.0 2.9 %collective-permute-done.1.refs_1_ = bf16[24,512]{1,0:T(8,128)(2,1)S(1)} collective-permute-done((bf16[24,512]{1,0:T(8,128)(2,1)S(1)}, bf16[24,512]{1,0:T(8,128)(2,1)S(1)}, u32[]{:S(2)}, u32[]{:S(2)}) %collective-permute-start.1) | collective-permute-done | bytes 24608 | tf_op jit(solution)/shard_map/ppermute | solution.py:292
  9.9 0.0 collective-permute-start.4
  9.9 0.5 %collective-permute-start.2 = (bf16[24,512]{1,0:T(8,128)(2,1)S(1)}, bf16[24,512]{1,0:T(8,128)(2,1)S(1)}, u32[]{:S(2)}, u32[]{:S(2)}) collective-permute-start(bf16[24,512]{1,0:T(8,128)(2,1)S(1)} %collective-permute-done.refs_0_), channel_id=1, source_target_pairs={{0,1},{1,0},{2,3},{3,2},{4,5},{5,4},{6,7},{7,6},{8,9},{9,8},{10,11... | collective-permute-start | bytes 73736 | tf_op jit(solution)/shard_map/ppermute | solution.py:284
  10.5 0.0 collective-permute-start.3
  10.5 0.6 %across.1 = (bf16[384,1280]{1,0:T(8,128)(2,1)S(1)}, f32[384,128]{1,0:T(8,128)S(1)}) custom-call(bf16[24,512]{1,0:T(8,128)(2,1)S(1)} %collective-permute-done.refs_0_, bf16[24,512]{1,0:T(8,128)(2,1)S(1)} %collective-permute-done.1.refs_1_, f32[384,128]{1,0:T(8,128)S(1)} %get-tuple-element.28.refs_2_), custom_call_target="tpu_custom_call" | custom-call | tf_op jit(solution)/shard_map/across/pallas_call | solution.py:316
  11.0 0.1 collective-permute-done.4.other_ref
  11.2 0.5 %near.1.refs_4_ = f32[384,128]{1,0:T(8,128)S(1)} custom-call(bf16[48,512]{1,0:T(8,128)(2,1)S(1)} %collective-permute-done.4.other_ref, bf16[384,1280]{1,0:T(8,128)(2,1)S(1)} %get-tuple-element.32.toeplitz_ref), custom_call_target="tpu_custom_call" | custom-call | tf_op jit(solution)/shard_map/near/pallas_call | solution.py:316
  11.7 0.0 collective-permute-done.2.refs_0_
  11.7 0.0 collective-permute-done.3.refs_1_
  11.7 0.5 %finish.1 = (f32[80,256]{1,0:T(8,128)S(1)}, bf16[80,256]{1,0:T(8,128)(2,1)S(1)}, bf16[80,256]{1,0:T(8,128)(2,1)S(1)}, bf16[80,256]{1,0:T(8,128)(2,1)S(1)}) custom-call(bf16[24,512]{1,0:T(8,128)(2,1)S(1)} %collective-permute-done.2.refs_0_, bf16[24,512]{1,0:T(8,128)(2,1)S(1)} %collective-permute-done.3.refs_1_, ...), custom_call_target="tpu_custom_call" | custom-call | tf_op jit(solution)/shard_map/finish/pallas_call | solution.py:316
  12.2 2.6 %collective-permute-start.5 = (bf16[80,256]{1,0:T(8,128)(2,1)S(1)}, bf16[80,256]{1,0:T(8,128)(2,1)S(1)}, u32[]{:S(2)}, u32[]{:S(2)}) collective-permute-start(bf16[80,256]{1,0:T(8,128)(2,1)S(1)} %get-tuple-element.34), channel_id=1, source_target_pairs={{0,6},{1,5},{2,4},{3,7},{4,2},{5,1},{6,0},{7,3},{8,14},{9,13},{10,... | collective-permute-start | bytes 122888 | tf_op jit(solution)/shard_map/ppermute | solution.py:292
  14.8 0.5 %collective-permute-start.6 = (bf16[80,256]{1,0:T(8,128)(2,1)S(1)}, bf16[80,256]{1,0:T(8,128)(2,1)S(1)}, u32[]{:S(2)}, u32[]{:S(2)}) collective-permute-start(bf16[80,256]{1,0:T(8,128)(2,1)S(1)} %get-tuple-element.35), channel_id=1, source_target_pairs={{0,2},{1,7},{2,0},{3,5},{4,6},{5,3},{6,4},{7,1},{8,10},{9,15},{10,... | collective-permute-start | bytes 122888 | tf_op jit(solution)/shard_map/ppermute | solution.py:292
  15.3 0.4 %collective-permute-start.7 = (bf16[80,256]{1,0:T(8,128)(2,1)S(1)}, bf16[80,256]{1,0:T(8,128)(2,1)S(1)}, u32[]{:S(2)}, u32[]{:S(2)}) collective-permute-start(bf16[80,256]{1,0:T(8,128)(2,1)S(1)} %get-tuple-element.36), channel_id=1, source_target_pairs={{0,4},{1,3},{2,6},{3,1},{4,0},{5,7},{6,2},{7,5},{8,12},{9,11},{10,... | collective-permute-start | bytes 122888 | tf_op jit(solution)/shard_map/ppermute | solution.py:292
  15.8 0.4 %prepare.1.base_ref = f32[400,256]{1,0:T(8,128)S(1)} custom-call(bf16[80,240]{1,0:T(8,128)(2,1)S(1)} %get-tuple-element.23.order_ref, bf16[256,256]{1,0:T(8,128)(2,1)S(1)} %get-tuple-element.24.chosen_ref, f32[80,256]{1,0:T(8,128)S(1)} %get-tuple-element.33.kept_ref), custom_call_target="tpu_custom_call" | custom-call | tf_op jit(solution)/shard_map/prepare/pallas_call | solution.py:316
  16.2 1.0 %collective-permute-done.5.refs_0_ = bf16[80,256]{1,0:T(8,128)(2,1)S(1)} collective-permute-done((bf16[80,256]{1,0:T(8,128)(2,1)S(1)}, bf16[80,256]{1,0:T(8,128)(2,1)S(1)}, u32[]{:S(2)}, u32[]{:S(2)}) %collective-permute-start.5) | collective-permute-done | bytes 40992 | tf_op jit(solution)/shard_map/ppermute | solution.py:292
  17.2 1.6 %collective-permute-done.6.refs_1_ = bf16[80,256]{1,0:T(8,128)(2,1)S(1)} collective-permute-done((bf16[80,256]{1,0:T(8,128)(2,1)S(1)}, bf16[80,256]{1,0:T(8,128)(2,1)S(1)}, u32[]{:S(2)}, u32[]{:S(2)}) %collective-permute-start.6) | collective-permute-done | bytes 40992 | tf_op jit(solution)/shard_map/ppermute | solution.py:292
  18.8 0.5 %collective-permute-done.7.refs_2_ = bf16[80,256]{1,0:T(8,128)(2,1)S(1)} collective-permute-done((bf16[80,256]{1,0:T(8,128)(2,1)S(1)}, bf16[80,256]{1,0:T(8,128)(2,1)S(1)}, u32[]{:S(2)}, u32[]{:S(2)}) %collective-permute-start.7) | collective-permute-done | bytes 40992 | tf_op jit(solution)/shard_map/ppermute | solution.py:292
  19.3 1.2 %expand.1 = f32[3,129,256]{2,1,0:T(8,128)} custom-call(bf16[80,240]{1,0:T(8,128)(2,1)S(1)} %get-tuple-element.23.order_ref, bf16[256,256]{1,0:T(8,128)(2,1)S(1)} %get-tuple-element.24.chosen_ref, f32[400,256]{1,0:T(8,128)S(1)} %prepare.1.base_ref, bf16[80,256]{1,0:T(8,128)(2,1)S(1)} %collective-permute-done.5.refs_0_, ...), custom_call_target="tpu_custom_call" | custom-call | tf_op jit(solution)/shard_map/expand/pallas_call | solution.py:368
Async XLA Ops:
  1.1 5.9 %collective-permute-start = (bf16[24,512]{1,0:T(8,128)(2,1)S(1)}, bf16[24,512]{1,0:T(8,128)(2,1)S(1)}, u32[]{:S(2)}, u32[]{:S(2)}) collective-permute-start(bf16[24,512]{1,0:T(8,128)(2,1)S(1)} %get-tuple-element.21.refs_0_), channel_id=1, source_target_pairs={{0,8},{1,9},{2,10},{3,11},{4,12},{5,13},{6,14},{7,15},{8,0},{9,1},... | collective-permute-start | bytes 73736 | tf_op jit(solution)/shard_map/ppermute | solution.py:292
  5.2 0.7 %copy-start = (s32[256]{0:T(256)S(1)}, s32[256]{0:T(256)}, u32[]{:S(2)}) copy-start(s32[256]{0:T(256)} %param.5) | copy-start | bytes 3076
  5.2 4.7 %collective-permute-start.1 = (bf16[24,512]{1,0:T(8,128)(2,1)S(1)}, bf16[24,512]{1,0:T(8,128)(2,1)S(1)}, u32[]{:S(2)}, u32[]{:S(2)}) collective-permute-start(bf16[24,512]{1,0:T(8,128)(2,1)S(1)} %get-tuple-element.22.refs_1_), channel_id=1, source_target_pairs={{0,8},{1,9},{2,10},{3,11},{4,12},{5,13},{6,14},{7,15},{8,0},{9,1},... | collective-permute-start | bytes 73736 | tf_op jit(solution)/shard_map/ppermute | solution.py:292
  9.9 1.2 %collective-permute-start.4 = (bf16[48,512]{1,0:T(8,128)(2,1)S(1)}, bf16[48,512]{1,0:T(8,128)(2,1)S(1)}, u32[]{:S(2)}, u32[]{:S(2)}) collective-permute-start(bf16[48,512]{1,0:T(8,128)(2,1)S(1)} %get-tuple-element.31), channel_id=1, source_target_pairs={{0,1},{1,0},{2,3},{3,2},{4,5},{5,4},{6,7},{7,6},{8,9},{9,8},{10,11... | collective-permute-start | bytes 147464 | tf_op jit(solution)/shard_map/ppermute | solution.py:284
  9.9 1.7 %collective-permute-start.2 = (bf16[24,512]{1,0:T(8,128)(2,1)S(1)}, bf16[24,512]{1,0:T(8,128)(2,1)S(1)}, u32[]{:S(2)}, u32[]{:S(2)}) collective-permute-start(bf16[24,512]{1,0:T(8,128)(2,1)S(1)} %collective-permute-done.refs_0_), channel_id=1, source_target_pairs={{0,1},{1,0},{2,3},{3,2},{4,5},{5,4},{6,7},{7,6},{8,9},{9,8},{10,11... | collective-permute-start | bytes 73736 | tf_op jit(solution)/shard_map/ppermute | solution.py:284
  10.5 1.3 %collective-permute-start.3 = (bf16[24,512]{1,0:T(8,128)(2,1)S(1)}, bf16[24,512]{1,0:T(8,128)(2,1)S(1)}, u32[]{:S(2)}, u32[]{:S(2)}) collective-permute-start(bf16[24,512]{1,0:T(8,128)(2,1)S(1)} %collective-permute-done.1.refs_1_), channel_id=1, source_target_pairs={{0,1},{1,0},{2,3},{3,2},{4,5},{5,4},{6,7},{7,6},{8,9},{9,8},{10,11... | collective-permute-start | bytes 73736 | tf_op jit(solution)/shard_map/ppermute | solution.py:284
  12.2 5.0 %collective-permute-start.5 = (bf16[80,256]{1,0:T(8,128)(2,1)S(1)}, bf16[80,256]{1,0:T(8,128)(2,1)S(1)}, u32[]{:S(2)}, u32[]{:S(2)}) collective-permute-start(bf16[80,256]{1,0:T(8,128)(2,1)S(1)} %get-tuple-element.34), channel_id=1, source_target_pairs={{0,6},{1,5},{2,4},{3,7},{4,2},{5,1},{6,0},{7,3},{8,14},{9,13},{10,... | collective-permute-start | bytes 122888 | tf_op jit(solution)/shard_map/ppermute | solution.py:292
  14.8 4.0 %collective-permute-start.6 = (bf16[80,256]{1,0:T(8,128)(2,1)S(1)}, bf16[80,256]{1,0:T(8,128)(2,1)S(1)}, u32[]{:S(2)}, u32[]{:S(2)}) collective-permute-start(bf16[80,256]{1,0:T(8,128)(2,1)S(1)} %get-tuple-element.35), channel_id=1, source_target_pairs={{0,2},{1,7},{2,0},{3,5},{4,6},{5,3},{6,4},{7,1},{8,10},{9,15},{10,... | collective-permute-start | bytes 122888 | tf_op jit(solution)/shard_map/ppermute | solution.py:292
  15.3 4.0 %collective-permute-start.7 = (bf16[80,256]{1,0:T(8,128)(2,1)S(1)}, bf16[80,256]{1,0:T(8,128)(2,1)S(1)}, u32[]{:S(2)}, u32[]{:S(2)}) collective-permute-start(bf16[80,256]{1,0:T(8,128)(2,1)S(1)} %get-tuple-element.36), channel_id=1, source_target_pairs={{0,4},{1,3},{2,6},{3,1},{4,0},{5,7},{6,2},{7,5},{8,12},{9,11},{10,... | collective-permute-start | bytes 122888 | tf_op jit(solution)/shard_map/ppermute | solution.py:292

commit v19 on v16

--- a/solution.py
+++ b/solution.py
@@ -12,7 +12,7 @@
 LAG_COUNT = 2 * MAXLAG + 1
 LANES = 256
 GROUP = 8
-HOPS = ((3, 2), (1, 3), (2, 1))
+HOPS = (3, 1, 2)
 
 
 def broadcast(value, axis, source):
@@ -124,8 +124,7 @@
 def lag_rows(plan, rows_ref, toeplitz_ref):
     span = plan.span
     me = lax.axis_index("blk")
-    on_first = lax.axis_index("src") == 0
-    hops = [0] + [jnp.where(on_first, *pair) for pair in HOPS]
+    hops = (0,) + HOPS
     filler = jnp.zeros((1, span - plan.segment), jnp.float32)
     for window in range(plan.windows):
         at = slice(window * span, (window + 1) * span)
@@ -161,10 +160,12 @@
     )
 
 
-def near_kernel(plan, other_ref, toeplitz_ref, prior_ref, sum_ref, columns_ref):
+def near_kernel(plan, mine_ref, other_ref, sum_ref, rows_ref, toeplitz_ref, columns_ref):
+    rows_ref[...] = mine_ref[...].astype(jnp.float32)
+    lag_rows(plan, rows_ref, toeplitz_ref)
     other = other_ref[...].astype(jnp.float32)
-    sum_ref[:, : plan.half_lanes] = prior_ref[...]
-    sum_ref[:, plan.half_lanes :] = half_product(plan, other, toeplitz_ref, columns_ref)
+    sum_ref[:, : plan.half_lanes] = half_product(plan, rows_ref[...], toeplitz_ref, columns_ref.at[0])
+    sum_ref[:, plan.half_lanes :] = half_product(plan, other, toeplitz_ref, columns_ref.at[1])
 
 
 def across_kernel(plan, mine_ref, prior_ref, toeplitz_ref, sum_ref, rows_ref, columns_ref):
@@ -223,13 +224,8 @@
     return jnp.concatenate(pieces, axis=0)
 
 
-def first_kernel(
-    plan, index_ref, mine_ref, order_ref, chosen_ref, same_ref, toeplitz_ref, sum_ref, rows_ref, columns_ref
-):
-    same_ref[...] = mine_ref[...]
-    rows_ref[...] = mine_ref[...].astype(jnp.float32)
-    lag_rows(plan, rows_ref, toeplitz_ref)
-    sum_ref[...] = half_product(plan, rows_ref[...], toeplitz_ref, columns_ref)
+def choose_kernel(plan, index_ref, whitened_ref, order_ref, chosen_ref, same_ref):
+    same_ref[...] = whitened_ref[...]
     first = lax.axis_index("src") * plan.half
     index = index_ref[...] - first
     index = jnp.where(index < 0, index + plan.channels, index)
@@ -280,9 +276,9 @@
     def swap_cores(array):
         return lax.ppermute(array, "src", [(0, 1), (1, 0)])
 
-    def swap_blk(array, hops):
+    def swap_blk(array, hop):
         pairs = [
-            (place * plan.src_size + core, (place ^ hops[core]) * plan.src_size + core)
+            (place * plan.src_size + core, (place ^ hop) * plan.src_size + 1 - core)
             for place in range(plan.blk_size)
             for core in range(plan.src_size)
         ]
@@ -320,22 +316,23 @@
             name=name,
         )(*operands)
 
-    across = swap_blk(whitened, (plan.targets, plan.targets))
-    order, chosen, same, lagged, total = call(
-        first_kernel,
-        "first",
+    across = swap_blk(whitened, plan.targets)
+    order, chosen, same = call(
+        choose_kernel,
+        "choose",
         (source_index.reshape(1, -1), whitened),
         (
             jax.ShapeDtypeStruct((plan.rows, (plan.targets - 1) * plan.rows), jnp.bfloat16),
             jax.ShapeDtypeStruct((LANES, plan.source_count), jnp.bfloat16),
             jax.ShapeDtypeStruct(whitened.shape, whitened.dtype),
-            jax.ShapeDtypeStruct(toeplitz, jnp.bfloat16),
-            jax.ShapeDtypeStruct((height, plan.half_lanes), jnp.float32),
         ),
-        (rows, pltpu.VMEM(columns, jnp.bfloat16)),
     )
     (total,) = call(
-        near_kernel, "near", (swap_cores(same), lagged, total), (sums,), (pltpu.VMEM(columns, jnp.bfloat16),)
+        near_kernel,
+        "near",
+        (swap_cores(same), whitened),
+        (sums,),
+        (rows, pltpu.VMEM(toeplitz, jnp.bfloat16), pltpu.VMEM((2,) + columns, jnp.bfloat16)),
     )
     across_other = swap_cores(across)
     lagged, total = call(
@@ -355,7 +352,8 @@
         ),
         (pltpu.VMEM(columns, jnp.bfloat16),),
     )
-    arrived = [swap_blk(array, hops) for array, hops in zip(sent, HOPS)]
+    arrived = [swap_blk(array, hop) for array, hop in zip(sent, HOPS)]
+    kept = swap_cores(kept)
     (base,) = call(
         prepare_kernel,
         "prepare",

time: 17.8 us -> 17.8 us (level)
  starting transfers between devices: 7.73 us -> 8.57 us
  waiting for transfers between devices: 4.77 us -> 4.16 us
  Pallas kernels: 5.11 us -> 4.89 us
    ppermute x2 -> x3, starting transfers between devices: 0.07 us -> 1.32 us  [swap_cores(): return lax.ppermute(array, 'src', [(0, 1), (1, 0)])]
    ppermute x4, waiting for transfers between devices: 4.65 us -> 4.15 us  [swap_blk(): return lax.ppermute(array, ('blk', 'src'), pairs)]
    ppermute x4, starting transfers between devices: 7.65 us -> 7.25 us  [swap_blk(): return lax.ppermute(array, ('blk', 'src'), pairs)]
    pallas_call x5, Pallas kernels: 2.79 us -> 2.58 us  [call(): pl.pallas_call(functools.partial(kernel, plan), out_shape=outputs, in_spe...]
  transfers between devices with their start and end apart: 6 -> 7, of which waited for: 5 -> 4; matrix products, arithmetic and copies ran while one was open for 0% -> 0% of each run, Pallas kernels for 13% -> 12%
where the time goes in v19:
time: 17.8 us; the launch traced here: 17.7 us
  starting transfers between devices  8.57 us (48%)
  Pallas kernels  4.89 us (27%)
  waiting for transfers between devices  4.16 us (23%)
    ppermute x4, starting transfers between devices, swap_blk(): return lax.ppermute(array, ('blk', 'src'), pairs)  7.25 us
    ppermute x4, waiting for transfers between devices, swap_blk(): return lax.ppermute(array, ('blk', 'src'), pairs)  4.15 us
    pallas_call x5, Pallas kernels, call(): pl.pallas_call(functools.partial(kernel, plan), out_shape=outputs, in_spe...  2.58 us
    ppermute x3, starting transfers between devices, swap_cores(): return lax.ppermute(array, 'src', [(0, 1), (1, 0)])  1.32 us
    pallas_call x1, Pallas kernels, few_channels(): pl.pallas_call(functools.partial(expand_kernel, plan), out_shape=jax.Shap...  1.21 us
    pallas_call x1, Pallas kernels, few_channels(): pl.pallas_call(functools.partial(whiten_kernel, plan), out_shape=pltpu.VM...  1.1 us
  transfers between devices with their start and end apart: 7, of which 4 were waited for; matrix products, arithmetic and copies ran while one was open for 0% of the time, Pallas kernels for 12%

profile of v19, /device:TPU:0, one launch (start us, length us, event | category | flops | bytes accessed | tf_op | source)
XLA Modules:
  0.0 17.7 jit_solution(6183333392211977032)
XLA Ops:
  0.0 1.1 %whiten.1.whitened_ref.other_ref = bf16[48,512]{1,0:T(8,128)(2,1)S(1)} custom-call(f32[24,2,512]{2,1,0:T(2,128)} %traces_hbm.1, s32[2,24]{1,0:T(2,128)} %bitcast.3), custom_call_target="tpu_custom_call" | custom-call | tf_op jit(solution)/shard_map/whiten/pallas_call | solution.py:287
  1.1 0.0 copy-start
  1.1 3.5 %collective-permute-start = (bf16[48,512]{1,0:T(8,128)(2,1)S(1)}, bf16[48,512]{1,0:T(8,128)(2,1)S(1)}, u32[]{:S(2)}, u32[]{:S(2)}) collective-permute-start(bf16[48,512]{1,0:T(8,128)(2,1)S(1)} %whiten.1.whitened_ref.other_ref), channel_id=1, source_target_pairs={{0,9},{1,8},{2,11},{3,10},{4,13},{5,12},{6,15},{7,14},{8,1},{9,0},... | collective-permute-start | bytes 147464 | tf_op jit(solution)/shard_map/ppermute | solution.py:285
  4.7 0.0 copy-done
  4.7 0.3 %choose.1 = (bf16[80,240]{1,0:T(8,128)(2,1)S(1)}, bf16[256,256]{1,0:T(8,128)(2,1)S(1)}, bf16[48,512]{1,0:T(8,128)(2,1)S(1)}) custom-call(s32[1,256]{1,0:T(1,128)S(1)} %bitcast.2, bf16[48,512]{1,0:T(8,128)(2,1)S(1)} %whiten.1.whitened_ref.other_ref), custom_call_target="tpu_custom_call" | custom-call | tf_op jit(solution)/shard_map/choose/pallas_call | solution.py:309
  5.0 0.7 %collective-permute-start.2 = (bf16[48,512]{1,0:T(8,128)(2,1)S(1)}, bf16[48,512]{1,0:T(8,128)(2,1)S(1)}, u32[]{:S(2)}, u32[]{:S(2)}) collective-permute-start(bf16[48,512]{1,0:T(8,128)(2,1)S(1)} %get-tuple-element.16), channel_id=1, source_target_pairs={{0,1},{1,0},{2,3},{3,2},{4,5},{5,4},{6,7},{7,6},{8,9},{9,8},{10,11... | collective-permute-start | bytes 147464 | tf_op jit(solution)/shard_map/ppermute | solution.py:277
  5.7 1.1 %collective-permute-done.mine_ref = bf16[48,512]{1,0:T(8,128)(2,1)S(1)} collective-permute-done((bf16[48,512]{1,0:T(8,128)(2,1)S(1)}, bf16[48,512]{1,0:T(8,128)(2,1)S(1)}, u32[]{:S(2)}, u32[]{:S(2)}) %collective-permute-start) | collective-permute-done | bytes 49184 | tf_op jit(solution)/shard_map/ppermute | solution.py:285
  6.8 0.3 %collective-permute-start.1 = (bf16[48,512]{1,0:T(8,128)(2,1)S(1)}, bf16[48,512]{1,0:T(8,128)(2,1)S(1)}, u32[]{:S(2)}, u32[]{:S(2)}) collective-permute-start(bf16[48,512]{1,0:T(8,128)(2,1)S(1)} %collective-permute-done.mine_ref), channel_id=1, source_target_pairs={{0,1},{1,0},{2,3},{3,2},{4,5},{5,4},{6,7},{7,6},{8,9},{9,8},{10,11... | collective-permute-start | bytes 147464 | tf_op jit(solution)/shard_map/ppermute | solution.py:277
  7.1 0.0 collective-permute-done.2.mine_ref
  7.1 0.8 %near.1.prior_ref = f32[384,256]{1,0:T(8,128)S(1)} custom-call(bf16[48,512]{1,0:T(8,128)(2,1)S(1)} %collective-permute-done.2.mine_ref, bf16[48,512]{1,0:T(8,128)(2,1)S(1)} %whiten.1.whitened_ref.other_ref), custom_call_target="tpu_custom_call" | custom-call | tf_op jit(solution)/shard_map/near/pallas_call | solution.py:309
  7.9 0.6 %across.1 = (bf16[384,1280]{1,0:T(8,128)(2,1)S(1)}, f32[384,256]{1,0:T(8,128)S(1)}) custom-call(bf16[48,512]{1,0:T(8,128)(2,1)S(1)} %collective-permute-done.mine_ref, f32[384,256]{1,0:T(8,128)S(1)} %near.1.prior_ref), custom_call_target="tpu_custom_call" | custom-call | tf_op jit(solution)/shard_map/across/pallas_call | solution.py:309
  8.5 0.0 collective-permute-done.1.other_ref
  8.5 0.5 %finish.1 = (f32[80,256]{1,0:T(8,128)S(1)}, bf16[80,256]{1,0:T(8,128)(2,1)S(1)}, bf16[80,256]{1,0:T(8,128)(2,1)S(1)}, bf16[80,256]{1,0:T(8,128)(2,1)S(1)}) custom-call(bf16[48,512]{1,0:T(8,128)(2,1)S(1)} %collective-permute-done.1.other_ref, bf16[384,1280]{1,0:T(8,128)(2,1)S(1)} %get-tuple-element.17.toeplitz_ref, f32[384,256]{1,0:T(8,128)S(1)} %get-tuple-element.18.prior_ref), custom_call_target="tpu_custom_call" | custom-call | tf_op jit(solution)/shard_map/finish/pallas_call | solution.py:309
  9.0 0.3 %collective-permute-start.3 = (f32[80,256]{1,0:T(8,128)S(1)}, f32[80,256]{1,0:T(8,128)S(1)}, u32[]{:S(2)}, u32[]{:S(2)}) collective-permute-start(f32[80,256]{1,0:T(8,128)S(1)} %get-tuple-element.19), channel_id=1, source_target_pairs={{0,1},{1,0},{2,3},{3,2},{4,5},{5,4},{6,7},{7,6},{8,9},{9,8},{10,11... | collective-permute-start | bytes 245768 | tf_op jit(solution)/shard_map/ppermute | solution.py:277
  9.2 3.2 %collective-permute-start.4 = (bf16[80,256]{1,0:T(8,128)(2,1)S(1)}, bf16[80,256]{1,0:T(8,128)(2,1)S(1)}, u32[]{:S(2)}, u32[]{:S(2)}) collective-permute-start(bf16[80,256]{1,0:T(8,128)(2,1)S(1)} %get-tuple-element.20), channel_id=1, source_target_pairs={{0,7},{1,6},{2,5},{3,4},{4,3},{5,2},{6,1},{7,0},{8,15},{9,14},{10,... | collective-permute-start | bytes 122888 | tf_op jit(solution)/shard_map/ppermute | solution.py:285
  12.4 0.5 %collective-permute-start.5 = (bf16[80,256]{1,0:T(8,128)(2,1)S(1)}, bf16[80,256]{1,0:T(8,128)(2,1)S(1)}, u32[]{:S(2)}, u32[]{:S(2)}) collective-permute-start(bf16[80,256]{1,0:T(8,128)(2,1)S(1)} %get-tuple-element.21), channel_id=1, source_target_pairs={{0,3},{1,2},{2,1},{3,0},{4,7},{5,6},{6,5},{7,4},{8,11},{9,10},{10,... | collective-permute-start | bytes 122888 | tf_op jit(solution)/shard_map/ppermute | solution.py:285
  12.9 0.0 collective-permute-start.6
  13.0 0.0 collective-permute-done.3.kept_ref
  13.0 0.4 %prepare.1.base_ref = f32[400,256]{1,0:T(8,128)S(1)} custom-call(bf16[80,240]{1,0:T(8,128)(2,1)S(1)} %get-tuple-element.14.order_ref, bf16[256,256]{1,0:T(8,128)(2,1)S(1)} %get-tuple-element.15.chosen_ref, f32[80,256]{1,0:T(8,128)S(1)} %collective-permute-done.3.kept_ref), custom_call_target="tpu_custom_call" | custom-call | tf_op jit(solution)/shard_map/prepare/pallas_call | solution.py:309
  13.4 0.9 %collective-permute-done.4.refs_0_ = bf16[80,256]{1,0:T(8,128)(2,1)S(1)} collective-permute-done((bf16[80,256]{1,0:T(8,128)(2,1)S(1)}, bf16[80,256]{1,0:T(8,128)(2,1)S(1)}, u32[]{:S(2)}, u32[]{:S(2)}) %collective-permute-start.4) | collective-permute-done | bytes 40992 | tf_op jit(solution)/shard_map/ppermute | solution.py:285
  14.4 1.5 %collective-permute-done.5.refs_1_ = bf16[80,256]{1,0:T(8,128)(2,1)S(1)} collective-permute-done((bf16[80,256]{1,0:T(8,128)(2,1)S(1)}, bf16[80,256]{1,0:T(8,128)(2,1)S(1)}, u32[]{:S(2)}, u32[]{:S(2)}) %collective-permute-start.5) | collective-permute-done | bytes 40992 | tf_op jit(solution)/shard_map/ppermute | solution.py:285
  15.9 0.6 %collective-permute-done.6.refs_2_ = bf16[80,256]{1,0:T(8,128)(2,1)S(1)} collective-permute-done((bf16[80,256]{1,0:T(8,128)(2,1)S(1)}, bf16[80,256]{1,0:T(8,128)(2,1)S(1)}, u32[]{:S(2)}, u32[]{:S(2)}) %collective-permute-start.6) | collective-permute-done | bytes 40992 | tf_op jit(solution)/shard_map/ppermute | solution.py:285
  16.5 1.2 %expand.1 = f32[3,129,256]{2,1,0:T(8,128)} custom-call(bf16[80,240]{1,0:T(8,128)(2,1)S(1)} %get-tuple-element.14.order_ref, bf16[256,256]{1,0:T(8,128)(2,1)S(1)} %get-tuple-element.15.chosen_ref, f32[400,256]{1,0:T(8,128)S(1)} %prepare.1.base_ref, bf16[80,256]{1,0:T(8,128)(2,1)S(1)} %collective-permute-done.4.refs_0_, ...), custom_call_target="tpu_custom_call" | custom-call | tf_op jit(solution)/shard_map/expand/pallas_call | solution.py:364
Async XLA Ops:
  1.1 3.6 %copy-start = (s32[256]{0:T(256)S(1)}, s32[256]{0:T(256)}, u32[]{:S(2)}) copy-start(s32[256]{0:T(256)} %param.5) | copy-start | bytes 3076
  1.1 5.7 %collective-permute-start = (bf16[48,512]{1,0:T(8,128)(2,1)S(1)}, bf16[48,512]{1,0:T(8,128)(2,1)S(1)}, u32[]{:S(2)}, u32[]{:S(2)}) collective-permute-start(bf16[48,512]{1,0:T(8,128)(2,1)S(1)} %whiten.1.whitened_ref.other_ref), channel_id=1, source_target_pairs={{0,9},{1,8},{2,11},{3,10},{4,13},{5,12},{6,15},{7,14},{8,1},{9,0},... | collective-permute-start | bytes 147464 | tf_op jit(solution)/shard_map/ppermute | solution.py:285
  5.0 2.2 %collective-permute-start.2 = (bf16[48,512]{1,0:T(8,128)(2,1)S(1)}, bf16[48,512]{1,0:T(8,128)(2,1)S(1)}, u32[]{:S(2)}, u32[]{:S(2)}) collective-permute-start(bf16[48,512]{1,0:T(8,128)(2,1)S(1)} %get-tuple-element.16), channel_id=1, source_target_pairs={{0,1},{1,0},{2,3},{3,2},{4,5},{5,4},{6,7},{7,6},{8,9},{9,8},{10,11... | collective-permute-start | bytes 147464 | tf_op jit(solution)/shard_map/ppermute | solution.py:277
  6.8 1.7 %collective-permute-start.1 = (bf16[48,512]{1,0:T(8,128)(2,1)S(1)}, bf16[48,512]{1,0:T(8,128)(2,1)S(1)}, u32[]{:S(2)}, u32[]{:S(2)}) collective-permute-start(bf16[48,512]{1,0:T(8,128)(2,1)S(1)} %collective-permute-done.mine_ref), channel_id=1, source_target_pairs={{0,1},{1,0},{2,3},{3,2},{4,5},{5,4},{6,7},{7,6},{8,9},{9,8},{10,11... | collective-permute-start | bytes 147464 | tf_op jit(solution)/shard_map/ppermute | solution.py:277
  9.0 4.0 %collective-permute-start.3 = (f32[80,256]{1,0:T(8,128)S(1)}, f32[80,256]{1,0:T(8,128)S(1)}, u32[]{:S(2)}, u32[]{:S(2)}) collective-permute-start(f32[80,256]{1,0:T(8,128)S(1)} %get-tuple-element.19), channel_id=1, source_target_pairs={{0,1},{1,0},{2,3},{3,2},{4,5},{5,4},{6,7},{7,6},{8,9},{9,8},{10,11... | collective-permute-start | bytes 245768 | tf_op jit(solution)/shard_map/ppermute | solution.py:277
  9.2 5.1 %collective-permute-start.4 = (bf16[80,256]{1,0:T(8,128)(2,1)S(1)}, bf16[80,256]{1,0:T(8,128)(2,1)S(1)}, u32[]{:S(2)}, u32[]{:S(2)}) collective-permute-start(bf16[80,256]{1,0:T(8,128)(2,1)S(1)} %get-tuple-element.20), channel_id=1, source_target_pairs={{0,7},{1,6},{2,5},{3,4},{4,3},{5,2},{6,1},{7,0},{8,15},{9,14},{10,... | collective-permute-start | bytes 122888 | tf_op jit(solution)/shard_map/ppermute | solution.py:285
  12.4 3.5 %collective-permute-start.5 = (bf16[80,256]{1,0:T(8,128)(2,1)S(1)}, bf16[80,256]{1,0:T(8,128)(2,1)S(1)}, u32[]{:S(2)}, u32[]{:S(2)}) collective-permute-start(bf16[80,256]{1,0:T(8,128)(2,1)S(1)} %get-tuple-element.21), channel_id=1, source_target_pairs={{0,3},{1,2},{2,1},{3,0},{4,7},{5,6},{6,5},{7,4},{8,11},{9,10},{10,... | collective-permute-start | bytes 122888 | tf_op jit(solution)/shard_map/ppermute | solution.py:285
  12.9 3.5 %collective-permute-start.6 = (bf16[80,256]{1,0:T(8,128)(2,1)S(1)}, bf16[80,256]{1,0:T(8,128)(2,1)S(1)}, u32[]{:S(2)}, u32[]{:S(2)}) collective-permute-start(bf16[80,256]{1,0:T(8,128)(2,1)S(1)} %get-tuple-element.22), channel_id=1, source_target_pairs={{0,5},{1,4},{2,7},{3,6},{4,1},{5,0},{6,3},{7,2},{8,13},{9,12},{10,... | collective-permute-start | bytes 122888 | tf_op jit(solution)/shard_map/ppermute | solution.py:285

commit v20 on v19

--- a/solution.py
+++ b/solution.py
@@ -12,7 +12,7 @@
 LAG_COUNT = 2 * MAXLAG + 1
 LANES = 256
 GROUP = 8
-HOPS = (3, 1, 2)
+HOPS = (3, 1, 2, 0)
 
 
 def broadcast(value, axis, source):
@@ -124,11 +124,10 @@
 def lag_rows(plan, rows_ref, toeplitz_ref):
     span = plan.span
     me = lax.axis_index("blk")
-    hops = (0,) + HOPS
     filler = jnp.zeros((1, span - plan.segment), jnp.float32)
     for window in range(plan.windows):
         at = slice(window * span, (window + 1) * span)
-        for place, hop in enumerate(hops):
+        for place, hop in enumerate(HOPS):
             for member in range(plan.own):
                 channel = window * plan.half + (me ^ hop) * plan.own + member
                 row = jnp.concatenate([rows_ref[pl.ds(channel, 1), :], filler], axis=1)
@@ -143,7 +142,7 @@
                 )
 
 
-def half_product(plan, values, toeplitz_ref, columns_ref):
+def fill_columns(plan, values, columns_ref):
     span = plan.span
     filled = plan.coarse * plan.half
     if filled < plan.half_lanes:
@@ -155,6 +154,9 @@
         for step in range(plan.coarse):
             moved = pltpu.roll(rows, step * plan.fine, 1) if step else rows
             columns_ref[step * plan.half : (step + 1) * plan.half, at] = moved.astype(jnp.bfloat16)
+
+
+def product(toeplitz_ref, columns_ref):
     return lax.dot_general(
         toeplitz_ref[...], columns_ref[...], (((1,), (1,)), ((), ())), preferred_element_type=jnp.float32
     )
@@ -163,25 +165,23 @@
 def near_kernel(plan, mine_ref, other_ref, sum_ref, rows_ref, toeplitz_ref, columns_ref):
     rows_ref[...] = mine_ref[...].astype(jnp.float32)
     lag_rows(plan, rows_ref, toeplitz_ref)
-    other = other_ref[...].astype(jnp.float32)
-    sum_ref[:, : plan.half_lanes] = half_product(plan, rows_ref[...], toeplitz_ref, columns_ref.at[0])
-    sum_ref[:, plan.half_lanes :] = half_product(plan, other, toeplitz_ref, columns_ref.at[1])
+    fill_columns(plan, rows_ref[...], columns_ref.at[: plan.half_lanes])
+    fill_columns(plan, other_ref[...].astype(jnp.float32), columns_ref.at[plan.half_lanes :])
+    sum_ref[...] = product(toeplitz_ref, columns_ref)
 
 
 def across_kernel(plan, mine_ref, prior_ref, toeplitz_ref, sum_ref, rows_ref, columns_ref):
     rows_ref[...] = mine_ref[...].astype(jnp.float32)
     lag_rows(plan, rows_ref, toeplitz_ref)
-    sum_ref[:, : plan.half_lanes] = prior_ref[:, : plan.half_lanes] + half_product(
-        plan, rows_ref[...], toeplitz_ref, columns_ref
-    )
+    fill_columns(plan, rows_ref[...], columns_ref)
+    sum_ref[:, : plan.half_lanes] = prior_ref[:, : plan.half_lanes] + product(toeplitz_ref, columns_ref)
     sum_ref[:, plan.half_lanes :] = prior_ref[:, plan.half_lanes :]
 
 
 def finish_kernel(plan, other_ref, toeplitz_ref, prior_ref, *refs):
     *out_refs, columns_ref = refs
-    right = prior_ref[:, plan.half_lanes :] + half_product(
-        plan, other_ref[...].astype(jnp.float32), toeplitz_ref, columns_ref
-    )
+    fill_columns(plan, other_ref[...].astype(jnp.float32), columns_ref)
+    right = prior_ref[:, plan.half_lanes :] + product(toeplitz_ref, columns_ref)
     products = jnp.concatenate([prior_ref[:, : plan.half_lanes], right], axis=1)
     products = products.reshape(plan.targets, plan.own, plan.fine_padded, LANES)
     for hop in range(plan.targets):
@@ -236,24 +236,15 @@
         chosen = chosen | (at_column == lane + step * plan.half)
     chosen_ref[...] = chosen.astype(jnp.float32).astype(jnp.bfloat16)
     order = order_matrix(plan)
-    for block in range(plan.targets - 1):
+    for block in range(plan.targets):
         order_ref[:, block * plan.rows : (block + 1) * plan.rows] = order
 
 
-def prepare_kernel(plan, order_ref, chosen_ref, kept_ref, base_ref):
-    kept = kept_ref[...] * plan.norm_factor
-    high = kept.astype(jnp.bfloat16)
-    low = (kept - high.astype(jnp.float32)).astype(jnp.bfloat16)
-    order = order_ref[:, : plan.rows]
-    ordered = sum(jnp.dot(order, part, preferred_element_type=jnp.float32) for part in (high, low))
-    base_ref[...] = jnp.dot(spread(plan, ordered), chosen_ref[...], preferred_element_type=jnp.float32)
-
-
-def expand_kernel(plan, order_ref, chosen_ref, base_ref, *refs):
+def expand_kernel(plan, order_ref, chosen_ref, *refs):
     *arrived_refs, out_hbm, out_ref, sems = refs
     blocks = jnp.concatenate([ref[...] for ref in arrived_refs], axis=0)
-    arrived = jnp.dot(order_ref[...], blocks, preferred_element_type=jnp.float32) * plan.norm_factor
-    expanded = base_ref[...] + jnp.dot(spread(plan, arrived), chosen_ref[...], preferred_element_type=jnp.float32)
+    total = jnp.dot(order_ref[...], blocks, preferred_element_type=jnp.float32) * plan.norm_factor
+    expanded = jnp.dot(spread(plan, total), chosen_ref[...], preferred_element_type=jnp.float32)
     copies = []
     for member in range(plan.own):
         for step in range(plan.coarse):
@@ -322,7 +313,7 @@
         "choose",
         (source_index.reshape(1, -1), whitened),
         (
-            jax.ShapeDtypeStruct((plan.rows, (plan.targets - 1) * plan.rows), jnp.bfloat16),
+            jax.ShapeDtypeStruct((plan.rows, plan.targets * plan.rows), jnp.bfloat16),
             jax.ShapeDtypeStruct((LANES, plan.source_count), jnp.bfloat16),
             jax.ShapeDtypeStruct(whitened.shape, whitened.dtype),
         ),
@@ -332,7 +323,7 @@
         "near",
         (swap_cores(same), whitened),
         (sums,),
-        (rows, pltpu.VMEM(toeplitz, jnp.bfloat16), pltpu.VMEM((2,) + columns, jnp.bfloat16)),
+        (rows, pltpu.VMEM(toeplitz, jnp.bfloat16), pltpu.VMEM((LANES, width), jnp.bfloat16)),
     )
     across_other = swap_cores(across)
     lagged, total = call(
@@ -342,34 +333,24 @@
         (jax.ShapeDtypeStruct(toeplitz, jnp.bfloat16), sums),
         (rows, pltpu.VMEM(columns, jnp.bfloat16)),
     )
-    kept, *sent = call(
+    sent = call(
         finish_kernel,
         "finish",
         (across_other, lagged, total),
-        tuple(
-            jax.ShapeDtypeStruct((plan.rows, LANES), jnp.bfloat16 if hop else jnp.float32)
-            for hop in range(plan.targets)
-        ),
+        (jax.ShapeDtypeStruct((plan.rows, LANES), jnp.bfloat16),) * plan.targets,
         (pltpu.VMEM(columns, jnp.bfloat16),),
     )
     arrived = [swap_blk(array, hop) for array, hop in zip(sent, HOPS)]
-    kept = swap_cores(kept)
-    (base,) = call(
-        prepare_kernel,
-        "prepare",
-        (order, chosen, kept),
-        (jax.ShapeDtypeStruct((plan.coarse * plan.rows, plan.source_count), jnp.float32),),
-    )
     out_shape = (plan.own, LAG_COUNT, plan.source_count)
     return pl.pallas_call(
         functools.partial(expand_kernel, plan),
         out_shape=jax.ShapeDtypeStruct(out_shape, jnp.float32),
-        in_specs=[vmem] * (3 + len(arrived)),
+        in_specs=[vmem] * (2 + len(arrived)),
         out_specs=pl.BlockSpec(memory_space=pl.ANY),
         scratch_shapes=[pltpu.VMEM(out_shape, jnp.float32), pltpu.SemaphoreType.DMA((plan.own,))],
         compiler_params=params,
         name="expand",
-    )(order, chosen, base, *arrived)
+    )(order, chosen, *arrived)
 
 
 def body(traces, valid_flags, source_index):

time: 17.8 us -> 17.3 us (0.972)
  Pallas kernels: 4.89 us -> 4.39 us
    pallas_call x5 -> x4, Pallas kernels: 2.58 us -> 2.06 us  [call(): pl.pallas_call(functools.partial(kernel, plan), out_shape=outputs, in_spe...]
    ppermute x4 -> x5, starting transfers between devices: 7.25 us -> 7.59 us  [swap_blk(): return lax.ppermute(array, ('blk', 'src'), pairs)]
    ppermute x3 -> x2, starting transfers between devices: 1.32 us -> 1.06 us  [swap_cores(): return lax.ppermute(array, 'src', [(0, 1), (1, 0)])]
    ppermute x4 -> x5, waiting for transfers between devices: 4.15 us -> 4.06 us  [swap_blk(): return lax.ppermute(array, ('blk', 'src'), pairs)]
  transfers between devices with their start and end apart: 7 -> 7, of which waited for: 4 -> 4; matrix products, arithmetic and copies ran while one was open for 0% -> 0% of each run, Pallas kernels for 12% -> 9%
where the time goes in v20:
time: 17.3 us; the launch traced here: 17.2 us
  starting transfers between devices  8.65 us (50%)
  Pallas kernels  4.39 us (25%)
  waiting for transfers between devices  4.06 us (23%)
    ppermute x5, starting transfers between devices, swap_blk(): return lax.ppermute(array, ('blk', 'src'), pairs)  7.59 us
    ppermute x5, waiting for transfers between devices, swap_blk(): return lax.ppermute(array, ('blk', 'src'), pairs)  4.06 us
    pallas_call x4, Pallas kernels, call(): pl.pallas_call(functools.partial(kernel, plan), out_shape=outputs, in_spe...  2.06 us
    pallas_call x1, Pallas kernels, few_channels(): pl.pallas_call(functools.partial(expand_kernel, plan), out_shape=jax.Shap...  1.22 us
    pallas_call x1, Pallas kernels, few_channels(): pl.pallas_call(functools.partial(whiten_kernel, plan), out_shape=pltpu.VM...  1.1 us
    ppermute x2, starting transfers between devices, swap_cores(): return lax.ppermute(array, 'src', [(0, 1), (1, 0)])  1.06 us
  transfers between devices with their start and end apart: 7, of which 4 were waited for; matrix products, arithmetic and copies ran while one was open for 0% of the time, Pallas kernels for 9%

profile of v20, /device:TPU:0, one launch (start us, length us, event | category | flops | bytes accessed | tf_op | source)
XLA Modules:
  0.0 17.2 jit_solution(17545570974893783639)
XLA Ops:
  0.0 1.1 %whiten.1.whitened_ref.other_ref = bf16[48,512]{1,0:T(8,128)(2,1)S(1)} custom-call(f32[24,2,512]{2,1,0:T(2,128)} %traces_hbm.1, s32[2,24]{1,0:T(2,128)} %bitcast.3), custom_call_target="tpu_custom_call" | custom-call | tf_op jit(solution)/shard_map/whiten/pallas_call | solution.py:278
  1.1 0.0 copy-start
  1.1 3.5 %collective-permute-start = (bf16[48,512]{1,0:T(8,128)(2,1)S(1)}, bf16[48,512]{1,0:T(8,128)(2,1)S(1)}, u32[]{:S(2)}, u32[]{:S(2)}) collective-permute-start(bf16[48,512]{1,0:T(8,128)(2,1)S(1)} %whiten.1.whitened_ref.other_ref), channel_id=1, source_target_pairs={{0,9},{1,8},{2,11},{3,10},{4,13},{5,12},{6,15},{7,14},{8,1},{9,0},... | collective-permute-start | bytes 147464 | tf_op jit(solution)/shard_map/ppermute | solution.py:276
  4.7 0.0 copy-done
  4.7 0.3 %choose.1 = (bf16[80,320]{1,0:T(8,128)(2,1)S(1)}, bf16[256,256]{1,0:T(8,128)(2,1)S(1)}, bf16[48,512]{1,0:T(8,128)(2,1)S(1)}) custom-call(s32[1,256]{1,0:T(1,128)S(1)} %bitcast.2, bf16[48,512]{1,0:T(8,128)(2,1)S(1)} %whiten.1.whitened_ref.other_ref), custom_call_target="tpu_custom_call" | custom-call | tf_op jit(solution)/shard_map/choose/pallas_call | solution.py:300
  5.0 0.7 %collective-permute-start.2 = (bf16[48,512]{1,0:T(8,128)(2,1)S(1)}, bf16[48,512]{1,0:T(8,128)(2,1)S(1)}, u32[]{:S(2)}, u32[]{:S(2)}) collective-permute-start(bf16[48,512]{1,0:T(8,128)(2,1)S(1)} %get-tuple-element.16), channel_id=1, source_target_pairs={{0,1},{1,0},{2,3},{3,2},{4,5},{5,4},{6,7},{7,6},{8,9},{9,8},{10,11... | collective-permute-start | bytes 147464 | tf_op jit(solution)/shard_map/ppermute | solution.py:268
  5.7 1.1 %collective-permute-done.mine_ref = bf16[48,512]{1,0:T(8,128)(2,1)S(1)} collective-permute-done((bf16[48,512]{1,0:T(8,128)(2,1)S(1)}, bf16[48,512]{1,0:T(8,128)(2,1)S(1)}, u32[]{:S(2)}, u32[]{:S(2)}) %collective-permute-start) | collective-permute-done | bytes 49184 | tf_op jit(solution)/shard_map/ppermute | solution.py:276
  6.8 0.3 %collective-permute-start.1 = (bf16[48,512]{1,0:T(8,128)(2,1)S(1)}, bf16[48,512]{1,0:T(8,128)(2,1)S(1)}, u32[]{:S(2)}, u32[]{:S(2)}) collective-permute-start(bf16[48,512]{1,0:T(8,128)(2,1)S(1)} %collective-permute-done.mine_ref), channel_id=1, source_target_pairs={{0,1},{1,0},{2,3},{3,2},{4,5},{5,4},{6,7},{7,6},{8,9},{9,8},{10,11... | collective-permute-start | bytes 147464 | tf_op jit(solution)/shard_map/ppermute | solution.py:268
  7.1 0.0 collective-permute-done.2.mine_ref
  7.1 0.7 %near.1.prior_ref = f32[384,256]{1,0:T(8,128)S(1)} custom-call(bf16[48,512]{1,0:T(8,128)(2,1)S(1)} %collective-permute-done.2.mine_ref, bf16[48,512]{1,0:T(8,128)(2,1)S(1)} %whiten.1.whitened_ref.other_ref), custom_call_target="tpu_custom_call" | custom-call | tf_op jit(solution)/shard_map/near/pallas_call | solution.py:300
  7.8 0.6 %across.1 = (bf16[384,1280]{1,0:T(8,128)(2,1)S(1)}, f32[384,256]{1,0:T(8,128)S(1)}) custom-call(bf16[48,512]{1,0:T(8,128)(2,1)S(1)} %collective-permute-done.mine_ref, f32[384,256]{1,0:T(8,128)S(1)} %near.1.prior_ref), custom_call_target="tpu_custom_call" | custom-call | tf_op jit(solution)/shard_map/across/pallas_call | solution.py:300
  8.4 0.0 collective-permute-done.1.other_ref
  8.4 0.5 %finish.1 = (bf16[80,256]{1,0:T(8,128)(2,1)S(1)}, bf16[80,256]{1,0:T(8,128)(2,1)S(1)}, bf16[80,256]{1,0:T(8,128)(2,1)S(1)}, bf16[80,256]{1,0:T(8,128)(2,1)S(1)}) custom-call(bf16[48,512]{1,0:T(8,128)(2,1)S(1)} %collective-permute-done.1.other_ref, bf16[384,1280]{1,0:T(8,128)(2,1)S(1)} %get-tuple-element.17.toeplitz_ref, ...), custom_call_target="tpu_custom_call" | custom-call | tf_op jit(solution)/shard_map/finish/pallas_call | solution.py:300
  8.9 3.3 %collective-permute-start.3 = (bf16[80,256]{1,0:T(8,128)(2,1)S(1)}, bf16[80,256]{1,0:T(8,128)(2,1)S(1)}, u32[]{:S(2)}, u32[]{:S(2)}) collective-permute-start(bf16[80,256]{1,0:T(8,128)(2,1)S(1)} %get-tuple-element.19), channel_id=1, source_target_pairs={{0,7},{1,6},{2,5},{3,4},{4,3},{5,2},{6,1},{7,0},{8,15},{9,14},{10,... | collective-permute-start | bytes 122888 | tf_op jit(solution)/shard_map/ppermute | solution.py:276
  12.2 0.3 %collective-permute-start.4 = (bf16[80,256]{1,0:T(8,128)(2,1)S(1)}, bf16[80,256]{1,0:T(8,128)(2,1)S(1)}, u32[]{:S(2)}, u32[]{:S(2)}) collective-permute-start(bf16[80,256]{1,0:T(8,128)(2,1)S(1)} %get-tuple-element.20), channel_id=1, source_target_pairs={{0,3},{1,2},{2,1},{3,0},{4,7},{5,6},{6,5},{7,4},{8,11},{9,10},{10,... | collective-permute-start | bytes 122888 | tf_op jit(solution)/shard_map/ppermute | solution.py:276
  12.5 0.1 collective-permute-start.5
  12.6 0.4 %collective-permute-start.6 = (bf16[80,256]{1,0:T(8,128)(2,1)S(1)}, bf16[80,256]{1,0:T(8,128)(2,1)S(1)}, u32[]{:S(2)}, u32[]{:S(2)}) collective-permute-start(bf16[80,256]{1,0:T(8,128)(2,1)S(1)} %get-tuple-element.22), channel_id=1, source_target_pairs={{0,1},{1,0},{2,3},{3,2},{4,5},{5,4},{6,7},{7,6},{8,9},{9,8},{10,11... | collective-permute-start | bytes 122888 | tf_op jit(solution)/shard_map/ppermute | solution.py:276
  13.0 1.1 %collective-permute-done.3.refs_0_ = bf16[80,256]{1,0:T(8,128)(2,1)S(1)} collective-permute-done((bf16[80,256]{1,0:T(8,128)(2,1)S(1)}, bf16[80,256]{1,0:T(8,128)(2,1)S(1)}, u32[]{:S(2)}, u32[]{:S(2)}) %collective-permute-start.3) | collective-permute-done | bytes 40992 | tf_op jit(solution)/shard_map/ppermute | solution.py:276
  14.1 1.6 %collective-permute-done.4.refs_1_ = bf16[80,256]{1,0:T(8,128)(2,1)S(1)} collective-permute-done((bf16[80,256]{1,0:T(8,128)(2,1)S(1)}, bf16[80,256]{1,0:T(8,128)(2,1)S(1)}, u32[]{:S(2)}, u32[]{:S(2)}) %collective-permute-start.4) | collective-permute-done | bytes 40992 | tf_op jit(solution)/shard_map/ppermute | solution.py:276
  15.7 0.2 %collective-permute-done.5.refs_2_ = bf16[80,256]{1,0:T(8,128)(2,1)S(1)} collective-permute-done((bf16[80,256]{1,0:T(8,128)(2,1)S(1)}, bf16[80,256]{1,0:T(8,128)(2,1)S(1)}, u32[]{:S(2)}, u32[]{:S(2)}) %collective-permute-start.5) | collective-permute-done | bytes 40992 | tf_op jit(solution)/shard_map/ppermute | solution.py:276
  15.9 0.0 collective-permute-done.6.refs_3_
  15.9 1.2 %expand.1 = f32[3,129,256]{2,1,0:T(8,128)} custom-call(bf16[80,320]{1,0:T(8,128)(2,1)S(1)} %get-tuple-element.14.order_ref, bf16[256,256]{1,0:T(8,128)(2,1)S(1)} %get-tuple-element.15.chosen_ref, bf16[80,256]{1,0:T(8,128)(2,1)S(1)} %collective-permute-done.3.refs_0_, bf16[80,256]{1,0:T(8,128)(2,1)S(1)} %collective-permute-done.4.refs_1_, ...), custom_call_target="tpu_custom_call" | custom-call | tf_op jit(solution)/shard_map/expand/pallas_call | solution.py:345
Async XLA Ops:
  1.1 3.6 %copy-start = (s32[256]{0:T(256)S(1)}, s32[256]{0:T(256)}, u32[]{:S(2)}) copy-start(s32[256]{0:T(256)} %param.5) | copy-start | bytes 3076
  1.1 5.7 %collective-permute-start = (bf16[48,512]{1,0:T(8,128)(2,1)S(1)}, bf16[48,512]{1,0:T(8,128)(2,1)S(1)}, u32[]{:S(2)}, u32[]{:S(2)}) collective-permute-start(bf16[48,512]{1,0:T(8,128)(2,1)S(1)} %whiten.1.whitened_ref.other_ref), channel_id=1, source_target_pairs={{0,9},{1,8},{2,11},{3,10},{4,13},{5,12},{6,15},{7,14},{8,1},{9,0},... | collective-permute-start | bytes 147464 | tf_op jit(solution)/shard_map/ppermute | solution.py:276
  5.0 2.1 %collective-permute-start.2 = (bf16[48,512]{1,0:T(8,128)(2,1)S(1)}, bf16[48,512]{1,0:T(8,128)(2,1)S(1)}, u32[]{:S(2)}, u32[]{:S(2)}) collective-permute-start(bf16[48,512]{1,0:T(8,128)(2,1)S(1)} %get-tuple-element.16), channel_id=1, source_target_pairs={{0,1},{1,0},{2,3},{3,2},{4,5},{5,4},{6,7},{7,6},{8,9},{9,8},{10,11... | collective-permute-start | bytes 147464 | tf_op jit(solution)/shard_map/ppermute | solution.py:268
  6.8 1.6 %collective-permute-start.1 = (bf16[48,512]{1,0:T(8,128)(2,1)S(1)}, bf16[48,512]{1,0:T(8,128)(2,1)S(1)}, u32[]{:S(2)}, u32[]{:S(2)}) collective-permute-start(bf16[48,512]{1,0:T(8,128)(2,1)S(1)} %collective-permute-done.mine_ref), channel_id=1, source_target_pairs={{0,1},{1,0},{2,3},{3,2},{4,5},{5,4},{6,7},{7,6},{8,9},{9,8},{10,11... | collective-permute-start | bytes 147464 | tf_op jit(solution)/shard_map/ppermute | solution.py:268
  8.9 5.2 %collective-permute-start.3 = (bf16[80,256]{1,0:T(8,128)(2,1)S(1)}, bf16[80,256]{1,0:T(8,128)(2,1)S(1)}, u32[]{:S(2)}, u32[]{:S(2)}) collective-permute-start(bf16[80,256]{1,0:T(8,128)(2,1)S(1)} %get-tuple-element.19), channel_id=1, source_target_pairs={{0,7},{1,6},{2,5},{3,4},{4,3},{5,2},{6,1},{7,0},{8,15},{9,14},{10,... | collective-permute-start | bytes 122888 | tf_op jit(solution)/shard_map/ppermute | solution.py:276
  12.2 3.5 %collective-permute-start.4 = (bf16[80,256]{1,0:T(8,128)(2,1)S(1)}, bf16[80,256]{1,0:T(8,128)(2,1)S(1)}, u32[]{:S(2)}, u32[]{:S(2)}) collective-permute-start(bf16[80,256]{1,0:T(8,128)(2,1)S(1)} %get-tuple-element.20), channel_id=1, source_target_pairs={{0,3},{1,2},{2,1},{3,0},{4,7},{5,6},{6,5},{7,4},{8,11},{9,10},{10,... | collective-permute-start | bytes 122888 | tf_op jit(solution)/shard_map/ppermute | solution.py:276
  12.5 3.4 %collective-permute-start.5 = (bf16[80,256]{1,0:T(8,128)(2,1)S(1)}, bf16[80,256]{1,0:T(8,128)(2,1)S(1)}, u32[]{:S(2)}, u32[]{:S(2)}) collective-permute-start(bf16[80,256]{1,0:T(8,128)(2,1)S(1)} %get-tuple-element.21), channel_id=1, source_target_pairs={{0,5},{1,4},{2,7},{3,6},{4,1},{5,0},{6,3},{7,2},{8,13},{9,12},{10,... | collective-permute-start | bytes 122888 | tf_op jit(solution)/shard_map/ppermute | solution.py:276
  12.6 3.3 %collective-permute-start.6 = (bf16[80,256]{1,0:T(8,128)(2,1)S(1)}, bf16[80,256]{1,0:T(8,128)(2,1)S(1)}, u32[]{:S(2)}, u32[]{:S(2)}) collective-permute-start(bf16[80,256]{1,0:T(8,128)(2,1)S(1)} %get-tuple-element.22), channel_id=1, source_target_pairs={{0,1},{1,0},{2,3},{3,2},{4,5},{5,4},{6,7},{7,6},{8,9},{9,8},{10,11... | collective-permute-start | bytes 122888 | tf_op jit(solution)/shard_map/ppermute | solution.py:276

commit v21 on v20

--- a/solution.py
+++ b/solution.py
@@ -196,11 +196,11 @@
 
 
 def order_matrix(plan):
-    at_row = lax.broadcasted_iota(jnp.int32, (plan.rows, plan.rows), 0)
-    at_part = lax.broadcasted_iota(jnp.int32, (plan.rows, plan.rows), 1)
-    order = jnp.zeros((plan.rows, plan.rows), jnp.bool_)
+    at_row = lax.broadcasted_iota(jnp.int32, (plan.height, plan.rows), 0)
+    at_part = lax.broadcasted_iota(jnp.int32, (plan.height, plan.rows), 1)
+    order = jnp.zeros((plan.height, plan.rows), jnp.bool_)
     for member in range(plan.own):
-        reverse = plan.fine - 1 - (at_row - member * plan.fine)
+        reverse = plan.fine - 1 - (at_row - member * plan.fine_padded)
         whole = (reverse >= 0) & (reverse < plan.whole_groups) & (at_part == member * plan.whole_groups + reverse)
         tail = plan.own * plan.whole_groups + member * plan.rest + reverse - plan.whole_groups
         rest = (reverse >= plan.whole_groups) & (reverse < plan.fine) & (at_part == tail)
@@ -244,13 +244,15 @@
     *arrived_refs, out_hbm, out_ref, sems = refs
     blocks = jnp.concatenate([ref[...] for ref in arrived_refs], axis=0)
     total = jnp.dot(order_ref[...], blocks, preferred_element_type=jnp.float32) * plan.norm_factor
-    expanded = jnp.dot(spread(plan, total), chosen_ref[...], preferred_element_type=jnp.float32)
+    chosen = chosen_ref[...]
     copies = []
     for member in range(plan.own):
+        rows = total[member * plan.fine_padded : (member + 1) * plan.fine_padded]
+        expanded = jnp.dot(spread(plan, rows), chosen, preferred_element_type=jnp.float32)
         for step in range(plan.coarse):
             start = step * plan.fine
             count = min(plan.fine, LAG_COUNT - start)
-            first = step * plan.rows + member * plan.fine
+            first = step * plan.fine_padded
             out_ref[member, start : start + count, :] = expanded[first : first + count]
         copies.append(pltpu.make_async_copy(out_ref.at[member], out_hbm.at[member], sems.at[member]))
         copies[-1].start()
@@ -313,7 +315,7 @@
         "choose",
         (source_index.reshape(1, -1), whitened),
         (
-            jax.ShapeDtypeStruct((plan.rows, plan.targets * plan.rows), jnp.bfloat16),
+            jax.ShapeDtypeStruct((plan.height, plan.targets * plan.rows), jnp.bfloat16),
             jax.ShapeDtypeStruct((LANES, plan.source_count), jnp.bfloat16),
             jax.ShapeDtypeStruct(whitened.shape, whitened.dtype),
         ),

time: 17.3 us -> 17.3 us (level)
  no operation moved by 1% of the time
where the time goes in v21:
time: 17.3 us; the launch traced here: 17.1 us
  starting transfers between devices  8.65 us (50%)
  Pallas kernels  4.27 us (25%)
  waiting for transfers between devices  4.13 us (24%)
    ppermute x5, starting transfers between devices, swap_blk(): return lax.ppermute(array, ('blk', 'src'), pairs)  7.59 us
    ppermute x5, waiting for transfers between devices, swap_blk(): return lax.ppermute(array, ('blk', 'src'), pairs)  4.13 us
    pallas_call x4, Pallas kernels, call(): pl.pallas_call(functools.partial(kernel, plan), out_shape=outputs, in_spe...  1.99 us
    pallas_call x1, Pallas kernels, few_channels(): pl.pallas_call(functools.partial(expand_kernel, plan), out_shape=jax.Shap...  1.18 us
    pallas_call x1, Pallas kernels, few_channels(): pl.pallas_call(functools.partial(whiten_kernel, plan), out_shape=pltpu.VM...  1.1 us
    ppermute x2, starting transfers between devices, swap_cores(): return lax.ppermute(array, 'src', [(0, 1), (1, 0)])  1.06 us
  transfers between devices with their start and end apart: 7, of which 4 were waited for; matrix products, arithmetic and copies ran while one was open for 0% of the time, Pallas kernels for 9%

profile of v21, /device:TPU:0, one launch (start us, length us, event | category | flops | bytes accessed | tf_op | source)
XLA Modules:
  0.0 17.1 jit_solution(5230588075605708305)
XLA Ops:
  0.0 1.1 %whiten.1.whitened_ref.other_ref = bf16[48,512]{1,0:T(8,128)(2,1)S(1)} custom-call(f32[24,2,512]{2,1,0:T(2,128)} %traces_hbm.1, s32[2,24]{1,0:T(2,128)} %bitcast.3), custom_call_target="tpu_custom_call" | custom-call | tf_op jit(solution)/shard_map/whiten/pallas_call | solution.py:280
  1.1 0.0 copy-start
  1.1 3.5 %collective-permute-start = (bf16[48,512]{1,0:T(8,128)(2,1)S(1)}, bf16[48,512]{1,0:T(8,128)(2,1)S(1)}, u32[]{:S(2)}, u32[]{:S(2)}) collective-permute-start(bf16[48,512]{1,0:T(8,128)(2,1)S(1)} %whiten.1.whitened_ref.other_ref), channel_id=1, source_target_pairs={{0,9},{1,8},{2,11},{3,10},{4,13},{5,12},{6,15},{7,14},{8,1},{9,0},... | collective-permute-start | bytes 147464 | tf_op jit(solution)/shard_map/ppermute | solution.py:278
  4.7 0.0 copy-done
  4.7 0.2 %choose.1 = (bf16[96,320]{1,0:T(8,128)(2,1)S(1)}, bf16[256,256]{1,0:T(8,128)(2,1)S(1)}, bf16[48,512]{1,0:T(8,128)(2,1)S(1)}) custom-call(s32[1,256]{1,0:T(1,128)S(1)} %bitcast.2, bf16[48,512]{1,0:T(8,128)(2,1)S(1)} %whiten.1.whitened_ref.other_ref), custom_call_target="tpu_custom_call" | custom-call | tf_op jit(solution)/shard_map/choose/pallas_call | solution.py:302
  4.9 0.7 %collective-permute-start.2 = (bf16[48,512]{1,0:T(8,128)(2,1)S(1)}, bf16[48,512]{1,0:T(8,128)(2,1)S(1)}, u32[]{:S(2)}, u32[]{:S(2)}) collective-permute-start(bf16[48,512]{1,0:T(8,128)(2,1)S(1)} %get-tuple-element.16), channel_id=1, source_target_pairs={{0,1},{1,0},{2,3},{3,2},{4,5},{5,4},{6,7},{7,6},{8,9},{9,8},{10,11... | collective-permute-start | bytes 147464 | tf_op jit(solution)/shard_map/ppermute | solution.py:270
  5.6 1.2 %collective-permute-done.mine_ref = bf16[48,512]{1,0:T(8,128)(2,1)S(1)} collective-permute-done((bf16[48,512]{1,0:T(8,128)(2,1)S(1)}, bf16[48,512]{1,0:T(8,128)(2,1)S(1)}, u32[]{:S(2)}, u32[]{:S(2)}) %collective-permute-start) | collective-permute-done | bytes 49184 | tf_op jit(solution)/shard_map/ppermute | solution.py:278
  6.8 0.3 %collective-permute-start.1 = (bf16[48,512]{1,0:T(8,128)(2,1)S(1)}, bf16[48,512]{1,0:T(8,128)(2,1)S(1)}, u32[]{:S(2)}, u32[]{:S(2)}) collective-permute-start(bf16[48,512]{1,0:T(8,128)(2,1)S(1)} %collective-permute-done.mine_ref), channel_id=1, source_target_pairs={{0,1},{1,0},{2,3},{3,2},{4,5},{5,4},{6,7},{7,6},{8,9},{9,8},{10,11... | collective-permute-start | bytes 147464 | tf_op jit(solution)/shard_map/ppermute | solution.py:270
  7.1 0.0 collective-permute-done.2.mine_ref
  7.1 0.7 %near.1.prior_ref = f32[384,256]{1,0:T(8,128)S(1)} custom-call(bf16[48,512]{1,0:T(8,128)(2,1)S(1)} %collective-permute-done.2.mine_ref, bf16[48,512]{1,0:T(8,128)(2,1)S(1)} %whiten.1.whitened_ref.other_ref), custom_call_target="tpu_custom_call" | custom-call | tf_op jit(solution)/shard_map/near/pallas_call | solution.py:302
  7.8 0.6 %across.1 = (bf16[384,1280]{1,0:T(8,128)(2,1)S(1)}, f32[384,256]{1,0:T(8,128)S(1)}) custom-call(bf16[48,512]{1,0:T(8,128)(2,1)S(1)} %collective-permute-done.mine_ref, f32[384,256]{1,0:T(8,128)S(1)} %near.1.prior_ref), custom_call_target="tpu_custom_call" | custom-call | tf_op jit(solution)/shard_map/across/pallas_call | solution.py:302
  8.4 0.0 collective-permute-done.1.other_ref
  8.4 0.5 %finish.1 = (bf16[80,256]{1,0:T(8,128)(2,1)S(1)}, bf16[80,256]{1,0:T(8,128)(2,1)S(1)}, bf16[80,256]{1,0:T(8,128)(2,1)S(1)}, bf16[80,256]{1,0:T(8,128)(2,1)S(1)}) custom-call(bf16[48,512]{1,0:T(8,128)(2,1)S(1)} %collective-permute-done.1.other_ref, bf16[384,1280]{1,0:T(8,128)(2,1)S(1)} %get-tuple-element.17.toeplitz_ref, ...), custom_call_target="tpu_custom_call" | custom-call | tf_op jit(solution)/shard_map/finish/pallas_call | solution.py:302
  8.9 3.3 %collective-permute-start.3 = (bf16[80,256]{1,0:T(8,128)(2,1)S(1)}, bf16[80,256]{1,0:T(8,128)(2,1)S(1)}, u32[]{:S(2)}, u32[]{:S(2)}) collective-permute-start(bf16[80,256]{1,0:T(8,128)(2,1)S(1)} %get-tuple-element.19), channel_id=1, source_target_pairs={{0,7},{1,6},{2,5},{3,4},{4,3},{5,2},{6,1},{7,0},{8,15},{9,14},{10,... | collective-permute-start | bytes 122888 | tf_op jit(solution)/shard_map/ppermute | solution.py:278
  12.2 0.3 %collective-permute-start.4 = (bf16[80,256]{1,0:T(8,128)(2,1)S(1)}, bf16[80,256]{1,0:T(8,128)(2,1)S(1)}, u32[]{:S(2)}, u32[]{:S(2)}) collective-permute-start(bf16[80,256]{1,0:T(8,128)(2,1)S(1)} %get-tuple-element.20), channel_id=1, source_target_pairs={{0,3},{1,2},{2,1},{3,0},{4,7},{5,6},{6,5},{7,4},{8,11},{9,10},{10,... | collective-permute-start | bytes 122888 | tf_op jit(solution)/shard_map/ppermute | solution.py:278
  12.5 0.1 collective-permute-start.5
  12.6 0.4 %collective-permute-start.6 = (bf16[80,256]{1,0:T(8,128)(2,1)S(1)}, bf16[80,256]{1,0:T(8,128)(2,1)S(1)}, u32[]{:S(2)}, u32[]{:S(2)}) collective-permute-start(bf16[80,256]{1,0:T(8,128)(2,1)S(1)} %get-tuple-element.22), channel_id=1, source_target_pairs={{0,1},{1,0},{2,3},{3,2},{4,5},{5,4},{6,7},{7,6},{8,9},{9,8},{10,11... | collective-permute-start | bytes 122888 | tf_op jit(solution)/shard_map/ppermute | solution.py:278
  13.0 1.1 %collective-permute-done.3.refs_0_ = bf16[80,256]{1,0:T(8,128)(2,1)S(1)} collective-permute-done((bf16[80,256]{1,0:T(8,128)(2,1)S(1)}, bf16[80,256]{1,0:T(8,128)(2,1)S(1)}, u32[]{:S(2)}, u32[]{:S(2)}) %collective-permute-start.3) | collective-permute-done | bytes 40992 | tf_op jit(solution)/shard_map/ppermute | solution.py:278
  14.1 1.6 %collective-permute-done.4.refs_1_ = bf16[80,256]{1,0:T(8,128)(2,1)S(1)} collective-permute-done((bf16[80,256]{1,0:T(8,128)(2,1)S(1)}, bf16[80,256]{1,0:T(8,128)(2,1)S(1)}, u32[]{:S(2)}, u32[]{:S(2)}) %collective-permute-start.4) | collective-permute-done | bytes 40992 | tf_op jit(solution)/shard_map/ppermute | solution.py:278
  15.7 0.2 %collective-permute-done.5.refs_2_ = bf16[80,256]{1,0:T(8,128)(2,1)S(1)} collective-permute-done((bf16[80,256]{1,0:T(8,128)(2,1)S(1)}, bf16[80,256]{1,0:T(8,128)(2,1)S(1)}, u32[]{:S(2)}, u32[]{:S(2)}) %collective-permute-start.5) | collective-permute-done | bytes 40992 | tf_op jit(solution)/shard_map/ppermute | solution.py:278
  15.9 0.0 collective-permute-done.6.refs_3_
  15.9 1.2 %expand.1 = f32[3,129,256]{2,1,0:T(8,128)} custom-call(bf16[96,320]{1,0:T(8,128)(2,1)S(1)} %get-tuple-element.14.order_ref, bf16[256,256]{1,0:T(8,128)(2,1)S(1)} %get-tuple-element.15.chosen_ref, bf16[80,256]{1,0:T(8,128)(2,1)S(1)} %collective-permute-done.3.refs_0_, bf16[80,256]{1,0:T(8,128)(2,1)S(1)} %collective-permute-done.4.refs_1_, ...), custom_call_target="tpu_custom_call" | custom-call | tf_op jit(solution)/shard_map/expand/pallas_call | solution.py:347
Async XLA Ops:
  1.1 3.6 %copy-start = (s32[256]{0:T(256)S(1)}, s32[256]{0:T(256)}, u32[]{:S(2)}) copy-start(s32[256]{0:T(256)} %param.5) | copy-start | bytes 3076
  1.1 5.7 %collective-permute-start = (bf16[48,512]{1,0:T(8,128)(2,1)S(1)}, bf16[48,512]{1,0:T(8,128)(2,1)S(1)}, u32[]{:S(2)}, u32[]{:S(2)}) collective-permute-start(bf16[48,512]{1,0:T(8,128)(2,1)S(1)} %whiten.1.whitened_ref.other_ref), channel_id=1, source_target_pairs={{0,9},{1,8},{2,11},{3,10},{4,13},{5,12},{6,15},{7,14},{8,1},{9,0},... | collective-permute-start | bytes 147464 | tf_op jit(solution)/shard_map/ppermute | solution.py:278
  4.9 2.2 %collective-permute-start.2 = (bf16[48,512]{1,0:T(8,128)(2,1)S(1)}, bf16[48,512]{1,0:T(8,128)(2,1)S(1)}, u32[]{:S(2)}, u32[]{:S(2)}) collective-permute-start(bf16[48,512]{1,0:T(8,128)(2,1)S(1)} %get-tuple-element.16), channel_id=1, source_target_pairs={{0,1},{1,0},{2,3},{3,2},{4,5},{5,4},{6,7},{7,6},{8,9},{9,8},{10,11... | collective-permute-start | bytes 147464 | tf_op jit(solution)/shard_map/ppermute | solution.py:270
  6.8 1.6 %collective-permute-start.1 = (bf16[48,512]{1,0:T(8,128)(2,1)S(1)}, bf16[48,512]{1,0:T(8,128)(2,1)S(1)}, u32[]{:S(2)}, u32[]{:S(2)}) collective-permute-start(bf16[48,512]{1,0:T(8,128)(2,1)S(1)} %collective-permute-done.mine_ref), channel_id=1, source_target_pairs={{0,1},{1,0},{2,3},{3,2},{4,5},{5,4},{6,7},{7,6},{8,9},{9,8},{10,11... | collective-permute-start | bytes 147464 | tf_op jit(solution)/shard_map/ppermute | solution.py:270
  8.9 5.2 %collective-permute-start.3 = (bf16[80,256]{1,0:T(8,128)(2,1)S(1)}, bf16[80,256]{1,0:T(8,128)(2,1)S(1)}, u32[]{:S(2)}, u32[]{:S(2)}) collective-permute-start(bf16[80,256]{1,0:T(8,128)(2,1)S(1)} %get-tuple-element.19), channel_id=1, source_target_pairs={{0,7},{1,6},{2,5},{3,4},{4,3},{5,2},{6,1},{7,0},{8,15},{9,14},{10,... | collective-permute-start | bytes 122888 | tf_op jit(solution)/shard_map/ppermute | solution.py:278
  12.2 3.5 %collective-permute-start.4 = (bf16[80,256]{1,0:T(8,128)(2,1)S(1)}, bf16[80,256]{1,0:T(8,128)(2,1)S(1)}, u32[]{:S(2)}, u32[]{:S(2)}) collective-permute-start(bf16[80,256]{1,0:T(8,128)(2,1)S(1)} %get-tuple-element.20), channel_id=1, source_target_pairs={{0,3},{1,2},{2,1},{3,0},{4,7},{5,6},{6,5},{7,4},{8,11},{9,10},{10,... | collective-permute-start | bytes 122888 | tf_op jit(solution)/shard_map/ppermute | solution.py:278
  12.5 3.4 %collective-permute-start.5 = (bf16[80,256]{1,0:T(8,128)(2,1)S(1)}, bf16[80,256]{1,0:T(8,128)(2,1)S(1)}, u32[]{:S(2)}, u32[]{:S(2)}) collective-permute-start(bf16[80,256]{1,0:T(8,128)(2,1)S(1)} %get-tuple-element.21), channel_id=1, source_target_pairs={{0,5},{1,4},{2,7},{3,6},{4,1},{5,0},{6,3},{7,2},{8,13},{9,12},{10,... | collective-permute-start | bytes 122888 | tf_op jit(solution)/shard_map/ppermute | solution.py:278
  12.6 3.3 %collective-permute-start.6 = (bf16[80,256]{1,0:T(8,128)(2,1)S(1)}, bf16[80,256]{1,0:T(8,128)(2,1)S(1)}, u32[]{:S(2)}, u32[]{:S(2)}) collective-permute-start(bf16[80,256]{1,0:T(8,128)(2,1)S(1)} %get-tuple-element.22), channel_id=1, source_target_pairs={{0,1},{1,0},{2,3},{3,2},{4,5},{5,4},{6,7},{7,6},{8,9},{9,8},{10,11... | collective-permute-start | bytes 122888 | tf_op jit(solution)/shard_map/ppermute | solution.py:278

commit v22 on v21

--- a/solution.py
+++ b/solution.py
@@ -11,6 +11,9 @@
 MAXLAG = 64
 LAG_COUNT = 2 * MAXLAG + 1
 LANES = 256
+IN_PARTS = 4
+OUT_PARTS = 4
+OUT_ROWS = 32
 GROUP = 8
 HOPS = (3, 1, 2, 0)
 
@@ -103,10 +106,11 @@
 
 
 def whiten_kernel(plan, traces_hbm, flags_hbm, out_ref, traces_ref, flags_ref, sems):
-    copies = [
-        pltpu.make_async_copy(traces_hbm, traces_ref, sems.at[0]),
-        pltpu.make_async_copy(flags_hbm, flags_ref, sems.at[1]),
-    ]
+    part = plan.half // IN_PARTS
+    copies = [pltpu.make_async_copy(flags_hbm, flags_ref, sems.at[IN_PARTS])]
+    for index in range(IN_PARTS):
+        at = pl.ds(index * part, part)
+        copies.append(pltpu.make_async_copy(traces_hbm.at[at], traces_ref.at[at], sems.at[index]))
     for copy in copies:
         copy.start()
     for copy in copies:
@@ -254,8 +258,12 @@
             count = min(plan.fine, LAG_COUNT - start)
             first = step * plan.fine_padded
             out_ref[member, start : start + count, :] = expanded[first : first + count]
-        copies.append(pltpu.make_async_copy(out_ref.at[member], out_hbm.at[member], sems.at[member]))
-        copies[-1].start()
+        for part in range(OUT_PARTS):
+            start = part * OUT_ROWS
+            count = OUT_ROWS if part + 1 < OUT_PARTS else LAG_COUNT - start
+            at = (member, pl.ds(start, count))
+            copies.append(pltpu.make_async_copy(out_ref.at[at], out_hbm.at[at], sems.at[member, part]))
+            copies[-1].start()
     for copy in copies:
         copy.wait()
 
@@ -285,7 +293,7 @@
         scratch_shapes=[
             pltpu.VMEM(traces.shape, jnp.float32),
             pltpu.VMEM(flags.shape, jnp.int32),
-            pltpu.SemaphoreType.DMA((2,)),
+            pltpu.SemaphoreType.DMA((IN_PARTS + 1,)),
         ],
         compiler_params=pltpu.CompilerParams(vmem_limit_bytes=60 * 1024 * 1024),
         name="whiten",
@@ -349,7 +357,7 @@
         out_shape=jax.ShapeDtypeStruct(out_shape, jnp.float32),
         in_specs=[vmem] * (2 + len(arrived)),
         out_specs=pl.BlockSpec(memory_space=pl.ANY),
-        scratch_shapes=[pltpu.VMEM(out_shape, jnp.float32), pltpu.SemaphoreType.DMA((plan.own,))],
+        scratch_shapes=[pltpu.VMEM(out_shape, jnp.float32), pltpu.SemaphoreType.DMA((plan.own, OUT_PARTS))],
         compiler_params=params,
         name="expand",
     )(order, chosen, *arrived)

time: 17.3 us -> 17.3 us (level)
  no operation moved by 1% of the time
where the time goes in v22:
time: 17.3 us; the launch traced here: 17.1 us
  starting transfers between devices  8.65 us (50%)
  Pallas kernels  4.28 us (25%)
  waiting for transfers between devices  4.13 us (24%)
    ppermute x5, starting transfers between devices, swap_blk(): return lax.ppermute(array, ('blk', 'src'), pairs)  7.59 us
    ppermute x5, waiting for transfers between devices, swap_blk(): return lax.ppermute(array, ('blk', 'src'), pairs)  4.13 us
    pallas_call x4, Pallas kernels, call(): pl.pallas_call(functools.partial(kernel, plan), out_shape=outputs, in_spe...  1.99 us
    pallas_call x1, Pallas kernels, few_channels(): pl.pallas_call(functools.partial(expand_kernel, plan), out_shape=jax.Shap...  1.25 us
    ppermute x2, starting transfers between devices, swap_cores(): return lax.ppermute(array, 'src', [(0, 1), (1, 0)])  1.06 us
    pallas_call x1, Pallas kernels, few_channels(): pl.pallas_call(functools.partial(whiten_kernel, plan), out_shape=pltpu.VM...  1.04 us
  transfers between devices with their start and end apart: 7, of which 4 were waited for; matrix products, arithmetic and copies ran while one was open for 0% of the time, Pallas kernels for 9%

profile of v22, /device:TPU:0, one launch (start us, length us, event | category | flops | bytes accessed | tf_op | source)
XLA Modules:
  0.0 17.1 jit_solution(14292466976875751385)
XLA Ops:
  0.0 1.0 %whiten.1.whitened_ref.other_ref = bf16[48,512]{1,0:T(8,128)(2,1)S(1)} custom-call(f32[24,2,512]{2,1,0:T(2,128)} %traces_hbm.1, s32[2,24]{1,0:T(2,128)} %bitcast.3), custom_call_target="tpu_custom_call" | custom-call | tf_op jit(solution)/shard_map/whiten/pallas_call | solution.py:288
  1.1 0.0 copy-start
  1.1 3.5 %collective-permute-start = (bf16[48,512]{1,0:T(8,128)(2,1)S(1)}, bf16[48,512]{1,0:T(8,128)(2,1)S(1)}, u32[]{:S(2)}, u32[]{:S(2)}) collective-permute-start(bf16[48,512]{1,0:T(8,128)(2,1)S(1)} %whiten.1.whitened_ref.other_ref), channel_id=1, source_target_pairs={{0,9},{1,8},{2,11},{3,10},{4,13},{5,12},{6,15},{7,14},{8,1},{9,0},... | collective-permute-start | bytes 147464 | tf_op jit(solution)/shard_map/ppermute | solution.py:286
  4.6 0.0 copy-done
  4.6 0.2 %choose.1 = (bf16[96,320]{1,0:T(8,128)(2,1)S(1)}, bf16[256,256]{1,0:T(8,128)(2,1)S(1)}, bf16[48,512]{1,0:T(8,128)(2,1)S(1)}) custom-call(s32[1,256]{1,0:T(1,128)S(1)} %bitcast.2, bf16[48,512]{1,0:T(8,128)(2,1)S(1)} %whiten.1.whitened_ref.other_ref), custom_call_target="tpu_custom_call" | custom-call | tf_op jit(solution)/shard_map/choose/pallas_call | solution.py:310
  4.8 0.7 %collective-permute-start.2 = (bf16[48,512]{1,0:T(8,128)(2,1)S(1)}, bf16[48,512]{1,0:T(8,128)(2,1)S(1)}, u32[]{:S(2)}, u32[]{:S(2)}) collective-permute-start(bf16[48,512]{1,0:T(8,128)(2,1)S(1)} %get-tuple-element.16), channel_id=1, source_target_pairs={{0,1},{1,0},{2,3},{3,2},{4,5},{5,4},{6,7},{7,6},{8,9},{9,8},{10,11... | collective-permute-start | bytes 147464 | tf_op jit(solution)/shard_map/ppermute | solution.py:278
  5.6 1.2 %collective-permute-done.mine_ref = bf16[48,512]{1,0:T(8,128)(2,1)S(1)} collective-permute-done((bf16[48,512]{1,0:T(8,128)(2,1)S(1)}, bf16[48,512]{1,0:T(8,128)(2,1)S(1)}, u32[]{:S(2)}, u32[]{:S(2)}) %collective-permute-start) | collective-permute-done | bytes 49184 | tf_op jit(solution)/shard_map/ppermute | solution.py:286
  6.7 0.3 %collective-permute-start.1 = (bf16[48,512]{1,0:T(8,128)(2,1)S(1)}, bf16[48,512]{1,0:T(8,128)(2,1)S(1)}, u32[]{:S(2)}, u32[]{:S(2)}) collective-permute-start(bf16[48,512]{1,0:T(8,128)(2,1)S(1)} %collective-permute-done.mine_ref), channel_id=1, source_target_pairs={{0,1},{1,0},{2,3},{3,2},{4,5},{5,4},{6,7},{7,6},{8,9},{9,8},{10,11... | collective-permute-start | bytes 147464 | tf_op jit(solution)/shard_map/ppermute | solution.py:278
  7.1 0.0 collective-permute-done.2.mine_ref
  7.1 0.7 %near.1.prior_ref = f32[384,256]{1,0:T(8,128)S(1)} custom-call(bf16[48,512]{1,0:T(8,128)(2,1)S(1)} %collective-permute-done.2.mine_ref, bf16[48,512]{1,0:T(8,128)(2,1)S(1)} %whiten.1.whitened_ref.other_ref), custom_call_target="tpu_custom_call" | custom-call | tf_op jit(solution)/shard_map/near/pallas_call | solution.py:310
  7.8 0.6 %across.1 = (bf16[384,1280]{1,0:T(8,128)(2,1)S(1)}, f32[384,256]{1,0:T(8,128)S(1)}) custom-call(bf16[48,512]{1,0:T(8,128)(2,1)S(1)} %collective-permute-done.mine_ref, f32[384,256]{1,0:T(8,128)S(1)} %near.1.prior_ref), custom_call_target="tpu_custom_call" | custom-call | tf_op jit(solution)/shard_map/across/pallas_call | solution.py:310
  8.3 0.0 collective-permute-done.1.other_ref
  8.3 0.5 %finish.1 = (bf16[80,256]{1,0:T(8,128)(2,1)S(1)}, bf16[80,256]{1,0:T(8,128)(2,1)S(1)}, bf16[80,256]{1,0:T(8,128)(2,1)S(1)}, bf16[80,256]{1,0:T(8,128)(2,1)S(1)}) custom-call(bf16[48,512]{1,0:T(8,128)(2,1)S(1)} %collective-permute-done.1.other_ref, bf16[384,1280]{1,0:T(8,128)(2,1)S(1)} %get-tuple-element.17.toeplitz_ref, ...), custom_call_target="tpu_custom_call" | custom-call | tf_op jit(solution)/shard_map/finish/pallas_call | solution.py:310
  8.8 3.3 %collective-permute-start.3 = (bf16[80,256]{1,0:T(8,128)(2,1)S(1)}, bf16[80,256]{1,0:T(8,128)(2,1)S(1)}, u32[]{:S(2)}, u32[]{:S(2)}) collective-permute-start(bf16[80,256]{1,0:T(8,128)(2,1)S(1)} %get-tuple-element.19), channel_id=1, source_target_pairs={{0,7},{1,6},{2,5},{3,4},{4,3},{5,2},{6,1},{7,0},{8,15},{9,14},{10,... | collective-permute-start | bytes 122888 | tf_op jit(solution)/shard_map/ppermute | solution.py:286
  12.1 0.3 %collective-permute-start.4 = (bf16[80,256]{1,0:T(8,128)(2,1)S(1)}, bf16[80,256]{1,0:T(8,128)(2,1)S(1)}, u32[]{:S(2)}, u32[]{:S(2)}) collective-permute-start(bf16[80,256]{1,0:T(8,128)(2,1)S(1)} %get-tuple-element.20), channel_id=1, source_target_pairs={{0,3},{1,2},{2,1},{3,0},{4,7},{5,6},{6,5},{7,4},{8,11},{9,10},{10,... | collective-permute-start | bytes 122888 | tf_op jit(solution)/shard_map/ppermute | solution.py:286
  12.4 0.1 collective-permute-start.5
  12.5 0.4 %collective-permute-start.6 = (bf16[80,256]{1,0:T(8,128)(2,1)S(1)}, bf16[80,256]{1,0:T(8,128)(2,1)S(1)}, u32[]{:S(2)}, u32[]{:S(2)}) collective-permute-start(bf16[80,256]{1,0:T(8,128)(2,1)S(1)} %get-tuple-element.22), channel_id=1, source_target_pairs={{0,1},{1,0},{2,3},{3,2},{4,5},{5,4},{6,7},{7,6},{8,9},{9,8},{10,11... | collective-permute-start | bytes 122888 | tf_op jit(solution)/shard_map/ppermute | solution.py:286
  12.9 1.1 %collective-permute-done.3.refs_0_ = bf16[80,256]{1,0:T(8,128)(2,1)S(1)} collective-permute-done((bf16[80,256]{1,0:T(8,128)(2,1)S(1)}, bf16[80,256]{1,0:T(8,128)(2,1)S(1)}, u32[]{:S(2)}, u32[]{:S(2)}) %collective-permute-start.3) | collective-permute-done | bytes 40992 | tf_op jit(solution)/shard_map/ppermute | solution.py:286
  14.0 1.6 %collective-permute-done.4.refs_1_ = bf16[80,256]{1,0:T(8,128)(2,1)S(1)} collective-permute-done((bf16[80,256]{1,0:T(8,128)(2,1)S(1)}, bf16[80,256]{1,0:T(8,128)(2,1)S(1)}, u32[]{:S(2)}, u32[]{:S(2)}) %collective-permute-start.4) | collective-permute-done | bytes 40992 | tf_op jit(solution)/shard_map/ppermute | solution.py:286
  15.7 0.2 %collective-permute-done.5.refs_2_ = bf16[80,256]{1,0:T(8,128)(2,1)S(1)} collective-permute-done((bf16[80,256]{1,0:T(8,128)(2,1)S(1)}, bf16[80,256]{1,0:T(8,128)(2,1)S(1)}, u32[]{:S(2)}, u32[]{:S(2)}) %collective-permute-start.5) | collective-permute-done | bytes 40992 | tf_op jit(solution)/shard_map/ppermute | solution.py:286
  15.9 0.0 collective-permute-done.6.refs_3_
  15.9 1.2 %expand.1 = f32[3,129,256]{2,1,0:T(8,128)} custom-call(bf16[96,320]{1,0:T(8,128)(2,1)S(1)} %get-tuple-element.14.order_ref, bf16[256,256]{1,0:T(8,128)(2,1)S(1)} %get-tuple-element.15.chosen_ref, bf16[80,256]{1,0:T(8,128)(2,1)S(1)} %collective-permute-done.3.refs_0_, bf16[80,256]{1,0:T(8,128)(2,1)S(1)} %collective-permute-done.4.refs_1_, ...), custom_call_target="tpu_custom_call" | custom-call | tf_op jit(solution)/shard_map/expand/pallas_call | solution.py:355
Async XLA Ops:
  1.1 3.6 %copy-start = (s32[256]{0:T(256)S(1)}, s32[256]{0:T(256)}, u32[]{:S(2)}) copy-start(s32[256]{0:T(256)} %param.5) | copy-start | bytes 3076
  1.1 5.7 %collective-permute-start = (bf16[48,512]{1,0:T(8,128)(2,1)S(1)}, bf16[48,512]{1,0:T(8,128)(2,1)S(1)}, u32[]{:S(2)}, u32[]{:S(2)}) collective-permute-start(bf16[48,512]{1,0:T(8,128)(2,1)S(1)} %whiten.1.whitened_ref.other_ref), channel_id=1, source_target_pairs={{0,9},{1,8},{2,11},{3,10},{4,13},{5,12},{6,15},{7,14},{8,1},{9,0},... | collective-permute-start | bytes 147464 | tf_op jit(solution)/shard_map/ppermute | solution.py:286
  4.8 2.2 %collective-permute-start.2 = (bf16[48,512]{1,0:T(8,128)(2,1)S(1)}, bf16[48,512]{1,0:T(8,128)(2,1)S(1)}, u32[]{:S(2)}, u32[]{:S(2)}) collective-permute-start(bf16[48,512]{1,0:T(8,128)(2,1)S(1)} %get-tuple-element.16), channel_id=1, source_target_pairs={{0,1},{1,0},{2,3},{3,2},{4,5},{5,4},{6,7},{7,6},{8,9},{9,8},{10,11... | collective-permute-start | bytes 147464 | tf_op jit(solution)/shard_map/ppermute | solution.py:278
  6.7 1.6 %collective-permute-start.1 = (bf16[48,512]{1,0:T(8,128)(2,1)S(1)}, bf16[48,512]{1,0:T(8,128)(2,1)S(1)}, u32[]{:S(2)}, u32[]{:S(2)}) collective-permute-start(bf16[48,512]{1,0:T(8,128)(2,1)S(1)} %collective-permute-done.mine_ref), channel_id=1, source_target_pairs={{0,1},{1,0},{2,3},{3,2},{4,5},{5,4},{6,7},{7,6},{8,9},{9,8},{10,11... | collective-permute-start | bytes 147464 | tf_op jit(solution)/shard_map/ppermute | solution.py:278
  8.8 5.2 %collective-permute-start.3 = (bf16[80,256]{1,0:T(8,128)(2,1)S(1)}, bf16[80,256]{1,0:T(8,128)(2,1)S(1)}, u32[]{:S(2)}, u32[]{:S(2)}) collective-permute-start(bf16[80,256]{1,0:T(8,128)(2,1)S(1)} %get-tuple-element.19), channel_id=1, source_target_pairs={{0,7},{1,6},{2,5},{3,4},{4,3},{5,2},{6,1},{7,0},{8,15},{9,14},{10,... | collective-permute-start | bytes 122888 | tf_op jit(solution)/shard_map/ppermute | solution.py:286
  12.1 3.5 %collective-permute-start.4 = (bf16[80,256]{1,0:T(8,128)(2,1)S(1)}, bf16[80,256]{1,0:T(8,128)(2,1)S(1)}, u32[]{:S(2)}, u32[]{:S(2)}) collective-permute-start(bf16[80,256]{1,0:T(8,128)(2,1)S(1)} %get-tuple-element.20), channel_id=1, source_target_pairs={{0,3},{1,2},{2,1},{3,0},{4,7},{5,6},{6,5},{7,4},{8,11},{9,10},{10,... | collective-permute-start | bytes 122888 | tf_op jit(solution)/shard_map/ppermute | solution.py:286
  12.4 3.4 %collective-permute-start.5 = (bf16[80,256]{1,0:T(8,128)(2,1)S(1)}, bf16[80,256]{1,0:T(8,128)(2,1)S(1)}, u32[]{:S(2)}, u32[]{:S(2)}) collective-permute-start(bf16[80,256]{1,0:T(8,128)(2,1)S(1)} %get-tuple-element.21), channel_id=1, source_target_pairs={{0,5},{1,4},{2,7},{3,6},{4,1},{5,0},{6,3},{7,2},{8,13},{9,12},{10,... | collective-permute-start | bytes 122888 | tf_op jit(solution)/shard_map/ppermute | solution.py:286
  12.5 3.3 %collective-permute-start.6 = (bf16[80,256]{1,0:T(8,128)(2,1)S(1)}, bf16[80,256]{1,0:T(8,128)(2,1)S(1)}, u32[]{:S(2)}, u32[]{:S(2)}) collective-permute-start(bf16[80,256]{1,0:T(8,128)(2,1)S(1)} %get-tuple-element.22), channel_id=1, source_target_pairs={{0,1},{1,0},{2,3},{3,2},{4,5},{5,4},{6,7},{7,6},{8,9},{9,8},{10,11... | collective-permute-start | bytes 122888 | tf_op jit(solution)/shard_map/ppermute | solution.py:286

commit v23 on v22

--- a/solution.py
+++ b/solution.py
@@ -12,8 +12,6 @@
 LAG_COUNT = 2 * MAXLAG + 1
 LANES = 256
 IN_PARTS = 4
-OUT_PARTS = 4
-OUT_ROWS = 32
 GROUP = 8
 HOPS = (3, 1, 2, 0)
 
@@ -166,8 +164,10 @@
     )
 
 
-def near_kernel(plan, mine_ref, other_ref, sum_ref, rows_ref, toeplitz_ref, columns_ref):
-    rows_ref[...] = mine_ref[...].astype(jnp.float32)
+def near_kernel(plan, *refs):
+    mine_refs, (other_ref, sum_ref, rows_ref, toeplitz_ref, columns_ref) = refs[: plan.windows], refs[plan.windows :]
+    for window, mine_ref in enumerate(mine_refs):
+        rows_ref[window * plan.half : (window + 1) * plan.half, :] = mine_ref[...].astype(jnp.float32)
     lag_rows(plan, rows_ref, toeplitz_ref)
     fill_columns(plan, rows_ref[...], columns_ref.at[: plan.half_lanes])
     fill_columns(plan, other_ref[...].astype(jnp.float32), columns_ref.at[plan.half_lanes :])
@@ -228,8 +228,10 @@
     return jnp.concatenate(pieces, axis=0)
 
 
-def choose_kernel(plan, index_ref, whitened_ref, order_ref, chosen_ref, same_ref):
-    same_ref[...] = whitened_ref[...]
+def choose_kernel(plan, index_ref, whitened_ref, order_ref, chosen_ref, *same_refs):
+    whitened = whitened_ref[...].astype(jnp.float32)
+    for window, same_ref in enumerate(same_refs):
+        same_ref[...] = whitened[window * plan.half : (window + 1) * plan.half].astype(jnp.bfloat16)
     first = lax.axis_index("src") * plan.half
     index = index_ref[...] - first
     index = jnp.where(index < 0, index + plan.channels, index)
@@ -258,12 +260,8 @@
             count = min(plan.fine, LAG_COUNT - start)
             first = step * plan.fine_padded
             out_ref[member, start : start + count, :] = expanded[first : first + count]
-        for part in range(OUT_PARTS):
-            start = part * OUT_ROWS
-            count = OUT_ROWS if part + 1 < OUT_PARTS else LAG_COUNT - start
-            at = (member, pl.ds(start, count))
-            copies.append(pltpu.make_async_copy(out_ref.at[at], out_hbm.at[at], sems.at[member, part]))
-            copies[-1].start()
+        copies.append(pltpu.make_async_copy(out_ref.at[member], out_hbm.at[member], sems.at[member]))
+        copies[-1].start()
     for copy in copies:
         copy.wait()
 
@@ -318,23 +316,24 @@
         )(*operands)
 
     across = swap_blk(whitened, plan.targets)
-    order, chosen, same = call(
+    order, chosen, *same = call(
         choose_kernel,
         "choose",
         (source_index.reshape(1, -1), whitened),
         (
             jax.ShapeDtypeStruct((plan.height, plan.targets * plan.rows), jnp.bfloat16),
             jax.ShapeDtypeStruct((LANES, plan.source_count), jnp.bfloat16),
-            jax.ShapeDtypeStruct(whitened.shape, whitened.dtype),
+            *[jax.ShapeDtypeStruct((plan.half, plan.segment), whitened.dtype)] * plan.windows,
         ),
     )
     (total,) = call(
         near_kernel,
         "near",
-        (swap_cores(same), whitened),
+        (*[swap_cores(array) for array in same], whitened),
         (sums,),
         (rows, pltpu.VMEM(toeplitz, jnp.bfloat16), pltpu.VMEM((LANES, width), jnp.bfloat16)),
     )
+    across, total = lax.optimization_barrier((across, total))
     across_other = swap_cores(across)
     lagged, total = call(
         across_kernel,
@@ -357,7 +356,7 @@
         out_shape=jax.ShapeDtypeStruct(out_shape, jnp.float32),
         in_specs=[vmem] * (2 + len(arrived)),
         out_specs=pl.BlockSpec(memory_space=pl.ANY),
-        scratch_shapes=[pltpu.VMEM(out_shape, jnp.float32), pltpu.SemaphoreType.DMA((plan.own, OUT_PARTS))],
+        scratch_shapes=[pltpu.VMEM(out_shape, jnp.float32), pltpu.SemaphoreType.DMA((plan.own,))],
         compiler_params=params,
         name="expand",
     )(order, chosen, *arrived)

time: 17.3 us -> 17.1 us (0.988)
  starting transfers between devices: 8.65 us -> 7.98 us
  waiting for transfers between devices: 4.13 us -> 4.67 us
    ppermute x2 -> x3, waiting for transfers between devices: 0.01 us -> 1.6 us  [swap_cores(): return lax.ppermute(array, 'src', [(0, 1), (1, 0)])]
    ppermute x5, waiting for transfers between devices: 4.13 us -> 3.07 us  [swap_blk(): return lax.ppermute(array, ('blk', 'src'), pairs)]
    ppermute x5, starting transfers between devices: 7.59 us -> 6.93 us  [swap_blk(): return lax.ppermute(array, ('blk', 'src'), pairs)]
    ppermute x2 -> x3, starting transfers between devices: 1.06 us -> 1.05 us  [swap_cores(): return lax.ppermute(array, 'src', [(0, 1), (1, 0)])]
  transfers between devices with their start and end apart: 7 -> 8, of which waited for: 4 -> 6; matrix products, arithmetic and copies ran while one was open for 0% -> 0% of each run, Pallas kernels for 9% -> 9%
where the time goes in v23:
time: 17.1 us; the launch traced here: 16.9 us
  starting transfers between devices  7.98 us (47%)
  waiting for transfers between devices  4.67 us (27%)
  Pallas kernels  4.21 us (25%)
    ppermute x5, starting transfers between devices, swap_blk(): return lax.ppermute(array, ('blk', 'src'), pairs)  6.93 us
    ppermute x5, waiting for transfers between devices, swap_blk(): return lax.ppermute(array, ('blk', 'src'), pairs)  3.07 us
    pallas_call x4, Pallas kernels, call(): pl.pallas_call(functools.partial(kernel, plan), out_shape=outputs, in_spe...  1.99 us
    ppermute x3, waiting for transfers between devices, swap_cores(): return lax.ppermute(array, 'src', [(0, 1), (1, 0)])  1.6 us
    pallas_call x1, Pallas kernels, few_channels(): pl.pallas_call(functools.partial(expand_kernel, plan), out_shape=jax.Shap...  1.18 us
    ppermute x3, starting transfers between devices, swap_cores(): return lax.ppermute(array, 'src', [(0, 1), (1, 0)])  1.05 us
    pallas_call x1, Pallas kernels, few_channels(): pl.pallas_call(functools.partial(whiten_kernel, plan), out_shape=pltpu.VM...  1.04 us
  transfers between devices with their start and end apart: 8, of which 6 were waited for; matrix products, arithmetic and copies ran while one was open for 0% of the time, Pallas kernels for 9%

profile of v23, /device:TPU:0, one launch (start us, length us, event | category | flops | bytes accessed | tf_op | source)
XLA Modules:
  0.0 16.9 jit_solution(4539427921785155914)
XLA Ops:
  0.0 1.0 %whiten.1.whitened_ref.refs_2_ = bf16[48,512]{1,0:T(8,128)(2,1)S(1)} custom-call(f32[24,2,512]{2,1,0:T(2,128)} %traces_hbm.1, s32[2,24]{1,0:T(2,128)} %bitcast.3), custom_call_target="tpu_custom_call" | custom-call | tf_op jit(solution)/shard_map/whiten/pallas_call | solution.py:286
  1.1 0.0 copy-start
  1.1 3.5 %collective-permute-start = (bf16[48,512]{1,0:T(8,128)(2,1)S(1)}, bf16[48,512]{1,0:T(8,128)(2,1)S(1)}, u32[]{:S(2)}, u32[]{:S(2)}) collective-permute-start(bf16[48,512]{1,0:T(8,128)(2,1)S(1)} %whiten.1.whitened_ref.refs_2_), channel_id=1, source_target_pairs={{0,9},{1,8},{2,11},{3,10},{4,13},{5,12},{6,15},{7,14},{8,1},{9,0},... | collective-permute-start | bytes 147464 | tf_op jit(solution)/shard_map/ppermute | solution.py:284
  4.6 0.0 copy-done
  4.6 0.2 %choose.1 = (bf16[96,320]{1,0:T(8,128)(2,1)S(1)}, bf16[256,256]{1,0:T(8,128)(2,1)S(1)}, bf16[24,512]{1,0:T(8,128)(2,1)S(1)}, bf16[24,512]{1,0:T(8,128)(2,1)S(1)}) custom-call(s32[1,256]{1,0:T(1,128)S(1)} %bitcast.2, bf16[48,512]{1,0:T(8,128)(2,1)S(1)} %whiten.1.whitened_ref.refs_2_), custom_call_target="tpu_custom_call" | custom-call | tf_op jit(solution)/shard_map/choose/pallas_call | solution.py:308
  4.8 0.7 %collective-permute-start.1 = (bf16[24,512]{1,0:T(8,128)(2,1)S(1)}, bf16[24,512]{1,0:T(8,128)(2,1)S(1)}, u32[]{:S(2)}, u32[]{:S(2)}) collective-permute-start(bf16[24,512]{1,0:T(8,128)(2,1)S(1)} %get-tuple-element.19), channel_id=1, source_target_pairs={{0,1},{1,0},{2,3},{3,2},{4,5},{5,4},{6,7},{7,6},{8,9},{9,8},{10,11... | collective-permute-start | bytes 73736 | tf_op jit(solution)/shard_map/ppermute | solution.py:276
  5.6 0.1 collective-permute-start.2
  5.7 0.8 %collective-permute-done.1.refs_0_ = bf16[24,512]{1,0:T(8,128)(2,1)S(1)} collective-permute-done((bf16[24,512]{1,0:T(8,128)(2,1)S(1)}, bf16[24,512]{1,0:T(8,128)(2,1)S(1)}, u32[]{:S(2)}, u32[]{:S(2)}) %collective-permute-start.1) | collective-permute-done | bytes 24608 | tf_op jit(solution)/shard_map/ppermute | solution.py:276
  6.4 0.3 %collective-permute-done.2.refs_1_ = bf16[24,512]{1,0:T(8,128)(2,1)S(1)} collective-permute-done((bf16[24,512]{1,0:T(8,128)(2,1)S(1)}, bf16[24,512]{1,0:T(8,128)(2,1)S(1)}, u32[]{:S(2)}, u32[]{:S(2)}) %collective-permute-start.2) | collective-permute-done | bytes 24608 | tf_op jit(solution)/shard_map/ppermute | solution.py:276
  6.8 0.7 %near.1.prior_ref = f32[384,256]{1,0:T(8,128)S(1)} custom-call(bf16[24,512]{1,0:T(8,128)(2,1)S(1)} %collective-permute-done.1.refs_0_, bf16[24,512]{1,0:T(8,128)(2,1)S(1)} %collective-permute-done.2.refs_1_, bf16[48,512]{1,0:T(8,128)(2,1)S(1)} %whiten.1.whitened_ref.refs_2_), custom_call_target="tpu_custom_call" | custom-call | tf_op jit(solution)/shard_map/near/pallas_call | solution.py:308
  7.5 0.0 collective-permute-done.mine_ref
  7.5 0.2 %collective-permute-start.3 = (bf16[48,512]{1,0:T(8,128)(2,1)S(1)}, bf16[48,512]{1,0:T(8,128)(2,1)S(1)}, u32[]{:S(2)}, u32[]{:S(2)}) collective-permute-start(bf16[48,512]{1,0:T(8,128)(2,1)S(1)} %collective-permute-done.mine_ref), channel_id=1, source_target_pairs={{0,1},{1,0},{2,3},{3,2},{4,5},{5,4},{6,7},{7,6},{8,9},{9,8},{10,11... | collective-permute-start | bytes 147464 | tf_op jit(solution)/shard_map/ppermute | solution.py:276
  7.7 0.6 %across.1 = (bf16[384,1280]{1,0:T(8,128)(2,1)S(1)}, f32[384,256]{1,0:T(8,128)S(1)}) custom-call(bf16[48,512]{1,0:T(8,128)(2,1)S(1)} %collective-permute-done.mine_ref, f32[384,256]{1,0:T(8,128)S(1)} %near.1.prior_ref), custom_call_target="tpu_custom_call" | custom-call | tf_op jit(solution)/shard_map/across/pallas_call | solution.py:308
  8.3 0.5 %collective-permute-done.3.other_ref = bf16[48,512]{1,0:T(8,128)(2,1)S(1)} collective-permute-done((bf16[48,512]{1,0:T(8,128)(2,1)S(1)}, bf16[48,512]{1,0:T(8,128)(2,1)S(1)}, u32[]{:S(2)}, u32[]{:S(2)}) %collective-permute-start.3) | collective-permute-done | bytes 49184 | tf_op jit(solution)/shard_map/ppermute | solution.py:276
  8.8 0.5 %finish.1 = (bf16[80,256]{1,0:T(8,128)(2,1)S(1)}, bf16[80,256]{1,0:T(8,128)(2,1)S(1)}, bf16[80,256]{1,0:T(8,128)(2,1)S(1)}, bf16[80,256]{1,0:T(8,128)(2,1)S(1)}) custom-call(bf16[48,512]{1,0:T(8,128)(2,1)S(1)} %collective-permute-done.3.other_ref, bf16[384,1280]{1,0:T(8,128)(2,1)S(1)} %get-tuple-element.23.toeplitz_ref, ...), custom_call_target="tpu_custom_call" | custom-call | tf_op jit(solution)/shard_map/finish/pallas_call | solution.py:308
  9.3 2.4 %collective-permute-start.4 = (bf16[80,256]{1,0:T(8,128)(2,1)S(1)}, bf16[80,256]{1,0:T(8,128)(2,1)S(1)}, u32[]{:S(2)}, u32[]{:S(2)}) collective-permute-start(bf16[80,256]{1,0:T(8,128)(2,1)S(1)} %get-tuple-element.25), channel_id=1, source_target_pairs={{0,7},{1,6},{2,5},{3,4},{4,3},{5,2},{6,1},{7,0},{8,15},{9,14},{10,... | collective-permute-start | bytes 122888 | tf_op jit(solution)/shard_map/ppermute | solution.py:284
  11.7 0.5 %collective-permute-start.5 = (bf16[80,256]{1,0:T(8,128)(2,1)S(1)}, bf16[80,256]{1,0:T(8,128)(2,1)S(1)}, u32[]{:S(2)}, u32[]{:S(2)}) collective-permute-start(bf16[80,256]{1,0:T(8,128)(2,1)S(1)} %get-tuple-element.26), channel_id=1, source_target_pairs={{0,3},{1,2},{2,1},{3,0},{4,7},{5,6},{6,5},{7,4},{8,11},{9,10},{10,... | collective-permute-start | bytes 122888 | tf_op jit(solution)/shard_map/ppermute | solution.py:284
  12.2 0.1 collective-permute-start.6
  12.3 0.3 %collective-permute-start.7 = (bf16[80,256]{1,0:T(8,128)(2,1)S(1)}, bf16[80,256]{1,0:T(8,128)(2,1)S(1)}, u32[]{:S(2)}, u32[]{:S(2)}) collective-permute-start(bf16[80,256]{1,0:T(8,128)(2,1)S(1)} %get-tuple-element.28), channel_id=1, source_target_pairs={{0,1},{1,0},{2,3},{3,2},{4,5},{5,4},{6,7},{7,6},{8,9},{9,8},{10,11... | collective-permute-start | bytes 122888 | tf_op jit(solution)/shard_map/ppermute | solution.py:284
  12.7 1.1 %collective-permute-done.4.refs_0_ = bf16[80,256]{1,0:T(8,128)(2,1)S(1)} collective-permute-done((bf16[80,256]{1,0:T(8,128)(2,1)S(1)}, bf16[80,256]{1,0:T(8,128)(2,1)S(1)}, u32[]{:S(2)}, u32[]{:S(2)}) %collective-permute-start.4) | collective-permute-done | bytes 40992 | tf_op jit(solution)/shard_map/ppermute | solution.py:284
  13.8 1.4 %collective-permute-done.5.refs_1_ = bf16[80,256]{1,0:T(8,128)(2,1)S(1)} collective-permute-done((bf16[80,256]{1,0:T(8,128)(2,1)S(1)}, bf16[80,256]{1,0:T(8,128)(2,1)S(1)}, u32[]{:S(2)}, u32[]{:S(2)}) %collective-permute-start.5) | collective-permute-done | bytes 40992 | tf_op jit(solution)/shard_map/ppermute | solution.py:284
  15.2 0.6 %collective-permute-done.6.refs_2_ = bf16[80,256]{1,0:T(8,128)(2,1)S(1)} collective-permute-done((bf16[80,256]{1,0:T(8,128)(2,1)S(1)}, bf16[80,256]{1,0:T(8,128)(2,1)S(1)}, u32[]{:S(2)}, u32[]{:S(2)}) %collective-permute-start.6) | collective-permute-done | bytes 40992 | tf_op jit(solution)/shard_map/ppermute | solution.py:284
  15.7 0.0 collective-permute-done.7.refs_3_
  15.7 1.2 %expand.1 = f32[3,129,256]{2,1,0:T(8,128)} custom-call(bf16[96,320]{1,0:T(8,128)(2,1)S(1)} %get-tuple-element.17.order_ref, bf16[256,256]{1,0:T(8,128)(2,1)S(1)} %get-tuple-element.18.chosen_ref, bf16[80,256]{1,0:T(8,128)(2,1)S(1)} %collective-permute-done.4.refs_0_, bf16[80,256]{1,0:T(8,128)(2,1)S(1)} %collective-permute-done.5.refs_1_, ...), custom_call_target="tpu_custom_call" | custom-call | tf_op jit(solution)/shard_map/expand/pallas_call | solution.py:354
Async XLA Ops:
  1.1 3.6 %copy-start = (s32[256]{0:T(256)S(1)}, s32[256]{0:T(256)}, u32[]{:S(2)}) copy-start(s32[256]{0:T(256)} %param.5) | copy-start | bytes 3076
  1.1 6.4 %collective-permute-start = (bf16[48,512]{1,0:T(8,128)(2,1)S(1)}, bf16[48,512]{1,0:T(8,128)(2,1)S(1)}, u32[]{:S(2)}, u32[]{:S(2)}) collective-permute-start(bf16[48,512]{1,0:T(8,128)(2,1)S(1)} %whiten.1.whitened_ref.refs_2_), channel_id=1, source_target_pairs={{0,9},{1,8},{2,11},{3,10},{4,13},{5,12},{6,15},{7,14},{8,1},{9,0},... | collective-permute-start | bytes 147464 | tf_op jit(solution)/shard_map/ppermute | solution.py:284
  4.8 1.6 %collective-permute-start.1 = (bf16[24,512]{1,0:T(8,128)(2,1)S(1)}, bf16[24,512]{1,0:T(8,128)(2,1)S(1)}, u32[]{:S(2)}, u32[]{:S(2)}) collective-permute-start(bf16[24,512]{1,0:T(8,128)(2,1)S(1)} %get-tuple-element.19), channel_id=1, source_target_pairs={{0,1},{1,0},{2,3},{3,2},{4,5},{5,4},{6,7},{7,6},{8,9},{9,8},{10,11... | collective-permute-start | bytes 73736 | tf_op jit(solution)/shard_map/ppermute | solution.py:276
  5.6 1.2 %collective-permute-start.2 = (bf16[24,512]{1,0:T(8,128)(2,1)S(1)}, bf16[24,512]{1,0:T(8,128)(2,1)S(1)}, u32[]{:S(2)}, u32[]{:S(2)}) collective-permute-start(bf16[24,512]{1,0:T(8,128)(2,1)S(1)} %get-tuple-element.20), channel_id=1, source_target_pairs={{0,1},{1,0},{2,3},{3,2},{4,5},{5,4},{6,7},{7,6},{8,9},{9,8},{10,11... | collective-permute-start | bytes 73736 | tf_op jit(solution)/shard_map/ppermute | solution.py:276
  7.5 1.3 %collective-permute-start.3 = (bf16[48,512]{1,0:T(8,128)(2,1)S(1)}, bf16[48,512]{1,0:T(8,128)(2,1)S(1)}, u32[]{:S(2)}, u32[]{:S(2)}) collective-permute-start(bf16[48,512]{1,0:T(8,128)(2,1)S(1)} %collective-permute-done.mine_ref), channel_id=1, source_target_pairs={{0,1},{1,0},{2,3},{3,2},{4,5},{5,4},{6,7},{7,6},{8,9},{9,8},{10,11... | collective-permute-start | bytes 147464 | tf_op jit(solution)/shard_map/ppermute | solution.py:276
  9.3 4.5 %collective-permute-start.4 = (bf16[80,256]{1,0:T(8,128)(2,1)S(1)}, bf16[80,256]{1,0:T(8,128)(2,1)S(1)}, u32[]{:S(2)}, u32[]{:S(2)}) collective-permute-start(bf16[80,256]{1,0:T(8,128)(2,1)S(1)} %get-tuple-element.25), channel_id=1, source_target_pairs={{0,7},{1,6},{2,5},{3,4},{4,3},{5,2},{6,1},{7,0},{8,15},{9,14},{10,... | collective-permute-start | bytes 122888 | tf_op jit(solution)/shard_map/ppermute | solution.py:284
  11.7 3.4 %collective-permute-start.5 = (bf16[80,256]{1,0:T(8,128)(2,1)S(1)}, bf16[80,256]{1,0:T(8,128)(2,1)S(1)}, u32[]{:S(2)}, u32[]{:S(2)}) collective-permute-start(bf16[80,256]{1,0:T(8,128)(2,1)S(1)} %get-tuple-element.26), channel_id=1, source_target_pairs={{0,3},{1,2},{2,1},{3,0},{4,7},{5,6},{6,5},{7,4},{8,11},{9,10},{10,... | collective-permute-start | bytes 122888 | tf_op jit(solution)/shard_map/ppermute | solution.py:284
  12.2 3.5 %collective-permute-start.6 = (bf16[80,256]{1,0:T(8,128)(2,1)S(1)}, bf16[80,256]{1,0:T(8,128)(2,1)S(1)}, u32[]{:S(2)}, u32[]{:S(2)}) collective-permute-start(bf16[80,256]{1,0:T(8,128)(2,1)S(1)} %get-tuple-element.27), channel_id=1, source_target_pairs={{0,5},{1,4},{2,7},{3,6},{4,1},{5,0},{6,3},{7,2},{8,13},{9,12},{10,... | collective-permute-start | bytes 122888 | tf_op jit(solution)/shard_map/ppermute | solution.py:284
  12.3 3.4 %collective-permute-start.7 = (bf16[80,256]{1,0:T(8,128)(2,1)S(1)}, bf16[80,256]{1,0:T(8,128)(2,1)S(1)}, u32[]{:S(2)}, u32[]{:S(2)}) collective-permute-start(bf16[80,256]{1,0:T(8,128)(2,1)S(1)} %get-tuple-element.28), channel_id=1, source_target_pairs={{0,1},{1,0},{2,3},{3,2},{4,5},{5,4},{6,7},{7,6},{8,9},{9,8},{10,11... | collective-permute-start | bytes 122888 | tf_op jit(solution)/shard_map/ppermute | solution.py:284

commit v24 on v23

--- a/solution.py
+++ b/solution.py
@@ -135,7 +135,7 @@
                 row = jnp.concatenate([rows_ref[pl.ds(channel, 1), :], filler], axis=1)
                 row = jnp.broadcast_to(row, (GROUP, span))
                 pieces = [
-                    pltpu.roll(row, (MAXLAG - plan.fine + 1 + lag) % span, 1, stride=1, stride_axis=0)
+                    pltpu.roll(row, (MAXLAG - plan.fine_padded + 1 + lag) % span, 1, stride=1, stride_axis=0)
                     for lag in range(0, plan.fine_padded, GROUP)
                 ]
                 first = place * plan.height + member * plan.fine_padded
@@ -187,29 +187,22 @@
     fill_columns(plan, other_ref[...].astype(jnp.float32), columns_ref)
     right = prior_ref[:, plan.half_lanes :] + product(toeplitz_ref, columns_ref)
     products = jnp.concatenate([prior_ref[:, : plan.half_lanes], right], axis=1)
-    products = products.reshape(plan.targets, plan.own, plan.fine_padded, LANES)
-    for hop in range(plan.targets):
-        part = products[hop]
-        pieces = [part[member, : plan.whole_groups] for member in range(plan.own)]
-        if plan.rest:
-            pieces += [part[member, plan.whole_groups : plan.fine] for member in range(plan.own)]
+    back = GROUP - 1 - lax.broadcasted_iota(jnp.int32, (GROUP, LANES), 0)
+    for place in range(plan.targets):
+        whole, rest = [], []
+        for member in range(plan.own):
+            last = place * plan.height + (member + 1) * plan.fine_padded
+            tiles = [
+                jnp.take_along_axis(products[last - lag - GROUP : last - lag], back, axis=0)
+                for lag in range(0, plan.fine, GROUP)
+            ]
+            whole += tiles[: plan.whole_groups // GROUP]
+            if plan.rest:
+                rest.append(tiles[-1][: plan.rest])
+        pieces = whole + rest
         if plan.rows > plan.own * plan.fine:
             pieces.append(jnp.zeros((plan.rows - plan.own * plan.fine, LANES), jnp.float32))
-        packed = jnp.concatenate(pieces, axis=0)
-        out_refs[hop][...] = packed.astype(out_refs[hop].dtype)
-
-
-def order_matrix(plan):
-    at_row = lax.broadcasted_iota(jnp.int32, (plan.height, plan.rows), 0)
-    at_part = lax.broadcasted_iota(jnp.int32, (plan.height, plan.rows), 1)
-    order = jnp.zeros((plan.height, plan.rows), jnp.bool_)
-    for member in range(plan.own):
-        reverse = plan.fine - 1 - (at_row - member * plan.fine_padded)
-        whole = (reverse >= 0) & (reverse < plan.whole_groups) & (at_part == member * plan.whole_groups + reverse)
-        tail = plan.own * plan.whole_groups + member * plan.rest + reverse - plan.whole_groups
-        rest = (reverse >= plan.whole_groups) & (reverse < plan.fine) & (at_part == tail)
-        order = order | whole | rest
-    return order.astype(jnp.float32).astype(jnp.bfloat16)
+        out_refs[place][...] = jnp.concatenate(pieces, axis=0).astype(jnp.bfloat16)
 
 
 def spread(plan, values):
@@ -228,7 +221,7 @@
     return jnp.concatenate(pieces, axis=0)
 
 
-def choose_kernel(plan, index_ref, whitened_ref, order_ref, chosen_ref, *same_refs):
+def choose_kernel(plan, index_ref, whitened_ref, chosen_ref, *same_refs):
     whitened = whitened_ref[...].astype(jnp.float32)
     for window, same_ref in enumerate(same_refs):
         same_ref[...] = whitened[window * plan.half : (window + 1) * plan.half].astype(jnp.bfloat16)
@@ -241,19 +234,24 @@
     for step in range(plan.coarse):
         chosen = chosen | (at_column == lane + step * plan.half)
     chosen_ref[...] = chosen.astype(jnp.float32).astype(jnp.bfloat16)
-    order = order_matrix(plan)
-    for block in range(plan.targets):
-        order_ref[:, block * plan.rows : (block + 1) * plan.rows] = order
-
-
-def expand_kernel(plan, order_ref, chosen_ref, *refs):
+
+
+def expand_kernel(plan, chosen_ref, *refs):
     *arrived_refs, out_hbm, out_ref, sems = refs
-    blocks = jnp.concatenate([ref[...] for ref in arrived_refs], axis=0)
-    total = jnp.dot(order_ref[...], blocks, preferred_element_type=jnp.float32) * plan.norm_factor
+    total = sum(ref[...].astype(jnp.float32) for ref in arrived_refs) * plan.norm_factor
     chosen = chosen_ref[...]
+    filler = jnp.zeros((plan.fine_padded - plan.fine, LANES), jnp.float32)
     copies = []
     for member in range(plan.own):
-        rows = total[member * plan.fine_padded : (member + 1) * plan.fine_padded]
+        rest = plan.own * plan.whole_groups + member * plan.rest
+        rows = jnp.concatenate(
+            [
+                total[member * plan.whole_groups : (member + 1) * plan.whole_groups],
+                total[rest : rest + plan.rest],
+                filler,
+            ],
+            axis=0,
+        )
         expanded = jnp.dot(spread(plan, rows), chosen, preferred_element_type=jnp.float32)
         for step in range(plan.coarse):
             start = step * plan.fine
@@ -316,12 +314,11 @@
         )(*operands)
 
     across = swap_blk(whitened, plan.targets)
-    order, chosen, *same = call(
+    chosen, *same = call(
         choose_kernel,
         "choose",
         (source_index.reshape(1, -1), whitened),
         (
-            jax.ShapeDtypeStruct((plan.height, plan.targets * plan.rows), jnp.bfloat16),
             jax.ShapeDtypeStruct((LANES, plan.source_count), jnp.bfloat16),
             *[jax.ShapeDtypeStruct((plan.half, plan.segment), whitened.dtype)] * plan.windows,
         ),
@@ -354,12 +351,12 @@
     return pl.pallas_call(
         functools.partial(expand_kernel, plan),
         out_shape=jax.ShapeDtypeStruct(out_shape, jnp.float32),
-        in_specs=[vmem] * (2 + len(arrived)),
+        in_specs=[vmem] * (1 + len(arrived)),
         out_specs=pl.BlockSpec(memory_space=pl.ANY),
         scratch_shapes=[pltpu.VMEM(out_shape, jnp.float32), pltpu.SemaphoreType.DMA((plan.own,))],
         compiler_params=params,
         name="expand",
-    )(order, chosen, *arrived)
+    )(chosen, *arrived)
 
 
 def body(traces, valid_flags, source_index):

time: 17.1 us -> 16.9 us (0.988)
  Pallas kernels: 4.21 us -> 3.98 us
  transfers between devices with their start and end apart: 8 -> 8, of which waited for: 6 -> 6; matrix products, arithmetic and copies ran while one was open for 0% -> 0% of each run, Pallas kernels for 9% -> 8%
where the time goes in v24:
time: 16.9 us; the launch traced here: 16.8 us
  starting transfers between devices  7.98 us (47%)
  waiting for transfers between devices  4.75 us (28%)
  Pallas kernels  3.98 us (24%)
    ppermute x5, starting transfers between devices, swap_blk(): return lax.ppermute(array, ('blk', 'src'), pairs)  6.93 us
    ppermute x5, waiting for transfers between devices, swap_blk(): return lax.ppermute(array, ('blk', 'src'), pairs)  3.15 us
    pallas_call x4, Pallas kernels, call(): pl.pallas_call(functools.partial(kernel, plan), out_shape=outputs, in_spe...  1.91 us
    ppermute x3, waiting for transfers between devices, swap_cores(): return lax.ppermute(array, 'src', [(0, 1), (1, 0)])  1.6 us
    ppermute x3, starting transfers between devices, swap_cores(): return lax.ppermute(array, 'src', [(0, 1), (1, 0)])  1.05 us
    pallas_call x1, Pallas kernels, few_channels(): pl.pallas_call(functools.partial(whiten_kernel, plan), out_shape=pltpu.VM...  1.04 us
    pallas_call x1, Pallas kernels, few_channels(): pl.pallas_call(functools.partial(expand_kernel, plan), out_shape=jax.Shap...  1.03 us
  transfers between devices with their start and end apart: 8, of which 6 were waited for; matrix products, arithmetic and copies ran while one was open for 0% of the time, Pallas kernels for 8%

profile of v24, /device:TPU:0, one launch (start us, length us, event | category | flops | bytes accessed | tf_op | source)
XLA Modules:
  0.0 16.8 jit_solution(15836550545536955743)
XLA Ops:
  0.0 1.0 %whiten.1.whitened_ref.refs_2_ = bf16[48,512]{1,0:T(8,128)(2,1)S(1)} custom-call(f32[24,2,512]{2,1,0:T(2,128)} %traces_hbm.1, s32[2,24]{1,0:T(2,128)} %bitcast.3), custom_call_target="tpu_custom_call" | custom-call | tf_op jit(solution)/shard_map/whiten/pallas_call | solution.py:284
  1.1 0.0 copy-start
  1.1 3.5 %collective-permute-start = (bf16[48,512]{1,0:T(8,128)(2,1)S(1)}, bf16[48,512]{1,0:T(8,128)(2,1)S(1)}, u32[]{:S(2)}, u32[]{:S(2)}) collective-permute-start(bf16[48,512]{1,0:T(8,128)(2,1)S(1)} %whiten.1.whitened_ref.refs_2_), channel_id=1, source_target_pairs={{0,9},{1,8},{2,11},{3,10},{4,13},{5,12},{6,15},{7,14},{8,1},{9,0},... | collective-permute-start | bytes 147464 | tf_op jit(solution)/shard_map/ppermute | solution.py:282
  4.6 0.0 copy-done
  4.6 0.2 choose.1
  4.8 0.7 %collective-permute-start.1 = (bf16[24,512]{1,0:T(8,128)(2,1)S(1)}, bf16[24,512]{1,0:T(8,128)(2,1)S(1)}, u32[]{:S(2)}, u32[]{:S(2)}) collective-permute-start(bf16[24,512]{1,0:T(8,128)(2,1)S(1)} %get-tuple-element.17), channel_id=1, source_target_pairs={{0,1},{1,0},{2,3},{3,2},{4,5},{5,4},{6,7},{7,6},{8,9},{9,8},{10,11... | collective-permute-start | bytes 73736 | tf_op jit(solution)/shard_map/ppermute | solution.py:274
  5.5 0.1 collective-permute-start.2
  5.6 0.8 %collective-permute-done.1.refs_0_ = bf16[24,512]{1,0:T(8,128)(2,1)S(1)} collective-permute-done((bf16[24,512]{1,0:T(8,128)(2,1)S(1)}, bf16[24,512]{1,0:T(8,128)(2,1)S(1)}, u32[]{:S(2)}, u32[]{:S(2)}) %collective-permute-start.1) | collective-permute-done | bytes 24608 | tf_op jit(solution)/shard_map/ppermute | solution.py:274
  6.4 0.3 %collective-permute-done.2.refs_1_ = bf16[24,512]{1,0:T(8,128)(2,1)S(1)} collective-permute-done((bf16[24,512]{1,0:T(8,128)(2,1)S(1)}, bf16[24,512]{1,0:T(8,128)(2,1)S(1)}, u32[]{:S(2)}, u32[]{:S(2)}) %collective-permute-start.2) | collective-permute-done | bytes 24608 | tf_op jit(solution)/shard_map/ppermute | solution.py:274
  6.7 0.7 %near.1.prior_ref = f32[384,256]{1,0:T(8,128)S(1)} custom-call(bf16[24,512]{1,0:T(8,128)(2,1)S(1)} %collective-permute-done.1.refs_0_, bf16[24,512]{1,0:T(8,128)(2,1)S(1)} %collective-permute-done.2.refs_1_, bf16[48,512]{1,0:T(8,128)(2,1)S(1)} %whiten.1.whitened_ref.refs_2_), custom_call_target="tpu_custom_call" | custom-call | tf_op jit(solution)/shard_map/near/pallas_call | solution.py:306
  7.4 0.0 collective-permute-done.mine_ref
  7.4 0.2 %collective-permute-start.3 = (bf16[48,512]{1,0:T(8,128)(2,1)S(1)}, bf16[48,512]{1,0:T(8,128)(2,1)S(1)}, u32[]{:S(2)}, u32[]{:S(2)}) collective-permute-start(bf16[48,512]{1,0:T(8,128)(2,1)S(1)} %collective-permute-done.mine_ref), channel_id=1, source_target_pairs={{0,1},{1,0},{2,3},{3,2},{4,5},{5,4},{6,7},{7,6},{8,9},{9,8},{10,11... | collective-permute-start | bytes 147464 | tf_op jit(solution)/shard_map/ppermute | solution.py:274
  7.6 0.6 %across.1 = (bf16[384,1280]{1,0:T(8,128)(2,1)S(1)}, f32[384,256]{1,0:T(8,128)S(1)}) custom-call(bf16[48,512]{1,0:T(8,128)(2,1)S(1)} %collective-permute-done.mine_ref, f32[384,256]{1,0:T(8,128)S(1)} %near.1.prior_ref), custom_call_target="tpu_custom_call" | custom-call | tf_op jit(solution)/shard_map/across/pallas_call | solution.py:306
  8.2 0.5 %collective-permute-done.3.other_ref = bf16[48,512]{1,0:T(8,128)(2,1)S(1)} collective-permute-done((bf16[48,512]{1,0:T(8,128)(2,1)S(1)}, bf16[48,512]{1,0:T(8,128)(2,1)S(1)}, u32[]{:S(2)}, u32[]{:S(2)}) %collective-permute-start.3) | collective-permute-done | bytes 49184 | tf_op jit(solution)/shard_map/ppermute | solution.py:274
  8.7 0.5 %finish.1 = (bf16[80,256]{1,0:T(8,128)(2,1)S(1)}, bf16[80,256]{1,0:T(8,128)(2,1)S(1)}, bf16[80,256]{1,0:T(8,128)(2,1)S(1)}, bf16[80,256]{1,0:T(8,128)(2,1)S(1)}) custom-call(bf16[48,512]{1,0:T(8,128)(2,1)S(1)} %collective-permute-done.3.other_ref, bf16[384,1280]{1,0:T(8,128)(2,1)S(1)} %get-tuple-element.21.toeplitz_ref, ...), custom_call_target="tpu_custom_call" | custom-call | tf_op jit(solution)/shard_map/finish/pallas_call | solution.py:306
  9.2 2.5 %collective-permute-start.4 = (bf16[80,256]{1,0:T(8,128)(2,1)S(1)}, bf16[80,256]{1,0:T(8,128)(2,1)S(1)}, u32[]{:S(2)}, u32[]{:S(2)}) collective-permute-start(bf16[80,256]{1,0:T(8,128)(2,1)S(1)} %get-tuple-element.23), channel_id=1, source_target_pairs={{0,7},{1,6},{2,5},{3,4},{4,3},{5,2},{6,1},{7,0},{8,15},{9,14},{10,... | collective-permute-start | bytes 122888 | tf_op jit(solution)/shard_map/ppermute | solution.py:282
  11.7 0.5 %collective-permute-start.5 = (bf16[80,256]{1,0:T(8,128)(2,1)S(1)}, bf16[80,256]{1,0:T(8,128)(2,1)S(1)}, u32[]{:S(2)}, u32[]{:S(2)}) collective-permute-start(bf16[80,256]{1,0:T(8,128)(2,1)S(1)} %get-tuple-element.24), channel_id=1, source_target_pairs={{0,3},{1,2},{2,1},{3,0},{4,7},{5,6},{6,5},{7,4},{8,11},{9,10},{10,... | collective-permute-start | bytes 122888 | tf_op jit(solution)/shard_map/ppermute | solution.py:282
  12.2 0.1 collective-permute-start.6
  12.3 0.3 %collective-permute-start.7 = (bf16[80,256]{1,0:T(8,128)(2,1)S(1)}, bf16[80,256]{1,0:T(8,128)(2,1)S(1)}, u32[]{:S(2)}, u32[]{:S(2)}) collective-permute-start(bf16[80,256]{1,0:T(8,128)(2,1)S(1)} %get-tuple-element.26), channel_id=1, source_target_pairs={{0,1},{1,0},{2,3},{3,2},{4,5},{5,4},{6,7},{7,6},{8,9},{9,8},{10,11... | collective-permute-start | bytes 122888 | tf_op jit(solution)/shard_map/ppermute | solution.py:282
  12.6 1.2 %collective-permute-done.4.refs_0_ = bf16[80,256]{1,0:T(8,128)(2,1)S(1)} collective-permute-done((bf16[80,256]{1,0:T(8,128)(2,1)S(1)}, bf16[80,256]{1,0:T(8,128)(2,1)S(1)}, u32[]{:S(2)}, u32[]{:S(2)}) %collective-permute-start.4) | collective-permute-done | bytes 40992 | tf_op jit(solution)/shard_map/ppermute | solution.py:282
  13.8 1.4 %collective-permute-done.5.refs_1_ = bf16[80,256]{1,0:T(8,128)(2,1)S(1)} collective-permute-done((bf16[80,256]{1,0:T(8,128)(2,1)S(1)}, bf16[80,256]{1,0:T(8,128)(2,1)S(1)}, u32[]{:S(2)}, u32[]{:S(2)}) %collective-permute-start.5) | collective-permute-done | bytes 40992 | tf_op jit(solution)/shard_map/ppermute | solution.py:282
  15.2 0.6 %collective-permute-done.6.refs_2_ = bf16[80,256]{1,0:T(8,128)(2,1)S(1)} collective-permute-done((bf16[80,256]{1,0:T(8,128)(2,1)S(1)}, bf16[80,256]{1,0:T(8,128)(2,1)S(1)}, u32[]{:S(2)}, u32[]{:S(2)}) %collective-permute-start.6) | collective-permute-done | bytes 40992 | tf_op jit(solution)/shard_map/ppermute | solution.py:282
  15.7 0.0 collective-permute-done.7.refs_3_
  15.7 1.0 %expand.1 = f32[3,129,256]{2,1,0:T(8,128)} custom-call(bf16[256,256]{1,0:T(8,128)(2,1)S(1)} %get-tuple-element.16.chosen_ref, bf16[80,256]{1,0:T(8,128)(2,1)S(1)} %collective-permute-done.4.refs_0_, bf16[80,256]{1,0:T(8,128)(2,1)S(1)} %collective-permute-done.5.refs_1_, bf16[80,256]{1,0:T(8,128)(2,1)S(1)} %collective-permute-done.6.refs_2_, ...), custom_call_target="tpu_custom_call" | custom-call | tf_op jit(solution)/shard_map/expand/pallas_call | solution.py:351
Async XLA Ops:
  1.1 3.6 %copy-start = (s32[256]{0:T(256)S(1)}, s32[256]{0:T(256)}, u32[]{:S(2)}) copy-start(s32[256]{0:T(256)} %param.5) | copy-start | bytes 3076
  1.1 6.3 %collective-permute-start = (bf16[48,512]{1,0:T(8,128)(2,1)S(1)}, bf16[48,512]{1,0:T(8,128)(2,1)S(1)}, u32[]{:S(2)}, u32[]{:S(2)}) collective-permute-start(bf16[48,512]{1,0:T(8,128)(2,1)S(1)} %whiten.1.whitened_ref.refs_2_), channel_id=1, source_target_pairs={{0,9},{1,8},{2,11},{3,10},{4,13},{5,12},{6,15},{7,14},{8,1},{9,0},... | collective-permute-start | bytes 147464 | tf_op jit(solution)/shard_map/ppermute | solution.py:282
  4.8 1.6 %collective-permute-start.1 = (bf16[24,512]{1,0:T(8,128)(2,1)S(1)}, bf16[24,512]{1,0:T(8,128)(2,1)S(1)}, u32[]{:S(2)}, u32[]{:S(2)}) collective-permute-start(bf16[24,512]{1,0:T(8,128)(2,1)S(1)} %get-tuple-element.17), channel_id=1, source_target_pairs={{0,1},{1,0},{2,3},{3,2},{4,5},{5,4},{6,7},{7,6},{8,9},{9,8},{10,11... | collective-permute-start | bytes 73736 | tf_op jit(solution)/shard_map/ppermute | solution.py:274
  5.5 1.2 %collective-permute-start.2 = (bf16[24,512]{1,0:T(8,128)(2,1)S(1)}, bf16[24,512]{1,0:T(8,128)(2,1)S(1)}, u32[]{:S(2)}, u32[]{:S(2)}) collective-permute-start(bf16[24,512]{1,0:T(8,128)(2,1)S(1)} %get-tuple-element.18), channel_id=1, source_target_pairs={{0,1},{1,0},{2,3},{3,2},{4,5},{5,4},{6,7},{7,6},{8,9},{9,8},{10,11... | collective-permute-start | bytes 73736 | tf_op jit(solution)/shard_map/ppermute | solution.py:274
  7.4 1.3 %collective-permute-start.3 = (bf16[48,512]{1,0:T(8,128)(2,1)S(1)}, bf16[48,512]{1,0:T(8,128)(2,1)S(1)}, u32[]{:S(2)}, u32[]{:S(2)}) collective-permute-start(bf16[48,512]{1,0:T(8,128)(2,1)S(1)} %collective-permute-done.mine_ref), channel_id=1, source_target_pairs={{0,1},{1,0},{2,3},{3,2},{4,5},{5,4},{6,7},{7,6},{8,9},{9,8},{10,11... | collective-permute-start | bytes 147464 | tf_op jit(solution)/shard_map/ppermute | solution.py:274
  9.2 4.6 %collective-permute-start.4 = (bf16[80,256]{1,0:T(8,128)(2,1)S(1)}, bf16[80,256]{1,0:T(8,128)(2,1)S(1)}, u32[]{:S(2)}, u32[]{:S(2)}) collective-permute-start(bf16[80,256]{1,0:T(8,128)(2,1)S(1)} %get-tuple-element.23), channel_id=1, source_target_pairs={{0,7},{1,6},{2,5},{3,4},{4,3},{5,2},{6,1},{7,0},{8,15},{9,14},{10,... | collective-permute-start | bytes 122888 | tf_op jit(solution)/shard_map/ppermute | solution.py:282
  11.7 3.4 %collective-permute-start.5 = (bf16[80,256]{1,0:T(8,128)(2,1)S(1)}, bf16[80,256]{1,0:T(8,128)(2,1)S(1)}, u32[]{:S(2)}, u32[]{:S(2)}) collective-permute-start(bf16[80,256]{1,0:T(8,128)(2,1)S(1)} %get-tuple-element.24), channel_id=1, source_target_pairs={{0,3},{1,2},{2,1},{3,0},{4,7},{5,6},{6,5},{7,4},{8,11},{9,10},{10,... | collective-permute-start | bytes 122888 | tf_op jit(solution)/shard_map/ppermute | solution.py:282
  12.2 3.5 %collective-permute-start.6 = (bf16[80,256]{1,0:T(8,128)(2,1)S(1)}, bf16[80,256]{1,0:T(8,128)(2,1)S(1)}, u32[]{:S(2)}, u32[]{:S(2)}) collective-permute-start(bf16[80,256]{1,0:T(8,128)(2,1)S(1)} %get-tuple-element.25), channel_id=1, source_target_pairs={{0,5},{1,4},{2,7},{3,6},{4,1},{5,0},{6,3},{7,2},{8,13},{9,12},{10,... | collective-permute-start | bytes 122888 | tf_op jit(solution)/shard_map/ppermute | solution.py:282
  12.3 3.4 %collective-permute-start.7 = (bf16[80,256]{1,0:T(8,128)(2,1)S(1)}, bf16[80,256]{1,0:T(8,128)(2,1)S(1)}, u32[]{:S(2)}, u32[]{:S(2)}) collective-permute-start(bf16[80,256]{1,0:T(8,128)(2,1)S(1)} %get-tuple-element.26), channel_id=1, source_target_pairs={{0,1},{1,0},{2,3},{3,2},{4,5},{5,4},{6,7},{7,6},{8,9},{9,8},{10,11... | collective-permute-start | bytes 122888 | tf_op jit(solution)/shard_map/ppermute | solution.py:282

commit v25 on v24

--- a/solution.py
+++ b/solution.py
@@ -313,7 +313,7 @@
             name=name,
         )(*operands)
 
-    across = swap_blk(whitened, plan.targets)
+    across = swap_blk(whitened, plan.blk_size - 2)
     chosen, *same = call(
         choose_kernel,
         "choose",

time: 16.9 us -> 17 us (level)
  starting transfers between devices: 7.98 us -> 8.99 us
  waiting for transfers between devices: 4.75 us -> 3.84 us
    ppermute x5, starting transfers between devices: 6.93 us -> 7.94 us  [swap_blk(): return lax.ppermute(array, ('blk', 'src'), pairs)]
    ppermute x5, waiting for transfers between devices: 3.15 us -> 2.24 us  [swap_blk(): return lax.ppermute(array, ('blk', 'src'), pairs)]
  transfers between devices with their start and end apart: 8 -> 8, of which waited for: 6 -> 5; matrix products, arithmetic and copies ran while one was open for 0% -> 0% of each run, Pallas kernels for 8% -> 8%
where the time goes in v25:
time: 17 us; the launch traced here: 16.9 us
  starting transfers between devices  8.99 us (53%)
  Pallas kernels  3.98 us (23%)
  waiting for transfers between devices  3.84 us (23%)
    ppermute x5, starting transfers between devices, swap_blk(): return lax.ppermute(array, ('blk', 'src'), pairs)  7.94 us
    ppermute x5, waiting for transfers between devices, swap_blk(): return lax.ppermute(array, ('blk', 'src'), pairs)  2.24 us
    pallas_call x4, Pallas kernels, call(): pl.pallas_call(functools.partial(kernel, plan), out_shape=outputs, in_spe...  1.91 us
    ppermute x3, waiting for transfers between devices, swap_cores(): return lax.ppermute(array, 'src', [(0, 1), (1, 0)])  1.6 us
    ppermute x3, starting transfers between devices, swap_cores(): return lax.ppermute(array, 'src', [(0, 1), (1, 0)])  1.05 us
    pallas_call x1, Pallas kernels, few_channels(): pl.pallas_call(functools.partial(whiten_kernel, plan), out_shape=pltpu.VM...  1.04 us
    pallas_call x1, Pallas kernels, few_channels(): pl.pallas_call(functools.partial(expand_kernel, plan), out_shape=jax.Shap...  1.03 us
  transfers between devices with their start and end apart: 8, of which 5 were waited for; matrix products, arithmetic and copies ran while one was open for 0% of the time, Pallas kernels for 8%

profile of v25, /device:TPU:0, one launch (start us, length us, event | category | flops | bytes accessed | tf_op | source)
XLA Modules:
  0.0 16.9 jit_solution(5167048979447046998)
XLA Ops:
  0.0 1.0 %whiten.1.whitened_ref.refs_2_ = bf16[48,512]{1,0:T(8,128)(2,1)S(1)} custom-call(f32[24,2,512]{2,1,0:T(2,128)} %traces_hbm.1, s32[2,24]{1,0:T(2,128)} %bitcast.3), custom_call_target="tpu_custom_call" | custom-call | tf_op jit(solution)/shard_map/whiten/pallas_call | solution.py:284
  1.1 0.0 copy-start
  1.1 4.6 %collective-permute-start = (bf16[48,512]{1,0:T(8,128)(2,1)S(1)}, bf16[48,512]{1,0:T(8,128)(2,1)S(1)}, u32[]{:S(2)}, u32[]{:S(2)}) collective-permute-start(bf16[48,512]{1,0:T(8,128)(2,1)S(1)} %whiten.1.whitened_ref.refs_2_), channel_id=1, source_target_pairs={{0,13},{1,12},{2,15},{3,14},{4,9},{5,8},{6,11},{7,10},{8,5},{9,4},... | collective-permute-start | bytes 147464 | tf_op jit(solution)/shard_map/ppermute | solution.py:282
  5.6 0.0 copy-done
  5.6 0.2 choose.1
  5.8 0.7 %collective-permute-start.1 = (bf16[24,512]{1,0:T(8,128)(2,1)S(1)}, bf16[24,512]{1,0:T(8,128)(2,1)S(1)}, u32[]{:S(2)}, u32[]{:S(2)}) collective-permute-start(bf16[24,512]{1,0:T(8,128)(2,1)S(1)} %get-tuple-element.17), channel_id=1, source_target_pairs={{0,1},{1,0},{2,3},{3,2},{4,5},{5,4},{6,7},{7,6},{8,9},{9,8},{10,11... | collective-permute-start | bytes 73736 | tf_op jit(solution)/shard_map/ppermute | solution.py:274
  6.5 0.1 collective-permute-start.2
  6.6 0.8 %collective-permute-done.1.refs_0_ = bf16[24,512]{1,0:T(8,128)(2,1)S(1)} collective-permute-done((bf16[24,512]{1,0:T(8,128)(2,1)S(1)}, bf16[24,512]{1,0:T(8,128)(2,1)S(1)}, u32[]{:S(2)}, u32[]{:S(2)}) %collective-permute-start.1) | collective-permute-done | bytes 24608 | tf_op jit(solution)/shard_map/ppermute | solution.py:274
  7.4 0.3 %collective-permute-done.2.refs_1_ = bf16[24,512]{1,0:T(8,128)(2,1)S(1)} collective-permute-done((bf16[24,512]{1,0:T(8,128)(2,1)S(1)}, bf16[24,512]{1,0:T(8,128)(2,1)S(1)}, u32[]{:S(2)}, u32[]{:S(2)}) %collective-permute-start.2) | collective-permute-done | bytes 24608 | tf_op jit(solution)/shard_map/ppermute | solution.py:274
  7.7 0.7 %near.1.prior_ref = f32[384,256]{1,0:T(8,128)S(1)} custom-call(bf16[24,512]{1,0:T(8,128)(2,1)S(1)} %collective-permute-done.1.refs_0_, bf16[24,512]{1,0:T(8,128)(2,1)S(1)} %collective-permute-done.2.refs_1_, bf16[48,512]{1,0:T(8,128)(2,1)S(1)} %whiten.1.whitened_ref.refs_2_), custom_call_target="tpu_custom_call" | custom-call | tf_op jit(solution)/shard_map/near/pallas_call | solution.py:306
  8.4 0.0 collective-permute-done.mine_ref
  8.4 0.2 %collective-permute-start.3 = (bf16[48,512]{1,0:T(8,128)(2,1)S(1)}, bf16[48,512]{1,0:T(8,128)(2,1)S(1)}, u32[]{:S(2)}, u32[]{:S(2)}) collective-permute-start(bf16[48,512]{1,0:T(8,128)(2,1)S(1)} %collective-permute-done.mine_ref), channel_id=1, source_target_pairs={{0,1},{1,0},{2,3},{3,2},{4,5},{5,4},{6,7},{7,6},{8,9},{9,8},{10,11... | collective-permute-start | bytes 147464 | tf_op jit(solution)/shard_map/ppermute | solution.py:274
  8.6 0.6 %across.1 = (bf16[384,1280]{1,0:T(8,128)(2,1)S(1)}, f32[384,256]{1,0:T(8,128)S(1)}) custom-call(bf16[48,512]{1,0:T(8,128)(2,1)S(1)} %collective-permute-done.mine_ref, f32[384,256]{1,0:T(8,128)S(1)} %near.1.prior_ref), custom_call_target="tpu_custom_call" | custom-call | tf_op jit(solution)/shard_map/across/pallas_call | solution.py:306
  9.2 0.5 %collective-permute-done.3.other_ref = bf16[48,512]{1,0:T(8,128)(2,1)S(1)} collective-permute-done((bf16[48,512]{1,0:T(8,128)(2,1)S(1)}, bf16[48,512]{1,0:T(8,128)(2,1)S(1)}, u32[]{:S(2)}, u32[]{:S(2)}) %collective-permute-start.3) | collective-permute-done | bytes 49184 | tf_op jit(solution)/shard_map/ppermute | solution.py:274
  9.7 0.5 %finish.1 = (bf16[80,256]{1,0:T(8,128)(2,1)S(1)}, bf16[80,256]{1,0:T(8,128)(2,1)S(1)}, bf16[80,256]{1,0:T(8,128)(2,1)S(1)}, bf16[80,256]{1,0:T(8,128)(2,1)S(1)}) custom-call(bf16[48,512]{1,0:T(8,128)(2,1)S(1)} %collective-permute-done.3.other_ref, bf16[384,1280]{1,0:T(8,128)(2,1)S(1)} %get-tuple-element.21.toeplitz_ref, ...), custom_call_target="tpu_custom_call" | custom-call | tf_op jit(solution)/shard_map/finish/pallas_call | solution.py:306
  10.2 1.4 %collective-permute-start.4 = (bf16[80,256]{1,0:T(8,128)(2,1)S(1)}, bf16[80,256]{1,0:T(8,128)(2,1)S(1)}, u32[]{:S(2)}, u32[]{:S(2)}) collective-permute-start(bf16[80,256]{1,0:T(8,128)(2,1)S(1)} %get-tuple-element.23), channel_id=1, source_target_pairs={{0,7},{1,6},{2,5},{3,4},{4,3},{5,2},{6,1},{7,0},{8,15},{9,14},{10,... | collective-permute-start | bytes 122888 | tf_op jit(solution)/shard_map/ppermute | solution.py:282
  11.6 0.5 %collective-permute-start.5 = (bf16[80,256]{1,0:T(8,128)(2,1)S(1)}, bf16[80,256]{1,0:T(8,128)(2,1)S(1)}, u32[]{:S(2)}, u32[]{:S(2)}) collective-permute-start(bf16[80,256]{1,0:T(8,128)(2,1)S(1)} %get-tuple-element.24), channel_id=1, source_target_pairs={{0,3},{1,2},{2,1},{3,0},{4,7},{5,6},{6,5},{7,4},{8,11},{9,10},{10,... | collective-permute-start | bytes 122888 | tf_op jit(solution)/shard_map/ppermute | solution.py:282
  12.1 1.2 %collective-permute-start.6 = (bf16[80,256]{1,0:T(8,128)(2,1)S(1)}, bf16[80,256]{1,0:T(8,128)(2,1)S(1)}, u32[]{:S(2)}, u32[]{:S(2)}) collective-permute-start(bf16[80,256]{1,0:T(8,128)(2,1)S(1)} %get-tuple-element.25), channel_id=1, source_target_pairs={{0,5},{1,4},{2,7},{3,6},{4,1},{5,0},{6,3},{7,2},{8,13},{9,12},{10,... | collective-permute-start | bytes 122888 | tf_op jit(solution)/shard_map/ppermute | solution.py:282
  13.3 0.3 %collective-permute-start.7 = (bf16[80,256]{1,0:T(8,128)(2,1)S(1)}, bf16[80,256]{1,0:T(8,128)(2,1)S(1)}, u32[]{:S(2)}, u32[]{:S(2)}) collective-permute-start(bf16[80,256]{1,0:T(8,128)(2,1)S(1)} %get-tuple-element.26), channel_id=1, source_target_pairs={{0,1},{1,0},{2,3},{3,2},{4,5},{5,4},{6,7},{7,6},{8,9},{9,8},{10,11... | collective-permute-start | bytes 122888 | tf_op jit(solution)/shard_map/ppermute | solution.py:282
  13.6 1.1 %collective-permute-done.4.refs_0_ = bf16[80,256]{1,0:T(8,128)(2,1)S(1)} collective-permute-done((bf16[80,256]{1,0:T(8,128)(2,1)S(1)}, bf16[80,256]{1,0:T(8,128)(2,1)S(1)}, u32[]{:S(2)}, u32[]{:S(2)}) %collective-permute-start.4) | collective-permute-done | bytes 40992 | tf_op jit(solution)/shard_map/ppermute | solution.py:282
  14.7 1.1 %collective-permute-done.5.refs_1_ = bf16[80,256]{1,0:T(8,128)(2,1)S(1)} collective-permute-done((bf16[80,256]{1,0:T(8,128)(2,1)S(1)}, bf16[80,256]{1,0:T(8,128)(2,1)S(1)}, u32[]{:S(2)}, u32[]{:S(2)}) %collective-permute-start.5) | collective-permute-done | bytes 40992 | tf_op jit(solution)/shard_map/ppermute | solution.py:282
  15.8 0.0 collective-permute-done.6.refs_2_
  15.8 0.0 collective-permute-done.7.refs_3_
  15.8 1.0 %expand.1 = f32[3,129,256]{2,1,0:T(8,128)} custom-call(bf16[256,256]{1,0:T(8,128)(2,1)S(1)} %get-tuple-element.16.chosen_ref, bf16[80,256]{1,0:T(8,128)(2,1)S(1)} %collective-permute-done.4.refs_0_, bf16[80,256]{1,0:T(8,128)(2,1)S(1)} %collective-permute-done.5.refs_1_, bf16[80,256]{1,0:T(8,128)(2,1)S(1)} %collective-permute-done.6.refs_2_, ...), custom_call_target="tpu_custom_call" | custom-call | tf_op jit(solution)/shard_map/expand/pallas_call | solution.py:351
Async XLA Ops:
  1.1 4.6 %copy-start = (s32[256]{0:T(256)S(1)}, s32[256]{0:T(256)}, u32[]{:S(2)}) copy-start(s32[256]{0:T(256)} %param.5) | copy-start | bytes 3076
  1.1 7.3 %collective-permute-start = (bf16[48,512]{1,0:T(8,128)(2,1)S(1)}, bf16[48,512]{1,0:T(8,128)(2,1)S(1)}, u32[]{:S(2)}, u32[]{:S(2)}) collective-permute-start(bf16[48,512]{1,0:T(8,128)(2,1)S(1)} %whiten.1.whitened_ref.refs_2_), channel_id=1, source_target_pairs={{0,13},{1,12},{2,15},{3,14},{4,9},{5,8},{6,11},{7,10},{8,5},{9,4},... | collective-permute-start | bytes 147464 | tf_op jit(solution)/shard_map/ppermute | solution.py:282
  5.8 1.6 %collective-permute-start.1 = (bf16[24,512]{1,0:T(8,128)(2,1)S(1)}, bf16[24,512]{1,0:T(8,128)(2,1)S(1)}, u32[]{:S(2)}, u32[]{:S(2)}) collective-permute-start(bf16[24,512]{1,0:T(8,128)(2,1)S(1)} %get-tuple-element.17), channel_id=1, source_target_pairs={{0,1},{1,0},{2,3},{3,2},{4,5},{5,4},{6,7},{7,6},{8,9},{9,8},{10,11... | collective-permute-start | bytes 73736 | tf_op jit(solution)/shard_map/ppermute | solution.py:274
  6.5 1.2 %collective-permute-start.2 = (bf16[24,512]{1,0:T(8,128)(2,1)S(1)}, bf16[24,512]{1,0:T(8,128)(2,1)S(1)}, u32[]{:S(2)}, u32[]{:S(2)}) collective-permute-start(bf16[24,512]{1,0:T(8,128)(2,1)S(1)} %get-tuple-element.18), channel_id=1, source_target_pairs={{0,1},{1,0},{2,3},{3,2},{4,5},{5,4},{6,7},{7,6},{8,9},{9,8},{10,11... | collective-permute-start | bytes 73736 | tf_op jit(solution)/shard_map/ppermute | solution.py:274
  8.4 1.3 %collective-permute-start.3 = (bf16[48,512]{1,0:T(8,128)(2,1)S(1)}, bf16[48,512]{1,0:T(8,128)(2,1)S(1)}, u32[]{:S(2)}, u32[]{:S(2)}) collective-permute-start(bf16[48,512]{1,0:T(8,128)(2,1)S(1)} %collective-permute-done.mine_ref), channel_id=1, source_target_pairs={{0,1},{1,0},{2,3},{3,2},{4,5},{5,4},{6,7},{7,6},{8,9},{9,8},{10,11... | collective-permute-start | bytes 147464 | tf_op jit(solution)/shard_map/ppermute | solution.py:274
  10.2 4.5 %collective-permute-start.4 = (bf16[80,256]{1,0:T(8,128)(2,1)S(1)}, bf16[80,256]{1,0:T(8,128)(2,1)S(1)}, u32[]{:S(2)}, u32[]{:S(2)}) collective-permute-start(bf16[80,256]{1,0:T(8,128)(2,1)S(1)} %get-tuple-element.23), channel_id=1, source_target_pairs={{0,7},{1,6},{2,5},{3,4},{4,3},{5,2},{6,1},{7,0},{8,15},{9,14},{10,... | collective-permute-start | bytes 122888 | tf_op jit(solution)/shard_map/ppermute | solution.py:282
  11.6 4.2 %collective-permute-start.5 = (bf16[80,256]{1,0:T(8,128)(2,1)S(1)}, bf16[80,256]{1,0:T(8,128)(2,1)S(1)}, u32[]{:S(2)}, u32[]{:S(2)}) collective-permute-start(bf16[80,256]{1,0:T(8,128)(2,1)S(1)} %get-tuple-element.24), channel_id=1, source_target_pairs={{0,3},{1,2},{2,1},{3,0},{4,7},{5,6},{6,5},{7,4},{8,11},{9,10},{10,... | collective-permute-start | bytes 122888 | tf_op jit(solution)/shard_map/ppermute | solution.py:282
  12.1 3.7 %collective-permute-start.6 = (bf16[80,256]{1,0:T(8,128)(2,1)S(1)}, bf16[80,256]{1,0:T(8,128)(2,1)S(1)}, u32[]{:S(2)}, u32[]{:S(2)}) collective-permute-start(bf16[80,256]{1,0:T(8,128)(2,1)S(1)} %get-tuple-element.25), channel_id=1, source_target_pairs={{0,5},{1,4},{2,7},{3,6},{4,1},{5,0},{6,3},{7,2},{8,13},{9,12},{10,... | collective-permute-start | bytes 122888 | tf_op jit(solution)/shard_map/ppermute | solution.py:282
  13.3 2.6 %collective-permute-start.7 = (bf16[80,256]{1,0:T(8,128)(2,1)S(1)}, bf16[80,256]{1,0:T(8,128)(2,1)S(1)}, u32[]{:S(2)}, u32[]{:S(2)}) collective-permute-start(bf16[80,256]{1,0:T(8,128)(2,1)S(1)} %get-tuple-element.26), channel_id=1, source_target_pairs={{0,1},{1,0},{2,3},{3,2},{4,5},{5,4},{6,7},{7,6},{8,9},{9,8},{10,11... | collective-permute-start | bytes 122888 | tf_op jit(solution)/shard_map/ppermute | solution.py:282

commit v26 on v24

--- a/solution.py
+++ b/solution.py
@@ -146,16 +146,14 @@
 
 def fill_columns(plan, values, columns_ref):
     span = plan.span
-    filled = plan.coarse * plan.half
-    if filled < plan.half_lanes:
-        columns_ref[filled:, :] = jnp.zeros((plan.half_lanes - filled, columns_ref.shape[1]), jnp.bfloat16)
     filler = jnp.zeros((plan.half, span - plan.segment), jnp.float32)
+    spare = jnp.zeros((plan.half_lanes - plan.coarse * plan.half, span), jnp.float32)
     for window in range(plan.windows):
-        at = slice(window * span, (window + 1) * span)
         rows = jnp.concatenate([values[window * plan.half : (window + 1) * plan.half], filler], axis=1)
-        for step in range(plan.coarse):
-            moved = pltpu.roll(rows, step * plan.fine, 1) if step else rows
-            columns_ref[step * plan.half : (step + 1) * plan.half, at] = moved.astype(jnp.bfloat16)
+        pieces = [rows] + [pltpu.roll(rows, step * plan.fine, 1) for step in range(1, plan.coarse)]
+        if spare.shape[0]:
+            pieces.append(spare)
+        columns_ref[:, window * span : (window + 1) * span] = jnp.concatenate(pieces, axis=0).astype(jnp.bfloat16)
 
 
 def product(toeplitz_ref, columns_ref):
@@ -174,20 +172,20 @@
     sum_ref[...] = product(toeplitz_ref, columns_ref)
 
 
-def across_kernel(plan, mine_ref, prior_ref, toeplitz_ref, sum_ref, rows_ref, columns_ref):
+def across_kernel(plan, mine_ref, prior_ref, toeplitz_ref, left_ref, right_ref, rows_ref, columns_ref):
     rows_ref[...] = mine_ref[...].astype(jnp.float32)
     lag_rows(plan, rows_ref, toeplitz_ref)
     fill_columns(plan, rows_ref[...], columns_ref)
-    sum_ref[:, : plan.half_lanes] = prior_ref[:, : plan.half_lanes] + product(toeplitz_ref, columns_ref)
-    sum_ref[:, plan.half_lanes :] = prior_ref[:, plan.half_lanes :]
-
-
-def finish_kernel(plan, other_ref, toeplitz_ref, prior_ref, *refs):
-    *out_refs, columns_ref = refs
-    fill_columns(plan, other_ref[...].astype(jnp.float32), columns_ref)
-    right = prior_ref[:, plan.half_lanes :] + product(toeplitz_ref, columns_ref)
-    products = jnp.concatenate([prior_ref[:, : plan.half_lanes], right], axis=1)
-    back = GROUP - 1 - lax.broadcasted_iota(jnp.int32, (GROUP, LANES), 0)
+    left = prior_ref[:, : plan.half_lanes] + product(toeplitz_ref, columns_ref)
+    for place, block in enumerate(pack(plan, left)):
+        left_ref[place * plan.rows : (place + 1) * plan.rows, :] = block
+    right_ref[...] = prior_ref[:, plan.half_lanes :]
+
+
+def pack(plan, products):
+    width = products.shape[1]
+    back = GROUP - 1 - lax.broadcasted_iota(jnp.int32, (GROUP, width), 0)
+    packed = []
     for place in range(plan.targets):
         whole, rest = [], []
         for member in range(plan.own):
@@ -201,8 +199,18 @@
                 rest.append(tiles[-1][: plan.rest])
         pieces = whole + rest
         if plan.rows > plan.own * plan.fine:
-            pieces.append(jnp.zeros((plan.rows - plan.own * plan.fine, LANES), jnp.float32))
-        out_refs[place][...] = jnp.concatenate(pieces, axis=0).astype(jnp.bfloat16)
+            pieces.append(jnp.zeros((plan.rows - plan.own * plan.fine, width), jnp.float32))
+        packed.append(jnp.concatenate(pieces, axis=0))
+    return packed
+
+
+def finish_kernel(plan, other_ref, toeplitz_ref, left_ref, right_ref, *refs):
+    *out_refs, columns_ref = refs
+    fill_columns(plan, other_ref[...].astype(jnp.float32), columns_ref)
+    right = pack(plan, right_ref[...] + product(toeplitz_ref, columns_ref))
+    for place, out_ref in enumerate(out_refs):
+        rows = slice(place * plan.rows, (place + 1) * plan.rows)
+        out_ref[...] = jnp.concatenate([left_ref[rows, :], right[place]], axis=1).astype(jnp.bfloat16)
 
 
 def spread(plan, values):
@@ -332,17 +340,21 @@
     )
     across, total = lax.optimization_barrier((across, total))
     across_other = swap_cores(across)
-    lagged, total = call(
+    lagged, left, right = call(
         across_kernel,
         "across",
         (across, total),
-        (jax.ShapeDtypeStruct(toeplitz, jnp.bfloat16), sums),
+        (
+            jax.ShapeDtypeStruct(toeplitz, jnp.bfloat16),
+            jax.ShapeDtypeStruct((plan.targets * plan.rows, plan.half_lanes), jnp.float32),
+            jax.ShapeDtypeStruct((height, plan.half_lanes), jnp.float32),
+        ),
         (rows, pltpu.VMEM(columns, jnp.bfloat16)),
     )
     sent = call(
         finish_kernel,
         "finish",
-        (across_other, lagged, total),
+        (across_other, lagged, left, right),
         (jax.ShapeDtypeStruct((plan.rows, LANES), jnp.bfloat16),) * plan.targets,
         (pltpu.VMEM(columns, jnp.bfloat16),),
     )

time: 16.9 us -> 16.9 us (level)
  no operation moved by 1% of the time
where the time goes in v26:
time: 16.9 us; the launch traced here: 16.8 us
  starting transfers between devices  7.98 us (47%)
  waiting for transfers between devices  4.76 us (28%)
  Pallas kernels  3.97 us (23%)
    ppermute x5, starting transfers between devices, swap_blk(): return lax.ppermute(array, ('blk', 'src'), pairs)  6.93 us
    ppermute x5, waiting for transfers between devices, swap_blk(): return lax.ppermute(array, ('blk', 'src'), pairs)  3.16 us
    pallas_call x4, Pallas kernels, call(): pl.pallas_call(functools.partial(kernel, plan), out_shape=outputs, in_spe...  1.9 us
    ppermute x3, waiting for transfers between devices, swap_cores(): return lax.ppermute(array, 'src', [(0, 1), (1, 0)])  1.6 us
    ppermute x3, starting transfers between devices, swap_cores(): return lax.ppermute(array, 'src', [(0, 1), (1, 0)])  1.05 us
    pallas_call x1, Pallas kernels, few_channels(): pl.pallas_call(functools.partial(whiten_kernel, plan), out_shape=pltpu.VM...  1.04 us
    pallas_call x1, Pallas kernels, few_channels(): pl.pallas_call(functools.partial(expand_kernel, plan), out_shape=jax.Shap...  1.03 us
  transfers between devices with their start and end apart: 8, of which 6 were waited for; matrix products, arithmetic and copies ran while one was open for 0% of the time, Pallas kernels for 8%

profile of v26, /device:TPU:0, one launch (start us, length us, event | category | flops | bytes accessed | tf_op | source)
XLA Modules:
  0.0 16.8 jit_solution(6864368372821889530)
XLA Ops:
  0.0 1.0 %whiten.1.whitened_ref.refs_2_ = bf16[48,512]{1,0:T(8,128)(2,1)S(1)} custom-call(f32[24,2,512]{2,1,0:T(2,128)} %traces_hbm.1, s32[2,24]{1,0:T(2,128)} %bitcast.3), custom_call_target="tpu_custom_call" | custom-call | tf_op jit(solution)/shard_map/whiten/pallas_call | solution.py:292
  1.1 0.0 copy-start
  1.1 3.5 %collective-permute-start = (bf16[48,512]{1,0:T(8,128)(2,1)S(1)}, bf16[48,512]{1,0:T(8,128)(2,1)S(1)}, u32[]{:S(2)}, u32[]{:S(2)}) collective-permute-start(bf16[48,512]{1,0:T(8,128)(2,1)S(1)} %whiten.1.whitened_ref.refs_2_), channel_id=1, source_target_pairs={{0,9},{1,8},{2,11},{3,10},{4,13},{5,12},{6,15},{7,14},{8,1},{9,0},... | collective-permute-start | bytes 147464 | tf_op jit(solution)/shard_map/ppermute | solution.py:290
  4.6 0.0 copy-done
  4.6 0.2 choose.1
  4.8 0.7 %collective-permute-start.1 = (bf16[24,512]{1,0:T(8,128)(2,1)S(1)}, bf16[24,512]{1,0:T(8,128)(2,1)S(1)}, u32[]{:S(2)}, u32[]{:S(2)}) collective-permute-start(bf16[24,512]{1,0:T(8,128)(2,1)S(1)} %get-tuple-element.18), channel_id=1, source_target_pairs={{0,1},{1,0},{2,3},{3,2},{4,5},{5,4},{6,7},{7,6},{8,9},{9,8},{10,11... | collective-permute-start | bytes 73736 | tf_op jit(solution)/shard_map/ppermute | solution.py:282
  5.5 0.1 collective-permute-start.2
  5.6 0.8 %collective-permute-done.1.refs_0_ = bf16[24,512]{1,0:T(8,128)(2,1)S(1)} collective-permute-done((bf16[24,512]{1,0:T(8,128)(2,1)S(1)}, bf16[24,512]{1,0:T(8,128)(2,1)S(1)}, u32[]{:S(2)}, u32[]{:S(2)}) %collective-permute-start.1) | collective-permute-done | bytes 24608 | tf_op jit(solution)/shard_map/ppermute | solution.py:282
  6.4 0.3 %collective-permute-done.2.refs_1_ = bf16[24,512]{1,0:T(8,128)(2,1)S(1)} collective-permute-done((bf16[24,512]{1,0:T(8,128)(2,1)S(1)}, bf16[24,512]{1,0:T(8,128)(2,1)S(1)}, u32[]{:S(2)}, u32[]{:S(2)}) %collective-permute-start.2) | collective-permute-done | bytes 24608 | tf_op jit(solution)/shard_map/ppermute | solution.py:282
  6.7 0.7 %near.1.prior_ref = f32[384,256]{1,0:T(8,128)S(1)} custom-call(bf16[24,512]{1,0:T(8,128)(2,1)S(1)} %collective-permute-done.1.refs_0_, bf16[24,512]{1,0:T(8,128)(2,1)S(1)} %collective-permute-done.2.refs_1_, bf16[48,512]{1,0:T(8,128)(2,1)S(1)} %whiten.1.whitened_ref.refs_2_), custom_call_target="tpu_custom_call" | custom-call | tf_op jit(solution)/shard_map/near/pallas_call | solution.py:314
  7.4 0.0 collective-permute-done.mine_ref
  7.4 0.2 %collective-permute-start.3 = (bf16[48,512]{1,0:T(8,128)(2,1)S(1)}, bf16[48,512]{1,0:T(8,128)(2,1)S(1)}, u32[]{:S(2)}, u32[]{:S(2)}) collective-permute-start(bf16[48,512]{1,0:T(8,128)(2,1)S(1)} %collective-permute-done.mine_ref), channel_id=1, source_target_pairs={{0,1},{1,0},{2,3},{3,2},{4,5},{5,4},{6,7},{7,6},{8,9},{9,8},{10,11... | collective-permute-start | bytes 147464 | tf_op jit(solution)/shard_map/ppermute | solution.py:282
  7.6 0.6 %across.1 = (bf16[384,1280]{1,0:T(8,128)(2,1)S(1)}, f32[320,128]{1,0:T(8,128)S(1)}, f32[384,128]{1,0:T(8,128)S(1)}) custom-call(bf16[48,512]{1,0:T(8,128)(2,1)S(1)} %collective-permute-done.mine_ref, f32[384,256]{1,0:T(8,128)S(1)} %near.1.prior_ref), custom_call_target="tpu_custom_call" | custom-call | tf_op jit(solution)/shard_map/across/pallas_call | solution.py:314
  8.2 0.5 %collective-permute-done.3.other_ref = bf16[48,512]{1,0:T(8,128)(2,1)S(1)} collective-permute-done((bf16[48,512]{1,0:T(8,128)(2,1)S(1)}, bf16[48,512]{1,0:T(8,128)(2,1)S(1)}, u32[]{:S(2)}, u32[]{:S(2)}) %collective-permute-start.3) | collective-permute-done | bytes 49184 | tf_op jit(solution)/shard_map/ppermute | solution.py:282
  8.7 0.5 %finish.1 = (bf16[80,256]{1,0:T(8,128)(2,1)S(1)}, bf16[80,256]{1,0:T(8,128)(2,1)S(1)}, bf16[80,256]{1,0:T(8,128)(2,1)S(1)}, bf16[80,256]{1,0:T(8,128)(2,1)S(1)}) custom-call(bf16[48,512]{1,0:T(8,128)(2,1)S(1)} %collective-permute-done.3.other_ref, bf16[384,1280]{1,0:T(8,128)(2,1)S(1)} %get-tuple-element.22.toeplitz_ref, ...), custom_call_target="tpu_custom_call" | custom-call | tf_op jit(solution)/shard_map/finish/pallas_call | solution.py:314
  9.2 2.5 %collective-permute-start.4 = (bf16[80,256]{1,0:T(8,128)(2,1)S(1)}, bf16[80,256]{1,0:T(8,128)(2,1)S(1)}, u32[]{:S(2)}, u32[]{:S(2)}) collective-permute-start(bf16[80,256]{1,0:T(8,128)(2,1)S(1)} %get-tuple-element.25), channel_id=1, source_target_pairs={{0,7},{1,6},{2,5},{3,4},{4,3},{5,2},{6,1},{7,0},{8,15},{9,14},{10,... | collective-permute-start | bytes 122888 | tf_op jit(solution)/shard_map/ppermute | solution.py:290
  11.7 0.5 %collective-permute-start.5 = (bf16[80,256]{1,0:T(8,128)(2,1)S(1)}, bf16[80,256]{1,0:T(8,128)(2,1)S(1)}, u32[]{:S(2)}, u32[]{:S(2)}) collective-permute-start(bf16[80,256]{1,0:T(8,128)(2,1)S(1)} %get-tuple-element.26), channel_id=1, source_target_pairs={{0,3},{1,2},{2,1},{3,0},{4,7},{5,6},{6,5},{7,4},{8,11},{9,10},{10,... | collective-permute-start | bytes 122888 | tf_op jit(solution)/shard_map/ppermute | solution.py:290
  12.2 0.1 collective-permute-start.6
  12.3 0.3 %collective-permute-start.7 = (bf16[80,256]{1,0:T(8,128)(2,1)S(1)}, bf16[80,256]{1,0:T(8,128)(2,1)S(1)}, u32[]{:S(2)}, u32[]{:S(2)}) collective-permute-start(bf16[80,256]{1,0:T(8,128)(2,1)S(1)} %get-tuple-element.28), channel_id=1, source_target_pairs={{0,1},{1,0},{2,3},{3,2},{4,5},{5,4},{6,7},{7,6},{8,9},{9,8},{10,11... | collective-permute-start | bytes 122888 | tf_op jit(solution)/shard_map/ppermute | solution.py:290
  12.6 1.2 %collective-permute-done.4.refs_0_ = bf16[80,256]{1,0:T(8,128)(2,1)S(1)} collective-permute-done((bf16[80,256]{1,0:T(8,128)(2,1)S(1)}, bf16[80,256]{1,0:T(8,128)(2,1)S(1)}, u32[]{:S(2)}, u32[]{:S(2)}) %collective-permute-start.4) | collective-permute-done | bytes 40992 | tf_op jit(solution)/shard_map/ppermute | solution.py:290
  13.8 1.4 %collective-permute-done.5.refs_1_ = bf16[80,256]{1,0:T(8,128)(2,1)S(1)} collective-permute-done((bf16[80,256]{1,0:T(8,128)(2,1)S(1)}, bf16[80,256]{1,0:T(8,128)(2,1)S(1)}, u32[]{:S(2)}, u32[]{:S(2)}) %collective-permute-start.5) | collective-permute-done | bytes 40992 | tf_op jit(solution)/shard_map/ppermute | solution.py:290
  15.2 0.6 %collective-permute-done.6.refs_2_ = bf16[80,256]{1,0:T(8,128)(2,1)S(1)} collective-permute-done((bf16[80,256]{1,0:T(8,128)(2,1)S(1)}, bf16[80,256]{1,0:T(8,128)(2,1)S(1)}, u32[]{:S(2)}, u32[]{:S(2)}) %collective-permute-start.6) | collective-permute-done | bytes 40992 | tf_op jit(solution)/shard_map/ppermute | solution.py:290
  15.7 0.0 collective-permute-done.7.refs_3_
  15.7 1.0 %expand.1 = f32[3,129,256]{2,1,0:T(8,128)} custom-call(bf16[256,256]{1,0:T(8,128)(2,1)S(1)} %get-tuple-element.17.chosen_ref, bf16[80,256]{1,0:T(8,128)(2,1)S(1)} %collective-permute-done.4.refs_0_, bf16[80,256]{1,0:T(8,128)(2,1)S(1)} %collective-permute-done.5.refs_1_, bf16[80,256]{1,0:T(8,128)(2,1)S(1)} %collective-permute-done.6.refs_2_, ...), custom_call_target="tpu_custom_call" | custom-call | tf_op jit(solution)/shard_map/expand/pallas_call | solution.py:363
Async XLA Ops:
  1.1 3.6 %copy-start = (s32[256]{0:T(256)S(1)}, s32[256]{0:T(256)}, u32[]{:S(2)}) copy-start(s32[256]{0:T(256)} %param.5) | copy-start | bytes 3076
  1.1 6.3 %collective-permute-start = (bf16[48,512]{1,0:T(8,128)(2,1)S(1)}, bf16[48,512]{1,0:T(8,128)(2,1)S(1)}, u32[]{:S(2)}, u32[]{:S(2)}) collective-permute-start(bf16[48,512]{1,0:T(8,128)(2,1)S(1)} %whiten.1.whitened_ref.refs_2_), channel_id=1, source_target_pairs={{0,9},{1,8},{2,11},{3,10},{4,13},{5,12},{6,15},{7,14},{8,1},{9,0},... | collective-permute-start | bytes 147464 | tf_op jit(solution)/shard_map/ppermute | solution.py:290
  4.8 1.6 %collective-permute-start.1 = (bf16[24,512]{1,0:T(8,128)(2,1)S(1)}, bf16[24,512]{1,0:T(8,128)(2,1)S(1)}, u32[]{:S(2)}, u32[]{:S(2)}) collective-permute-start(bf16[24,512]{1,0:T(8,128)(2,1)S(1)} %get-tuple-element.18), channel_id=1, source_target_pairs={{0,1},{1,0},{2,3},{3,2},{4,5},{5,4},{6,7},{7,6},{8,9},{9,8},{10,11... | collective-permute-start | bytes 73736 | tf_op jit(solution)/shard_map/ppermute | solution.py:282
  5.5 1.2 %collective-permute-start.2 = (bf16[24,512]{1,0:T(8,128)(2,1)S(1)}, bf16[24,512]{1,0:T(8,128)(2,1)S(1)}, u32[]{:S(2)}, u32[]{:S(2)}) collective-permute-start(bf16[24,512]{1,0:T(8,128)(2,1)S(1)} %get-tuple-element.19), channel_id=1, source_target_pairs={{0,1},{1,0},{2,3},{3,2},{4,5},{5,4},{6,7},{7,6},{8,9},{9,8},{10,11... | collective-permute-start | bytes 73736 | tf_op jit(solution)/shard_map/ppermute | solution.py:282
  7.4 1.3 %collective-permute-start.3 = (bf16[48,512]{1,0:T(8,128)(2,1)S(1)}, bf16[48,512]{1,0:T(8,128)(2,1)S(1)}, u32[]{:S(2)}, u32[]{:S(2)}) collective-permute-start(bf16[48,512]{1,0:T(8,128)(2,1)S(1)} %collective-permute-done.mine_ref), channel_id=1, source_target_pairs={{0,1},{1,0},{2,3},{3,2},{4,5},{5,4},{6,7},{7,6},{8,9},{9,8},{10,11... | collective-permute-start | bytes 147464 | tf_op jit(solution)/shard_map/ppermute | solution.py:282
  9.2 4.6 %collective-permute-start.4 = (bf16[80,256]{1,0:T(8,128)(2,1)S(1)}, bf16[80,256]{1,0:T(8,128)(2,1)S(1)}, u32[]{:S(2)}, u32[]{:S(2)}) collective-permute-start(bf16[80,256]{1,0:T(8,128)(2,1)S(1)} %get-tuple-element.25), channel_id=1, source_target_pairs={{0,7},{1,6},{2,5},{3,4},{4,3},{5,2},{6,1},{7,0},{8,15},{9,14},{10,... | collective-permute-start | bytes 122888 | tf_op jit(solution)/shard_map/ppermute | solution.py:290
  11.7 3.4 %collective-permute-start.5 = (bf16[80,256]{1,0:T(8,128)(2,1)S(1)}, bf16[80,256]{1,0:T(8,128)(2,1)S(1)}, u32[]{:S(2)}, u32[]{:S(2)}) collective-permute-start(bf16[80,256]{1,0:T(8,128)(2,1)S(1)} %get-tuple-element.26), channel_id=1, source_target_pairs={{0,3},{1,2},{2,1},{3,0},{4,7},{5,6},{6,5},{7,4},{8,11},{9,10},{10,... | collective-permute-start | bytes 122888 | tf_op jit(solution)/shard_map/ppermute | solution.py:290
  12.2 3.5 %collective-permute-start.6 = (bf16[80,256]{1,0:T(8,128)(2,1)S(1)}, bf16[80,256]{1,0:T(8,128)(2,1)S(1)}, u32[]{:S(2)}, u32[]{:S(2)}) collective-permute-start(bf16[80,256]{1,0:T(8,128)(2,1)S(1)} %get-tuple-element.27), channel_id=1, source_target_pairs={{0,5},{1,4},{2,7},{3,6},{4,1},{5,0},{6,3},{7,2},{8,13},{9,12},{10,... | collective-permute-start | bytes 122888 | tf_op jit(solution)/shard_map/ppermute | solution.py:290
  12.3 3.4 %collective-permute-start.7 = (bf16[80,256]{1,0:T(8,128)(2,1)S(1)}, bf16[80,256]{1,0:T(8,128)(2,1)S(1)}, u32[]{:S(2)}, u32[]{:S(2)}) collective-permute-start(bf16[80,256]{1,0:T(8,128)(2,1)S(1)} %get-tuple-element.28), channel_id=1, source_target_pairs={{0,1},{1,0},{2,3},{3,2},{4,5},{5,4},{6,7},{7,6},{8,9},{9,8},{10,11... | collective-permute-start | bytes 122888 | tf_op jit(solution)/shard_map/ppermute | solution.py:290

commit v27 on v26

--- a/solution.py
+++ b/solution.py
@@ -13,7 +13,7 @@
 LANES = 256
 IN_PARTS = 4
 GROUP = 8
-HOPS = (3, 1, 2, 0)
+HOPS = (3, 2, 1, 0)
 
 
 def broadcast(value, axis, source):

time: 16.9 us -> 16.7 us (0.988)
  waiting for transfers between devices: 4.76 us -> 4.47 us
    ppermute x5, waiting for transfers between devices: 3.16 us -> 2.87 us  [swap_blk(): return lax.ppermute(array, ('blk', 'src'), pairs)]
  transfers between devices with their start and end apart: 8 -> 8, of which waited for: 6 -> 6; matrix products, arithmetic and copies ran while one was open for 0% -> 0% of each run, Pallas kernels for 8% -> 9%
where the time goes in v27:
time: 16.7 us; the launch traced here: 16.5 us
  starting transfers between devices  7.98 us (48%)
  waiting for transfers between devices  4.47 us (27%)
  Pallas kernels  3.97 us (24%)
    ppermute x5, starting transfers between devices, swap_blk(): return lax.ppermute(array, ('blk', 'src'), pairs)  6.93 us
    ppermute x5, waiting for transfers between devices, swap_blk(): return lax.ppermute(array, ('blk', 'src'), pairs)  2.87 us
    pallas_call x4, Pallas kernels, call(): pl.pallas_call(functools.partial(kernel, plan), out_shape=outputs, in_spe...  1.9 us
    ppermute x3, waiting for transfers between devices, swap_cores(): return lax.ppermute(array, 'src', [(0, 1), (1, 0)])  1.6 us
    ppermute x3, starting transfers between devices, swap_cores(): return lax.ppermute(array, 'src', [(0, 1), (1, 0)])  1.05 us
    pallas_call x1, Pallas kernels, few_channels(): pl.pallas_call(functools.partial(whiten_kernel, plan), out_shape=pltpu.VM...  1.04 us
    pallas_call x1, Pallas kernels, few_channels(): pl.pallas_call(functools.partial(expand_kernel, plan), out_shape=jax.Shap...  1.03 us
  transfers between devices with their start and end apart: 8, of which 6 were waited for; matrix products, arithmetic and copies ran while one was open for 0% of the time, Pallas kernels for 9%

profile of v27, /device:TPU:0, one launch (start us, length us, event | category | flops | bytes accessed | tf_op | source)
XLA Modules:
  0.0 16.5 jit_solution(695928386842975451)
XLA Ops:
  0.0 1.0 %whiten.1.whitened_ref.refs_2_ = bf16[48,512]{1,0:T(8,128)(2,1)S(1)} custom-call(f32[24,2,512]{2,1,0:T(2,128)} %traces_hbm.1, s32[2,24]{1,0:T(2,128)} %bitcast.3), custom_call_target="tpu_custom_call" | custom-call | tf_op jit(solution)/shard_map/whiten/pallas_call | solution.py:292
  1.1 0.0 copy-start
  1.1 3.5 %collective-permute-start = (bf16[48,512]{1,0:T(8,128)(2,1)S(1)}, bf16[48,512]{1,0:T(8,128)(2,1)S(1)}, u32[]{:S(2)}, u32[]{:S(2)}) collective-permute-start(bf16[48,512]{1,0:T(8,128)(2,1)S(1)} %whiten.1.whitened_ref.refs_2_), channel_id=1, source_target_pairs={{0,9},{1,8},{2,11},{3,10},{4,13},{5,12},{6,15},{7,14},{8,1},{9,0},... | collective-permute-start | bytes 147464 | tf_op jit(solution)/shard_map/ppermute | solution.py:290
  4.6 0.0 copy-done
  4.6 0.2 choose.1
  4.8 0.7 %collective-permute-start.1 = (bf16[24,512]{1,0:T(8,128)(2,1)S(1)}, bf16[24,512]{1,0:T(8,128)(2,1)S(1)}, u32[]{:S(2)}, u32[]{:S(2)}) collective-permute-start(bf16[24,512]{1,0:T(8,128)(2,1)S(1)} %get-tuple-element.18), channel_id=1, source_target_pairs={{0,1},{1,0},{2,3},{3,2},{4,5},{5,4},{6,7},{7,6},{8,9},{9,8},{10,11... | collective-permute-start | bytes 73736 | tf_op jit(solution)/shard_map/ppermute | solution.py:282
  5.5 0.1 collective-permute-start.2
  5.6 0.8 %collective-permute-done.1.refs_0_ = bf16[24,512]{1,0:T(8,128)(2,1)S(1)} collective-permute-done((bf16[24,512]{1,0:T(8,128)(2,1)S(1)}, bf16[24,512]{1,0:T(8,128)(2,1)S(1)}, u32[]{:S(2)}, u32[]{:S(2)}) %collective-permute-start.1) | collective-permute-done | bytes 24608 | tf_op jit(solution)/shard_map/ppermute | solution.py:282
  6.4 0.3 %collective-permute-done.2.refs_1_ = bf16[24,512]{1,0:T(8,128)(2,1)S(1)} collective-permute-done((bf16[24,512]{1,0:T(8,128)(2,1)S(1)}, bf16[24,512]{1,0:T(8,128)(2,1)S(1)}, u32[]{:S(2)}, u32[]{:S(2)}) %collective-permute-start.2) | collective-permute-done | bytes 24608 | tf_op jit(solution)/shard_map/ppermute | solution.py:282
  6.7 0.7 %near.1.prior_ref = f32[384,256]{1,0:T(8,128)S(1)} custom-call(bf16[24,512]{1,0:T(8,128)(2,1)S(1)} %collective-permute-done.1.refs_0_, bf16[24,512]{1,0:T(8,128)(2,1)S(1)} %collective-permute-done.2.refs_1_, bf16[48,512]{1,0:T(8,128)(2,1)S(1)} %whiten.1.whitened_ref.refs_2_), custom_call_target="tpu_custom_call" | custom-call | tf_op jit(solution)/shard_map/near/pallas_call | solution.py:314
  7.4 0.0 collective-permute-done.mine_ref
  7.4 0.2 %collective-permute-start.3 = (bf16[48,512]{1,0:T(8,128)(2,1)S(1)}, bf16[48,512]{1,0:T(8,128)(2,1)S(1)}, u32[]{:S(2)}, u32[]{:S(2)}) collective-permute-start(bf16[48,512]{1,0:T(8,128)(2,1)S(1)} %collective-permute-done.mine_ref), channel_id=1, source_target_pairs={{0,1},{1,0},{2,3},{3,2},{4,5},{5,4},{6,7},{7,6},{8,9},{9,8},{10,11... | collective-permute-start | bytes 147464 | tf_op jit(solution)/shard_map/ppermute | solution.py:282
  7.6 0.6 %across.1 = (bf16[384,1280]{1,0:T(8,128)(2,1)S(1)}, f32[320,128]{1,0:T(8,128)S(1)}, f32[384,128]{1,0:T(8,128)S(1)}) custom-call(bf16[48,512]{1,0:T(8,128)(2,1)S(1)} %collective-permute-done.mine_ref, f32[384,256]{1,0:T(8,128)S(1)} %near.1.prior_ref), custom_call_target="tpu_custom_call" | custom-call | tf_op jit(solution)/shard_map/across/pallas_call | solution.py:314
  8.2 0.5 %collective-permute-done.3.other_ref = bf16[48,512]{1,0:T(8,128)(2,1)S(1)} collective-permute-done((bf16[48,512]{1,0:T(8,128)(2,1)S(1)}, bf16[48,512]{1,0:T(8,128)(2,1)S(1)}, u32[]{:S(2)}, u32[]{:S(2)}) %collective-permute-start.3) | collective-permute-done | bytes 49184 | tf_op jit(solution)/shard_map/ppermute | solution.py:282
  8.7 0.5 %finish.1 = (bf16[80,256]{1,0:T(8,128)(2,1)S(1)}, bf16[80,256]{1,0:T(8,128)(2,1)S(1)}, bf16[80,256]{1,0:T(8,128)(2,1)S(1)}, bf16[80,256]{1,0:T(8,128)(2,1)S(1)}) custom-call(bf16[48,512]{1,0:T(8,128)(2,1)S(1)} %collective-permute-done.3.other_ref, bf16[384,1280]{1,0:T(8,128)(2,1)S(1)} %get-tuple-element.22.toeplitz_ref, ...), custom_call_target="tpu_custom_call" | custom-call | tf_op jit(solution)/shard_map/finish/pallas_call | solution.py:314
  9.2 2.5 %collective-permute-start.4 = (bf16[80,256]{1,0:T(8,128)(2,1)S(1)}, bf16[80,256]{1,0:T(8,128)(2,1)S(1)}, u32[]{:S(2)}, u32[]{:S(2)}) collective-permute-start(bf16[80,256]{1,0:T(8,128)(2,1)S(1)} %get-tuple-element.25), channel_id=1, source_target_pairs={{0,7},{1,6},{2,5},{3,4},{4,3},{5,2},{6,1},{7,0},{8,15},{9,14},{10,... | collective-permute-start | bytes 122888 | tf_op jit(solution)/shard_map/ppermute | solution.py:290
  11.7 0.2 %collective-permute-start.5 = (bf16[80,256]{1,0:T(8,128)(2,1)S(1)}, bf16[80,256]{1,0:T(8,128)(2,1)S(1)}, u32[]{:S(2)}, u32[]{:S(2)}) collective-permute-start(bf16[80,256]{1,0:T(8,128)(2,1)S(1)} %get-tuple-element.26), channel_id=1, source_target_pairs={{0,5},{1,4},{2,7},{3,6},{4,1},{5,0},{6,3},{7,2},{8,13},{9,12},{10,... | collective-permute-start | bytes 122888 | tf_op jit(solution)/shard_map/ppermute | solution.py:290
  11.9 0.4 %collective-permute-start.6 = (bf16[80,256]{1,0:T(8,128)(2,1)S(1)}, bf16[80,256]{1,0:T(8,128)(2,1)S(1)}, u32[]{:S(2)}, u32[]{:S(2)}) collective-permute-start(bf16[80,256]{1,0:T(8,128)(2,1)S(1)} %get-tuple-element.27), channel_id=1, source_target_pairs={{0,3},{1,2},{2,1},{3,0},{4,7},{5,6},{6,5},{7,4},{8,11},{9,10},{10,... | collective-permute-start | bytes 122888 | tf_op jit(solution)/shard_map/ppermute | solution.py:290
  12.3 0.3 %collective-permute-start.7 = (bf16[80,256]{1,0:T(8,128)(2,1)S(1)}, bf16[80,256]{1,0:T(8,128)(2,1)S(1)}, u32[]{:S(2)}, u32[]{:S(2)}) collective-permute-start(bf16[80,256]{1,0:T(8,128)(2,1)S(1)} %get-tuple-element.28), channel_id=1, source_target_pairs={{0,1},{1,0},{2,3},{3,2},{4,5},{5,4},{6,7},{7,6},{8,9},{9,8},{10,11... | collective-permute-start | bytes 122888 | tf_op jit(solution)/shard_map/ppermute | solution.py:290
  12.6 1.2 %collective-permute-done.4.refs_0_ = bf16[80,256]{1,0:T(8,128)(2,1)S(1)} collective-permute-done((bf16[80,256]{1,0:T(8,128)(2,1)S(1)}, bf16[80,256]{1,0:T(8,128)(2,1)S(1)}, u32[]{:S(2)}, u32[]{:S(2)}) %collective-permute-start.4) | collective-permute-done | bytes 40992 | tf_op jit(solution)/shard_map/ppermute | solution.py:290
  13.8 1.4 %collective-permute-done.5.refs_1_ = bf16[80,256]{1,0:T(8,128)(2,1)S(1)} collective-permute-done((bf16[80,256]{1,0:T(8,128)(2,1)S(1)}, bf16[80,256]{1,0:T(8,128)(2,1)S(1)}, u32[]{:S(2)}, u32[]{:S(2)}) %collective-permute-start.5) | collective-permute-done | bytes 40992 | tf_op jit(solution)/shard_map/ppermute | solution.py:290
  15.2 0.3 %collective-permute-done.6.refs_2_ = bf16[80,256]{1,0:T(8,128)(2,1)S(1)} collective-permute-done((bf16[80,256]{1,0:T(8,128)(2,1)S(1)}, bf16[80,256]{1,0:T(8,128)(2,1)S(1)}, u32[]{:S(2)}, u32[]{:S(2)}) %collective-permute-start.6) | collective-permute-done | bytes 40992 | tf_op jit(solution)/shard_map/ppermute | solution.py:290
  15.5 0.0 collective-permute-done.7.refs_3_
  15.5 1.0 %expand.1 = f32[3,129,256]{2,1,0:T(8,128)} custom-call(bf16[256,256]{1,0:T(8,128)(2,1)S(1)} %get-tuple-element.17.chosen_ref, bf16[80,256]{1,0:T(8,128)(2,1)S(1)} %collective-permute-done.4.refs_0_, bf16[80,256]{1,0:T(8,128)(2,1)S(1)} %collective-permute-done.5.refs_1_, bf16[80,256]{1,0:T(8,128)(2,1)S(1)} %collective-permute-done.6.refs_2_, ...), custom_call_target="tpu_custom_call" | custom-call | tf_op jit(solution)/shard_map/expand/pallas_call | solution.py:363
Async XLA Ops:
  1.1 3.6 %copy-start = (s32[256]{0:T(256)S(1)}, s32[256]{0:T(256)}, u32[]{:S(2)}) copy-start(s32[256]{0:T(256)} %param.5) | copy-start | bytes 3076
  1.1 6.3 %collective-permute-start = (bf16[48,512]{1,0:T(8,128)(2,1)S(1)}, bf16[48,512]{1,0:T(8,128)(2,1)S(1)}, u32[]{:S(2)}, u32[]{:S(2)}) collective-permute-start(bf16[48,512]{1,0:T(8,128)(2,1)S(1)} %whiten.1.whitened_ref.refs_2_), channel_id=1, source_target_pairs={{0,9},{1,8},{2,11},{3,10},{4,13},{5,12},{6,15},{7,14},{8,1},{9,0},... | collective-permute-start | bytes 147464 | tf_op jit(solution)/shard_map/ppermute | solution.py:290
  4.8 1.6 %collective-permute-start.1 = (bf16[24,512]{1,0:T(8,128)(2,1)S(1)}, bf16[24,512]{1,0:T(8,128)(2,1)S(1)}, u32[]{:S(2)}, u32[]{:S(2)}) collective-permute-start(bf16[24,512]{1,0:T(8,128)(2,1)S(1)} %get-tuple-element.18), channel_id=1, source_target_pairs={{0,1},{1,0},{2,3},{3,2},{4,5},{5,4},{6,7},{7,6},{8,9},{9,8},{10,11... | collective-permute-start | bytes 73736 | tf_op jit(solution)/shard_map/ppermute | solution.py:282
  5.5 1.2 %collective-permute-start.2 = (bf16[24,512]{1,0:T(8,128)(2,1)S(1)}, bf16[24,512]{1,0:T(8,128)(2,1)S(1)}, u32[]{:S(2)}, u32[]{:S(2)}) collective-permute-start(bf16[24,512]{1,0:T(8,128)(2,1)S(1)} %get-tuple-element.19), channel_id=1, source_target_pairs={{0,1},{1,0},{2,3},{3,2},{4,5},{5,4},{6,7},{7,6},{8,9},{9,8},{10,11... | collective-permute-start | bytes 73736 | tf_op jit(solution)/shard_map/ppermute | solution.py:282
  7.4 1.3 %collective-permute-start.3 = (bf16[48,512]{1,0:T(8,128)(2,1)S(1)}, bf16[48,512]{1,0:T(8,128)(2,1)S(1)}, u32[]{:S(2)}, u32[]{:S(2)}) collective-permute-start(bf16[48,512]{1,0:T(8,128)(2,1)S(1)} %collective-permute-done.mine_ref), channel_id=1, source_target_pairs={{0,1},{1,0},{2,3},{3,2},{4,5},{5,4},{6,7},{7,6},{8,9},{9,8},{10,11... | collective-permute-start | bytes 147464 | tf_op jit(solution)/shard_map/ppermute | solution.py:282
  9.2 4.6 %collective-permute-start.4 = (bf16[80,256]{1,0:T(8,128)(2,1)S(1)}, bf16[80,256]{1,0:T(8,128)(2,1)S(1)}, u32[]{:S(2)}, u32[]{:S(2)}) collective-permute-start(bf16[80,256]{1,0:T(8,128)(2,1)S(1)} %get-tuple-element.25), channel_id=1, source_target_pairs={{0,7},{1,6},{2,5},{3,4},{4,3},{5,2},{6,1},{7,0},{8,15},{9,14},{10,... | collective-permute-start | bytes 122888 | tf_op jit(solution)/shard_map/ppermute | solution.py:290
  11.7 3.4 %collective-permute-start.5 = (bf16[80,256]{1,0:T(8,128)(2,1)S(1)}, bf16[80,256]{1,0:T(8,128)(2,1)S(1)}, u32[]{:S(2)}, u32[]{:S(2)}) collective-permute-start(bf16[80,256]{1,0:T(8,128)(2,1)S(1)} %get-tuple-element.26), channel_id=1, source_target_pairs={{0,5},{1,4},{2,7},{3,6},{4,1},{5,0},{6,3},{7,2},{8,13},{9,12},{10,... | collective-permute-start | bytes 122888 | tf_op jit(solution)/shard_map/ppermute | solution.py:290
  11.9 3.5 %collective-permute-start.6 = (bf16[80,256]{1,0:T(8,128)(2,1)S(1)}, bf16[80,256]{1,0:T(8,128)(2,1)S(1)}, u32[]{:S(2)}, u32[]{:S(2)}) collective-permute-start(bf16[80,256]{1,0:T(8,128)(2,1)S(1)} %get-tuple-element.27), channel_id=1, source_target_pairs={{0,3},{1,2},{2,1},{3,0},{4,7},{5,6},{6,5},{7,4},{8,11},{9,10},{10,... | collective-permute-start | bytes 122888 | tf_op jit(solution)/shard_map/ppermute | solution.py:290
  12.3 3.1 %collective-permute-start.7 = (bf16[80,256]{1,0:T(8,128)(2,1)S(1)}, bf16[80,256]{1,0:T(8,128)(2,1)S(1)}, u32[]{:S(2)}, u32[]{:S(2)}) collective-permute-start(bf16[80,256]{1,0:T(8,128)(2,1)S(1)} %get-tuple-element.28), channel_id=1, source_target_pairs={{0,1},{1,0},{2,3},{3,2},{4,5},{5,4},{6,7},{7,6},{8,9},{9,8},{10,11... | collective-permute-start | bytes 122888 | tf_op jit(solution)/shard_map/ppermute | solution.py:290

commit v28 on v27

--- a/solution.py
+++ b/solution.py
@@ -87,8 +87,9 @@
         self.rest = self.fine - self.whole_groups
         rows = self.own * self.fine
         self.rows = -(-rows // 16) * 16
-        self.height = self.own * self.fine_padded
         self.targets = blk_size // 2
+        self.receivers = self.targets * self.own
+        self.lag_rows = -(-self.receivers * self.fine // 32) * 32
         self.norm_factor = 1.0 / math.sqrt(windows * blk_size * segment)
 
     def fits(self):
@@ -100,6 +101,11 @@
             and self.channels % 16 == 0
             and self.windows * self.half % 16 == 0
             and self.blk_size == 8
+            and self.rest > 0
+            and GROUP % self.rest == 0
+            and self.receivers * self.rest % GROUP == 0
+            and self.receivers % 2 == 0
+            and self.receivers * self.whole_groups % 16 == 0
         )
 
 
@@ -127,21 +133,38 @@
     span = plan.span
     me = lax.axis_index("blk")
     filler = jnp.zeros((1, span - plan.segment), jnp.float32)
+    spare = jnp.zeros((plan.lag_rows - plan.receivers * plan.fine, span), jnp.float32)
+    sublane = lax.broadcasted_iota(jnp.int32, (GROUP, span), 0)
     for window in range(plan.windows):
         at = slice(window * span, (window + 1) * span)
-        for place, hop in enumerate(HOPS):
+        spread_rows = []
+        for hop in HOPS:
             for member in range(plan.own):
                 channel = window * plan.half + (me ^ hop) * plan.own + member
                 row = jnp.concatenate([rows_ref[pl.ds(channel, 1), :], filler], axis=1)
-                row = jnp.broadcast_to(row, (GROUP, span))
-                pieces = [
-                    pltpu.roll(row, (MAXLAG - plan.fine_padded + 1 + lag) % span, 1, stride=1, stride_axis=0)
-                    for lag in range(0, plan.fine_padded, GROUP)
-                ]
-                first = place * plan.height + member * plan.fine_padded
-                toeplitz_ref[first : first + plan.fine_padded, at] = jnp.concatenate(pieces, axis=0).astype(
-                    jnp.bfloat16
-                )
+                spread_rows.append(jnp.broadcast_to(row, (GROUP, span)))
+        for first in range(0, plan.receivers, 2):
+            pieces = [
+                pltpu.roll(row, (MAXLAG - plan.whole_groups + 1 + lag) % span, 1, stride=1, stride_axis=0)
+                for row in spread_rows[first : first + 2]
+                for lag in range(0, plan.whole_groups, GROUP)
+            ]
+            start = first * plan.whole_groups
+            toeplitz_ref[start : start + 2 * plan.whole_groups, at] = jnp.concatenate(pieces, axis=0).astype(
+                jnp.bfloat16
+            )
+        pieces = []
+        for first in range(0, plan.receivers, GROUP // plan.rest):
+            mixed = spread_rows[first]
+            for index in range(1, GROUP // plan.rest):
+                mixed = jnp.where(sublane >= index * plan.rest, spread_rows[first + index], mixed)
+            tile = pltpu.roll(mixed, (MAXLAG - plan.whole_groups) % span, 1)
+            for lag in range(1, plan.rest):
+                later = pltpu.roll(mixed, (MAXLAG - plan.whole_groups - lag) % span, 1)
+                tile = jnp.where(sublane % plan.rest == lag, later, tile)
+            pieces.append(tile)
+        start = plan.receivers * plan.whole_groups
+        toeplitz_ref[start:, at] = jnp.concatenate(pieces + [spare], axis=0).astype(jnp.bfloat16)
 
 
 def fill_columns(plan, values, columns_ref):
@@ -187,17 +210,15 @@
     back = GROUP - 1 - lax.broadcasted_iota(jnp.int32, (GROUP, width), 0)
     packed = []
     for place in range(plan.targets):
-        whole, rest = [], []
-        for member in range(plan.own):
-            last = place * plan.height + (member + 1) * plan.fine_padded
-            tiles = [
+        pieces = []
+        for receiver in range(place * plan.own, (place + 1) * plan.own):
+            last = (receiver + 1) * plan.whole_groups
+            pieces += [
                 jnp.take_along_axis(products[last - lag - GROUP : last - lag], back, axis=0)
-                for lag in range(0, plan.fine, GROUP)
+                for lag in range(0, plan.whole_groups, GROUP)
             ]
-            whole += tiles[: plan.whole_groups // GROUP]
-            if plan.rest:
-                rest.append(tiles[-1][: plan.rest])
-        pieces = whole + rest
+        first = plan.receivers * plan.whole_groups + place * plan.own * plan.rest
+        pieces.append(products[first : first + plan.own * plan.rest])
         if plan.rows > plan.own * plan.fine:
             pieces.append(jnp.zeros((plan.rows - plan.own * plan.fine, width), jnp.float32))
         packed.append(jnp.concatenate(pieces, axis=0))
@@ -303,7 +324,7 @@
         name="whiten",
     )(traces, flags)
 
-    height = plan.targets * plan.height
+    height = plan.lag_rows
     width = plan.windows * plan.span
     rows = pltpu.VMEM((packed_rows, plan.segment), jnp.float32)
     toeplitz = (height, width)

time: 16.7 us -> 16.6 us (level)
  transfers between devices with their start and end apart: 8 -> 8, of which waited for: 6 -> 6; matrix products, arithmetic and copies ran while one was open for 0% -> 0% of each run, Pallas kernels for 9% -> 8%
where the time goes in v28:
time: 16.6 us; the launch traced here: 16.4 us
  starting transfers between devices  7.98 us (48%)
  waiting for transfers between devices  4.57 us (28%)
  Pallas kernels  3.84 us (23%)
    ppermute x5, starting transfers between devices, swap_blk(): return lax.ppermute(array, ('blk', 'src'), pairs)  6.93 us
    ppermute x5, waiting for transfers between devices, swap_blk(): return lax.ppermute(array, ('blk', 'src'), pairs)  2.93 us
    pallas_call x4, Pallas kernels, call(): pl.pallas_call(functools.partial(kernel, plan), out_shape=outputs, in_spe...  1.77 us
    ppermute x3, waiting for transfers between devices, swap_cores(): return lax.ppermute(array, 'src', [(0, 1), (1, 0)])  1.64 us
    ppermute x3, starting transfers between devices, swap_cores(): return lax.ppermute(array, 'src', [(0, 1), (1, 0)])  1.05 us
    pallas_call x1, Pallas kernels, few_channels(): pl.pallas_call(functools.partial(whiten_kernel, plan), out_shape=pltpu.VM...  1.04 us
    pallas_call x1, Pallas kernels, few_channels(): pl.pallas_call(functools.partial(expand_kernel, plan), out_shape=jax.Shap...  1.03 us
  transfers between devices with their start and end apart: 8, of which 6 were waited for; matrix products, arithmetic and copies ran while one was open for 0% of the time, Pallas kernels for 8%

profile of v28, /device:TPU:0, one launch (start us, length us, event | category | flops | bytes accessed | tf_op | source)
XLA Modules:
  0.0 16.4 jit_solution(12209775654730767520)
XLA Ops:
  0.0 1.0 %whiten.1.whitened_ref.refs_2_ = bf16[48,512]{1,0:T(8,128)(2,1)S(1)} custom-call(f32[24,2,512]{2,1,0:T(2,128)} %traces_hbm.1, s32[2,24]{1,0:T(2,128)} %bitcast.3), custom_call_target="tpu_custom_call" | custom-call | tf_op jit(solution)/shard_map/whiten/pallas_call | solution.py:313
  1.1 0.0 copy-start
  1.1 3.5 %collective-permute-start = (bf16[48,512]{1,0:T(8,128)(2,1)S(1)}, bf16[48,512]{1,0:T(8,128)(2,1)S(1)}, u32[]{:S(2)}, u32[]{:S(2)}) collective-permute-start(bf16[48,512]{1,0:T(8,128)(2,1)S(1)} %whiten.1.whitened_ref.refs_2_), channel_id=1, source_target_pairs={{0,9},{1,8},{2,11},{3,10},{4,13},{5,12},{6,15},{7,14},{8,1},{9,0},... | collective-permute-start | bytes 147464 | tf_op jit(solution)/shard_map/ppermute | solution.py:311
  4.6 0.0 copy-done
  4.6 0.2 choose.1
  4.8 0.7 %collective-permute-start.1 = (bf16[24,512]{1,0:T(8,128)(2,1)S(1)}, bf16[24,512]{1,0:T(8,128)(2,1)S(1)}, u32[]{:S(2)}, u32[]{:S(2)}) collective-permute-start(bf16[24,512]{1,0:T(8,128)(2,1)S(1)} %get-tuple-element.18), channel_id=1, source_target_pairs={{0,1},{1,0},{2,3},{3,2},{4,5},{5,4},{6,7},{7,6},{8,9},{9,8},{10,11... | collective-permute-start | bytes 73736 | tf_op jit(solution)/shard_map/ppermute | solution.py:303
  5.5 0.1 collective-permute-start.2
  5.6 0.8 %collective-permute-done.1.refs_0_ = bf16[24,512]{1,0:T(8,128)(2,1)S(1)} collective-permute-done((bf16[24,512]{1,0:T(8,128)(2,1)S(1)}, bf16[24,512]{1,0:T(8,128)(2,1)S(1)}, u32[]{:S(2)}, u32[]{:S(2)}) %collective-permute-start.1) | collective-permute-done | bytes 24608 | tf_op jit(solution)/shard_map/ppermute | solution.py:303
  6.4 0.3 %collective-permute-done.2.refs_1_ = bf16[24,512]{1,0:T(8,128)(2,1)S(1)} collective-permute-done((bf16[24,512]{1,0:T(8,128)(2,1)S(1)}, bf16[24,512]{1,0:T(8,128)(2,1)S(1)}, u32[]{:S(2)}, u32[]{:S(2)}) %collective-permute-start.2) | collective-permute-done | bytes 24608 | tf_op jit(solution)/shard_map/ppermute | solution.py:303
  6.7 0.6 %near.1.prior_ref = f32[320,256]{1,0:T(8,128)S(1)} custom-call(bf16[24,512]{1,0:T(8,128)(2,1)S(1)} %collective-permute-done.1.refs_0_, bf16[24,512]{1,0:T(8,128)(2,1)S(1)} %collective-permute-done.2.refs_1_, bf16[48,512]{1,0:T(8,128)(2,1)S(1)} %whiten.1.whitened_ref.refs_2_), custom_call_target="tpu_custom_call" | custom-call | tf_op jit(solution)/shard_map/near/pallas_call | solution.py:335
  7.3 0.0 collective-permute-done.mine_ref
  7.3 0.2 %collective-permute-start.3 = (bf16[48,512]{1,0:T(8,128)(2,1)S(1)}, bf16[48,512]{1,0:T(8,128)(2,1)S(1)}, u32[]{:S(2)}, u32[]{:S(2)}) collective-permute-start(bf16[48,512]{1,0:T(8,128)(2,1)S(1)} %collective-permute-done.mine_ref), channel_id=1, source_target_pairs={{0,1},{1,0},{2,3},{3,2},{4,5},{5,4},{6,7},{7,6},{8,9},{9,8},{10,11... | collective-permute-start | bytes 147464 | tf_op jit(solution)/shard_map/ppermute | solution.py:303
  7.6 0.5 %across.1 = (bf16[320,1280]{1,0:T(8,128)(2,1)S(1)}, f32[320,128]{1,0:T(8,128)S(1)}, f32[320,128]{1,0:T(8,128)S(1)}) custom-call(bf16[48,512]{1,0:T(8,128)(2,1)S(1)} %collective-permute-done.mine_ref, f32[320,256]{1,0:T(8,128)S(1)} %near.1.prior_ref), custom_call_target="tpu_custom_call" | custom-call | tf_op jit(solution)/shard_map/across/pallas_call | solution.py:335
  8.1 0.5 %collective-permute-done.3.other_ref = bf16[48,512]{1,0:T(8,128)(2,1)S(1)} collective-permute-done((bf16[48,512]{1,0:T(8,128)(2,1)S(1)}, bf16[48,512]{1,0:T(8,128)(2,1)S(1)}, u32[]{:S(2)}, u32[]{:S(2)}) %collective-permute-start.3) | collective-permute-done | bytes 49184 | tf_op jit(solution)/shard_map/ppermute | solution.py:303
  8.6 0.4 %finish.1 = (bf16[80,256]{1,0:T(8,128)(2,1)S(1)}, bf16[80,256]{1,0:T(8,128)(2,1)S(1)}, bf16[80,256]{1,0:T(8,128)(2,1)S(1)}, bf16[80,256]{1,0:T(8,128)(2,1)S(1)}) custom-call(bf16[48,512]{1,0:T(8,128)(2,1)S(1)} %collective-permute-done.3.other_ref, bf16[320,1280]{1,0:T(8,128)(2,1)S(1)} %get-tuple-element.22.toeplitz_ref, ...), custom_call_target="tpu_custom_call" | custom-call | tf_op jit(solution)/shard_map/finish/pallas_call | solution.py:335
  9.1 2.6 %collective-permute-start.4 = (bf16[80,256]{1,0:T(8,128)(2,1)S(1)}, bf16[80,256]{1,0:T(8,128)(2,1)S(1)}, u32[]{:S(2)}, u32[]{:S(2)}) collective-permute-start(bf16[80,256]{1,0:T(8,128)(2,1)S(1)} %get-tuple-element.25), channel_id=1, source_target_pairs={{0,7},{1,6},{2,5},{3,4},{4,3},{5,2},{6,1},{7,0},{8,15},{9,14},{10,... | collective-permute-start | bytes 122888 | tf_op jit(solution)/shard_map/ppermute | solution.py:311
  11.7 0.2 collective-permute-start.5
  11.8 0.4 %collective-permute-start.6 = (bf16[80,256]{1,0:T(8,128)(2,1)S(1)}, bf16[80,256]{1,0:T(8,128)(2,1)S(1)}, u32[]{:S(2)}, u32[]{:S(2)}) collective-permute-start(bf16[80,256]{1,0:T(8,128)(2,1)S(1)} %get-tuple-element.27), channel_id=1, source_target_pairs={{0,3},{1,2},{2,1},{3,0},{4,7},{5,6},{6,5},{7,4},{8,11},{9,10},{10,... | collective-permute-start | bytes 122888 | tf_op jit(solution)/shard_map/ppermute | solution.py:311
  12.3 0.2 %collective-permute-start.7 = (bf16[80,256]{1,0:T(8,128)(2,1)S(1)}, bf16[80,256]{1,0:T(8,128)(2,1)S(1)}, u32[]{:S(2)}, u32[]{:S(2)}) collective-permute-start(bf16[80,256]{1,0:T(8,128)(2,1)S(1)} %get-tuple-element.28), channel_id=1, source_target_pairs={{0,1},{1,0},{2,3},{3,2},{4,5},{5,4},{6,7},{7,6},{8,9},{9,8},{10,11... | collective-permute-start | bytes 122888 | tf_op jit(solution)/shard_map/ppermute | solution.py:311
  12.5 1.1 %collective-permute-done.4.refs_0_ = bf16[80,256]{1,0:T(8,128)(2,1)S(1)} collective-permute-done((bf16[80,256]{1,0:T(8,128)(2,1)S(1)}, bf16[80,256]{1,0:T(8,128)(2,1)S(1)}, u32[]{:S(2)}, u32[]{:S(2)}) %collective-permute-start.4) | collective-permute-done | bytes 40992 | tf_op jit(solution)/shard_map/ppermute | solution.py:311
  13.6 1.5 %collective-permute-done.5.refs_1_ = bf16[80,256]{1,0:T(8,128)(2,1)S(1)} collective-permute-done((bf16[80,256]{1,0:T(8,128)(2,1)S(1)}, bf16[80,256]{1,0:T(8,128)(2,1)S(1)}, u32[]{:S(2)}, u32[]{:S(2)}) %collective-permute-start.5) | collective-permute-done | bytes 40992 | tf_op jit(solution)/shard_map/ppermute | solution.py:311
  15.1 0.3 %collective-permute-done.6.refs_2_ = bf16[80,256]{1,0:T(8,128)(2,1)S(1)} collective-permute-done((bf16[80,256]{1,0:T(8,128)(2,1)S(1)}, bf16[80,256]{1,0:T(8,128)(2,1)S(1)}, u32[]{:S(2)}, u32[]{:S(2)}) %collective-permute-start.6) | collective-permute-done | bytes 40992 | tf_op jit(solution)/shard_map/ppermute | solution.py:311
  15.4 0.0 collective-permute-done.7.refs_3_
  15.4 1.0 %expand.1 = f32[3,129,256]{2,1,0:T(8,128)} custom-call(bf16[256,256]{1,0:T(8,128)(2,1)S(1)} %get-tuple-element.17.chosen_ref, bf16[80,256]{1,0:T(8,128)(2,1)S(1)} %collective-permute-done.4.refs_0_, bf16[80,256]{1,0:T(8,128)(2,1)S(1)} %collective-permute-done.5.refs_1_, bf16[80,256]{1,0:T(8,128)(2,1)S(1)} %collective-permute-done.6.refs_2_, ...), custom_call_target="tpu_custom_call" | custom-call | tf_op jit(solution)/shard_map/expand/pallas_call | solution.py:384
Async XLA Ops:
  1.1 3.6 %copy-start = (s32[256]{0:T(256)S(1)}, s32[256]{0:T(256)}, u32[]{:S(2)}) copy-start(s32[256]{0:T(256)} %param.5) | copy-start | bytes 3076
  1.1 6.3 %collective-permute-start = (bf16[48,512]{1,0:T(8,128)(2,1)S(1)}, bf16[48,512]{1,0:T(8,128)(2,1)S(1)}, u32[]{:S(2)}, u32[]{:S(2)}) collective-permute-start(bf16[48,512]{1,0:T(8,128)(2,1)S(1)} %whiten.1.whitened_ref.refs_2_), channel_id=1, source_target_pairs={{0,9},{1,8},{2,11},{3,10},{4,13},{5,12},{6,15},{7,14},{8,1},{9,0},... | collective-permute-start | bytes 147464 | tf_op jit(solution)/shard_map/ppermute | solution.py:311
  4.8 1.6 %collective-permute-start.1 = (bf16[24,512]{1,0:T(8,128)(2,1)S(1)}, bf16[24,512]{1,0:T(8,128)(2,1)S(1)}, u32[]{:S(2)}, u32[]{:S(2)}) collective-permute-start(bf16[24,512]{1,0:T(8,128)(2,1)S(1)} %get-tuple-element.18), channel_id=1, source_target_pairs={{0,1},{1,0},{2,3},{3,2},{4,5},{5,4},{6,7},{7,6},{8,9},{9,8},{10,11... | collective-permute-start | bytes 73736 | tf_op jit(solution)/shard_map/ppermute | solution.py:303
  5.5 1.2 %collective-permute-start.2 = (bf16[24,512]{1,0:T(8,128)(2,1)S(1)}, bf16[24,512]{1,0:T(8,128)(2,1)S(1)}, u32[]{:S(2)}, u32[]{:S(2)}) collective-permute-start(bf16[24,512]{1,0:T(8,128)(2,1)S(1)} %get-tuple-element.19), channel_id=1, source_target_pairs={{0,1},{1,0},{2,3},{3,2},{4,5},{5,4},{6,7},{7,6},{8,9},{9,8},{10,11... | collective-permute-start | bytes 73736 | tf_op jit(solution)/shard_map/ppermute | solution.py:303
  7.3 1.3 %collective-permute-start.3 = (bf16[48,512]{1,0:T(8,128)(2,1)S(1)}, bf16[48,512]{1,0:T(8,128)(2,1)S(1)}, u32[]{:S(2)}, u32[]{:S(2)}) collective-permute-start(bf16[48,512]{1,0:T(8,128)(2,1)S(1)} %collective-permute-done.mine_ref), channel_id=1, source_target_pairs={{0,1},{1,0},{2,3},{3,2},{4,5},{5,4},{6,7},{7,6},{8,9},{9,8},{10,11... | collective-permute-start | bytes 147464 | tf_op jit(solution)/shard_map/ppermute | solution.py:303
  9.1 4.5 %collective-permute-start.4 = (bf16[80,256]{1,0:T(8,128)(2,1)S(1)}, bf16[80,256]{1,0:T(8,128)(2,1)S(1)}, u32[]{:S(2)}, u32[]{:S(2)}) collective-permute-start(bf16[80,256]{1,0:T(8,128)(2,1)S(1)} %get-tuple-element.25), channel_id=1, source_target_pairs={{0,7},{1,6},{2,5},{3,4},{4,3},{5,2},{6,1},{7,0},{8,15},{9,14},{10,... | collective-permute-start | bytes 122888 | tf_op jit(solution)/shard_map/ppermute | solution.py:311
  11.7 3.4 %collective-permute-start.5 = (bf16[80,256]{1,0:T(8,128)(2,1)S(1)}, bf16[80,256]{1,0:T(8,128)(2,1)S(1)}, u32[]{:S(2)}, u32[]{:S(2)}) collective-permute-start(bf16[80,256]{1,0:T(8,128)(2,1)S(1)} %get-tuple-element.26), channel_id=1, source_target_pairs={{0,5},{1,4},{2,7},{3,6},{4,1},{5,0},{6,3},{7,2},{8,13},{9,12},{10,... | collective-permute-start | bytes 122888 | tf_op jit(solution)/shard_map/ppermute | solution.py:311
  11.8 3.6 %collective-permute-start.6 = (bf16[80,256]{1,0:T(8,128)(2,1)S(1)}, bf16[80,256]{1,0:T(8,128)(2,1)S(1)}, u32[]{:S(2)}, u32[]{:S(2)}) collective-permute-start(bf16[80,256]{1,0:T(8,128)(2,1)S(1)} %get-tuple-element.27), channel_id=1, source_target_pairs={{0,3},{1,2},{2,1},{3,0},{4,7},{5,6},{6,5},{7,4},{8,11},{9,10},{10,... | collective-permute-start | bytes 122888 | tf_op jit(solution)/shard_map/ppermute | solution.py:311
  12.3 3.1 %collective-permute-start.7 = (bf16[80,256]{1,0:T(8,128)(2,1)S(1)}, bf16[80,256]{1,0:T(8,128)(2,1)S(1)}, u32[]{:S(2)}, u32[]{:S(2)}) collective-permute-start(bf16[80,256]{1,0:T(8,128)(2,1)S(1)} %get-tuple-element.28), channel_id=1, source_target_pairs={{0,1},{1,0},{2,3},{3,2},{4,5},{5,4},{6,7},{7,6},{8,9},{9,8},{10,11... | collective-permute-start | bytes 122888 | tf_op jit(solution)/shard_map/ppermute | solution.py:311

commit v29 on v28

--- a/solution.py
+++ b/solution.py
@@ -117,15 +117,18 @@
         copies.append(pltpu.make_async_copy(traces_hbm.at[at], traces_ref.at[at], sems.at[index]))
     for copy in copies:
         copy.start()
-    for copy in copies:
+    copies[0].wait()
+    flag_values = [
+        flags_ref[window : window + 1, :].astype(jnp.float32).reshape(plan.half, 1) for window in range(plan.windows)
+    ]
+    for copy in copies[1:]:
         copy.wait()
     pieces = []
     for window in range(plan.windows):
         values = traces_ref[:, window, :]
         centered = values - jnp.mean(values, axis=1, keepdims=True)
         mean_power = jnp.mean(centered * centered, axis=1, keepdims=True)
-        flag_values = flags_ref[window : window + 1, :].astype(jnp.float32).reshape(plan.half, 1)
-        pieces.append(centered * lax.rsqrt(mean_power + 1e-05) * flag_values)
+        pieces.append(centered * lax.rsqrt(mean_power + 1e-05) * flag_values[window])
     out_ref[...] = jnp.concatenate(pieces, axis=0).astype(jnp.bfloat16)
 
 

time: 16.6 us -> 16.6 us (level)
  no operation moved by 1% of the time
where the time goes in v29:
time: 16.6 us; the launch traced here: 16.4 us
  starting transfers between devices  7.98 us (48%)
  waiting for transfers between devices  4.57 us (28%)
  Pallas kernels  3.84 us (23%)
    ppermute x5, starting transfers between devices, swap_blk(): return lax.ppermute(array, ('blk', 'src'), pairs)  6.93 us
    ppermute x5, waiting for transfers between devices, swap_blk(): return lax.ppermute(array, ('blk', 'src'), pairs)  2.93 us
    pallas_call x4, Pallas kernels, call(): pl.pallas_call(functools.partial(kernel, plan), out_shape=outputs, in_spe...  1.77 us
    ppermute x3, waiting for transfers between devices, swap_cores(): return lax.ppermute(array, 'src', [(0, 1), (1, 0)])  1.64 us
    ppermute x3, starting transfers between devices, swap_cores(): return lax.ppermute(array, 'src', [(0, 1), (1, 0)])  1.05 us
    pallas_call x1, Pallas kernels, few_channels(): pl.pallas_call(functools.partial(whiten_kernel, plan), out_shape=pltpu.VM...  1.04 us
    pallas_call x1, Pallas kernels, few_channels(): pl.pallas_call(functools.partial(expand_kernel, plan), out_shape=jax.Shap...  1.03 us
  transfers between devices with their start and end apart: 8, of which 6 were waited for; matrix products, arithmetic and copies ran while one was open for 0% of the time, Pallas kernels for 8%

profile of v29, /device:TPU:0, one launch (start us, length us, event | category | flops | bytes accessed | tf_op | source)
XLA Modules:
  0.0 16.4 jit_solution(11259094079890329208)
XLA Ops:
  0.0 1.0 %whiten.1.whitened_ref.refs_2_ = bf16[48,512]{1,0:T(8,128)(2,1)S(1)} custom-call(f32[24,2,512]{2,1,0:T(2,128)} %traces_hbm.1, s32[2,24]{1,0:T(2,128)} %bitcast.3), custom_call_target="tpu_custom_call" | custom-call | tf_op jit(solution)/shard_map/whiten/pallas_call | solution.py:316
  1.1 0.0 copy-start
  1.1 3.5 %collective-permute-start = (bf16[48,512]{1,0:T(8,128)(2,1)S(1)}, bf16[48,512]{1,0:T(8,128)(2,1)S(1)}, u32[]{:S(2)}, u32[]{:S(2)}) collective-permute-start(bf16[48,512]{1,0:T(8,128)(2,1)S(1)} %whiten.1.whitened_ref.refs_2_), channel_id=1, source_target_pairs={{0,9},{1,8},{2,11},{3,10},{4,13},{5,12},{6,15},{7,14},{8,1},{9,0},... | collective-permute-start | bytes 147464 | tf_op jit(solution)/shard_map/ppermute | solution.py:314
  4.6 0.0 copy-done
  4.6 0.2 choose.1
  4.8 0.7 %collective-permute-start.1 = (bf16[24,512]{1,0:T(8,128)(2,1)S(1)}, bf16[24,512]{1,0:T(8,128)(2,1)S(1)}, u32[]{:S(2)}, u32[]{:S(2)}) collective-permute-start(bf16[24,512]{1,0:T(8,128)(2,1)S(1)} %get-tuple-element.18), channel_id=1, source_target_pairs={{0,1},{1,0},{2,3},{3,2},{4,5},{5,4},{6,7},{7,6},{8,9},{9,8},{10,11... | collective-permute-start | bytes 73736 | tf_op jit(solution)/shard_map/ppermute | solution.py:306
  5.5 0.1 collective-permute-start.2
  5.6 0.8 %collective-permute-done.1.refs_0_ = bf16[24,512]{1,0:T(8,128)(2,1)S(1)} collective-permute-done((bf16[24,512]{1,0:T(8,128)(2,1)S(1)}, bf16[24,512]{1,0:T(8,128)(2,1)S(1)}, u32[]{:S(2)}, u32[]{:S(2)}) %collective-permute-start.1) | collective-permute-done | bytes 24608 | tf_op jit(solution)/shard_map/ppermute | solution.py:306
  6.4 0.3 %collective-permute-done.2.refs_1_ = bf16[24,512]{1,0:T(8,128)(2,1)S(1)} collective-permute-done((bf16[24,512]{1,0:T(8,128)(2,1)S(1)}, bf16[24,512]{1,0:T(8,128)(2,1)S(1)}, u32[]{:S(2)}, u32[]{:S(2)}) %collective-permute-start.2) | collective-permute-done | bytes 24608 | tf_op jit(solution)/shard_map/ppermute | solution.py:306
  6.7 0.6 %near.1.prior_ref = f32[320,256]{1,0:T(8,128)S(1)} custom-call(bf16[24,512]{1,0:T(8,128)(2,1)S(1)} %collective-permute-done.1.refs_0_, bf16[24,512]{1,0:T(8,128)(2,1)S(1)} %collective-permute-done.2.refs_1_, bf16[48,512]{1,0:T(8,128)(2,1)S(1)} %whiten.1.whitened_ref.refs_2_), custom_call_target="tpu_custom_call" | custom-call | tf_op jit(solution)/shard_map/near/pallas_call | solution.py:338
  7.3 0.0 collective-permute-done.mine_ref
  7.3 0.2 %collective-permute-start.3 = (bf16[48,512]{1,0:T(8,128)(2,1)S(1)}, bf16[48,512]{1,0:T(8,128)(2,1)S(1)}, u32[]{:S(2)}, u32[]{:S(2)}) collective-permute-start(bf16[48,512]{1,0:T(8,128)(2,1)S(1)} %collective-permute-done.mine_ref), channel_id=1, source_target_pairs={{0,1},{1,0},{2,3},{3,2},{4,5},{5,4},{6,7},{7,6},{8,9},{9,8},{10,11... | collective-permute-start | bytes 147464 | tf_op jit(solution)/shard_map/ppermute | solution.py:306
  7.6 0.5 %across.1 = (bf16[320,1280]{1,0:T(8,128)(2,1)S(1)}, f32[320,128]{1,0:T(8,128)S(1)}, f32[320,128]{1,0:T(8,128)S(1)}) custom-call(bf16[48,512]{1,0:T(8,128)(2,1)S(1)} %collective-permute-done.mine_ref, f32[320,256]{1,0:T(8,128)S(1)} %near.1.prior_ref), custom_call_target="tpu_custom_call" | custom-call | tf_op jit(solution)/shard_map/across/pallas_call | solution.py:338
  8.1 0.5 %collective-permute-done.3.other_ref = bf16[48,512]{1,0:T(8,128)(2,1)S(1)} collective-permute-done((bf16[48,512]{1,0:T(8,128)(2,1)S(1)}, bf16[48,512]{1,0:T(8,128)(2,1)S(1)}, u32[]{:S(2)}, u32[]{:S(2)}) %collective-permute-start.3) | collective-permute-done | bytes 49184 | tf_op jit(solution)/shard_map/ppermute | solution.py:306
  8.6 0.4 %finish.1 = (bf16[80,256]{1,0:T(8,128)(2,1)S(1)}, bf16[80,256]{1,0:T(8,128)(2,1)S(1)}, bf16[80,256]{1,0:T(8,128)(2,1)S(1)}, bf16[80,256]{1,0:T(8,128)(2,1)S(1)}) custom-call(bf16[48,512]{1,0:T(8,128)(2,1)S(1)} %collective-permute-done.3.other_ref, bf16[320,1280]{1,0:T(8,128)(2,1)S(1)} %get-tuple-element.22.toeplitz_ref, ...), custom_call_target="tpu_custom_call" | custom-call | tf_op jit(solution)/shard_map/finish/pallas_call | solution.py:338
  9.1 2.6 %collective-permute-start.4 = (bf16[80,256]{1,0:T(8,128)(2,1)S(1)}, bf16[80,256]{1,0:T(8,128)(2,1)S(1)}, u32[]{:S(2)}, u32[]{:S(2)}) collective-permute-start(bf16[80,256]{1,0:T(8,128)(2,1)S(1)} %get-tuple-element.25), channel_id=1, source_target_pairs={{0,7},{1,6},{2,5},{3,4},{4,3},{5,2},{6,1},{7,0},{8,15},{9,14},{10,... | collective-permute-start | bytes 122888 | tf_op jit(solution)/shard_map/ppermute | solution.py:314
  11.7 0.2 collective-permute-start.5
  11.8 0.4 %collective-permute-start.6 = (bf16[80,256]{1,0:T(8,128)(2,1)S(1)}, bf16[80,256]{1,0:T(8,128)(2,1)S(1)}, u32[]{:S(2)}, u32[]{:S(2)}) collective-permute-start(bf16[80,256]{1,0:T(8,128)(2,1)S(1)} %get-tuple-element.27), channel_id=1, source_target_pairs={{0,3},{1,2},{2,1},{3,0},{4,7},{5,6},{6,5},{7,4},{8,11},{9,10},{10,... | collective-permute-start | bytes 122888 | tf_op jit(solution)/shard_map/ppermute | solution.py:314
  12.3 0.2 %collective-permute-start.7 = (bf16[80,256]{1,0:T(8,128)(2,1)S(1)}, bf16[80,256]{1,0:T(8,128)(2,1)S(1)}, u32[]{:S(2)}, u32[]{:S(2)}) collective-permute-start(bf16[80,256]{1,0:T(8,128)(2,1)S(1)} %get-tuple-element.28), channel_id=1, source_target_pairs={{0,1},{1,0},{2,3},{3,2},{4,5},{5,4},{6,7},{7,6},{8,9},{9,8},{10,11... | collective-permute-start | bytes 122888 | tf_op jit(solution)/shard_map/ppermute | solution.py:314
  12.5 1.1 %collective-permute-done.4.refs_0_ = bf16[80,256]{1,0:T(8,128)(2,1)S(1)} collective-permute-done((bf16[80,256]{1,0:T(8,128)(2,1)S(1)}, bf16[80,256]{1,0:T(8,128)(2,1)S(1)}, u32[]{:S(2)}, u32[]{:S(2)}) %collective-permute-start.4) | collective-permute-done | bytes 40992 | tf_op jit(solution)/shard_map/ppermute | solution.py:314
  13.6 1.5 %collective-permute-done.5.refs_1_ = bf16[80,256]{1,0:T(8,128)(2,1)S(1)} collective-permute-done((bf16[80,256]{1,0:T(8,128)(2,1)S(1)}, bf16[80,256]{1,0:T(8,128)(2,1)S(1)}, u32[]{:S(2)}, u32[]{:S(2)}) %collective-permute-start.5) | collective-permute-done | bytes 40992 | tf_op jit(solution)/shard_map/ppermute | solution.py:314
  15.1 0.3 %collective-permute-done.6.refs_2_ = bf16[80,256]{1,0:T(8,128)(2,1)S(1)} collective-permute-done((bf16[80,256]{1,0:T(8,128)(2,1)S(1)}, bf16[80,256]{1,0:T(8,128)(2,1)S(1)}, u32[]{:S(2)}, u32[]{:S(2)}) %collective-permute-start.6) | collective-permute-done | bytes 40992 | tf_op jit(solution)/shard_map/ppermute | solution.py:314
  15.4 0.0 collective-permute-done.7.refs_3_
  15.4 1.0 %expand.1 = f32[3,129,256]{2,1,0:T(8,128)} custom-call(bf16[256,256]{1,0:T(8,128)(2,1)S(1)} %get-tuple-element.17.chosen_ref, bf16[80,256]{1,0:T(8,128)(2,1)S(1)} %collective-permute-done.4.refs_0_, bf16[80,256]{1,0:T(8,128)(2,1)S(1)} %collective-permute-done.5.refs_1_, bf16[80,256]{1,0:T(8,128)(2,1)S(1)} %collective-permute-done.6.refs_2_, ...), custom_call_target="tpu_custom_call" | custom-call | tf_op jit(solution)/shard_map/expand/pallas_call | solution.py:387
Async XLA Ops:
  1.1 3.6 %copy-start = (s32[256]{0:T(256)S(1)}, s32[256]{0:T(256)}, u32[]{:S(2)}) copy-start(s32[256]{0:T(256)} %param.5) | copy-start | bytes 3076
  1.1 6.3 %collective-permute-start = (bf16[48,512]{1,0:T(8,128)(2,1)S(1)}, bf16[48,512]{1,0:T(8,128)(2,1)S(1)}, u32[]{:S(2)}, u32[]{:S(2)}) collective-permute-start(bf16[48,512]{1,0:T(8,128)(2,1)S(1)} %whiten.1.whitened_ref.refs_2_), channel_id=1, source_target_pairs={{0,9},{1,8},{2,11},{3,10},{4,13},{5,12},{6,15},{7,14},{8,1},{9,0},... | collective-permute-start | bytes 147464 | tf_op jit(solution)/shard_map/ppermute | solution.py:314
  4.8 1.6 %collective-permute-start.1 = (bf16[24,512]{1,0:T(8,128)(2,1)S(1)}, bf16[24,512]{1,0:T(8,128)(2,1)S(1)}, u32[]{:S(2)}, u32[]{:S(2)}) collective-permute-start(bf16[24,512]{1,0:T(8,128)(2,1)S(1)} %get-tuple-element.18), channel_id=1, source_target_pairs={{0,1},{1,0},{2,3},{3,2},{4,5},{5,4},{6,7},{7,6},{8,9},{9,8},{10,11... | collective-permute-start | bytes 73736 | tf_op jit(solution)/shard_map/ppermute | solution.py:306
  5.5 1.2 %collective-permute-start.2 = (bf16[24,512]{1,0:T(8,128)(2,1)S(1)}, bf16[24,512]{1,0:T(8,128)(2,1)S(1)}, u32[]{:S(2)}, u32[]{:S(2)}) collective-permute-start(bf16[24,512]{1,0:T(8,128)(2,1)S(1)} %get-tuple-element.19), channel_id=1, source_target_pairs={{0,1},{1,0},{2,3},{3,2},{4,5},{5,4},{6,7},{7,6},{8,9},{9,8},{10,11... | collective-permute-start | bytes 73736 | tf_op jit(solution)/shard_map/ppermute | solution.py:306
  7.3 1.3 %collective-permute-start.3 = (bf16[48,512]{1,0:T(8,128)(2,1)S(1)}, bf16[48,512]{1,0:T(8,128)(2,1)S(1)}, u32[]{:S(2)}, u32[]{:S(2)}) collective-permute-start(bf16[48,512]{1,0:T(8,128)(2,1)S(1)} %collective-permute-done.mine_ref), channel_id=1, source_target_pairs={{0,1},{1,0},{2,3},{3,2},{4,5},{5,4},{6,7},{7,6},{8,9},{9,8},{10,11... | collective-permute-start | bytes 147464 | tf_op jit(solution)/shard_map/ppermute | solution.py:306
  9.1 4.5 %collective-permute-start.4 = (bf16[80,256]{1,0:T(8,128)(2,1)S(1)}, bf16[80,256]{1,0:T(8,128)(2,1)S(1)}, u32[]{:S(2)}, u32[]{:S(2)}) collective-permute-start(bf16[80,256]{1,0:T(8,128)(2,1)S(1)} %get-tuple-element.25), channel_id=1, source_target_pairs={{0,7},{1,6},{2,5},{3,4},{4,3},{5,2},{6,1},{7,0},{8,15},{9,14},{10,... | collective-permute-start | bytes 122888 | tf_op jit(solution)/shard_map/ppermute | solution.py:314
  11.7 3.4 %collective-permute-start.5 = (bf16[80,256]{1,0:T(8,128)(2,1)S(1)}, bf16[80,256]{1,0:T(8,128)(2,1)S(1)}, u32[]{:S(2)}, u32[]{:S(2)}) collective-permute-start(bf16[80,256]{1,0:T(8,128)(2,1)S(1)} %get-tuple-element.26), channel_id=1, source_target_pairs={{0,5},{1,4},{2,7},{3,6},{4,1},{5,0},{6,3},{7,2},{8,13},{9,12},{10,... | collective-permute-start | bytes 122888 | tf_op jit(solution)/shard_map/ppermute | solution.py:314
  11.8 3.6 %collective-permute-start.6 = (bf16[80,256]{1,0:T(8,128)(2,1)S(1)}, bf16[80,256]{1,0:T(8,128)(2,1)S(1)}, u32[]{:S(2)}, u32[]{:S(2)}) collective-permute-start(bf16[80,256]{1,0:T(8,128)(2,1)S(1)} %get-tuple-element.27), channel_id=1, source_target_pairs={{0,3},{1,2},{2,1},{3,0},{4,7},{5,6},{6,5},{7,4},{8,11},{9,10},{10,... | collective-permute-start | bytes 122888 | tf_op jit(solution)/shard_map/ppermute | solution.py:314
  12.3 3.1 %collective-permute-start.7 = (bf16[80,256]{1,0:T(8,128)(2,1)S(1)}, bf16[80,256]{1,0:T(8,128)(2,1)S(1)}, u32[]{:S(2)}, u32[]{:S(2)}) collective-permute-start(bf16[80,256]{1,0:T(8,128)(2,1)S(1)} %get-tuple-element.28), channel_id=1, source_target_pairs={{0,1},{1,0},{2,3},{3,2},{4,5},{5,4},{6,7},{7,6},{8,9},{9,8},{10,11... | collective-permute-start | bytes 122888 | tf_op jit(solution)/shard_map/ppermute | solution.py:314

commit v30 on v29

--- a/solution.py
+++ b/solution.py
@@ -345,7 +345,7 @@
             name=name,
         )(*operands)
 
-    across = swap_blk(whitened, plan.targets)
+    across = swap_blk(whitened, plan.blk_size - 2)
     chosen, *same = call(
         choose_kernel,
         "choose",

time: 16.6 us -> 17.6 us (1.060)
  starting transfers between devices: 7.98 us -> 8.99 us
    ppermute x5, starting transfers between devices: 6.93 us -> 7.94 us  [swap_blk(): return lax.ppermute(array, ('blk', 'src'), pairs)]
where the time goes in v30:
time: 17.6 us; the launch traced here: 17.4 us
  starting transfers between devices  8.99 us (51%)
  waiting for transfers between devices  4.52 us (26%)
  Pallas kernels  3.84 us (22%)
    ppermute x5, starting transfers between devices, swap_blk(): return lax.ppermute(array, ('blk', 'src'), pairs)  7.94 us
    ppermute x5, waiting for transfers between devices, swap_blk(): return lax.ppermute(array, ('blk', 'src'), pairs)  2.88 us
    pallas_call x4, Pallas kernels, call(): pl.pallas_call(functools.partial(kernel, plan), out_shape=outputs, in_spe...  1.77 us
    ppermute x3, waiting for transfers between devices, swap_cores(): return lax.ppermute(array, 'src', [(0, 1), (1, 0)])  1.64 us
    ppermute x3, starting transfers between devices, swap_cores(): return lax.ppermute(array, 'src', [(0, 1), (1, 0)])  1.05 us
    pallas_call x1, Pallas kernels, few_channels(): pl.pallas_call(functools.partial(whiten_kernel, plan), out_shape=pltpu.VM...  1.04 us
    pallas_call x1, Pallas kernels, few_channels(): pl.pallas_call(functools.partial(expand_kernel, plan), out_shape=jax.Shap...  1.03 us
  transfers between devices with their start and end apart: 8, of which 6 were waited for; matrix products, arithmetic and copies ran while one was open for 0% of the time, Pallas kernels for 8%

profile of v30, /device:TPU:0, one launch (start us, length us, event | category | flops | bytes accessed | tf_op | source)
XLA Modules:
  0.0 17.4 jit_solution(8626649287740252178)
XLA Ops:
  0.0 1.0 %whiten.1.whitened_ref.refs_2_ = bf16[48,512]{1,0:T(8,128)(2,1)S(1)} custom-call(f32[24,2,512]{2,1,0:T(2,128)} %traces_hbm.1, s32[2,24]{1,0:T(2,128)} %bitcast.3), custom_call_target="tpu_custom_call" | custom-call | tf_op jit(solution)/shard_map/whiten/pallas_call | solution.py:316
  1.1 0.0 copy-start
  1.1 4.6 %collective-permute-start = (bf16[48,512]{1,0:T(8,128)(2,1)S(1)}, bf16[48,512]{1,0:T(8,128)(2,1)S(1)}, u32[]{:S(2)}, u32[]{:S(2)}) collective-permute-start(bf16[48,512]{1,0:T(8,128)(2,1)S(1)} %whiten.1.whitened_ref.refs_2_), channel_id=1, source_target_pairs={{0,13},{1,12},{2,15},{3,14},{4,9},{5,8},{6,11},{7,10},{8,5},{9,4},... | collective-permute-start | bytes 147464 | tf_op jit(solution)/shard_map/ppermute | solution.py:314
  5.6 0.0 copy-done
  5.6 0.2 choose.1
  5.8 0.7 %collective-permute-start.1 = (bf16[24,512]{1,0:T(8,128)(2,1)S(1)}, bf16[24,512]{1,0:T(8,128)(2,1)S(1)}, u32[]{:S(2)}, u32[]{:S(2)}) collective-permute-start(bf16[24,512]{1,0:T(8,128)(2,1)S(1)} %get-tuple-element.18), channel_id=1, source_target_pairs={{0,1},{1,0},{2,3},{3,2},{4,5},{5,4},{6,7},{7,6},{8,9},{9,8},{10,11... | collective-permute-start | bytes 73736 | tf_op jit(solution)/shard_map/ppermute | solution.py:306
  6.5 0.1 collective-permute-start.2
  6.6 0.8 %collective-permute-done.1.refs_0_ = bf16[24,512]{1,0:T(8,128)(2,1)S(1)} collective-permute-done((bf16[24,512]{1,0:T(8,128)(2,1)S(1)}, bf16[24,512]{1,0:T(8,128)(2,1)S(1)}, u32[]{:S(2)}, u32[]{:S(2)}) %collective-permute-start.1) | collective-permute-done | bytes 24608 | tf_op jit(solution)/shard_map/ppermute | solution.py:306
  7.4 0.3 %collective-permute-done.2.refs_1_ = bf16[24,512]{1,0:T(8,128)(2,1)S(1)} collective-permute-done((bf16[24,512]{1,0:T(8,128)(2,1)S(1)}, bf16[24,512]{1,0:T(8,128)(2,1)S(1)}, u32[]{:S(2)}, u32[]{:S(2)}) %collective-permute-start.2) | collective-permute-done | bytes 24608 | tf_op jit(solution)/shard_map/ppermute | solution.py:306
  7.7 0.6 %near.1.prior_ref = f32[320,256]{1,0:T(8,128)S(1)} custom-call(bf16[24,512]{1,0:T(8,128)(2,1)S(1)} %collective-permute-done.1.refs_0_, bf16[24,512]{1,0:T(8,128)(2,1)S(1)} %collective-permute-done.2.refs_1_, bf16[48,512]{1,0:T(8,128)(2,1)S(1)} %whiten.1.whitened_ref.refs_2_), custom_call_target="tpu_custom_call" | custom-call | tf_op jit(solution)/shard_map/near/pallas_call | solution.py:338
  8.3 0.0 collective-permute-done.mine_ref
  8.4 0.2 %collective-permute-start.3 = (bf16[48,512]{1,0:T(8,128)(2,1)S(1)}, bf16[48,512]{1,0:T(8,128)(2,1)S(1)}, u32[]{:S(2)}, u32[]{:S(2)}) collective-permute-start(bf16[48,512]{1,0:T(8,128)(2,1)S(1)} %collective-permute-done.mine_ref), channel_id=1, source_target_pairs={{0,1},{1,0},{2,3},{3,2},{4,5},{5,4},{6,7},{7,6},{8,9},{9,8},{10,11... | collective-permute-start | bytes 147464 | tf_op jit(solution)/shard_map/ppermute | solution.py:306
  8.6 0.5 %across.1 = (bf16[320,1280]{1,0:T(8,128)(2,1)S(1)}, f32[320,128]{1,0:T(8,128)S(1)}, f32[320,128]{1,0:T(8,128)S(1)}) custom-call(bf16[48,512]{1,0:T(8,128)(2,1)S(1)} %collective-permute-done.mine_ref, f32[320,256]{1,0:T(8,128)S(1)} %near.1.prior_ref), custom_call_target="tpu_custom_call" | custom-call | tf_op jit(solution)/shard_map/across/pallas_call | solution.py:338
  9.1 0.5 %collective-permute-done.3.other_ref = bf16[48,512]{1,0:T(8,128)(2,1)S(1)} collective-permute-done((bf16[48,512]{1,0:T(8,128)(2,1)S(1)}, bf16[48,512]{1,0:T(8,128)(2,1)S(1)}, u32[]{:S(2)}, u32[]{:S(2)}) %collective-permute-start.3) | collective-permute-done | bytes 49184 | tf_op jit(solution)/shard_map/ppermute | solution.py:306
  9.7 0.5 %finish.1 = (bf16[80,256]{1,0:T(8,128)(2,1)S(1)}, bf16[80,256]{1,0:T(8,128)(2,1)S(1)}, bf16[80,256]{1,0:T(8,128)(2,1)S(1)}, bf16[80,256]{1,0:T(8,128)(2,1)S(1)}) custom-call(bf16[48,512]{1,0:T(8,128)(2,1)S(1)} %collective-permute-done.3.other_ref, bf16[320,1280]{1,0:T(8,128)(2,1)S(1)} %get-tuple-element.22.toeplitz_ref, ...), custom_call_target="tpu_custom_call" | custom-call | tf_op jit(solution)/shard_map/finish/pallas_call | solution.py:338
  10.1 1.5 %collective-permute-start.4 = (bf16[80,256]{1,0:T(8,128)(2,1)S(1)}, bf16[80,256]{1,0:T(8,128)(2,1)S(1)}, u32[]{:S(2)}, u32[]{:S(2)}) collective-permute-start(bf16[80,256]{1,0:T(8,128)(2,1)S(1)} %get-tuple-element.25), channel_id=1, source_target_pairs={{0,7},{1,6},{2,5},{3,4},{4,3},{5,2},{6,1},{7,0},{8,15},{9,14},{10,... | collective-permute-start | bytes 122888 | tf_op jit(solution)/shard_map/ppermute | solution.py:314
  11.6 1.3 %collective-permute-start.5 = (bf16[80,256]{1,0:T(8,128)(2,1)S(1)}, bf16[80,256]{1,0:T(8,128)(2,1)S(1)}, u32[]{:S(2)}, u32[]{:S(2)}) collective-permute-start(bf16[80,256]{1,0:T(8,128)(2,1)S(1)} %get-tuple-element.26), channel_id=1, source_target_pairs={{0,5},{1,4},{2,7},{3,6},{4,1},{5,0},{6,3},{7,2},{8,13},{9,12},{10,... | collective-permute-start | bytes 122888 | tf_op jit(solution)/shard_map/ppermute | solution.py:314
  12.9 0.3 %collective-permute-start.6 = (bf16[80,256]{1,0:T(8,128)(2,1)S(1)}, bf16[80,256]{1,0:T(8,128)(2,1)S(1)}, u32[]{:S(2)}, u32[]{:S(2)}) collective-permute-start(bf16[80,256]{1,0:T(8,128)(2,1)S(1)} %get-tuple-element.27), channel_id=1, source_target_pairs={{0,3},{1,2},{2,1},{3,0},{4,7},{5,6},{6,5},{7,4},{8,11},{9,10},{10,... | collective-permute-start | bytes 122888 | tf_op jit(solution)/shard_map/ppermute | solution.py:314
  13.2 0.3 %collective-permute-start.7 = (bf16[80,256]{1,0:T(8,128)(2,1)S(1)}, bf16[80,256]{1,0:T(8,128)(2,1)S(1)}, u32[]{:S(2)}, u32[]{:S(2)}) collective-permute-start(bf16[80,256]{1,0:T(8,128)(2,1)S(1)} %get-tuple-element.28), channel_id=1, source_target_pairs={{0,1},{1,0},{2,3},{3,2},{4,5},{5,4},{6,7},{7,6},{8,9},{9,8},{10,11... | collective-permute-start | bytes 122888 | tf_op jit(solution)/shard_map/ppermute | solution.py:314
  13.5 1.2 %collective-permute-done.4.refs_0_ = bf16[80,256]{1,0:T(8,128)(2,1)S(1)} collective-permute-done((bf16[80,256]{1,0:T(8,128)(2,1)S(1)}, bf16[80,256]{1,0:T(8,128)(2,1)S(1)}, u32[]{:S(2)}, u32[]{:S(2)}) %collective-permute-start.4) | collective-permute-done | bytes 40992 | tf_op jit(solution)/shard_map/ppermute | solution.py:314
  14.7 0.8 %collective-permute-done.5.refs_1_ = bf16[80,256]{1,0:T(8,128)(2,1)S(1)} collective-permute-done((bf16[80,256]{1,0:T(8,128)(2,1)S(1)}, bf16[80,256]{1,0:T(8,128)(2,1)S(1)}, u32[]{:S(2)}, u32[]{:S(2)}) %collective-permute-start.5) | collective-permute-done | bytes 40992 | tf_op jit(solution)/shard_map/ppermute | solution.py:314
  15.5 0.9 %collective-permute-done.6.refs_2_ = bf16[80,256]{1,0:T(8,128)(2,1)S(1)} collective-permute-done((bf16[80,256]{1,0:T(8,128)(2,1)S(1)}, bf16[80,256]{1,0:T(8,128)(2,1)S(1)}, u32[]{:S(2)}, u32[]{:S(2)}) %collective-permute-start.6) | collective-permute-done | bytes 40992 | tf_op jit(solution)/shard_map/ppermute | solution.py:314
  16.4 0.0 collective-permute-done.7.refs_3_
  16.4 1.0 %expand.1 = f32[3,129,256]{2,1,0:T(8,128)} custom-call(bf16[256,256]{1,0:T(8,128)(2,1)S(1)} %get-tuple-element.17.chosen_ref, bf16[80,256]{1,0:T(8,128)(2,1)S(1)} %collective-permute-done.4.refs_0_, bf16[80,256]{1,0:T(8,128)(2,1)S(1)} %collective-permute-done.5.refs_1_, bf16[80,256]{1,0:T(8,128)(2,1)S(1)} %collective-permute-done.6.refs_2_, ...), custom_call_target="tpu_custom_call" | custom-call | tf_op jit(solution)/shard_map/expand/pallas_call | solution.py:387
Async XLA Ops:
  1.1 4.6 %copy-start = (s32[256]{0:T(256)S(1)}, s32[256]{0:T(256)}, u32[]{:S(2)}) copy-start(s32[256]{0:T(256)} %param.5) | copy-start | bytes 3076
  1.1 7.3 %collective-permute-start = (bf16[48,512]{1,0:T(8,128)(2,1)S(1)}, bf16[48,512]{1,0:T(8,128)(2,1)S(1)}, u32[]{:S(2)}, u32[]{:S(2)}) collective-permute-start(bf16[48,512]{1,0:T(8,128)(2,1)S(1)} %whiten.1.whitened_ref.refs_2_), channel_id=1, source_target_pairs={{0,13},{1,12},{2,15},{3,14},{4,9},{5,8},{6,11},{7,10},{8,5},{9,4},... | collective-permute-start | bytes 147464 | tf_op jit(solution)/shard_map/ppermute | solution.py:314
  5.8 1.6 %collective-permute-start.1 = (bf16[24,512]{1,0:T(8,128)(2,1)S(1)}, bf16[24,512]{1,0:T(8,128)(2,1)S(1)}, u32[]{:S(2)}, u32[]{:S(2)}) collective-permute-start(bf16[24,512]{1,0:T(8,128)(2,1)S(1)} %get-tuple-element.18), channel_id=1, source_target_pairs={{0,1},{1,0},{2,3},{3,2},{4,5},{5,4},{6,7},{7,6},{8,9},{9,8},{10,11... | collective-permute-start | bytes 73736 | tf_op jit(solution)/shard_map/ppermute | solution.py:306
  6.5 1.2 %collective-permute-start.2 = (bf16[24,512]{1,0:T(8,128)(2,1)S(1)}, bf16[24,512]{1,0:T(8,128)(2,1)S(1)}, u32[]{:S(2)}, u32[]{:S(2)}) collective-permute-start(bf16[24,512]{1,0:T(8,128)(2,1)S(1)} %get-tuple-element.19), channel_id=1, source_target_pairs={{0,1},{1,0},{2,3},{3,2},{4,5},{5,4},{6,7},{7,6},{8,9},{9,8},{10,11... | collective-permute-start | bytes 73736 | tf_op jit(solution)/shard_map/ppermute | solution.py:306
  8.4 1.3 %collective-permute-start.3 = (bf16[48,512]{1,0:T(8,128)(2,1)S(1)}, bf16[48,512]{1,0:T(8,128)(2,1)S(1)}, u32[]{:S(2)}, u32[]{:S(2)}) collective-permute-start(bf16[48,512]{1,0:T(8,128)(2,1)S(1)} %collective-permute-done.mine_ref), channel_id=1, source_target_pairs={{0,1},{1,0},{2,3},{3,2},{4,5},{5,4},{6,7},{7,6},{8,9},{9,8},{10,11... | collective-permute-start | bytes 147464 | tf_op jit(solution)/shard_map/ppermute | solution.py:306
  10.1 4.6 %collective-permute-start.4 = (bf16[80,256]{1,0:T(8,128)(2,1)S(1)}, bf16[80,256]{1,0:T(8,128)(2,1)S(1)}, u32[]{:S(2)}, u32[]{:S(2)}) collective-permute-start(bf16[80,256]{1,0:T(8,128)(2,1)S(1)} %get-tuple-element.25), channel_id=1, source_target_pairs={{0,7},{1,6},{2,5},{3,4},{4,3},{5,2},{6,1},{7,0},{8,15},{9,14},{10,... | collective-permute-start | bytes 122888 | tf_op jit(solution)/shard_map/ppermute | solution.py:314
  11.6 3.9 %collective-permute-start.5 = (bf16[80,256]{1,0:T(8,128)(2,1)S(1)}, bf16[80,256]{1,0:T(8,128)(2,1)S(1)}, u32[]{:S(2)}, u32[]{:S(2)}) collective-permute-start(bf16[80,256]{1,0:T(8,128)(2,1)S(1)} %get-tuple-element.26), channel_id=1, source_target_pairs={{0,5},{1,4},{2,7},{3,6},{4,1},{5,0},{6,3},{7,2},{8,13},{9,12},{10,... | collective-permute-start | bytes 122888 | tf_op jit(solution)/shard_map/ppermute | solution.py:314
  12.9 3.5 %collective-permute-start.6 = (bf16[80,256]{1,0:T(8,128)(2,1)S(1)}, bf16[80,256]{1,0:T(8,128)(2,1)S(1)}, u32[]{:S(2)}, u32[]{:S(2)}) collective-permute-start(bf16[80,256]{1,0:T(8,128)(2,1)S(1)} %get-tuple-element.27), channel_id=1, source_target_pairs={{0,3},{1,2},{2,1},{3,0},{4,7},{5,6},{6,5},{7,4},{8,11},{9,10},{10,... | collective-permute-start | bytes 122888 | tf_op jit(solution)/shard_map/ppermute | solution.py:314
  13.2 3.2 %collective-permute-start.7 = (bf16[80,256]{1,0:T(8,128)(2,1)S(1)}, bf16[80,256]{1,0:T(8,128)(2,1)S(1)}, u32[]{:S(2)}, u32[]{:S(2)}) collective-permute-start(bf16[80,256]{1,0:T(8,128)(2,1)S(1)} %get-tuple-element.28), channel_id=1, source_target_pairs={{0,1},{1,0},{2,3},{3,2},{4,5},{5,4},{6,7},{7,6},{8,9},{9,8},{10,11... | collective-permute-start | bytes 122888 | tf_op jit(solution)/shard_map/ppermute | solution.py:314

commit v31 on v29

--- a/solution.py
+++ b/solution.py
@@ -290,8 +290,11 @@
             count = min(plan.fine, LAG_COUNT - start)
             first = step * plan.fine_padded
             out_ref[member, start : start + count, :] = expanded[first : first + count]
-        copies.append(pltpu.make_async_copy(out_ref.at[member], out_hbm.at[member], sems.at[member]))
-        copies[-1].start()
+        whole = LAG_COUNT // GROUP * GROUP
+        for part, rows in enumerate((pl.ds(0, whole), pl.ds(whole, LAG_COUNT - whole))):
+            at = (member, rows)
+            copies.append(pltpu.make_async_copy(out_ref.at[at], out_hbm.at[at], sems.at[member, part]))
+            copies[-1].start()
     for copy in copies:
         copy.wait()
 
@@ -389,7 +392,7 @@
         out_shape=jax.ShapeDtypeStruct(out_shape, jnp.float32),
         in_specs=[vmem] * (1 + len(arrived)),
         out_specs=pl.BlockSpec(memory_space=pl.ANY),
-        scratch_shapes=[pltpu.VMEM(out_shape, jnp.float32), pltpu.SemaphoreType.DMA((plan.own,))],
+        scratch_shapes=[pltpu.VMEM(out_shape, jnp.float32), pltpu.SemaphoreType.DMA((plan.own, 2))],
         compiler_params=params,
         name="expand",
     )(chosen, *arrived)

time: 16.6 us -> 16.7 us (level)
  no operation moved by 1% of the time
where the time goes in v31:
time: 16.7 us; the launch traced here: 16.5 us
  starting transfers between devices  7.98 us (48%)
  waiting for transfers between devices  4.57 us (27%)
  Pallas kernels  3.87 us (23%)
    ppermute x5, starting transfers between devices, swap_blk(): return lax.ppermute(array, ('blk', 'src'), pairs)  6.93 us
    ppermute x5, waiting for transfers between devices, swap_blk(): return lax.ppermute(array, ('blk', 'src'), pairs)  2.93 us
    pallas_call x4, Pallas kernels, call(): pl.pallas_call(functools.partial(kernel, plan), out_shape=outputs, in_spe...  1.77 us
    ppermute x3, waiting for transfers between devices, swap_cores(): return lax.ppermute(array, 'src', [(0, 1), (1, 0)])  1.64 us
    pallas_call x1, Pallas kernels, few_channels(): pl.pallas_call(functools.partial(expand_kernel, plan), out_shape=jax.Shap...  1.06 us
    ppermute x3, starting transfers between devices, swap_cores(): return lax.ppermute(array, 'src', [(0, 1), (1, 0)])  1.05 us
    pallas_call x1, Pallas kernels, few_channels(): pl.pallas_call(functools.partial(whiten_kernel, plan), out_shape=pltpu.VM...  1.04 us
  transfers between devices with their start and end apart: 8, of which 6 were waited for; matrix products, arithmetic and copies ran while one was open for 0% of the time, Pallas kernels for 8%

profile of v31, /device:TPU:0, one launch (start us, length us, event | category | flops | bytes accessed | tf_op | source)
XLA Modules:
  0.0 16.5 jit_solution(4176793315431177834)
XLA Ops:
  0.0 1.0 %whiten.1.whitened_ref.refs_2_ = bf16[48,512]{1,0:T(8,128)(2,1)S(1)} custom-call(f32[24,2,512]{2,1,0:T(2,128)} %traces_hbm.1, s32[2,24]{1,0:T(2,128)} %bitcast.3), custom_call_target="tpu_custom_call" | custom-call | tf_op jit(solution)/shard_map/whiten/pallas_call | solution.py:319
  1.1 0.0 copy-start
  1.1 3.5 %collective-permute-start = (bf16[48,512]{1,0:T(8,128)(2,1)S(1)}, bf16[48,512]{1,0:T(8,128)(2,1)S(1)}, u32[]{:S(2)}, u32[]{:S(2)}) collective-permute-start(bf16[48,512]{1,0:T(8,128)(2,1)S(1)} %whiten.1.whitened_ref.refs_2_), channel_id=1, source_target_pairs={{0,9},{1,8},{2,11},{3,10},{4,13},{5,12},{6,15},{7,14},{8,1},{9,0},... | collective-permute-start | bytes 147464 | tf_op jit(solution)/shard_map/ppermute | solution.py:317
  4.6 0.0 copy-done
  4.6 0.2 choose.1
  4.8 0.7 %collective-permute-start.1 = (bf16[24,512]{1,0:T(8,128)(2,1)S(1)}, bf16[24,512]{1,0:T(8,128)(2,1)S(1)}, u32[]{:S(2)}, u32[]{:S(2)}) collective-permute-start(bf16[24,512]{1,0:T(8,128)(2,1)S(1)} %get-tuple-element.18), channel_id=1, source_target_pairs={{0,1},{1,0},{2,3},{3,2},{4,5},{5,4},{6,7},{7,6},{8,9},{9,8},{10,11... | collective-permute-start | bytes 73736 | tf_op jit(solution)/shard_map/ppermute | solution.py:309
  5.5 0.1 collective-permute-start.2
  5.6 0.8 %collective-permute-done.1.refs_0_ = bf16[24,512]{1,0:T(8,128)(2,1)S(1)} collective-permute-done((bf16[24,512]{1,0:T(8,128)(2,1)S(1)}, bf16[24,512]{1,0:T(8,128)(2,1)S(1)}, u32[]{:S(2)}, u32[]{:S(2)}) %collective-permute-start.1) | collective-permute-done | bytes 24608 | tf_op jit(solution)/shard_map/ppermute | solution.py:309
  6.4 0.3 %collective-permute-done.2.refs_1_ = bf16[24,512]{1,0:T(8,128)(2,1)S(1)} collective-permute-done((bf16[24,512]{1,0:T(8,128)(2,1)S(1)}, bf16[24,512]{1,0:T(8,128)(2,1)S(1)}, u32[]{:S(2)}, u32[]{:S(2)}) %collective-permute-start.2) | collective-permute-done | bytes 24608 | tf_op jit(solution)/shard_map/ppermute | solution.py:309
  6.7 0.6 %near.1.prior_ref = f32[320,256]{1,0:T(8,128)S(1)} custom-call(bf16[24,512]{1,0:T(8,128)(2,1)S(1)} %collective-permute-done.1.refs_0_, bf16[24,512]{1,0:T(8,128)(2,1)S(1)} %collective-permute-done.2.refs_1_, bf16[48,512]{1,0:T(8,128)(2,1)S(1)} %whiten.1.whitened_ref.refs_2_), custom_call_target="tpu_custom_call" | custom-call | tf_op jit(solution)/shard_map/near/pallas_call | solution.py:341
  7.3 0.0 collective-permute-done.mine_ref
  7.3 0.2 %collective-permute-start.3 = (bf16[48,512]{1,0:T(8,128)(2,1)S(1)}, bf16[48,512]{1,0:T(8,128)(2,1)S(1)}, u32[]{:S(2)}, u32[]{:S(2)}) collective-permute-start(bf16[48,512]{1,0:T(8,128)(2,1)S(1)} %collective-permute-done.mine_ref), channel_id=1, source_target_pairs={{0,1},{1,0},{2,3},{3,2},{4,5},{5,4},{6,7},{7,6},{8,9},{9,8},{10,11... | collective-permute-start | bytes 147464 | tf_op jit(solution)/shard_map/ppermute | solution.py:309
  7.6 0.5 %across.1 = (bf16[320,1280]{1,0:T(8,128)(2,1)S(1)}, f32[320,128]{1,0:T(8,128)S(1)}, f32[320,128]{1,0:T(8,128)S(1)}) custom-call(bf16[48,512]{1,0:T(8,128)(2,1)S(1)} %collective-permute-done.mine_ref, f32[320,256]{1,0:T(8,128)S(1)} %near.1.prior_ref), custom_call_target="tpu_custom_call" | custom-call | tf_op jit(solution)/shard_map/across/pallas_call | solution.py:341
  8.1 0.5 %collective-permute-done.3.other_ref = bf16[48,512]{1,0:T(8,128)(2,1)S(1)} collective-permute-done((bf16[48,512]{1,0:T(8,128)(2,1)S(1)}, bf16[48,512]{1,0:T(8,128)(2,1)S(1)}, u32[]{:S(2)}, u32[]{:S(2)}) %collective-permute-start.3) | collective-permute-done | bytes 49184 | tf_op jit(solution)/shard_map/ppermute | solution.py:309
  8.6 0.4 %finish.1 = (bf16[80,256]{1,0:T(8,128)(2,1)S(1)}, bf16[80,256]{1,0:T(8,128)(2,1)S(1)}, bf16[80,256]{1,0:T(8,128)(2,1)S(1)}, bf16[80,256]{1,0:T(8,128)(2,1)S(1)}) custom-call(bf16[48,512]{1,0:T(8,128)(2,1)S(1)} %collective-permute-done.3.other_ref, bf16[320,1280]{1,0:T(8,128)(2,1)S(1)} %get-tuple-element.22.toeplitz_ref, ...), custom_call_target="tpu_custom_call" | custom-call | tf_op jit(solution)/shard_map/finish/pallas_call | solution.py:341
  9.1 2.6 %collective-permute-start.4 = (bf16[80,256]{1,0:T(8,128)(2,1)S(1)}, bf16[80,256]{1,0:T(8,128)(2,1)S(1)}, u32[]{:S(2)}, u32[]{:S(2)}) collective-permute-start(bf16[80,256]{1,0:T(8,128)(2,1)S(1)} %get-tuple-element.25), channel_id=1, source_target_pairs={{0,7},{1,6},{2,5},{3,4},{4,3},{5,2},{6,1},{7,0},{8,15},{9,14},{10,... | collective-permute-start | bytes 122888 | tf_op jit(solution)/shard_map/ppermute | solution.py:317
  11.7 0.2 collective-permute-start.5
  11.8 0.4 %collective-permute-start.6 = (bf16[80,256]{1,0:T(8,128)(2,1)S(1)}, bf16[80,256]{1,0:T(8,128)(2,1)S(1)}, u32[]{:S(2)}, u32[]{:S(2)}) collective-permute-start(bf16[80,256]{1,0:T(8,128)(2,1)S(1)} %get-tuple-element.27), channel_id=1, source_target_pairs={{0,3},{1,2},{2,1},{3,0},{4,7},{5,6},{6,5},{7,4},{8,11},{9,10},{10,... | collective-permute-start | bytes 122888 | tf_op jit(solution)/shard_map/ppermute | solution.py:317
  12.3 0.2 %collective-permute-start.7 = (bf16[80,256]{1,0:T(8,128)(2,1)S(1)}, bf16[80,256]{1,0:T(8,128)(2,1)S(1)}, u32[]{:S(2)}, u32[]{:S(2)}) collective-permute-start(bf16[80,256]{1,0:T(8,128)(2,1)S(1)} %get-tuple-element.28), channel_id=1, source_target_pairs={{0,1},{1,0},{2,3},{3,2},{4,5},{5,4},{6,7},{7,6},{8,9},{9,8},{10,11... | collective-permute-start | bytes 122888 | tf_op jit(solution)/shard_map/ppermute | solution.py:317
  12.5 1.1 %collective-permute-done.4.refs_0_ = bf16[80,256]{1,0:T(8,128)(2,1)S(1)} collective-permute-done((bf16[80,256]{1,0:T(8,128)(2,1)S(1)}, bf16[80,256]{1,0:T(8,128)(2,1)S(1)}, u32[]{:S(2)}, u32[]{:S(2)}) %collective-permute-start.4) | collective-permute-done | bytes 40992 | tf_op jit(solution)/shard_map/ppermute | solution.py:317
  13.6 1.5 %collective-permute-done.5.refs_1_ = bf16[80,256]{1,0:T(8,128)(2,1)S(1)} collective-permute-done((bf16[80,256]{1,0:T(8,128)(2,1)S(1)}, bf16[80,256]{1,0:T(8,128)(2,1)S(1)}, u32[]{:S(2)}, u32[]{:S(2)}) %collective-permute-start.5) | collective-permute-done | bytes 40992 | tf_op jit(solution)/shard_map/ppermute | solution.py:317
  15.1 0.3 %collective-permute-done.6.refs_2_ = bf16[80,256]{1,0:T(8,128)(2,1)S(1)} collective-permute-done((bf16[80,256]{1,0:T(8,128)(2,1)S(1)}, bf16[80,256]{1,0:T(8,128)(2,1)S(1)}, u32[]{:S(2)}, u32[]{:S(2)}) %collective-permute-start.6) | collective-permute-done | bytes 40992 | tf_op jit(solution)/shard_map/ppermute | solution.py:317
  15.4 0.0 collective-permute-done.7.refs_3_
  15.4 1.1 %expand.1 = f32[3,129,256]{2,1,0:T(8,128)} custom-call(bf16[256,256]{1,0:T(8,128)(2,1)S(1)} %get-tuple-element.17.chosen_ref, bf16[80,256]{1,0:T(8,128)(2,1)S(1)} %collective-permute-done.4.refs_0_, bf16[80,256]{1,0:T(8,128)(2,1)S(1)} %collective-permute-done.5.refs_1_, bf16[80,256]{1,0:T(8,128)(2,1)S(1)} %collective-permute-done.6.refs_2_, ...), custom_call_target="tpu_custom_call" | custom-call | tf_op jit(solution)/shard_map/expand/pallas_call | solution.py:390
Async XLA Ops:
  1.1 3.6 %copy-start = (s32[256]{0:T(256)S(1)}, s32[256]{0:T(256)}, u32[]{:S(2)}) copy-start(s32[256]{0:T(256)} %param.5) | copy-start | bytes 3076
  1.1 6.3 %collective-permute-start = (bf16[48,512]{1,0:T(8,128)(2,1)S(1)}, bf16[48,512]{1,0:T(8,128)(2,1)S(1)}, u32[]{:S(2)}, u32[]{:S(2)}) collective-permute-start(bf16[48,512]{1,0:T(8,128)(2,1)S(1)} %whiten.1.whitened_ref.refs_2_), channel_id=1, source_target_pairs={{0,9},{1,8},{2,11},{3,10},{4,13},{5,12},{6,15},{7,14},{8,1},{9,0},... | collective-permute-start | bytes 147464 | tf_op jit(solution)/shard_map/ppermute | solution.py:317
  4.8 1.6 %collective-permute-start.1 = (bf16[24,512]{1,0:T(8,128)(2,1)S(1)}, bf16[24,512]{1,0:T(8,128)(2,1)S(1)}, u32[]{:S(2)}, u32[]{:S(2)}) collective-permute-start(bf16[24,512]{1,0:T(8,128)(2,1)S(1)} %get-tuple-element.18), channel_id=1, source_target_pairs={{0,1},{1,0},{2,3},{3,2},{4,5},{5,4},{6,7},{7,6},{8,9},{9,8},{10,11... | collective-permute-start | bytes 73736 | tf_op jit(solution)/shard_map/ppermute | solution.py:309
  5.5 1.2 %collective-permute-start.2 = (bf16[24,512]{1,0:T(8,128)(2,1)S(1)}, bf16[24,512]{1,0:T(8,128)(2,1)S(1)}, u32[]{:S(2)}, u32[]{:S(2)}) collective-permute-start(bf16[24,512]{1,0:T(8,128)(2,1)S(1)} %get-tuple-element.19), channel_id=1, source_target_pairs={{0,1},{1,0},{2,3},{3,2},{4,5},{5,4},{6,7},{7,6},{8,9},{9,8},{10,11... | collective-permute-start | bytes 73736 | tf_op jit(solution)/shard_map/ppermute | solution.py:309
  7.3 1.3 %collective-permute-start.3 = (bf16[48,512]{1,0:T(8,128)(2,1)S(1)}, bf16[48,512]{1,0:T(8,128)(2,1)S(1)}, u32[]{:S(2)}, u32[]{:S(2)}) collective-permute-start(bf16[48,512]{1,0:T(8,128)(2,1)S(1)} %collective-permute-done.mine_ref), channel_id=1, source_target_pairs={{0,1},{1,0},{2,3},{3,2},{4,5},{5,4},{6,7},{7,6},{8,9},{9,8},{10,11... | collective-permute-start | bytes 147464 | tf_op jit(solution)/shard_map/ppermute | solution.py:309
  9.1 4.5 %collective-permute-start.4 = (bf16[80,256]{1,0:T(8,128)(2,1)S(1)}, bf16[80,256]{1,0:T(8,128)(2,1)S(1)}, u32[]{:S(2)}, u32[]{:S(2)}) collective-permute-start(bf16[80,256]{1,0:T(8,128)(2,1)S(1)} %get-tuple-element.25), channel_id=1, source_target_pairs={{0,7},{1,6},{2,5},{3,4},{4,3},{5,2},{6,1},{7,0},{8,15},{9,14},{10,... | collective-permute-start | bytes 122888 | tf_op jit(solution)/shard_map/ppermute | solution.py:317
  11.7 3.4 %collective-permute-start.5 = (bf16[80,256]{1,0:T(8,128)(2,1)S(1)}, bf16[80,256]{1,0:T(8,128)(2,1)S(1)}, u32[]{:S(2)}, u32[]{:S(2)}) collective-permute-start(bf16[80,256]{1,0:T(8,128)(2,1)S(1)} %get-tuple-element.26), channel_id=1, source_target_pairs={{0,5},{1,4},{2,7},{3,6},{4,1},{5,0},{6,3},{7,2},{8,13},{9,12},{10,... | collective-permute-start | bytes 122888 | tf_op jit(solution)/shard_map/ppermute | solution.py:317
  11.8 3.6 %collective-permute-start.6 = (bf16[80,256]{1,0:T(8,128)(2,1)S(1)}, bf16[80,256]{1,0:T(8,128)(2,1)S(1)}, u32[]{:S(2)}, u32[]{:S(2)}) collective-permute-start(bf16[80,256]{1,0:T(8,128)(2,1)S(1)} %get-tuple-element.27), channel_id=1, source_target_pairs={{0,3},{1,2},{2,1},{3,0},{4,7},{5,6},{6,5},{7,4},{8,11},{9,10},{10,... | collective-permute-start | bytes 122888 | tf_op jit(solution)/shard_map/ppermute | solution.py:317
  12.3 3.1 %collective-permute-start.7 = (bf16[80,256]{1,0:T(8,128)(2,1)S(1)}, bf16[80,256]{1,0:T(8,128)(2,1)S(1)}, u32[]{:S(2)}, u32[]{:S(2)}) collective-permute-start(bf16[80,256]{1,0:T(8,128)(2,1)S(1)} %get-tuple-element.28), channel_id=1, source_target_pairs={{0,1},{1,0},{2,3},{3,2},{4,5},{5,4},{6,7},{7,6},{8,9},{9,8},{10,11... | collective-permute-start | bytes 122888 | tf_op jit(solution)/shard_map/ppermute | solution.py:317

commit v32 on v29

--- a/solution.py
+++ b/solution.py
@@ -269,11 +269,10 @@
 
 
 def expand_kernel(plan, chosen_ref, *refs):
-    *arrived_refs, out_hbm, out_ref, sems = refs
+    *arrived_refs, out_hbm, out_ref, sem = refs
     total = sum(ref[...].astype(jnp.float32) for ref in arrived_refs) * plan.norm_factor
     chosen = chosen_ref[...]
     filler = jnp.zeros((plan.fine_padded - plan.fine, LANES), jnp.float32)
-    copies = []
     for member in range(plan.own):
         rest = plan.own * plan.whole_groups + member * plan.rest
         rows = jnp.concatenate(
@@ -290,10 +289,9 @@
             count = min(plan.fine, LAG_COUNT - start)
             first = step * plan.fine_padded
             out_ref[member, start : start + count, :] = expanded[first : first + count]
-        copies.append(pltpu.make_async_copy(out_ref.at[member], out_hbm.at[member], sems.at[member]))
-        copies[-1].start()
-    for copy in copies:
-        copy.wait()
+    copy = pltpu.make_async_copy(out_ref, out_hbm, sem)
+    copy.start()
+    copy.wait()
 
 
 def few_channels(plan, traces, valid_flags, source_index):
@@ -389,7 +387,7 @@
         out_shape=jax.ShapeDtypeStruct(out_shape, jnp.float32),
         in_specs=[vmem] * (1 + len(arrived)),
         out_specs=pl.BlockSpec(memory_space=pl.ANY),
-        scratch_shapes=[pltpu.VMEM(out_shape, jnp.float32), pltpu.SemaphoreType.DMA((plan.own,))],
+        scratch_shapes=[pltpu.VMEM(out_shape, jnp.float32), pltpu.SemaphoreType.DMA],
         compiler_params=params,
         name="expand",
     )(chosen, *arrived)

time: 16.6 us -> 16.6 us (level)
  no operation moved by 1% of the time
where the time goes in v32:
time: 16.6 us; the launch traced here: 16.5 us
  starting transfers between devices  7.98 us (48%)
  waiting for transfers between devices  4.57 us (28%)
  Pallas kernels  3.85 us (23%)
    ppermute x5, starting transfers between devices, swap_blk(): return lax.ppermute(array, ('blk', 'src'), pairs)  6.93 us
    ppermute x5, waiting for transfers between devices, swap_blk(): return lax.ppermute(array, ('blk', 'src'), pairs)  2.93 us
    pallas_call x4, Pallas kernels, call(): pl.pallas_call(functools.partial(kernel, plan), out_shape=outputs, in_spe...  1.77 us
    ppermute x3, waiting for transfers between devices, swap_cores(): return lax.ppermute(array, 'src', [(0, 1), (1, 0)])  1.64 us
    ppermute x3, starting transfers between devices, swap_cores(): return lax.ppermute(array, 'src', [(0, 1), (1, 0)])  1.05 us
    pallas_call x1, Pallas kernels, few_channels(): pl.pallas_call(functools.partial(whiten_kernel, plan), out_shape=pltpu.VM...  1.04 us
    pallas_call x1, Pallas kernels, few_channels(): pl.pallas_call(functools.partial(expand_kernel, plan), out_shape=jax.Shap...  1.04 us
  transfers between devices with their start and end apart: 8, of which 6 were waited for; matrix products, arithmetic and copies ran while one was open for 0% of the time, Pallas kernels for 8%

profile of v32, /device:TPU:0, one launch (start us, length us, event | category | flops | bytes accessed | tf_op | source)
XLA Modules:
  0.0 16.5 jit_solution(13030838745750350890)
XLA Ops:
  0.0 1.0 %whiten.1.whitened_ref.refs_2_ = bf16[48,512]{1,0:T(8,128)(2,1)S(1)} custom-call(f32[24,2,512]{2,1,0:T(2,128)} %traces_hbm.1, s32[2,24]{1,0:T(2,128)} %bitcast.3), custom_call_target="tpu_custom_call" | custom-call | tf_op jit(solution)/shard_map/whiten/pallas_call | solution.py:314
  1.1 0.0 copy-start
  1.1 3.5 %collective-permute-start = (bf16[48,512]{1,0:T(8,128)(2,1)S(1)}, bf16[48,512]{1,0:T(8,128)(2,1)S(1)}, u32[]{:S(2)}, u32[]{:S(2)}) collective-permute-start(bf16[48,512]{1,0:T(8,128)(2,1)S(1)} %whiten.1.whitened_ref.refs_2_), channel_id=1, source_target_pairs={{0,9},{1,8},{2,11},{3,10},{4,13},{5,12},{6,15},{7,14},{8,1},{9,0},... | collective-permute-start | bytes 147464 | tf_op jit(solution)/shard_map/ppermute | solution.py:312
  4.6 0.0 copy-done
  4.6 0.2 choose.1
  4.8 0.7 %collective-permute-start.1 = (bf16[24,512]{1,0:T(8,128)(2,1)S(1)}, bf16[24,512]{1,0:T(8,128)(2,1)S(1)}, u32[]{:S(2)}, u32[]{:S(2)}) collective-permute-start(bf16[24,512]{1,0:T(8,128)(2,1)S(1)} %get-tuple-element.18), channel_id=1, source_target_pairs={{0,1},{1,0},{2,3},{3,2},{4,5},{5,4},{6,7},{7,6},{8,9},{9,8},{10,11... | collective-permute-start | bytes 73736 | tf_op jit(solution)/shard_map/ppermute | solution.py:304
  5.5 0.1 collective-permute-start.2
  5.6 0.8 %collective-permute-done.1.refs_0_ = bf16[24,512]{1,0:T(8,128)(2,1)S(1)} collective-permute-done((bf16[24,512]{1,0:T(8,128)(2,1)S(1)}, bf16[24,512]{1,0:T(8,128)(2,1)S(1)}, u32[]{:S(2)}, u32[]{:S(2)}) %collective-permute-start.1) | collective-permute-done | bytes 24608 | tf_op jit(solution)/shard_map/ppermute | solution.py:304
  6.4 0.3 %collective-permute-done.2.refs_1_ = bf16[24,512]{1,0:T(8,128)(2,1)S(1)} collective-permute-done((bf16[24,512]{1,0:T(8,128)(2,1)S(1)}, bf16[24,512]{1,0:T(8,128)(2,1)S(1)}, u32[]{:S(2)}, u32[]{:S(2)}) %collective-permute-start.2) | collective-permute-done | bytes 24608 | tf_op jit(solution)/shard_map/ppermute | solution.py:304
  6.7 0.6 %near.1.prior_ref = f32[320,256]{1,0:T(8,128)S(1)} custom-call(bf16[24,512]{1,0:T(8,128)(2,1)S(1)} %collective-permute-done.1.refs_0_, bf16[24,512]{1,0:T(8,128)(2,1)S(1)} %collective-permute-done.2.refs_1_, bf16[48,512]{1,0:T(8,128)(2,1)S(1)} %whiten.1.whitened_ref.refs_2_), custom_call_target="tpu_custom_call" | custom-call | tf_op jit(solution)/shard_map/near/pallas_call | solution.py:336
  7.3 0.0 collective-permute-done.mine_ref
  7.3 0.2 %collective-permute-start.3 = (bf16[48,512]{1,0:T(8,128)(2,1)S(1)}, bf16[48,512]{1,0:T(8,128)(2,1)S(1)}, u32[]{:S(2)}, u32[]{:S(2)}) collective-permute-start(bf16[48,512]{1,0:T(8,128)(2,1)S(1)} %collective-permute-done.mine_ref), channel_id=1, source_target_pairs={{0,1},{1,0},{2,3},{3,2},{4,5},{5,4},{6,7},{7,6},{8,9},{9,8},{10,11... | collective-permute-start | bytes 147464 | tf_op jit(solution)/shard_map/ppermute | solution.py:304
  7.6 0.5 %across.1 = (bf16[320,1280]{1,0:T(8,128)(2,1)S(1)}, f32[320,128]{1,0:T(8,128)S(1)}, f32[320,128]{1,0:T(8,128)S(1)}) custom-call(bf16[48,512]{1,0:T(8,128)(2,1)S(1)} %collective-permute-done.mine_ref, f32[320,256]{1,0:T(8,128)S(1)} %near.1.prior_ref), custom_call_target="tpu_custom_call" | custom-call | tf_op jit(solution)/shard_map/across/pallas_call | solution.py:336
  8.1 0.5 %collective-permute-done.3.other_ref = bf16[48,512]{1,0:T(8,128)(2,1)S(1)} collective-permute-done((bf16[48,512]{1,0:T(8,128)(2,1)S(1)}, bf16[48,512]{1,0:T(8,128)(2,1)S(1)}, u32[]{:S(2)}, u32[]{:S(2)}) %collective-permute-start.3) | collective-permute-done | bytes 49184 | tf_op jit(solution)/shard_map/ppermute | solution.py:304
  8.6 0.4 %finish.1 = (bf16[80,256]{1,0:T(8,128)(2,1)S(1)}, bf16[80,256]{1,0:T(8,128)(2,1)S(1)}, bf16[80,256]{1,0:T(8,128)(2,1)S(1)}, bf16[80,256]{1,0:T(8,128)(2,1)S(1)}) custom-call(bf16[48,512]{1,0:T(8,128)(2,1)S(1)} %collective-permute-done.3.other_ref, bf16[320,1280]{1,0:T(8,128)(2,1)S(1)} %get-tuple-element.22.toeplitz_ref, ...), custom_call_target="tpu_custom_call" | custom-call | tf_op jit(solution)/shard_map/finish/pallas_call | solution.py:336
  9.1 2.6 %collective-permute-start.4 = (bf16[80,256]{1,0:T(8,128)(2,1)S(1)}, bf16[80,256]{1,0:T(8,128)(2,1)S(1)}, u32[]{:S(2)}, u32[]{:S(2)}) collective-permute-start(bf16[80,256]{1,0:T(8,128)(2,1)S(1)} %get-tuple-element.25), channel_id=1, source_target_pairs={{0,7},{1,6},{2,5},{3,4},{4,3},{5,2},{6,1},{7,0},{8,15},{9,14},{10,... | collective-permute-start | bytes 122888 | tf_op jit(solution)/shard_map/ppermute | solution.py:312
  11.7 0.2 collective-permute-start.5
  11.8 0.4 %collective-permute-start.6 = (bf16[80,256]{1,0:T(8,128)(2,1)S(1)}, bf16[80,256]{1,0:T(8,128)(2,1)S(1)}, u32[]{:S(2)}, u32[]{:S(2)}) collective-permute-start(bf16[80,256]{1,0:T(8,128)(2,1)S(1)} %get-tuple-element.27), channel_id=1, source_target_pairs={{0,3},{1,2},{2,1},{3,0},{4,7},{5,6},{6,5},{7,4},{8,11},{9,10},{10,... | collective-permute-start | bytes 122888 | tf_op jit(solution)/shard_map/ppermute | solution.py:312
  12.3 0.2 %collective-permute-start.7 = (bf16[80,256]{1,0:T(8,128)(2,1)S(1)}, bf16[80,256]{1,0:T(8,128)(2,1)S(1)}, u32[]{:S(2)}, u32[]{:S(2)}) collective-permute-start(bf16[80,256]{1,0:T(8,128)(2,1)S(1)} %get-tuple-element.28), channel_id=1, source_target_pairs={{0,1},{1,0},{2,3},{3,2},{4,5},{5,4},{6,7},{7,6},{8,9},{9,8},{10,11... | collective-permute-start | bytes 122888 | tf_op jit(solution)/shard_map/ppermute | solution.py:312
  12.5 1.1 %collective-permute-done.4.refs_0_ = bf16[80,256]{1,0:T(8,128)(2,1)S(1)} collective-permute-done((bf16[80,256]{1,0:T(8,128)(2,1)S(1)}, bf16[80,256]{1,0:T(8,128)(2,1)S(1)}, u32[]{:S(2)}, u32[]{:S(2)}) %collective-permute-start.4) | collective-permute-done | bytes 40992 | tf_op jit(solution)/shard_map/ppermute | solution.py:312
  13.6 1.5 %collective-permute-done.5.refs_1_ = bf16[80,256]{1,0:T(8,128)(2,1)S(1)} collective-permute-done((bf16[80,256]{1,0:T(8,128)(2,1)S(1)}, bf16[80,256]{1,0:T(8,128)(2,1)S(1)}, u32[]{:S(2)}, u32[]{:S(2)}) %collective-permute-start.5) | collective-permute-done | bytes 40992 | tf_op jit(solution)/shard_map/ppermute | solution.py:312
  15.1 0.3 %collective-permute-done.6.refs_2_ = bf16[80,256]{1,0:T(8,128)(2,1)S(1)} collective-permute-done((bf16[80,256]{1,0:T(8,128)(2,1)S(1)}, bf16[80,256]{1,0:T(8,128)(2,1)S(1)}, u32[]{:S(2)}, u32[]{:S(2)}) %collective-permute-start.6) | collective-permute-done | bytes 40992 | tf_op jit(solution)/shard_map/ppermute | solution.py:312
  15.4 0.0 collective-permute-done.7.refs_3_
  15.4 1.0 %expand.1 = f32[3,129,256]{2,1,0:T(8,128)} custom-call(bf16[256,256]{1,0:T(8,128)(2,1)S(1)} %get-tuple-element.17.chosen_ref, bf16[80,256]{1,0:T(8,128)(2,1)S(1)} %collective-permute-done.4.refs_0_, bf16[80,256]{1,0:T(8,128)(2,1)S(1)} %collective-permute-done.5.refs_1_, bf16[80,256]{1,0:T(8,128)(2,1)S(1)} %collective-permute-done.6.refs_2_, ...), custom_call_target="tpu_custom_call" | custom-call | tf_op jit(solution)/shard_map/expand/pallas_call | solution.py:385
Async XLA Ops:
  1.1 3.6 %copy-start = (s32[256]{0:T(256)S(1)}, s32[256]{0:T(256)}, u32[]{:S(2)}) copy-start(s32[256]{0:T(256)} %param.5) | copy-start | bytes 3076
  1.1 6.3 %collective-permute-start = (bf16[48,512]{1,0:T(8,128)(2,1)S(1)}, bf16[48,512]{1,0:T(8,128)(2,1)S(1)}, u32[]{:S(2)}, u32[]{:S(2)}) collective-permute-start(bf16[48,512]{1,0:T(8,128)(2,1)S(1)} %whiten.1.whitened_ref.refs_2_), channel_id=1, source_target_pairs={{0,9},{1,8},{2,11},{3,10},{4,13},{5,12},{6,15},{7,14},{8,1},{9,0},... | collective-permute-start | bytes 147464 | tf_op jit(solution)/shard_map/ppermute | solution.py:312
  4.8 1.6 %collective-permute-start.1 = (bf16[24,512]{1,0:T(8,128)(2,1)S(1)}, bf16[24,512]{1,0:T(8,128)(2,1)S(1)}, u32[]{:S(2)}, u32[]{:S(2)}) collective-permute-start(bf16[24,512]{1,0:T(8,128)(2,1)S(1)} %get-tuple-element.18), channel_id=1, source_target_pairs={{0,1},{1,0},{2,3},{3,2},{4,5},{5,4},{6,7},{7,6},{8,9},{9,8},{10,11... | collective-permute-start | bytes 73736 | tf_op jit(solution)/shard_map/ppermute | solution.py:304
  5.5 1.2 %collective-permute-start.2 = (bf16[24,512]{1,0:T(8,128)(2,1)S(1)}, bf16[24,512]{1,0:T(8,128)(2,1)S(1)}, u32[]{:S(2)}, u32[]{:S(2)}) collective-permute-start(bf16[24,512]{1,0:T(8,128)(2,1)S(1)} %get-tuple-element.19), channel_id=1, source_target_pairs={{0,1},{1,0},{2,3},{3,2},{4,5},{5,4},{6,7},{7,6},{8,9},{9,8},{10,11... | collective-permute-start | bytes 73736 | tf_op jit(solution)/shard_map/ppermute | solution.py:304
  7.3 1.3 %collective-permute-start.3 = (bf16[48,512]{1,0:T(8,128)(2,1)S(1)}, bf16[48,512]{1,0:T(8,128)(2,1)S(1)}, u32[]{:S(2)}, u32[]{:S(2)}) collective-permute-start(bf16[48,512]{1,0:T(8,128)(2,1)S(1)} %collective-permute-done.mine_ref), channel_id=1, source_target_pairs={{0,1},{1,0},{2,3},{3,2},{4,5},{5,4},{6,7},{7,6},{8,9},{9,8},{10,11... | collective-permute-start | bytes 147464 | tf_op jit(solution)/shard_map/ppermute | solution.py:304
  9.1 4.5 %collective-permute-start.4 = (bf16[80,256]{1,0:T(8,128)(2,1)S(1)}, bf16[80,256]{1,0:T(8,128)(2,1)S(1)}, u32[]{:S(2)}, u32[]{:S(2)}) collective-permute-start(bf16[80,256]{1,0:T(8,128)(2,1)S(1)} %get-tuple-element.25), channel_id=1, source_target_pairs={{0,7},{1,6},{2,5},{3,4},{4,3},{5,2},{6,1},{7,0},{8,15},{9,14},{10,... | collective-permute-start | bytes 122888 | tf_op jit(solution)/shard_map/ppermute | solution.py:312
  11.7 3.4 %collective-permute-start.5 = (bf16[80,256]{1,0:T(8,128)(2,1)S(1)}, bf16[80,256]{1,0:T(8,128)(2,1)S(1)}, u32[]{:S(2)}, u32[]{:S(2)}) collective-permute-start(bf16[80,256]{1,0:T(8,128)(2,1)S(1)} %get-tuple-element.26), channel_id=1, source_target_pairs={{0,5},{1,4},{2,7},{3,6},{4,1},{5,0},{6,3},{7,2},{8,13},{9,12},{10,... | collective-permute-start | bytes 122888 | tf_op jit(solution)/shard_map/ppermute | solution.py:312
  11.8 3.6 %collective-permute-start.6 = (bf16[80,256]{1,0:T(8,128)(2,1)S(1)}, bf16[80,256]{1,0:T(8,128)(2,1)S(1)}, u32[]{:S(2)}, u32[]{:S(2)}) collective-permute-start(bf16[80,256]{1,0:T(8,128)(2,1)S(1)} %get-tuple-element.27), channel_id=1, source_target_pairs={{0,3},{1,2},{2,1},{3,0},{4,7},{5,6},{6,5},{7,4},{8,11},{9,10},{10,... | collective-permute-start | bytes 122888 | tf_op jit(solution)/shard_map/ppermute | solution.py:312
  12.3 3.1 %collective-permute-start.7 = (bf16[80,256]{1,0:T(8,128)(2,1)S(1)}, bf16[80,256]{1,0:T(8,128)(2,1)S(1)}, u32[]{:S(2)}, u32[]{:S(2)}) collective-permute-start(bf16[80,256]{1,0:T(8,128)(2,1)S(1)} %get-tuple-element.28), channel_id=1, source_target_pairs={{0,1},{1,0},{2,3},{3,2},{4,5},{5,4},{6,7},{7,6},{8,9},{9,8},{10,11... | collective-permute-start | bytes 122888 | tf_op jit(solution)/shard_map/ppermute | solution.py:312

commit v33 on v29

--- a/solution.py
+++ b/solution.py
@@ -11,7 +11,7 @@
 MAXLAG = 64
 LAG_COUNT = 2 * MAXLAG + 1
 LANES = 256
-IN_PARTS = 4
+IN_PARTS = 8
 GROUP = 8
 HOPS = (3, 2, 1, 0)
 

time: 16.6 us -> 16.8 us (1.012)
  no operation moved by 1% of the time
where the time goes in v33:
time: 16.8 us; the launch traced here: 16.5 us
  starting transfers between devices  7.98 us (48%)
  waiting for transfers between devices  4.57 us (27%)
  Pallas kernels  3.91 us (23%)
    ppermute x5, starting transfers between devices, swap_blk(): return lax.ppermute(array, ('blk', 'src'), pairs)  6.93 us
    ppermute x5, waiting for transfers between devices, swap_blk(): return lax.ppermute(array, ('blk', 'src'), pairs)  2.94 us
    pallas_call x4, Pallas kernels, call(): pl.pallas_call(functools.partial(kernel, plan), out_shape=outputs, in_spe...  1.77 us
    ppermute x3, waiting for transfers between devices, swap_cores(): return lax.ppermute(array, 'src', [(0, 1), (1, 0)])  1.64 us
    pallas_call x1, Pallas kernels, few_channels(): pl.pallas_call(functools.partial(whiten_kernel, plan), out_shape=pltpu.VM...  1.11 us
    ppermute x3, starting transfers between devices, swap_cores(): return lax.ppermute(array, 'src', [(0, 1), (1, 0)])  1.05 us
    pallas_call x1, Pallas kernels, few_channels(): pl.pallas_call(functools.partial(expand_kernel, plan), out_shape=jax.Shap...  1.03 us
  transfers between devices with their start and end apart: 8, of which 6 were waited for; matrix products, arithmetic and copies ran while one was open for 0% of the time, Pallas kernels for 8%

profile of v33, /device:TPU:0, one launch (start us, length us, event | category | flops | bytes accessed | tf_op | source)
XLA Modules:
  0.0 16.5 jit_solution(11848264788131637739)
XLA Ops:
  0.0 1.1 %whiten.1.whitened_ref.refs_2_ = bf16[48,512]{1,0:T(8,128)(2,1)S(1)} custom-call(f32[24,2,512]{2,1,0:T(2,128)} %traces_hbm.1, s32[2,24]{1,0:T(2,128)} %bitcast.3), custom_call_target="tpu_custom_call" | custom-call | tf_op jit(solution)/shard_map/whiten/pallas_call | solution.py:316
  1.1 0.0 copy-start
  1.1 3.5 %collective-permute-start = (bf16[48,512]{1,0:T(8,128)(2,1)S(1)}, bf16[48,512]{1,0:T(8,128)(2,1)S(1)}, u32[]{:S(2)}, u32[]{:S(2)}) collective-permute-start(bf16[48,512]{1,0:T(8,128)(2,1)S(1)} %whiten.1.whitened_ref.refs_2_), channel_id=1, source_target_pairs={{0,9},{1,8},{2,11},{3,10},{4,13},{5,12},{6,15},{7,14},{8,1},{9,0},... | collective-permute-start | bytes 147464 | tf_op jit(solution)/shard_map/ppermute | solution.py:314
  4.7 0.0 copy-done
  4.7 0.2 choose.1
  4.8 0.7 %collective-permute-start.1 = (bf16[24,512]{1,0:T(8,128)(2,1)S(1)}, bf16[24,512]{1,0:T(8,128)(2,1)S(1)}, u32[]{:S(2)}, u32[]{:S(2)}) collective-permute-start(bf16[24,512]{1,0:T(8,128)(2,1)S(1)} %get-tuple-element.18), channel_id=1, source_target_pairs={{0,1},{1,0},{2,3},{3,2},{4,5},{5,4},{6,7},{7,6},{8,9},{9,8},{10,11... | collective-permute-start | bytes 73736 | tf_op jit(solution)/shard_map/ppermute | solution.py:306
  5.6 0.1 collective-permute-start.2
  5.7 0.8 %collective-permute-done.1.refs_0_ = bf16[24,512]{1,0:T(8,128)(2,1)S(1)} collective-permute-done((bf16[24,512]{1,0:T(8,128)(2,1)S(1)}, bf16[24,512]{1,0:T(8,128)(2,1)S(1)}, u32[]{:S(2)}, u32[]{:S(2)}) %collective-permute-start.1) | collective-permute-done | bytes 24608 | tf_op jit(solution)/shard_map/ppermute | solution.py:306
  6.4 0.3 %collective-permute-done.2.refs_1_ = bf16[24,512]{1,0:T(8,128)(2,1)S(1)} collective-permute-done((bf16[24,512]{1,0:T(8,128)(2,1)S(1)}, bf16[24,512]{1,0:T(8,128)(2,1)S(1)}, u32[]{:S(2)}, u32[]{:S(2)}) %collective-permute-start.2) | collective-permute-done | bytes 24608 | tf_op jit(solution)/shard_map/ppermute | solution.py:306
  6.8 0.6 %near.1.prior_ref = f32[320,256]{1,0:T(8,128)S(1)} custom-call(bf16[24,512]{1,0:T(8,128)(2,1)S(1)} %collective-permute-done.1.refs_0_, bf16[24,512]{1,0:T(8,128)(2,1)S(1)} %collective-permute-done.2.refs_1_, bf16[48,512]{1,0:T(8,128)(2,1)S(1)} %whiten.1.whitened_ref.refs_2_), custom_call_target="tpu_custom_call" | custom-call | tf_op jit(solution)/shard_map/near/pallas_call | solution.py:338
  7.4 0.0 collective-permute-done.mine_ref
  7.4 0.2 %collective-permute-start.3 = (bf16[48,512]{1,0:T(8,128)(2,1)S(1)}, bf16[48,512]{1,0:T(8,128)(2,1)S(1)}, u32[]{:S(2)}, u32[]{:S(2)}) collective-permute-start(bf16[48,512]{1,0:T(8,128)(2,1)S(1)} %collective-permute-done.mine_ref), channel_id=1, source_target_pairs={{0,1},{1,0},{2,3},{3,2},{4,5},{5,4},{6,7},{7,6},{8,9},{9,8},{10,11... | collective-permute-start | bytes 147464 | tf_op jit(solution)/shard_map/ppermute | solution.py:306
  7.6 0.5 %across.1 = (bf16[320,1280]{1,0:T(8,128)(2,1)S(1)}, f32[320,128]{1,0:T(8,128)S(1)}, f32[320,128]{1,0:T(8,128)S(1)}) custom-call(bf16[48,512]{1,0:T(8,128)(2,1)S(1)} %collective-permute-done.mine_ref, f32[320,256]{1,0:T(8,128)S(1)} %near.1.prior_ref), custom_call_target="tpu_custom_call" | custom-call | tf_op jit(solution)/shard_map/across/pallas_call | solution.py:338
  8.2 0.5 %collective-permute-done.3.other_ref = bf16[48,512]{1,0:T(8,128)(2,1)S(1)} collective-permute-done((bf16[48,512]{1,0:T(8,128)(2,1)S(1)}, bf16[48,512]{1,0:T(8,128)(2,1)S(1)}, u32[]{:S(2)}, u32[]{:S(2)}) %collective-permute-start.3) | collective-permute-done | bytes 49184 | tf_op jit(solution)/shard_map/ppermute | solution.py:306
  8.7 0.5 %finish.1 = (bf16[80,256]{1,0:T(8,128)(2,1)S(1)}, bf16[80,256]{1,0:T(8,128)(2,1)S(1)}, bf16[80,256]{1,0:T(8,128)(2,1)S(1)}, bf16[80,256]{1,0:T(8,128)(2,1)S(1)}) custom-call(bf16[48,512]{1,0:T(8,128)(2,1)S(1)} %collective-permute-done.3.other_ref, bf16[320,1280]{1,0:T(8,128)(2,1)S(1)} %get-tuple-element.22.toeplitz_ref, ...), custom_call_target="tpu_custom_call" | custom-call | tf_op jit(solution)/shard_map/finish/pallas_call | solution.py:338
  9.2 2.6 %collective-permute-start.4 = (bf16[80,256]{1,0:T(8,128)(2,1)S(1)}, bf16[80,256]{1,0:T(8,128)(2,1)S(1)}, u32[]{:S(2)}, u32[]{:S(2)}) collective-permute-start(bf16[80,256]{1,0:T(8,128)(2,1)S(1)} %get-tuple-element.25), channel_id=1, source_target_pairs={{0,7},{1,6},{2,5},{3,4},{4,3},{5,2},{6,1},{7,0},{8,15},{9,14},{10,... | collective-permute-start | bytes 122888 | tf_op jit(solution)/shard_map/ppermute | solution.py:314
  11.8 0.2 collective-permute-start.5
  11.9 0.4 %collective-permute-start.6 = (bf16[80,256]{1,0:T(8,128)(2,1)S(1)}, bf16[80,256]{1,0:T(8,128)(2,1)S(1)}, u32[]{:S(2)}, u32[]{:S(2)}) collective-permute-start(bf16[80,256]{1,0:T(8,128)(2,1)S(1)} %get-tuple-element.27), channel_id=1, source_target_pairs={{0,3},{1,2},{2,1},{3,0},{4,7},{5,6},{6,5},{7,4},{8,11},{9,10},{10,... | collective-permute-start | bytes 122888 | tf_op jit(solution)/shard_map/ppermute | solution.py:314
  12.4 0.2 %collective-permute-start.7 = (bf16[80,256]{1,0:T(8,128)(2,1)S(1)}, bf16[80,256]{1,0:T(8,128)(2,1)S(1)}, u32[]{:S(2)}, u32[]{:S(2)}) collective-permute-start(bf16[80,256]{1,0:T(8,128)(2,1)S(1)} %get-tuple-element.28), channel_id=1, source_target_pairs={{0,1},{1,0},{2,3},{3,2},{4,5},{5,4},{6,7},{7,6},{8,9},{9,8},{10,11... | collective-permute-start | bytes 122888 | tf_op jit(solution)/shard_map/ppermute | solution.py:314
  12.6 1.1 %collective-permute-done.4.refs_0_ = bf16[80,256]{1,0:T(8,128)(2,1)S(1)} collective-permute-done((bf16[80,256]{1,0:T(8,128)(2,1)S(1)}, bf16[80,256]{1,0:T(8,128)(2,1)S(1)}, u32[]{:S(2)}, u32[]{:S(2)}) %collective-permute-start.4) | collective-permute-done | bytes 40992 | tf_op jit(solution)/shard_map/ppermute | solution.py:314
  13.7 1.5 %collective-permute-done.5.refs_1_ = bf16[80,256]{1,0:T(8,128)(2,1)S(1)} collective-permute-done((bf16[80,256]{1,0:T(8,128)(2,1)S(1)}, bf16[80,256]{1,0:T(8,128)(2,1)S(1)}, u32[]{:S(2)}, u32[]{:S(2)}) %collective-permute-start.5) | collective-permute-done | bytes 40992 | tf_op jit(solution)/shard_map/ppermute | solution.py:314
  15.2 0.3 %collective-permute-done.6.refs_2_ = bf16[80,256]{1,0:T(8,128)(2,1)S(1)} collective-permute-done((bf16[80,256]{1,0:T(8,128)(2,1)S(1)}, bf16[80,256]{1,0:T(8,128)(2,1)S(1)}, u32[]{:S(2)}, u32[]{:S(2)}) %collective-permute-start.6) | collective-permute-done | bytes 40992 | tf_op jit(solution)/shard_map/ppermute | solution.py:314
  15.5 0.0 collective-permute-done.7.refs_3_
  15.5 1.0 %expand.1 = f32[3,129,256]{2,1,0:T(8,128)} custom-call(bf16[256,256]{1,0:T(8,128)(2,1)S(1)} %get-tuple-element.17.chosen_ref, bf16[80,256]{1,0:T(8,128)(2,1)S(1)} %collective-permute-done.4.refs_0_, bf16[80,256]{1,0:T(8,128)(2,1)S(1)} %collective-permute-done.5.refs_1_, bf16[80,256]{1,0:T(8,128)(2,1)S(1)} %collective-permute-done.6.refs_2_, ...), custom_call_target="tpu_custom_call" | custom-call | tf_op jit(solution)/shard_map/expand/pallas_call | solution.py:387
Async XLA Ops:
  1.1 3.6 %copy-start = (s32[256]{0:T(256)S(1)}, s32[256]{0:T(256)}, u32[]{:S(2)}) copy-start(s32[256]{0:T(256)} %param.5) | copy-start | bytes 3076
  1.1 6.3 %collective-permute-start = (bf16[48,512]{1,0:T(8,128)(2,1)S(1)}, bf16[48,512]{1,0:T(8,128)(2,1)S(1)}, u32[]{:S(2)}, u32[]{:S(2)}) collective-permute-start(bf16[48,512]{1,0:T(8,128)(2,1)S(1)} %whiten.1.whitened_ref.refs_2_), channel_id=1, source_target_pairs={{0,9},{1,8},{2,11},{3,10},{4,13},{5,12},{6,15},{7,14},{8,1},{9,0},... | collective-permute-start | bytes 147464 | tf_op jit(solution)/shard_map/ppermute | solution.py:314
  4.8 1.6 %collective-permute-start.1 = (bf16[24,512]{1,0:T(8,128)(2,1)S(1)}, bf16[24,512]{1,0:T(8,128)(2,1)S(1)}, u32[]{:S(2)}, u32[]{:S(2)}) collective-permute-start(bf16[24,512]{1,0:T(8,128)(2,1)S(1)} %get-tuple-element.18), channel_id=1, source_target_pairs={{0,1},{1,0},{2,3},{3,2},{4,5},{5,4},{6,7},{7,6},{8,9},{9,8},{10,11... | collective-permute-start | bytes 73736 | tf_op jit(solution)/shard_map/ppermute | solution.py:306
  5.6 1.2 %collective-permute-start.2 = (bf16[24,512]{1,0:T(8,128)(2,1)S(1)}, bf16[24,512]{1,0:T(8,128)(2,1)S(1)}, u32[]{:S(2)}, u32[]{:S(2)}) collective-permute-start(bf16[24,512]{1,0:T(8,128)(2,1)S(1)} %get-tuple-element.19), channel_id=1, source_target_pairs={{0,1},{1,0},{2,3},{3,2},{4,5},{5,4},{6,7},{7,6},{8,9},{9,8},{10,11... | collective-permute-start | bytes 73736 | tf_op jit(solution)/shard_map/ppermute | solution.py:306
  7.4 1.3 %collective-permute-start.3 = (bf16[48,512]{1,0:T(8,128)(2,1)S(1)}, bf16[48,512]{1,0:T(8,128)(2,1)S(1)}, u32[]{:S(2)}, u32[]{:S(2)}) collective-permute-start(bf16[48,512]{1,0:T(8,128)(2,1)S(1)} %collective-permute-done.mine_ref), channel_id=1, source_target_pairs={{0,1},{1,0},{2,3},{3,2},{4,5},{5,4},{6,7},{7,6},{8,9},{9,8},{10,11... | collective-permute-start | bytes 147464 | tf_op jit(solution)/shard_map/ppermute | solution.py:306
  9.2 4.5 %collective-permute-start.4 = (bf16[80,256]{1,0:T(8,128)(2,1)S(1)}, bf16[80,256]{1,0:T(8,128)(2,1)S(1)}, u32[]{:S(2)}, u32[]{:S(2)}) collective-permute-start(bf16[80,256]{1,0:T(8,128)(2,1)S(1)} %get-tuple-element.25), channel_id=1, source_target_pairs={{0,7},{1,6},{2,5},{3,4},{4,3},{5,2},{6,1},{7,0},{8,15},{9,14},{10,... | collective-permute-start | bytes 122888 | tf_op jit(solution)/shard_map/ppermute | solution.py:314
  11.8 3.4 %collective-permute-start.5 = (bf16[80,256]{1,0:T(8,128)(2,1)S(1)}, bf16[80,256]{1,0:T(8,128)(2,1)S(1)}, u32[]{:S(2)}, u32[]{:S(2)}) collective-permute-start(bf16[80,256]{1,0:T(8,128)(2,1)S(1)} %get-tuple-element.26), channel_id=1, source_target_pairs={{0,5},{1,4},{2,7},{3,6},{4,1},{5,0},{6,3},{7,2},{8,13},{9,12},{10,... | collective-permute-start | bytes 122888 | tf_op jit(solution)/shard_map/ppermute | solution.py:314
  11.9 3.6 %collective-permute-start.6 = (bf16[80,256]{1,0:T(8,128)(2,1)S(1)}, bf16[80,256]{1,0:T(8,128)(2,1)S(1)}, u32[]{:S(2)}, u32[]{:S(2)}) collective-permute-start(bf16[80,256]{1,0:T(8,128)(2,1)S(1)} %get-tuple-element.27), channel_id=1, source_target_pairs={{0,3},{1,2},{2,1},{3,0},{4,7},{5,6},{6,5},{7,4},{8,11},{9,10},{10,... | collective-permute-start | bytes 122888 | tf_op jit(solution)/shard_map/ppermute | solution.py:314
  12.4 3.1 %collective-permute-start.7 = (bf16[80,256]{1,0:T(8,128)(2,1)S(1)}, bf16[80,256]{1,0:T(8,128)(2,1)S(1)}, u32[]{:S(2)}, u32[]{:S(2)}) collective-permute-start(bf16[80,256]{1,0:T(8,128)(2,1)S(1)} %get-tuple-element.28), channel_id=1, source_target_pairs={{0,1},{1,0},{2,3},{3,2},{4,5},{5,4},{6,7},{7,6},{8,9},{9,8},{10,11... | collective-permute-start | bytes 122888 | tf_op jit(solution)/shard_map/ppermute | solution.py:314

commit v34 on v33

--- a/solution.py
+++ b/solution.py
@@ -11,7 +11,7 @@
 MAXLAG = 64
 LAG_COUNT = 2 * MAXLAG + 1
 LANES = 256
-IN_PARTS = 8
+IN_PARTS = 3
 GROUP = 8
 HOPS = (3, 2, 1, 0)
 
@@ -98,6 +98,7 @@
             and self.src_size == 2
             and self.half % self.blk_size == 0
             and self.half % GROUP == 0
+            and self.half % IN_PARTS == 0
             and self.channels % 16 == 0
             and self.windows * self.half % 16 == 0
             and self.blk_size == 8

time: 16.8 us -> 16.6 us (0.988)
  no operation moved by 1% of the time
where the time goes in v34:
time: 16.6 us; the launch traced here: 16.4 us
  starting transfers between devices  7.98 us (48%)
  waiting for transfers between devices  4.57 us (28%)
  Pallas kernels  3.83 us (23%)
    ppermute x5, starting transfers between devices, swap_blk(): return lax.ppermute(array, ('blk', 'src'), pairs)  6.93 us
    ppermute x5, waiting for transfers between devices, swap_blk(): return lax.ppermute(array, ('blk', 'src'), pairs)  2.93 us
    pallas_call x4, Pallas kernels, call(): pl.pallas_call(functools.partial(kernel, plan), out_shape=outputs, in_spe...  1.77 us
    ppermute x3, waiting for transfers between devices, swap_cores(): return lax.ppermute(array, 'src', [(0, 1), (1, 0)])  1.64 us
    ppermute x3, starting transfers between devices, swap_cores(): return lax.ppermute(array, 'src', [(0, 1), (1, 0)])  1.05 us
    pallas_call x1, Pallas kernels, few_channels(): pl.pallas_call(functools.partial(whiten_kernel, plan), out_shape=pltpu.VM...  1.03 us
    pallas_call x1, Pallas kernels, few_channels(): pl.pallas_call(functools.partial(expand_kernel, plan), out_shape=jax.Shap...  1.03 us
  transfers between devices with their start and end apart: 8, of which 6 were waited for; matrix products, arithmetic and copies ran while one was open for 0% of the time, Pallas kernels for 8%

profile of v34, /device:TPU:0, one launch (start us, length us, event | category | flops | bytes accessed | tf_op | source)
XLA Modules:
  0.0 16.4 jit_solution(550388138920847146)
XLA Ops:
  0.0 1.0 %whiten.1.whitened_ref.refs_2_ = bf16[48,512]{1,0:T(8,128)(2,1)S(1)} custom-call(f32[24,2,512]{2,1,0:T(2,128)} %traces_hbm.1, s32[2,24]{1,0:T(2,128)} %bitcast.3), custom_call_target="tpu_custom_call" | custom-call | tf_op jit(solution)/shard_map/whiten/pallas_call | solution.py:317
  1.0 0.0 copy-start
  1.1 3.5 %collective-permute-start = (bf16[48,512]{1,0:T(8,128)(2,1)S(1)}, bf16[48,512]{1,0:T(8,128)(2,1)S(1)}, u32[]{:S(2)}, u32[]{:S(2)}) collective-permute-start(bf16[48,512]{1,0:T(8,128)(2,1)S(1)} %whiten.1.whitened_ref.refs_2_), channel_id=1, source_target_pairs={{0,9},{1,8},{2,11},{3,10},{4,13},{5,12},{6,15},{7,14},{8,1},{9,0},... | collective-permute-start | bytes 147464 | tf_op jit(solution)/shard_map/ppermute | solution.py:315
  4.6 0.0 copy-done
  4.6 0.2 choose.1
  4.8 0.7 %collective-permute-start.1 = (bf16[24,512]{1,0:T(8,128)(2,1)S(1)}, bf16[24,512]{1,0:T(8,128)(2,1)S(1)}, u32[]{:S(2)}, u32[]{:S(2)}) collective-permute-start(bf16[24,512]{1,0:T(8,128)(2,1)S(1)} %get-tuple-element.18), channel_id=1, source_target_pairs={{0,1},{1,0},{2,3},{3,2},{4,5},{5,4},{6,7},{7,6},{8,9},{9,8},{10,11... | collective-permute-start | bytes 73736 | tf_op jit(solution)/shard_map/ppermute | solution.py:307
  5.5 0.1 collective-permute-start.2
  5.6 0.8 %collective-permute-done.1.refs_0_ = bf16[24,512]{1,0:T(8,128)(2,1)S(1)} collective-permute-done((bf16[24,512]{1,0:T(8,128)(2,1)S(1)}, bf16[24,512]{1,0:T(8,128)(2,1)S(1)}, u32[]{:S(2)}, u32[]{:S(2)}) %collective-permute-start.1) | collective-permute-done | bytes 24608 | tf_op jit(solution)/shard_map/ppermute | solution.py:307
  6.3 0.3 %collective-permute-done.2.refs_1_ = bf16[24,512]{1,0:T(8,128)(2,1)S(1)} collective-permute-done((bf16[24,512]{1,0:T(8,128)(2,1)S(1)}, bf16[24,512]{1,0:T(8,128)(2,1)S(1)}, u32[]{:S(2)}, u32[]{:S(2)}) %collective-permute-start.2) | collective-permute-done | bytes 24608 | tf_op jit(solution)/shard_map/ppermute | solution.py:307
  6.7 0.6 %near.1.prior_ref = f32[320,256]{1,0:T(8,128)S(1)} custom-call(bf16[24,512]{1,0:T(8,128)(2,1)S(1)} %collective-permute-done.1.refs_0_, bf16[24,512]{1,0:T(8,128)(2,1)S(1)} %collective-permute-done.2.refs_1_, bf16[48,512]{1,0:T(8,128)(2,1)S(1)} %whiten.1.whitened_ref.refs_2_), custom_call_target="tpu_custom_call" | custom-call | tf_op jit(solution)/shard_map/near/pallas_call | solution.py:339
  7.3 0.0 collective-permute-done.mine_ref
  7.3 0.2 %collective-permute-start.3 = (bf16[48,512]{1,0:T(8,128)(2,1)S(1)}, bf16[48,512]{1,0:T(8,128)(2,1)S(1)}, u32[]{:S(2)}, u32[]{:S(2)}) collective-permute-start(bf16[48,512]{1,0:T(8,128)(2,1)S(1)} %collective-permute-done.mine_ref), channel_id=1, source_target_pairs={{0,1},{1,0},{2,3},{3,2},{4,5},{5,4},{6,7},{7,6},{8,9},{9,8},{10,11... | collective-permute-start | bytes 147464 | tf_op jit(solution)/shard_map/ppermute | solution.py:307
  7.6 0.5 %across.1 = (bf16[320,1280]{1,0:T(8,128)(2,1)S(1)}, f32[320,128]{1,0:T(8,128)S(1)}, f32[320,128]{1,0:T(8,128)S(1)}) custom-call(bf16[48,512]{1,0:T(8,128)(2,1)S(1)} %collective-permute-done.mine_ref, f32[320,256]{1,0:T(8,128)S(1)} %near.1.prior_ref), custom_call_target="tpu_custom_call" | custom-call | tf_op jit(solution)/shard_map/across/pallas_call | solution.py:339
  8.1 0.5 %collective-permute-done.3.other_ref = bf16[48,512]{1,0:T(8,128)(2,1)S(1)} collective-permute-done((bf16[48,512]{1,0:T(8,128)(2,1)S(1)}, bf16[48,512]{1,0:T(8,128)(2,1)S(1)}, u32[]{:S(2)}, u32[]{:S(2)}) %collective-permute-start.3) | collective-permute-done | bytes 49184 | tf_op jit(solution)/shard_map/ppermute | solution.py:307
  8.6 0.5 %finish.1 = (bf16[80,256]{1,0:T(8,128)(2,1)S(1)}, bf16[80,256]{1,0:T(8,128)(2,1)S(1)}, bf16[80,256]{1,0:T(8,128)(2,1)S(1)}, bf16[80,256]{1,0:T(8,128)(2,1)S(1)}) custom-call(bf16[48,512]{1,0:T(8,128)(2,1)S(1)} %collective-permute-done.3.other_ref, bf16[320,1280]{1,0:T(8,128)(2,1)S(1)} %get-tuple-element.22.toeplitz_ref, ...), custom_call_target="tpu_custom_call" | custom-call | tf_op jit(solution)/shard_map/finish/pallas_call | solution.py:339
  9.1 2.6 %collective-permute-start.4 = (bf16[80,256]{1,0:T(8,128)(2,1)S(1)}, bf16[80,256]{1,0:T(8,128)(2,1)S(1)}, u32[]{:S(2)}, u32[]{:S(2)}) collective-permute-start(bf16[80,256]{1,0:T(8,128)(2,1)S(1)} %get-tuple-element.25), channel_id=1, source_target_pairs={{0,7},{1,6},{2,5},{3,4},{4,3},{5,2},{6,1},{7,0},{8,15},{9,14},{10,... | collective-permute-start | bytes 122888 | tf_op jit(solution)/shard_map/ppermute | solution.py:315
  11.7 0.2 collective-permute-start.5
  11.8 0.4 %collective-permute-start.6 = (bf16[80,256]{1,0:T(8,128)(2,1)S(1)}, bf16[80,256]{1,0:T(8,128)(2,1)S(1)}, u32[]{:S(2)}, u32[]{:S(2)}) collective-permute-start(bf16[80,256]{1,0:T(8,128)(2,1)S(1)} %get-tuple-element.27), channel_id=1, source_target_pairs={{0,3},{1,2},{2,1},{3,0},{4,7},{5,6},{6,5},{7,4},{8,11},{9,10},{10,... | collective-permute-start | bytes 122888 | tf_op jit(solution)/shard_map/ppermute | solution.py:315
  12.3 0.2 %collective-permute-start.7 = (bf16[80,256]{1,0:T(8,128)(2,1)S(1)}, bf16[80,256]{1,0:T(8,128)(2,1)S(1)}, u32[]{:S(2)}, u32[]{:S(2)}) collective-permute-start(bf16[80,256]{1,0:T(8,128)(2,1)S(1)} %get-tuple-element.28), channel_id=1, source_target_pairs={{0,1},{1,0},{2,3},{3,2},{4,5},{5,4},{6,7},{7,6},{8,9},{9,8},{10,11... | collective-permute-start | bytes 122888 | tf_op jit(solution)/shard_map/ppermute | solution.py:315
  12.5 1.1 %collective-permute-done.4.refs_0_ = bf16[80,256]{1,0:T(8,128)(2,1)S(1)} collective-permute-done((bf16[80,256]{1,0:T(8,128)(2,1)S(1)}, bf16[80,256]{1,0:T(8,128)(2,1)S(1)}, u32[]{:S(2)}, u32[]{:S(2)}) %collective-permute-start.4) | collective-permute-done | bytes 40992 | tf_op jit(solution)/shard_map/ppermute | solution.py:315
  13.6 1.5 %collective-permute-done.5.refs_1_ = bf16[80,256]{1,0:T(8,128)(2,1)S(1)} collective-permute-done((bf16[80,256]{1,0:T(8,128)(2,1)S(1)}, bf16[80,256]{1,0:T(8,128)(2,1)S(1)}, u32[]{:S(2)}, u32[]{:S(2)}) %collective-permute-start.5) | collective-permute-done | bytes 40992 | tf_op jit(solution)/shard_map/ppermute | solution.py:315
  15.1 0.3 %collective-permute-done.6.refs_2_ = bf16[80,256]{1,0:T(8,128)(2,1)S(1)} collective-permute-done((bf16[80,256]{1,0:T(8,128)(2,1)S(1)}, bf16[80,256]{1,0:T(8,128)(2,1)S(1)}, u32[]{:S(2)}, u32[]{:S(2)}) %collective-permute-start.6) | collective-permute-done | bytes 40992 | tf_op jit(solution)/shard_map/ppermute | solution.py:315
  15.4 0.0 collective-permute-done.7.refs_3_
  15.4 1.0 %expand.1 = f32[3,129,256]{2,1,0:T(8,128)} custom-call(bf16[256,256]{1,0:T(8,128)(2,1)S(1)} %get-tuple-element.17.chosen_ref, bf16[80,256]{1,0:T(8,128)(2,1)S(1)} %collective-permute-done.4.refs_0_, bf16[80,256]{1,0:T(8,128)(2,1)S(1)} %collective-permute-done.5.refs_1_, bf16[80,256]{1,0:T(8,128)(2,1)S(1)} %collective-permute-done.6.refs_2_, ...), custom_call_target="tpu_custom_call" | custom-call | tf_op jit(solution)/shard_map/expand/pallas_call | solution.py:388
Async XLA Ops:
  1.0 3.6 %copy-start = (s32[256]{0:T(256)S(1)}, s32[256]{0:T(256)}, u32[]{:S(2)}) copy-start(s32[256]{0:T(256)} %param.5) | copy-start | bytes 3076
  1.1 6.3 %collective-permute-start = (bf16[48,512]{1,0:T(8,128)(2,1)S(1)}, bf16[48,512]{1,0:T(8,128)(2,1)S(1)}, u32[]{:S(2)}, u32[]{:S(2)}) collective-permute-start(bf16[48,512]{1,0:T(8,128)(2,1)S(1)} %whiten.1.whitened_ref.refs_2_), channel_id=1, source_target_pairs={{0,9},{1,8},{2,11},{3,10},{4,13},{5,12},{6,15},{7,14},{8,1},{9,0},... | collective-permute-start | bytes 147464 | tf_op jit(solution)/shard_map/ppermute | solution.py:315
  4.8 1.6 %collective-permute-start.1 = (bf16[24,512]{1,0:T(8,128)(2,1)S(1)}, bf16[24,512]{1,0:T(8,128)(2,1)S(1)}, u32[]{:S(2)}, u32[]{:S(2)}) collective-permute-start(bf16[24,512]{1,0:T(8,128)(2,1)S(1)} %get-tuple-element.18), channel_id=1, source_target_pairs={{0,1},{1,0},{2,3},{3,2},{4,5},{5,4},{6,7},{7,6},{8,9},{9,8},{10,11... | collective-permute-start | bytes 73736 | tf_op jit(solution)/shard_map/ppermute | solution.py:307
  5.5 1.2 %collective-permute-start.2 = (bf16[24,512]{1,0:T(8,128)(2,1)S(1)}, bf16[24,512]{1,0:T(8,128)(2,1)S(1)}, u32[]{:S(2)}, u32[]{:S(2)}) collective-permute-start(bf16[24,512]{1,0:T(8,128)(2,1)S(1)} %get-tuple-element.19), channel_id=1, source_target_pairs={{0,1},{1,0},{2,3},{3,2},{4,5},{5,4},{6,7},{7,6},{8,9},{9,8},{10,11... | collective-permute-start | bytes 73736 | tf_op jit(solution)/shard_map/ppermute | solution.py:307
  7.3 1.3 %collective-permute-start.3 = (bf16[48,512]{1,0:T(8,128)(2,1)S(1)}, bf16[48,512]{1,0:T(8,128)(2,1)S(1)}, u32[]{:S(2)}, u32[]{:S(2)}) collective-permute-start(bf16[48,512]{1,0:T(8,128)(2,1)S(1)} %collective-permute-done.mine_ref), channel_id=1, source_target_pairs={{0,1},{1,0},{2,3},{3,2},{4,5},{5,4},{6,7},{7,6},{8,9},{9,8},{10,11... | collective-permute-start | bytes 147464 | tf_op jit(solution)/shard_map/ppermute | solution.py:307
  9.1 4.5 %collective-permute-start.4 = (bf16[80,256]{1,0:T(8,128)(2,1)S(1)}, bf16[80,256]{1,0:T(8,128)(2,1)S(1)}, u32[]{:S(2)}, u32[]{:S(2)}) collective-permute-start(bf16[80,256]{1,0:T(8,128)(2,1)S(1)} %get-tuple-element.25), channel_id=1, source_target_pairs={{0,7},{1,6},{2,5},{3,4},{4,3},{5,2},{6,1},{7,0},{8,15},{9,14},{10,... | collective-permute-start | bytes 122888 | tf_op jit(solution)/shard_map/ppermute | solution.py:315
  11.7 3.4 %collective-permute-start.5 = (bf16[80,256]{1,0:T(8,128)(2,1)S(1)}, bf16[80,256]{1,0:T(8,128)(2,1)S(1)}, u32[]{:S(2)}, u32[]{:S(2)}) collective-permute-start(bf16[80,256]{1,0:T(8,128)(2,1)S(1)} %get-tuple-element.26), channel_id=1, source_target_pairs={{0,5},{1,4},{2,7},{3,6},{4,1},{5,0},{6,3},{7,2},{8,13},{9,12},{10,... | collective-permute-start | bytes 122888 | tf_op jit(solution)/shard_map/ppermute | solution.py:315
  11.8 3.6 %collective-permute-start.6 = (bf16[80,256]{1,0:T(8,128)(2,1)S(1)}, bf16[80,256]{1,0:T(8,128)(2,1)S(1)}, u32[]{:S(2)}, u32[]{:S(2)}) collective-permute-start(bf16[80,256]{1,0:T(8,128)(2,1)S(1)} %get-tuple-element.27), channel_id=1, source_target_pairs={{0,3},{1,2},{2,1},{3,0},{4,7},{5,6},{6,5},{7,4},{8,11},{9,10},{10,... | collective-permute-start | bytes 122888 | tf_op jit(solution)/shard_map/ppermute | solution.py:315
  12.3 3.1 %collective-permute-start.7 = (bf16[80,256]{1,0:T(8,128)(2,1)S(1)}, bf16[80,256]{1,0:T(8,128)(2,1)S(1)}, u32[]{:S(2)}, u32[]{:S(2)}) collective-permute-start(bf16[80,256]{1,0:T(8,128)(2,1)S(1)} %get-tuple-element.28), channel_id=1, source_target_pairs={{0,1},{1,0},{2,3},{3,2},{4,5},{5,4},{6,7},{7,6},{8,9},{9,8},{10,11... | collective-permute-start | bytes 122888 | tf_op jit(solution)/shard_map/ppermute | solution.py:315

commit v35 on v34

--- a/solution.py
+++ b/solution.py
@@ -13,7 +13,7 @@
 LANES = 256
 IN_PARTS = 3
 GROUP = 8
-HOPS = (3, 2, 1, 0)
+HOPS = (3, 1, 2, 0)
 
 
 def broadcast(value, axis, source):

time: 16.6 us -> 16.9 us (1.018)
  waiting for transfers between devices: 4.57 us -> 4.84 us
    ppermute x5, waiting for transfers between devices: 2.93 us -> 3.2 us  [swap_blk(): return lax.ppermute(array, ('blk', 'src'), pairs)]
where the time goes in v35:
time: 16.9 us; the launch traced here: 16.7 us
  starting transfers between devices  7.98 us (47%)
  waiting for transfers between devices  4.84 us (29%)
  Pallas kernels  3.83 us (23%)
    ppermute x5, starting transfers between devices, swap_blk(): return lax.ppermute(array, ('blk', 'src'), pairs)  6.93 us
    ppermute x5, waiting for transfers between devices, swap_blk(): return lax.ppermute(array, ('blk', 'src'), pairs)  3.2 us
    pallas_call x4, Pallas kernels, call(): pl.pallas_call(functools.partial(kernel, plan), out_shape=outputs, in_spe...  1.77 us
    ppermute x3, waiting for transfers between devices, swap_cores(): return lax.ppermute(array, 'src', [(0, 1), (1, 0)])  1.64 us
    ppermute x3, starting transfers between devices, swap_cores(): return lax.ppermute(array, 'src', [(0, 1), (1, 0)])  1.05 us
    pallas_call x1, Pallas kernels, few_channels(): pl.pallas_call(functools.partial(whiten_kernel, plan), out_shape=pltpu.VM...  1.03 us
    pallas_call x1, Pallas kernels, few_channels(): pl.pallas_call(functools.partial(expand_kernel, plan), out_shape=jax.Shap...  1.03 us
  transfers between devices with their start and end apart: 8, of which 6 were waited for; matrix products, arithmetic and copies ran while one was open for 0% of the time, Pallas kernels for 8%

profile of v35, /device:TPU:0, one launch (start us, length us, event | category | flops | bytes accessed | tf_op | source)
XLA Modules:
  0.0 16.7 jit_solution(8472268876977338787)
XLA Ops:
  0.0 1.0 %whiten.1.whitened_ref.refs_2_ = bf16[48,512]{1,0:T(8,128)(2,1)S(1)} custom-call(f32[24,2,512]{2,1,0:T(2,128)} %traces_hbm.1, s32[2,24]{1,0:T(2,128)} %bitcast.3), custom_call_target="tpu_custom_call" | custom-call | tf_op jit(solution)/shard_map/whiten/pallas_call | solution.py:317
  1.0 0.0 copy-start
  1.1 3.5 %collective-permute-start = (bf16[48,512]{1,0:T(8,128)(2,1)S(1)}, bf16[48,512]{1,0:T(8,128)(2,1)S(1)}, u32[]{:S(2)}, u32[]{:S(2)}) collective-permute-start(bf16[48,512]{1,0:T(8,128)(2,1)S(1)} %whiten.1.whitened_ref.refs_2_), channel_id=1, source_target_pairs={{0,9},{1,8},{2,11},{3,10},{4,13},{5,12},{6,15},{7,14},{8,1},{9,0},... | collective-permute-start | bytes 147464 | tf_op jit(solution)/shard_map/ppermute | solution.py:315
  4.6 0.0 copy-done
  4.6 0.2 choose.1
  4.8 0.7 %collective-permute-start.1 = (bf16[24,512]{1,0:T(8,128)(2,1)S(1)}, bf16[24,512]{1,0:T(8,128)(2,1)S(1)}, u32[]{:S(2)}, u32[]{:S(2)}) collective-permute-start(bf16[24,512]{1,0:T(8,128)(2,1)S(1)} %get-tuple-element.18), channel_id=1, source_target_pairs={{0,1},{1,0},{2,3},{3,2},{4,5},{5,4},{6,7},{7,6},{8,9},{9,8},{10,11... | collective-permute-start | bytes 73736 | tf_op jit(solution)/shard_map/ppermute | solution.py:307
  5.5 0.1 collective-permute-start.2
  5.6 0.8 %collective-permute-done.1.refs_0_ = bf16[24,512]{1,0:T(8,128)(2,1)S(1)} collective-permute-done((bf16[24,512]{1,0:T(8,128)(2,1)S(1)}, bf16[24,512]{1,0:T(8,128)(2,1)S(1)}, u32[]{:S(2)}, u32[]{:S(2)}) %collective-permute-start.1) | collective-permute-done | bytes 24608 | tf_op jit(solution)/shard_map/ppermute | solution.py:307
  6.3 0.3 %collective-permute-done.2.refs_1_ = bf16[24,512]{1,0:T(8,128)(2,1)S(1)} collective-permute-done((bf16[24,512]{1,0:T(8,128)(2,1)S(1)}, bf16[24,512]{1,0:T(8,128)(2,1)S(1)}, u32[]{:S(2)}, u32[]{:S(2)}) %collective-permute-start.2) | collective-permute-done | bytes 24608 | tf_op jit(solution)/shard_map/ppermute | solution.py:307
  6.7 0.6 %near.1.prior_ref = f32[320,256]{1,0:T(8,128)S(1)} custom-call(bf16[24,512]{1,0:T(8,128)(2,1)S(1)} %collective-permute-done.1.refs_0_, bf16[24,512]{1,0:T(8,128)(2,1)S(1)} %collective-permute-done.2.refs_1_, bf16[48,512]{1,0:T(8,128)(2,1)S(1)} %whiten.1.whitened_ref.refs_2_), custom_call_target="tpu_custom_call" | custom-call | tf_op jit(solution)/shard_map/near/pallas_call | solution.py:339
  7.3 0.0 collective-permute-done.mine_ref
  7.3 0.2 %collective-permute-start.3 = (bf16[48,512]{1,0:T(8,128)(2,1)S(1)}, bf16[48,512]{1,0:T(8,128)(2,1)S(1)}, u32[]{:S(2)}, u32[]{:S(2)}) collective-permute-start(bf16[48,512]{1,0:T(8,128)(2,1)S(1)} %collective-permute-done.mine_ref), channel_id=1, source_target_pairs={{0,1},{1,0},{2,3},{3,2},{4,5},{5,4},{6,7},{7,6},{8,9},{9,8},{10,11... | collective-permute-start | bytes 147464 | tf_op jit(solution)/shard_map/ppermute | solution.py:307
  7.6 0.5 %across.1 = (bf16[320,1280]{1,0:T(8,128)(2,1)S(1)}, f32[320,128]{1,0:T(8,128)S(1)}, f32[320,128]{1,0:T(8,128)S(1)}) custom-call(bf16[48,512]{1,0:T(8,128)(2,1)S(1)} %collective-permute-done.mine_ref, f32[320,256]{1,0:T(8,128)S(1)} %near.1.prior_ref), custom_call_target="tpu_custom_call" | custom-call | tf_op jit(solution)/shard_map/across/pallas_call | solution.py:339
  8.1 0.5 %collective-permute-done.3.other_ref = bf16[48,512]{1,0:T(8,128)(2,1)S(1)} collective-permute-done((bf16[48,512]{1,0:T(8,128)(2,1)S(1)}, bf16[48,512]{1,0:T(8,128)(2,1)S(1)}, u32[]{:S(2)}, u32[]{:S(2)}) %collective-permute-start.3) | collective-permute-done | bytes 49184 | tf_op jit(solution)/shard_map/ppermute | solution.py:307
  8.6 0.5 %finish.1 = (bf16[80,256]{1,0:T(8,128)(2,1)S(1)}, bf16[80,256]{1,0:T(8,128)(2,1)S(1)}, bf16[80,256]{1,0:T(8,128)(2,1)S(1)}, bf16[80,256]{1,0:T(8,128)(2,1)S(1)}) custom-call(bf16[48,512]{1,0:T(8,128)(2,1)S(1)} %collective-permute-done.3.other_ref, bf16[320,1280]{1,0:T(8,128)(2,1)S(1)} %get-tuple-element.22.toeplitz_ref, ...), custom_call_target="tpu_custom_call" | custom-call | tf_op jit(solution)/shard_map/finish/pallas_call | solution.py:339
  9.1 2.6 %collective-permute-start.4 = (bf16[80,256]{1,0:T(8,128)(2,1)S(1)}, bf16[80,256]{1,0:T(8,128)(2,1)S(1)}, u32[]{:S(2)}, u32[]{:S(2)}) collective-permute-start(bf16[80,256]{1,0:T(8,128)(2,1)S(1)} %get-tuple-element.25), channel_id=1, source_target_pairs={{0,7},{1,6},{2,5},{3,4},{4,3},{5,2},{6,1},{7,0},{8,15},{9,14},{10,... | collective-permute-start | bytes 122888 | tf_op jit(solution)/shard_map/ppermute | solution.py:315
  11.7 0.5 %collective-permute-start.5 = (bf16[80,256]{1,0:T(8,128)(2,1)S(1)}, bf16[80,256]{1,0:T(8,128)(2,1)S(1)}, u32[]{:S(2)}, u32[]{:S(2)}) collective-permute-start(bf16[80,256]{1,0:T(8,128)(2,1)S(1)} %get-tuple-element.26), channel_id=1, source_target_pairs={{0,3},{1,2},{2,1},{3,0},{4,7},{5,6},{6,5},{7,4},{8,11},{9,10},{10,... | collective-permute-start | bytes 122888 | tf_op jit(solution)/shard_map/ppermute | solution.py:315
  12.2 0.1 collective-permute-start.6
  12.3 0.2 %collective-permute-start.7 = (bf16[80,256]{1,0:T(8,128)(2,1)S(1)}, bf16[80,256]{1,0:T(8,128)(2,1)S(1)}, u32[]{:S(2)}, u32[]{:S(2)}) collective-permute-start(bf16[80,256]{1,0:T(8,128)(2,1)S(1)} %get-tuple-element.28), channel_id=1, source_target_pairs={{0,1},{1,0},{2,3},{3,2},{4,5},{5,4},{6,7},{7,6},{8,9},{9,8},{10,11... | collective-permute-start | bytes 122888 | tf_op jit(solution)/shard_map/ppermute | solution.py:315
  12.5 1.1 %collective-permute-done.4.refs_0_ = bf16[80,256]{1,0:T(8,128)(2,1)S(1)} collective-permute-done((bf16[80,256]{1,0:T(8,128)(2,1)S(1)}, bf16[80,256]{1,0:T(8,128)(2,1)S(1)}, u32[]{:S(2)}, u32[]{:S(2)}) %collective-permute-start.4) | collective-permute-done | bytes 40992 | tf_op jit(solution)/shard_map/ppermute | solution.py:315
  13.6 1.5 %collective-permute-done.5.refs_1_ = bf16[80,256]{1,0:T(8,128)(2,1)S(1)} collective-permute-done((bf16[80,256]{1,0:T(8,128)(2,1)S(1)}, bf16[80,256]{1,0:T(8,128)(2,1)S(1)}, u32[]{:S(2)}, u32[]{:S(2)}) %collective-permute-start.5) | collective-permute-done | bytes 40992 | tf_op jit(solution)/shard_map/ppermute | solution.py:315
  15.1 0.6 %collective-permute-done.6.refs_2_ = bf16[80,256]{1,0:T(8,128)(2,1)S(1)} collective-permute-done((bf16[80,256]{1,0:T(8,128)(2,1)S(1)}, bf16[80,256]{1,0:T(8,128)(2,1)S(1)}, u32[]{:S(2)}, u32[]{:S(2)}) %collective-permute-start.6) | collective-permute-done | bytes 40992 | tf_op jit(solution)/shard_map/ppermute | solution.py:315
  15.7 0.0 collective-permute-done.7.refs_3_
  15.7 1.0 %expand.1 = f32[3,129,256]{2,1,0:T(8,128)} custom-call(bf16[256,256]{1,0:T(8,128)(2,1)S(1)} %get-tuple-element.17.chosen_ref, bf16[80,256]{1,0:T(8,128)(2,1)S(1)} %collective-permute-done.4.refs_0_, bf16[80,256]{1,0:T(8,128)(2,1)S(1)} %collective-permute-done.5.refs_1_, bf16[80,256]{1,0:T(8,128)(2,1)S(1)} %collective-permute-done.6.refs_2_, ...), custom_call_target="tpu_custom_call" | custom-call | tf_op jit(solution)/shard_map/expand/pallas_call | solution.py:388
Async XLA Ops:
  1.0 3.6 %copy-start = (s32[256]{0:T(256)S(1)}, s32[256]{0:T(256)}, u32[]{:S(2)}) copy-start(s32[256]{0:T(256)} %param.5) | copy-start | bytes 3076
  1.1 6.3 %collective-permute-start = (bf16[48,512]{1,0:T(8,128)(2,1)S(1)}, bf16[48,512]{1,0:T(8,128)(2,1)S(1)}, u32[]{:S(2)}, u32[]{:S(2)}) collective-permute-start(bf16[48,512]{1,0:T(8,128)(2,1)S(1)} %whiten.1.whitened_ref.refs_2_), channel_id=1, source_target_pairs={{0,9},{1,8},{2,11},{3,10},{4,13},{5,12},{6,15},{7,14},{8,1},{9,0},... | collective-permute-start | bytes 147464 | tf_op jit(solution)/shard_map/ppermute | solution.py:315
  4.8 1.6 %collective-permute-start.1 = (bf16[24,512]{1,0:T(8,128)(2,1)S(1)}, bf16[24,512]{1,0:T(8,128)(2,1)S(1)}, u32[]{:S(2)}, u32[]{:S(2)}) collective-permute-start(bf16[24,512]{1,0:T(8,128)(2,1)S(1)} %get-tuple-element.18), channel_id=1, source_target_pairs={{0,1},{1,0},{2,3},{3,2},{4,5},{5,4},{6,7},{7,6},{8,9},{9,8},{10,11... | collective-permute-start | bytes 73736 | tf_op jit(solution)/shard_map/ppermute | solution.py:307
  5.5 1.2 %collective-permute-start.2 = (bf16[24,512]{1,0:T(8,128)(2,1)S(1)}, bf16[24,512]{1,0:T(8,128)(2,1)S(1)}, u32[]{:S(2)}, u32[]{:S(2)}) collective-permute-start(bf16[24,512]{1,0:T(8,128)(2,1)S(1)} %get-tuple-element.19), channel_id=1, source_target_pairs={{0,1},{1,0},{2,3},{3,2},{4,5},{5,4},{6,7},{7,6},{8,9},{9,8},{10,11... | collective-permute-start | bytes 73736 | tf_op jit(solution)/shard_map/ppermute | solution.py:307
  7.3 1.3 %collective-permute-start.3 = (bf16[48,512]{1,0:T(8,128)(2,1)S(1)}, bf16[48,512]{1,0:T(8,128)(2,1)S(1)}, u32[]{:S(2)}, u32[]{:S(2)}) collective-permute-start(bf16[48,512]{1,0:T(8,128)(2,1)S(1)} %collective-permute-done.mine_ref), channel_id=1, source_target_pairs={{0,1},{1,0},{2,3},{3,2},{4,5},{5,4},{6,7},{7,6},{8,9},{9,8},{10,11... | collective-permute-start | bytes 147464 | tf_op jit(solution)/shard_map/ppermute | solution.py:307
  9.1 4.5 %collective-permute-start.4 = (bf16[80,256]{1,0:T(8,128)(2,1)S(1)}, bf16[80,256]{1,0:T(8,128)(2,1)S(1)}, u32[]{:S(2)}, u32[]{:S(2)}) collective-permute-start(bf16[80,256]{1,0:T(8,128)(2,1)S(1)} %get-tuple-element.25), channel_id=1, source_target_pairs={{0,7},{1,6},{2,5},{3,4},{4,3},{5,2},{6,1},{7,0},{8,15},{9,14},{10,... | collective-permute-start | bytes 122888 | tf_op jit(solution)/shard_map/ppermute | solution.py:315
  11.7 3.4 %collective-permute-start.5 = (bf16[80,256]{1,0:T(8,128)(2,1)S(1)}, bf16[80,256]{1,0:T(8,128)(2,1)S(1)}, u32[]{:S(2)}, u32[]{:S(2)}) collective-permute-start(bf16[80,256]{1,0:T(8,128)(2,1)S(1)} %get-tuple-element.26), channel_id=1, source_target_pairs={{0,3},{1,2},{2,1},{3,0},{4,7},{5,6},{6,5},{7,4},{8,11},{9,10},{10,... | collective-permute-start | bytes 122888 | tf_op jit(solution)/shard_map/ppermute | solution.py:315
  12.2 3.5 %collective-permute-start.6 = (bf16[80,256]{1,0:T(8,128)(2,1)S(1)}, bf16[80,256]{1,0:T(8,128)(2,1)S(1)}, u32[]{:S(2)}, u32[]{:S(2)}) collective-permute-start(bf16[80,256]{1,0:T(8,128)(2,1)S(1)} %get-tuple-element.27), channel_id=1, source_target_pairs={{0,5},{1,4},{2,7},{3,6},{4,1},{5,0},{6,3},{7,2},{8,13},{9,12},{10,... | collective-permute-start | bytes 122888 | tf_op jit(solution)/shard_map/ppermute | solution.py:315
  12.3 3.4 %collective-permute-start.7 = (bf16[80,256]{1,0:T(8,128)(2,1)S(1)}, bf16[80,256]{1,0:T(8,128)(2,1)S(1)}, u32[]{:S(2)}, u32[]{:S(2)}) collective-permute-start(bf16[80,256]{1,0:T(8,128)(2,1)S(1)} %get-tuple-element.28), channel_id=1, source_target_pairs={{0,1},{1,0},{2,3},{3,2},{4,5},{5,4},{6,7},{7,6},{8,9},{9,8},{10,11... | collective-permute-start | bytes 122888 | tf_op jit(solution)/shard_map/ppermute | solution.py:315
